TPU v7x, 32 devices: a whole 2x2x4 slice. The times are simulated.
32 devices in a mesh: scene: 1, space: 32 (over z, y, x, core).
Axes of the slice: x: 2, y: 2, z: 4, core: 2. Of those that a mesh axis runs over, the one named last changes fastest.
Arguments:
- feats: bfloat16 [16384, 256], P(('scene', 'space')), may hold values from -6 to 6
- pre_act: bfloat16 [16384, 256], P(('scene', 'space')), may hold values from -6 to 6
- coarse_grad: bfloat16 [4096, 512], P(('scene', 'space')), may hold values from -12 to 12
- w_sub: bfloat16 [6912, 256], replicated, may hold values from -0.078125 to 0.078125
- w_down: bfloat16 [2048, 512], replicated, may hold values from -0.125 to 0.125
- pair_src: int32 [32, 27, 8], P(('scene', 'space')), may hold values from 0 to 3, as said below
- pair_tgt: int32 [32, 27, 8], P(('scene', 'space')), may hold values from 0 to 7, as said below
- pair_rows: int32 [32, 27, 8, 128], P(('scene', 'space')), may hold values from 0 to 128, as said below
- down_rows: int32 [32, 8, 128], P(('scene', 'space')), may hold values from 0 to 512, as said below
- down_parent: int32 [32, 8, 128], P(('scene', 'space')), may hold values from 0 to 255, as said below
Outputs:
- grad_feats: bfloat16 [16384, 256], P(('scene', 'space'))
- sub_grads: float32 [1769472], P(('scene', 'space'))
- down_grads: float32 [2048, 512], P(('scene', 'space'))
Inputs may be any that keep to these rules, and one draw needn't show every extreme that they name: `pair_src`: source block of each slot among the device's own blocks; at every offset each block of a device is the source of at least one slot. `pair_tgt`: target block among the device's blocks extended by 2 blocks of the previous device in front and 2 of the next device behind (index 2 is its own first block); on every device and offset some slot names 0 and some slot names 7. `pair_rows`: for each row of the source block, the row of the target block that it is paired with, 128 for none; for one device, offset and source block the rows that are not 128 are disjoint between slots. `down_rows`: the device's fine rows of each child offset in no order, 512 marking an empty slot; every fine row of a device stands in exactly one of its lists, and on every device one list is full. `down_parent`: parent row among the device's coarse rows extended in front by the last coarse block of the previous device (indices below 128 are that block); any valid value in an empty slot.
All inputs are finite; a program needn't handle non-finite values.
Results may differ from a plain program's by a relative error of at most 0.0049.
Values may be sent and summed in bfloat16 or wider, within the bound.
No kernel may reach another device: no remote copies, remote signals or barrier semaphores. Data moves between devices by JAX's collectives and lax.ppermute only.
A program may use at most 128 MiB of HBM per device.

v0:
```python
import math

import jax
import jax.numpy as jnp
from jax import lax
from jax.sharding import PartitionSpec as P

HB = 2


def shifted(shard, axis, by):
    peers = lax.axis_size(axis)
    pairs = [(i, i + by) for i in range(peers) if 0 <= i + by < peers]
    return lax.ppermute(shard, axis, pairs)


def padded(shard, sides, width):
    for axis, dim in sides:
        peers, length = (lax.axis_size(axis), shard.shape[dim])
        up = [(i, (i + 1) % peers) for i in range(peers - 1)]
        down = [(j, i) for i, j in up]
        last = lax.slice_in_dim(shard, length - width, length, axis=dim)
        first = lax.slice_in_dim(shard, 0, width, axis=dim)
        before = lax.ppermute(last, axis, up)
        after = lax.ppermute(first, axis, down)
        shard = jnp.concatenate([before, shard, after], axis=dim)
    return shard


def slot_pieces(ext_blocks, targets, tables):
    block_count = ext_blocks.shape[0]
    block_rows = ext_blocks.shape[1]
    block_pick = (targets[:, None] == jnp.arange(block_count)[None, :]).astype(jnp.bfloat16)
    chosen = jnp.einsum(
        "pe,erc->prc", block_pick, ext_blocks, preferred_element_type=jnp.float32
    ).astype(jnp.bfloat16)
    row_pick = (tables[:, :, None] == jnp.arange(block_rows)[None, None, :]).astype(jnp.bfloat16)
    return jnp.einsum("prj,pjc->prc", row_pick, chosen, preferred_element_type=jnp.float32).astype(
        jnp.bfloat16
    )


def per_device(
    feats,
    pre_act,
    coarse_grad,
    w_sub,
    w_down,
    pair_src,
    pair_tgt,
    pair_rows,
    down_rows,
    down_parent,
):
    row_count = feats.shape[0]
    block_rows = pair_rows.shape[-1]
    nblocks = row_count // block_rows
    channels = feats.shape[1]
    out_width = coarse_grad.shape[1]
    kernel = pair_src.shape[1]
    children = down_rows.shape[1]
    grad_scale = 1.0 / math.sqrt(lax.axis_size("space") * row_count)
    previous = shifted(coarse_grad, "space", 1)
    coarse_ext = jnp.concatenate([previous, coarse_grad], 0)
    parent_pick = (
        down_parent[0][:, :, None] == jnp.arange(coarse_ext.shape[0])[None, None, :]
    ).astype(jnp.bfloat16)
    gathered = jnp.einsum(
        "cjq,qd->cjd", parent_pick, coarse_ext, preferred_element_type=jnp.float32
    ).astype(jnp.bfloat16)
    row_pick = (down_rows[0][:, :, None] == jnp.arange(row_count)[None, None, :]).astype(
        jnp.bfloat16
    )
    fine_parents = jnp.einsum(
        "cji,cjd->cid", row_pick, gathered, preferred_element_type=jnp.float32
    ).astype(jnp.bfloat16)
    w_children = w_down.reshape(children, channels, out_width)
    grad_out = jnp.einsum(
        "cid,cfd->if", fine_parents, w_children, preferred_element_type=jnp.float32
    )
    active = jnp.maximum(pre_act, 0)
    down_term = jnp.einsum("if,cid->cfd", active, fine_parents, preferred_element_type=jnp.float32)
    down_term = down_term.reshape(children * channels, out_width)
    grad_pre = jnp.where(pre_act > 0, grad_out, 0.0).astype(jnp.bfloat16)
    down_sum = lax.psum_scatter(down_term, "space", scatter_dimension=0, tiled=True)
    halo_rows = padded(grad_pre, (("space", 0),), HB * block_rows)
    ext_blocks = halo_rows.reshape(-1, block_rows, channels)
    w_kernel = w_sub.reshape(kernel, channels, channels)
    owners = pair_src[0][:, None, :] == jnp.arange(nblocks)[None, :, None]

    def offset_sum(inputs):
        targets, tables, owner_mask = inputs
        pieces = slot_pieces(ext_blocks, targets, tables)
        merged = jnp.einsum(
            "np,prf->nrf",
            owner_mask.astype(jnp.bfloat16),
            pieces,
            preferred_element_type=jnp.float32,
        )
        return merged.astype(jnp.bfloat16).reshape(row_count, channels)

    columns = lax.map(offset_sum, (pair_tgt[0], pair_rows[0], owners))
    grad_in = jnp.einsum("krf,kif->ri", columns, w_kernel, preferred_element_type=jnp.float32)
    sub_term = jnp.einsum("ri,krf->kif", feats, columns, preferred_element_type=jnp.float32)
    sub_term = sub_term.reshape(kernel * channels * channels)
    sub_sum = lax.psum_scatter(sub_term, "space", scatter_dimension=0, tiled=True)
    return (grad_in.astype(jnp.bfloat16), sub_sum * grad_scale, down_sum * grad_scale)


def solution(mesh):
    placed = (
        P(("scene", "space"), None),
        P(("scene", "space"), None),
        P(("scene", "space"), None),
        P(),
        P(),
        P(("scene", "space"), None, None),
        P(("scene", "space"), None, None),
        P(("scene", "space"), None, None, None),
        P(("scene", "space"), None, None),
        P(("scene", "space"), None, None),
    )
    return jax.shard_map(
        per_device,
        mesh=mesh,
        in_specs=placed,
        out_specs=(P(("scene", "space"), None), P(("scene", "space")), P(("scene", "space"), None)),
        check_vma=False,
    )
```

profile of v0, /device:TPU:0, one launch (start us, length us, event | category | flops | bytes accessed | tf_op | source)
XLA Modules:
  0.0 513.9 jit_solution(14181154073759063515)
XLA Ops:
  7.2 3.3 collective-permute-start
  11.3 1.4 copy.27
  12.7 4.6 convolution_convert_fusion.3
  17.2 4.1 fusion.11
  21.4 4.0 collective-permute-start.1
  25.3 1.3 collective-permute-start.2
  27.3 3.3 collective-permute-done.2
  30.6 1.1 copy.28
  31.6 133.8 %while.10 = (s32[]{:T(128)}, bf16[27,512,256]{2,1,0:T(8,128)(2,1)}, pred[27,4,8]{2,1,0:T(4,128)(4,1)}, s32[27,8,128]{2,1,0:T(8,128)}, s32[27,8]{1,0:T(8,128)}, /*index=5*/bf16[8,128,256]{2,0,1:T(8,128)(2,1)}, s32[]{:T(128)}) while((s32[]{:T(128)}, bf16[27,512,256]{2,1,0:T(8,128)(2,1)}, pred[27,4,8]{2,1,0:T(4,128)(4,1)}, ...), condition=%wide.region_1.2_spmd, body=%wide.region_0.1_spmd.sunk | while | flops 74186816 | bytes 3945157 | solution.py:102
  33.0 1.4 convolution_convert_fusion.8
  34.8 1.1 convolution_convert_fusion.10
  38.0 1.4 convolution_convert_fusion.8
  39.7 1.1 convolution_convert_fusion.10
  42.9 1.4 convolution_convert_fusion.8
  44.7 1.1 convolution_convert_fusion.10
  47.9 1.4 convolution_convert_fusion.8
  49.6 1.1 convolution_convert_fusion.10
  52.8 1.4 convolution_convert_fusion.8
  54.6 1.1 convolution_convert_fusion.10
  57.8 1.4 convolution_convert_fusion.8
  59.5 1.1 convolution_convert_fusion.10
  62.8 1.4 convolution_convert_fusion.8
  64.5 1.1 convolution_convert_fusion.10
  67.7 1.4 convolution_convert_fusion.8
  69.5 1.1 convolution_convert_fusion.10
  72.7 1.4 convolution_convert_fusion.8
  74.4 1.1 convolution_convert_fusion.10
  77.6 1.4 convolution_convert_fusion.8
  79.4 1.1 convolution_convert_fusion.10
  82.6 1.4 convolution_convert_fusion.8
  84.3 1.1 convolution_convert_fusion.10
  87.6 1.4 convolution_convert_fusion.8
  89.3 1.1 convolution_convert_fusion.10
  92.5 1.4 convolution_convert_fusion.8
  94.3 1.1 convolution_convert_fusion.10
  97.5 1.4 convolution_convert_fusion.8
  102.4 1.4 convolution_convert_fusion.8
  107.4 1.4 convolution_convert_fusion.8
  112.3 1.4 convolution_convert_fusion.8
  117.3 1.4 convolution_convert_fusion.8
  122.2 1.4 convolution_convert_fusion.8
  127.2 1.4 convolution_convert_fusion.8
  132.1 1.4 convolution_convert_fusion.8
  133.9 1.1 convolution_convert_fusion.10
  137.1 1.4 convolution_convert_fusion.8
  138.8 1.1 convolution_convert_fusion.10
  142.1 1.4 convolution_convert_fusion.8
  143.8 1.1 convolution_convert_fusion.10
  147.0 1.4 convolution_convert_fusion.8
  148.8 1.1 convolution_convert_fusion.10
  152.0 1.4 convolution_convert_fusion.8
  153.7 1.1 convolution_convert_fusion.10
  156.9 1.4 convolution_convert_fusion.8
  161.9 1.4 convolution_convert_fusion.8
  163.6 1.1 convolution_convert_fusion.10
  165.5 8.0 %convolution_bitcast_fusion = f32[27,256,256]{1,2,0:T(8,128)} fusion(bf16[27,512,256]{2,1,0:T(8,128)(2,1)} %get-tuple-element.35, bf16[512,256]{1,0:T(8,128)(2,1)} %param.12), kind=kOutput, calls=%fused_computation.17 | convolution fusion | flops 1811939328 | bytes 14417920 | tf_op jit(solution)/shard_map/ri,krf->kif/dot_general | solution.py:104
  173.4 8.0 %copy.30 = f32[27,256,256]{2,1,0:T(8,128)} copy(f32[27,256,256]{1,2,0:T(8,128)} %convolution_bitcast_fusion) | data formatting | bytes 14155776 | tf_op jit(solution)/shard_map/ri,krf->kif/transpose | solution.py:104
  181.4 9.6 %copy.35 = f32[864,2,8,128]{3,1,2,0:T(2,128)} copy(f32[864,2,8,128]{3,2,1,0:T(8,128)} %bitcast.71) | data formatting | bytes 14155776
  191.2 5.7 %fusion.20 = f32[8,512,256]{1,2,0:T(8,128)} fusion(bf16[8,512,512]{2,1,0:T(8,128)(2,1)} %convolution_convert_fusion.3, bf16[512,256]{1,0:T(8,128)(2,1)} %param.13), kind=kOutput, calls=%fused_computation.33 | convolution fusion | flops 1073872896 | bytes 8650752 | tf_op jit(solution)/shard_map/if,cid->cfd/dot_general | solution.py:82
  196.9 5.7 %fusion.12 = bf16[512,256]{1,0:T(8,128)(2,1)} fusion(bf16[27,512,256]{2,1,0:T(8,128)(2,1)} %get-tuple-element.35, bf16[27,256,256]{2,1,0:T(8,128)(2,1)S(1)} %bitcast.68), kind=kOutput, calls=%fused_computation.25 | convolution fusion | flops 1812070400 | bytes 10878976 | tf_op jit(solution)/shard_map/krf,kif->ri/dot_general | solution.py:103
  202.7 159.4 %all-reduce.3.cloned.1.call-done = f32[1769472]{0:T(1024)} async-done(((f32[1769472]{0:T(1024)}), f32[1769472]{0:T(1024)}) %all-reduce.3.cloned.1.call-update) | async-done | bytes 7077904
  362.0 1.6 dynamic-slice_multiply_fusion
  363.7 141.8 %reduce-scatter.2.cloned.1.call-done = f32[64,512]{1,0:T(8,128)} async-done(((f32[2048,512]{1,0:T(8,128)}), f32[64,512]{1,0:T(8,128)}) %reduce-scatter.2.cloned.1.call-update) | async-done | bytes 131088 | tf_op jit(solution)/shard_map/reduce_scatter | solution.py:85
  505.5 1.6 broadcast_multiply_fusion
  (156 shorter events, 77.3 us)
Async XLA Ops:
  7.2 189.8 %copy-start = (bf16[6912,256]{1,0:T(8,128)(2,1)S(1)}, bf16[6912,256]{1,0:T(8,128)(2,1)}, u32[]{:S(2)}) copy-start(bf16[6912,256]{1,0:T(8,128)(2,1)} %param.15) | copy-start | bytes 10616836
  7.2 354.9 %all-reduce.3.cloned.1.call-start = ((), (), s32[]{:S(2)}) async-start(), calls=%async_computation.2 | async-start | bytes 14155776
  7.2 5.4 %collective-permute-start = (bf16[128,512]{1,0:T(8,128)(2,1)}, bf16[128,512]{1,0:T(8,128)(2,1)}, u32[]{:S(2)}, u32[]{:S(2)}) collective-permute-start(bf16[128,512]{1,0:T(8,128)(2,1)} %param.14), channel_id=1, source_target_pairs={{0,1},{1,2},{2,3},{3,4},{4,5},{5,6},{6,7},{7,8},{8,9},{9,10},{10,1... | collective-permute-start | bytes 393224 | tf_op jit(solution)/shard_map/ppermute | solution.py:14
  21.4 5.9 %collective-permute-start.1 = (bf16[256,256]{1,0:T(8,128)(2,1)S(1)}, bf16[256,256]{1,0:T(8,128)(2,1)S(1)}, u32[]{:S(2)}, u32[]{:S(2)}) collective-permute-start(bf16[256,256]{1,0:T(8,128)(2,1)S(1)} %get-tuple-element.54), channel_id=1, source_target_pairs={{0,1},{1,2},{2,3},{3,4},{4,5},{5,6},{6,7},{7,8},{8,9},{9,10},{10,1... | collective-permute-start | bytes 393224 | tf_op jit(solution)/shard_map/ppermute | solution.py:24
  25.3 5.2 %collective-permute-start.2 = (bf16[256,256]{1,0:T(8,128)(2,1)S(1)}, bf16[256,256]{1,0:T(8,128)(2,1)S(1)}, u32[]{:S(2)}, u32[]{:S(2)}) collective-permute-start(bf16[256,256]{1,0:T(8,128)(2,1)S(1)} %get-tuple-element.55), channel_id=1, source_target_pairs={{1,0},{2,1},{3,2},{4,3},{5,4},{6,5},{7,6},{8,7},{9,8},{10,9},{11,1... | collective-permute-start | bytes 393224 | tf_op jit(solution)/shard_map/ppermute | solution.py:25
  191.0 314.5 %reduce-scatter.2.cloned.1.call-start = ((), (), s32[]{:S(2)}) async-start(), calls=%async_computation.1 | async-start | bytes 4325376 | tf_op jit(solution)/shard_map/reduce_scatter | solution.py:85
Sparse Core Ops, SparseCore 0:
  191.1 170.8 all-reduce.2
  364.4 141.0 reduce-scatter.1
where the time goes:
time: 518 us; the launch traced here: 514 us
  waiting for transfers between devices  305 us (59%)
  matrix products  104 us (20%)
  local copies, waits for them, and re-layouts  78.3 us (15%)
  between operations  14.1 us (3%)
  starting transfers between devices  8.79 us (2%)
    unnamed x3, waiting for transfers between devices  159 us
    reduce_scatter x1, waiting for transfers between devices, per_device(): lax.psum_scatter(down_term, 'space', scatter_dimension=0, tiled=True)  142 us
    dot_general x27, matrix products, slot_pieces(): jnp.einsum('pe,erc->prc', block_pick, ext_blocks, preferred_element_type=...  37.5 us
    dot_general x27, matrix products, offset_sum(): jnp.einsum('np,prf->nrf', owner_mask.astype(jnp.bfloat16), pieces, prefer...  28.7 us
    dynamic_update_slice x27, local copies, waits for them, and re-layouts, per_device(): columns = lax.map(offset_sum, (pair_tgt[0], pair_rows[0], owners))  19.6 us
    eq x27, local copies, waits for them, and re-layouts, slot_pieces(): targets[:, None] == jnp.arange(block_count)[None, :]  18.7 us
    eq x27, local copies, waits for them, and re-layouts, slot_pieces(): tables[:, :, None] == jnp.arange(block_rows)[None, None, :]  18.6 us
    unnamed x4, local copies, waits for them, and re-layouts  10.9 us
  transfers between devices with their start and end apart: 5, of which 3 were waited for; matrix products, arithmetic and copies ran while one was open for 3% of the time, Pallas kernels for 0%

commit v1 on v0

v1 whole, which is shorter than its diff:
```python
import functools
import math

import jax
import jax.numpy as jnp
from jax import lax
from jax.experimental import pallas as pl
from jax.experimental.pallas import tpu as pltpu
from jax.sharding import PartitionSpec as P

HB = 2
BF = jnp.bfloat16
F32 = jnp.float32


def dot(a, b):
    return lax.dot_general(a, b, (((1,), (0,)), ((), ())), preferred_element_type=F32)


def dot_nt(a, b):
    return lax.dot_general(a, b, (((1,), (1,)), ((), ())), preferred_element_type=F32)


def one_hot(index, shape, axis):
    return jnp.where(index == lax.broadcasted_iota(jnp.int32, shape, axis), 1.0, 0.0).astype(BF)


def cost(flops, nbytes):
    return pl.CostEstimate(flops=flops, bytes_accessed=nbytes, transcendentals=0)


def down_grad_kernel(prev, cur, par_t, rows, pre, w, gpre, gath, contrib, pick):
    children, slots = rows.shape
    count, channels = pre.shape
    ext = jnp.concatenate([prev[...], cur[...]], 0)
    for c in range(children):
        mine = pl.ds(c * slots, slots)
        parents = one_hot(par_t[:, c : c + 1], (slots, ext.shape[0]), 1)
        got = dot(parents, ext).astype(BF)
        gath[mine, :] = got
        contrib[mine, :] = dot_nt(got, w[pl.ds(c * channels, channels), :]).astype(BF)
        pick[:, mine] = one_hot(rows[c : c + 1, :], (count, slots), 0)
    grad = dot(pick[...], contrib[...])
    gpre[...] = jnp.where(pre[...].astype(F32) > 0, grad, 0.0).astype(BF)


def down_grad(prev, cur, par_t, rows, pre, w):
    children, slots = rows.shape
    count, channels = pre.shape
    width = cur.shape[1]
    return pl.pallas_call(
        down_grad_kernel,
        out_shape=(
            jax.ShapeDtypeStruct((count, channels), BF),
            jax.ShapeDtypeStruct((children * slots, width), BF),
        ),
        scratch_shapes=[
            pltpu.VMEM((children * slots, channels), BF),
            pltpu.VMEM((count, children * slots), BF),
        ],
        compiler_params=pltpu.CompilerParams(vmem_limit_bytes=24 << 20),
        cost_estimate=cost(1 << 30, 4 << 20),
        name="down_grad",
    )(prev, cur, par_t, rows, pre, w)


def down_weight_kernel(act_t, rows, gath, out):
    children, slots = rows.shape
    channels, count = act_t.shape
    for c in range(children):
        pick = one_hot(rows[c : c + 1, :], (count, slots), 0)
        chosen = dot(act_t[...], pick).astype(BF)
        out[pl.ds(c * channels, channels), :] = dot(chosen, gath[pl.ds(c * slots, slots), :])


def down_weight(act_t, rows, gath):
    channels = act_t.shape[0]
    children = rows.shape[0]
    width = gath.shape[1]
    return pl.pallas_call(
        down_weight_kernel,
        out_shape=jax.ShapeDtypeStruct((children * channels, width), F32),
        compiler_params=pltpu.CompilerParams(vmem_limit_bytes=24 << 20),
        cost_estimate=cost(1 << 30, 6 << 20),
        name="down_weight",
    )(act_t, rows, gath)


def conv_plan(kernel, channels, quarters):
    quarter = kernel * channels // 4
    plan, out = [], 0
    for q in quarters:
        row = q * quarter
        while row < (q + 1) * quarter:
            k, first = divmod(row, channels)
            last = min(channels, (q + 1) * quarter - k * channels)
            plan.append((k, first, last, out))
            out += last - first
            row += last - first
    return plan


def conv_kernel(plan, slots, final, *refs):
    src, tgt, tab, ext, feats_t, w, *rest = refs
    if final:
        before, *rest = rest
    grad, sub, wbuf, acc, col0, col1, sems = rest
    rows = tab.shape[0]
    cols = (col0, col1)
    channels = ext.shape[2]
    count = feats_t.shape[1]
    steps = len(plan)
    copies = []
    for at, (k, first, last, out) in enumerate(plan):
        if first == 0:
            copy = pltpu.make_async_copy(
                w.at[pl.ds(k * channels, channels), :], wbuf.at[at], sems.at[at]
            )
            copy.start()
            copies.append(copy)
        else:
            copies.append(None)
    if final:
        acc[...] = before[...]
    else:
        acc[...] = jnp.zeros_like(acc)

    def gather(k, col):
        col[...] = jnp.zeros_like(col)
        for p in range(slots):
            q = k * slots + p
            pick = one_hot(tab[:, q : q + 1], (rows, rows), 1)
            piece = dot(pick, ext[tgt[q]]).astype(BF)
            owner = src[q]
            col[owner] = col[owner] + piece

    gather(plan[0][0], cols[0])
    for at, (k, first, last, out) in enumerate(plan):
        if at + 1 < steps:
            gather(plan[at + 1][0], cols[(at + 1) % 2])
        column = cols[at % 2][...].reshape(count, channels)
        sub[pl.ds(out, last - first), :] = dot(feats_t[pl.ds(first, last - first), :], column)
        if copies[at] is not None:
            copies[at].wait()
            acc[...] += dot_nt(column, wbuf[at])
    grad[...] = acc[...].astype(grad.dtype)


def conv(src, tgt, tab, ext, feats_t, w, quarters, slots, before=None):
    channels, count = feats_t.shape
    kernel = w.shape[0] // channels
    plan = conv_plan(kernel, channels, quarters)
    final = before is not None
    smem = pl.BlockSpec(memory_space=pltpu.SMEM)
    vmem = pl.BlockSpec(memory_space=pltpu.VMEM)
    block = ext.shape[1:]
    return pl.pallas_call(
        functools.partial(conv_kernel, plan, slots, final),
        out_shape=(
            jax.ShapeDtypeStruct((count, channels), BF if final else F32),
            jax.ShapeDtypeStruct((len(quarters) * kernel * channels // 4, channels), F32),
        ),
        in_specs=[smem, smem, vmem, vmem, vmem, pl.BlockSpec(memory_space=pl.ANY)]
        + [vmem] * final,
        out_specs=(vmem, vmem),
        scratch_shapes=[
            pltpu.VMEM((len(plan), channels, channels), BF),
            pltpu.VMEM((count, channels), F32),
            pltpu.VMEM((count // block[0],) + block, BF),
            pltpu.VMEM((count // block[0],) + block, BF),
            pltpu.SemaphoreType.DMA((len(plan),)),
        ],
        compiler_params=pltpu.CompilerParams(vmem_limit_bytes=32 << 20),
        cost_estimate=cost(8 << 30, 8 << 20),
        name="conv",
    )(src, tgt, tab, ext, feats_t, w, *([before] if final else []))


def moved(x, peers, to):
    pairs = [(i, to(i)) for i in range(peers)]
    return lax.ppermute(x, "space", [(i, j) for i, j in pairs if j is not None and 0 <= j < peers])


def at_digit(x, digit):
    return lax.dynamic_index_in_dim(x, digit, axis=1, keepdims=False)


def fold(x, me, peers, radix, stride):
    digit = me // stride % radix
    total = at_digit(x, digit).astype(F32)
    for d in range(1, radix):
        sent = at_digit(x, digit ^ d).astype(BF)
        total = total + moved(sent, peers, lambda i: i ^ (d * stride)).astype(F32)
    return total


def fold_low(x, me, peers, high, rows, width):
    stride = 1
    low = peers // 4
    while stride < low:
        radix = 2 if (low // stride).bit_length() % 2 == 0 else 4
        x = fold(x.reshape(-1, radix, rows, width), me, peers, radix, stride)
        stride *= radix
    return x.reshape(high, rows, width)


def fold_top(x, me, peers, quarters):
    stride = peers // 4
    digit = me // stride
    place = (lambda g: g) if len(quarters) == 4 else (lambda g: g // 2)
    pick = lambda g: lax.dynamic_index_in_dim(x, place(g), axis=0, keepdims=False)
    total = pick(digit).astype(F32)
    for d in range(1, 4):
        to = lambda i: (i ^ (d * stride)) if (i // stride) ^ d in quarters else None
        total = total + moved(pick(digit ^ d).astype(BF), peers, to).astype(F32)
    return total


def per_device(
    feats,
    pre_act,
    coarse_grad,
    w_sub,
    w_down,
    pair_src,
    pair_tgt,
    pair_rows,
    down_rows,
    down_parent,
):
    peers = lax.axis_size("space")
    me = lax.axis_index("space")
    row_count, channels = feats.shape
    block_rows = pair_rows.shape[-1]
    out_width = coarse_grad.shape[1]
    kernel, slots = pair_src.shape[1:]
    children = down_rows.shape[1]
    scale = 1.0 / math.sqrt(peers * row_count)

    previous = moved(coarse_grad[-block_rows:], peers, lambda i: i + 1)
    feats_t = feats.T
    act_t = jnp.maximum(pre_act, 0).T
    tab = pair_rows[0].reshape(kernel * slots, block_rows).T
    src = pair_src[0].reshape(-1)
    tgt = pair_tgt[0].reshape(-1)

    grad_pre, gathered = down_grad(
        previous, coarse_grad, down_parent[0].T, down_rows[0], pre_act, w_down
    )
    halo = HB * block_rows
    before = moved(grad_pre[-halo:], peers, lambda i: i + 1)
    after = moved(grad_pre[:halo], peers, lambda i: i - 1)
    down_term = down_weight(act_t, down_rows[0], gathered)
    ext = jnp.concatenate([before, grad_pre, after], 0).reshape(-1, block_rows, channels)

    down_rows_own = children * channels // peers
    down = fold_low(down_term, me, peers, 4, down_rows_own, out_width)
    down_sum = fold_top(down, me, peers, (0, 1, 2, 3))

    sub_rows_own = kernel * channels // peers
    outer, inner = (0, 3), (1, 2)
    partial, sub_outer = conv(src, tgt, tab, ext, feats_t, w_sub, outer, slots)
    grad_in, sub_inner = conv(src, tgt, tab, ext, feats_t, w_sub, inner, slots, partial)
    sums = [
        fold_top(fold_low(x, me, peers, 2, sub_rows_own, channels), me, peers, quarters)
        for x, quarters in ((sub_outer, outer), (sub_inner, inner))
    ]
    digit = me // (peers // 4)
    sub_sum = jnp.where((digit == 0) | (digit == 3), sums[0], sums[1])
    return (grad_in, sub_sum.reshape(-1) * scale, down_sum * scale)


def solution(mesh):
    rows = ("scene", "space")
    placed = (
        P(rows, None),
        P(rows, None),
        P(rows, None),
        P(),
        P(),
        P(rows, None, None),
        P(rows, None, None),
        P(rows, None, None, None),
        P(rows, None, None),
        P(rows, None, None),
    )
    return jax.shard_map(
        per_device,
        mesh=mesh,
        in_specs=placed,
        out_specs=(P(rows, None), P(rows), P(rows, None)),
        check_vma=False,
    )
```

time: 518 us -> 119 us (0.23)
  waiting for transfers between devices: 305 us -> 12.5 us
  matrix products: 104 us -> 0 us
  local copies, waits for them, and re-layouts: 78.3 us -> 21.8 us
  starting transfers between devices: 8.79 us -> 51.2 us
  Pallas kernels: 0 us -> 24.8 us
  between operations: 14.1 us -> 1.02 us
    unnamed x3 -> x0, waiting for transfers between devices: 159 us -> none
    reduce_scatter x1 -> x0, waiting for transfers between devices: 142 us -> none  [per_device(): lax.psum_scatter(down_term, 'space', scatter_dimension=0, tiled=True)]
    dot_general x86 -> x0, matrix products: 104 us -> none  [the longest x27 37.5 us: slot_pieces(): jnp.einsum('pe,erc->prc', block_pick, ext_blocks, preferred_element_type=...]
    ppermute x3 -> x24, starting transfers between devices: 8.53 us -> 51.2 us  [moved(): lax.ppermute(x, 'space', [(i, j) for i, j in pairs if j is not None and 0...]
    eq x55 -> x0, local copies, waits for them, and re-layouts: 38 us -> none  [the longest x27 18.7 us: slot_pieces(): targets[:, None] == jnp.arange(block_count)[None, :]]
    pallas_call x0 -> x4, Pallas kernels: none -> 24.8 us  [the longest x2 21.5 us: conv(): pl.pallas_call(functools.partial(conv_kernel, plan, slots, final), out_sh...]
    dynamic_update_slice x27 -> x0, local copies, waits for them, and re-layouts: 19.6 us -> none  [per_device(): columns = lax.map(offset_sum, (pair_tgt[0], pair_rows[0], owners))]
    ppermute x3 -> x24, waiting for transfers between devices: 3.27 us -> 12.5 us  [moved(): lax.ppermute(x, 'space', [(i, j) for i, j in pairs if j is not None and 0...]
  transfers between devices with their start and end apart: 5 -> 24, of which waited for: 3 -> 5; matrix products, arithmetic and copies ran while one was open for 3% -> 11% of each run, Pallas kernels for 0% -> 11%
where the time goes in v1:
time: 119 us
  starting transfers between devices  51.2 us (43%)
  Pallas kernels  24.8 us (21%)
  local copies, waits for them, and re-layouts  21.8 us (18%)
  waiting for transfers between devices  12.5 us (11%)
  other arithmetic  7.17 us (6%)
    ppermute x24, starting transfers between devices, moved(): lax.ppermute(x, 'space', [(i, j) for i, j in pairs if j is not None and 0...  51.2 us
    pallas_call x2, Pallas kernels, conv(): pl.pallas_call(functools.partial(conv_kernel, plan, slots, final), out_sh...  21.5 us
    unnamed x50, local copies, waits for them, and re-layouts  17.2 us
    ppermute x24, waiting for transfers between devices, moved(): lax.ppermute(x, 'space', [(i, j) for i, j in pairs if j is not None and 0...  12.5 us
    add x6, other arithmetic, fold(): total = total + moved(sent, peers, lambda i: i ^ d * stride).astype(F32)  5.36 us
    convert_element_type x6, local copies, waits for them, and re-layouts, fold(): sent = at_digit(x, digit ^ d).astype(BF)  3.55 us
  transfers between devices with their start and end apart: 24, of which 5 were waited for; matrix products, arithmetic and copies ran while one was open for 11% of the time, Pallas kernels for 11%

profile of v1, /device:TPU:0, one launch (start us, length us, event | category | flops | bytes accessed | tf_op | source)
XLA Modules:
  0.0 118.6 jit_solution(2586113771891858994)
XLA Ops:
  0.6 2.4 %collective-permute-start = (bf16[128,512]{1,0:T(8,128)(2,1)}, bf16[128,512]{1,0:T(8,128)(2,1)S(1)}, u32[]{:S(2)}, u32[]{:S(2)}) collective-permute-start(bf16[128,512]{1,0:T(8,128)(2,1)} %cur.1), channel_id=1, source_target_pairs={{0,1},{1,2},{2,3},{3,4},{4,5},{5,6},{6,7},{7,8},{8,9},{9,10},{10,1... | collective-permute-start | bytes 393224 | tf_op jit(solution)/shard_map/ppermute | solution.py:181
  3.0 1.4 %copy.25 = s32[1,8,128]{1,2,0:T(8,128)} copy(s32[1,8,128]{2,1,0:T(8,128)} %param.19) | data formatting | bytes 8192 | tf_op args[9]
  4.4 0.7 copy-done.15
  5.1 0.9 copy-done.6
  6.0 0.8 copy-done.9
  6.9 0.7 copy-done.10
  7.6 1.6 %copy-done.13 = bf16[2048,512]{1,0:T(8,128)(2,1)S(1)} copy-done((bf16[2048,512]{1,0:T(8,128)(2,1)S(1)}, bf16[2048,512]{1,0:T(8,128)(2,1)}, u32[]{:S(2)}) %copy-start.13) | copy-done | bytes 2097176
  9.2 0.9 copy-done.14
  10.1 0.9 copy-done.16
  11.0 1.4 %down_grad.1 = (bf16[512,256]{1,0:T(8,128)(2,1)S(1)}, bf16[1024,512]{1,0:T(8,128)(2,1)S(1)}) custom-call(bf16[128,512]{1,0:T(8,128)(2,1)S(1)} %copy-done.16, bf16[128,512]{1,0:T(8,128)(2,1)S(1)} %copy-done.14, s32[128,8]{1,0:T(8,128)S(1)} %bitcast.157, s32[8,128]{1,0:T(8,128)S(1)} %bitcast.158, bf16[512,256]{1,0:T(8,128)(2,1)S(1)} %copy-done.6, ...), custom_call_target="tpu_custom_call" | custom-call | flops 1073741824 | bytes 4194304 | tf_op jit(solution)/shard_map/down_grad/pallas_call | solution.py:51
  12.4 0.7 copy-done.3
  13.1 5.3 %collective-permute-start.1 = (bf16[256,256]{1,0:T(8,128)(2,1)S(1)}, bf16[256,256]{1,0:T(8,128)(2,1)S(1)}, u32[]{:S(2)}, u32[]{:S(2)}) collective-permute-start(bf16[256,256]{1,0:T(8,128)(2,1)S(1)} %get-tuple-element.33), channel_id=1, source_target_pairs={{0,1},{1,2},{2,3},{3,4},{4,5},{5,6},{6,7},{7,8},{8,9},{9,10},{10,1... | collective-permute-start | bytes 393224 | tf_op jit(solution)/shard_map/ppermute | solution.py:181
  18.5 1.3 %collective-permute-start.2 = (bf16[256,256]{1,0:T(8,128)(2,1)S(1)}, bf16[256,256]{1,0:T(8,128)(2,1)S(1)}, u32[]{:S(2)}, u32[]{:S(2)}) collective-permute-start(bf16[256,256]{1,0:T(8,128)(2,1)S(1)} %get-tuple-element.34), channel_id=1, source_target_pairs={{1,0},{2,1},{3,2},{4,3},{5,4},{6,5},{7,6},{8,7},{9,8},{10,9},{11,1... | collective-permute-start | bytes 393224 | tf_op jit(solution)/shard_map/ppermute | solution.py:181
  19.8 0.8 copy.32
  20.6 0.8 copy.26
  21.5 0.8 copy.24
  22.4 0.1 copy.22
  22.6 0.9 collective-permute-done.2
  23.5 1.0 pad_maximum_fusion
  24.5 0.9 copy-done.7
  25.5 0.9 copy-done.8
  26.4 2.0 %copy-done.12 = bf16[6912,256]{1,0:T(8,128)(2,1)S(1)} copy-done((bf16[6912,256]{1,0:T(8,128)(2,1)S(1)}, bf16[6912,256]{1,0:T(8,128)(2,1)}, u32[]{:S(2)}) %copy-start.12) | copy-done | bytes 3538968
  28.4 9.9 %conv.2 = (f32[512,256]{1,0:T(8,128)S(1)}, f32[3456,256]{1,0:T(8,128)S(1)}) custom-call(s32[216]{0:T(256)S(1)} %reshape_squeeze.9.refs_0_, s32[216]{0:T(256)S(1)} %reshape_squeeze.10.refs_1_, s32[128,216]{1,0:T(8,128)S(1)} %bitcast.155, bf16[8,128,256]{2,1,0:T(8,128)(2,1)S(1)} %bitcast.151, bf16[256,512]{1,0:T(8,128)(2,1)S(1)} %bitcast.153, ...), custom_call_target="tpu_custom_call" | custom-call | flops 8589934592 | bytes 8388608 | tf_op jit(solution)/shard_map/conv/pallas_call | solution.py:157
  38.3 1.1 fusion.1
  39.4 3.5 %collective-permute-start.3 = (bf16[8,216,256]{2,1,0:T(8,128)(2,1)}, bf16[8,216,256]{2,1,0:T(8,128)(2,1)}, u32[]{:S(2)}, u32[]{:S(2)}) collective-permute-start(bf16[8,216,256]{2,1,0:T(8,128)(2,1)} %fusion.1), channel_id=1, source_target_pairs={{0,1},{1,0},{2,3},{3,2},{4,5},{5,4},{6,7},{7,6},{8,9},{9,8},{10,11... | collective-permute-start | bytes 2654216 | tf_op jit(solution)/shard_map/ppermute | solution.py:181
  43.0 11.6 %conv.3 = (bf16[512,256]{1,0:T(8,128)(2,1)}, f32[3456,256]{1,0:T(8,128)S(1)}) custom-call(s32[216]{0:T(256)S(1)} %reshape_squeeze.9.refs_0_, s32[216]{0:T(256)S(1)} %reshape_squeeze.10.refs_1_, s32[128,216]{1,0:T(8,128)S(1)} %bitcast.156, bf16[8,128,256]{2,1,0:T(8,128)(2,1)S(1)} %bitcast.152, bf16[256,512]{1,0:T(8,128)(2,1)S(1)} %bitcast.154, ...), custom_call_target="tpu_custom_call" | custom-call | flops 8589934592 | bytes 8388608 | tf_op jit(solution)/shard_map/conv/pallas_call | solution.py:157
  54.6 1.0 fusion.2
  55.6 0.9 collective-permute-start.10
  56.6 1.9 %down_weight.1 = f32[2048,512]{1,0:T(8,128)S(1)} custom-call(bf16[256,512]{1,0:T(8,128)(2,1)S(1)} %maximum_bitcast_fusion.act_t, s32[8,128]{1,0:T(8,128)S(1)} %bitcast.159, bf16[1024,512]{1,0:T(8,128)(2,1)S(1)} %copy-done.5), custom_call_target="tpu_custom_call" | custom-call | flops 1073741824 | bytes 6291456 | tf_op jit(solution)/shard_map/down_weight/pallas_call | solution.py:80
  58.5 2.0 %copy-done = f32[2048,512]{1,0:T(8,128)} copy-done((f32[2048,512]{1,0:T(8,128)}, f32[2048,512]{1,0:T(8,128)S(1)}, u32[]{:S(2)}) %copy-start) | copy-done | bytes 4194328
  60.5 1.1 fusion
  61.6 0.4 collective-permute-start.17
  62.0 1.9 %bitcast_add_fusion.2 = f32[8,216,256]{2,1,0:T(8,128)S(1)} fusion(bf16[8,216,256]{2,1,0:T(8,128)(2,1)} %collective-permute-done.3, f32[8,2,216,256]{3,2,1,0:T(8,128)} %bitcast.150, s32[]{:T(128)S(6)} %select_n.125), kind=kLoop, calls=%fused_computation.3 | loop fusion | flops 884736 | bytes 4423684 | tf_op jit(solution)/shard_map/add | solution.py:193
  64.0 0.1 fusion.13
  64.1 3.4 %collective-permute-start.4 = (bf16[2,216,256]{2,1,0:T(8,128)(2,1)S(1)}, bf16[2,216,256]{2,1,0:T(8,128)(2,1)S(1)}, u32[]{:S(2)}, u32[]{:S(2)}) collective-permute-start(bf16[2,216,256]{2,1,0:T(8,128)(2,1)S(1)} %get-tuple-element.18), channel_id=1, source_target_pairs={{0,2},{1,3},{2,0},{3,1},{4,6},{5,7},{6,4},{7,5},{8,10},{9,11},{10,... | collective-permute-start | bytes 663560 | tf_op jit(solution)/shard_map/ppermute | solution.py:181
  67.5 3.3 %collective-permute-start.5 = (bf16[2,216,256]{2,1,0:T(8,128)(2,1)S(1)}, bf16[2,216,256]{2,1,0:T(8,128)(2,1)S(1)}, u32[]{:S(2)}, u32[]{:S(2)}) collective-permute-start(bf16[2,216,256]{2,1,0:T(8,128)(2,1)S(1)} %get-tuple-element.19), channel_id=1, source_target_pairs={{0,4},{1,5},{2,6},{3,7},{4,0},{5,1},{6,2},{7,3},{8,12},{9,13},{10,... | collective-permute-start | bytes 663560 | tf_op jit(solution)/shard_map/ppermute | solution.py:181
  70.8 1.5 %bitcast_add_fusion.1 = f32[8,216,256]{2,1,0:T(8,128)S(1)} fusion(bf16[8,216,256]{2,1,0:T(8,128)(2,1)} %collective-permute-done.10, f32[8,2,216,256]{3,2,1,0:T(8,128)S(1)} %bitcast.148, s32[]{:T(128)S(6)} %select_n.125), kind=kLoop, calls=%fused_computation.2 | loop fusion | flops 884736 | bytes 4423684 | tf_op jit(solution)/shard_map/add | solution.py:193
  72.3 0.1 fusion.16
  72.4 1.4 %collective-permute-start.11 = (bf16[2,216,256]{2,1,0:T(8,128)(2,1)S(1)}, bf16[2,216,256]{2,1,0:T(8,128)(2,1)S(1)}, u32[]{:S(2)}, u32[]{:S(2)}) collective-permute-start(bf16[2,216,256]{2,1,0:T(8,128)(2,1)S(1)} %get-tuple-element.21), channel_id=1, source_target_pairs={{0,2},{1,3},{2,0},{3,1},{4,6},{5,7},{6,4},{7,5},{8,10},{9,11},{10,... | collective-permute-start | bytes 663560 | tf_op jit(solution)/shard_map/ppermute | solution.py:181
  73.8 2.0 %collective-permute-start.12 = (bf16[2,216,256]{2,1,0:T(8,128)(2,1)S(1)}, bf16[2,216,256]{2,1,0:T(8,128)(2,1)S(1)}, u32[]{:S(2)}, u32[]{:S(2)}) collective-permute-start(bf16[2,216,256]{2,1,0:T(8,128)(2,1)S(1)} %get-tuple-element.23), channel_id=1, source_target_pairs={{0,4},{1,5},{2,6},{3,7},{4,0},{5,1},{6,2},{7,3},{8,12},{9,13},{10,... | collective-permute-start | bytes 663560 | tf_op jit(solution)/shard_map/ppermute | solution.py:181
  75.8 1.6 %bitcast_add_fusion = f32[16,64,512]{2,1,0:T(8,128)S(1)} fusion(bf16[16,64,512]{2,1,0:T(8,128)(2,1)} %collective-permute-done.17, f32[16,2,64,512]{3,2,1,0:T(8,128)S(1)} %bitcast.146, s32[]{:T(128)S(6)} %select_n.125), kind=kLoop, calls=%fused_computation.1 | loop fusion | flops 1048576 | bytes 5242884 | tf_op jit(solution)/shard_map/add | solution.py:193
  77.3 0.1 fusion.10
  77.5 1.0 collective-permute-start.13
  78.5 2.9 %collective-permute-done.5 = bf16[2,216,256]{2,1,0:T(8,128)(2,1)S(1)} collective-permute-done((bf16[2,216,256]{2,1,0:T(8,128)(2,1)S(1)}, bf16[2,216,256]{2,1,0:T(8,128)(2,1)S(1)}, u32[]{:S(2)}, u32[]{:S(2)}) %collective-permute-start.5) | collective-permute-done | bytes 221216 | tf_op jit(solution)/shard_map/ppermute | solution.py:181
  81.4 2.5 %collective-permute-start.19 = (bf16[4,64,512]{2,1,0:T(8,128)(2,1)S(1)}, bf16[4,64,512]{2,1,0:T(8,128)(2,1)S(1)}, u32[]{:S(2)}, u32[]{:S(2)}) collective-permute-start(bf16[4,64,512]{2,1,0:T(8,128)(2,1)S(1)} %get-tuple-element.17), channel_id=1, source_target_pairs={{0,4},{1,5},{2,6},{3,7},{4,0},{5,1},{6,2},{7,3},{8,12},{9,13},{10,... | collective-permute-start | bytes 786440 | tf_op jit(solution)/shard_map/ppermute | solution.py:181
  84.0 0.1 fusion.8
  84.2 3.9 %collective-permute-start.20 = (bf16[4,64,512]{2,1,0:T(8,128)(2,1)S(1)}, bf16[4,64,512]{2,1,0:T(8,128)(2,1)S(1)}, u32[]{:S(2)}, u32[]{:S(2)}) collective-permute-start(bf16[4,64,512]{2,1,0:T(8,128)(2,1)S(1)} %get-tuple-element.16), channel_id=1, source_target_pairs={{0,6},{1,7},{2,4},{3,5},{4,2},{5,3},{6,0},{7,1},{8,14},{9,15},{10,... | collective-permute-start | bytes 786440 | tf_op jit(solution)/shard_map/ppermute | solution.py:181
  88.0 2.9 %collective-permute-done.12 = bf16[2,216,256]{2,1,0:T(8,128)(2,1)S(1)} collective-permute-done((bf16[2,216,256]{2,1,0:T(8,128)(2,1)S(1)}, bf16[2,216,256]{2,1,0:T(8,128)(2,1)S(1)}, u32[]{:S(2)}, u32[]{:S(2)}) %collective-permute-start.12) | collective-permute-done | bytes 221216 | tf_op jit(solution)/shard_map/ppermute | solution.py:181
  90.9 1.3 %collective-permute-start.7 = (bf16[216,256]{1,0:T(8,128)(2,1)S(1)}, bf16[216,256]{1,0:T(8,128)(2,1)S(1)}, u32[]{:S(2)}, u32[]{:S(2)}) collective-permute-start(bf16[216,256]{1,0:T(8,128)(2,1)S(1)} %get-tuple-element.27), channel_id=1, source_target_pairs={{8,0},{9,1},{10,2},{11,3},{12,4},{13,5},{14,6},{15,7},{16,24},{17,... | collective-permute-start | bytes 331784 | tf_op jit(solution)/shard_map/ppermute | solution.py:181
  92.2 1.3 %collective-permute-start.8 = (bf16[216,256]{1,0:T(8,128)(2,1)S(1)}, bf16[216,256]{1,0:T(8,128)(2,1)S(1)}, u32[]{:S(2)}, u32[]{:S(2)}) collective-permute-start(bf16[216,256]{1,0:T(8,128)(2,1)S(1)} %get-tuple-element.29), channel_id=1, source_target_pairs={{8,24},{9,25},{10,26},{11,27},{12,28},{13,29},{14,30},{15,31},{16,... | collective-permute-start | bytes 331784 | tf_op jit(solution)/shard_map/ppermute | solution.py:181
  93.5 0.1 fusion.6
  93.7 6.4 %collective-permute-start.9 = (bf16[216,256]{1,0:T(8,128)(2,1)S(1)}, bf16[216,256]{1,0:T(8,128)(2,1)S(1)}, u32[]{:S(2)}, u32[]{:S(2)}) collective-permute-start(bf16[216,256]{1,0:T(8,128)(2,1)S(1)} %get-tuple-element.28), channel_id=1, source_target_pairs={{0,24},{1,25},{2,26},{3,27},{4,28},{5,29},{6,30},{7,31},{24,0},{25... | collective-permute-start | bytes 331784 | tf_op jit(solution)/shard_map/ppermute | solution.py:181
  100.1 1.5 %collective-permute-done.19 = bf16[4,64,512]{2,1,0:T(8,128)(2,1)S(1)} collective-permute-done((bf16[4,64,512]{2,1,0:T(8,128)(2,1)S(1)}, bf16[4,64,512]{2,1,0:T(8,128)(2,1)S(1)}, u32[]{:S(2)}, u32[]{:S(2)}) %collective-permute-start.19) | collective-permute-done | bytes 262176 | tf_op jit(solution)/shard_map/ppermute | solution.py:181
  101.6 3.5 %collective-permute-start.14 = (bf16[216,256]{1,0:T(8,128)(2,1)S(1)}, bf16[216,256]{1,0:T(8,128)(2,1)S(1)}, u32[]{:S(2)}, u32[]{:S(2)}) collective-permute-start(bf16[216,256]{1,0:T(8,128)(2,1)S(1)} %get-tuple-element.30), channel_id=1, source_target_pairs={{0,8},{1,9},{2,10},{3,11},{4,12},{5,13},{6,14},{7,15},{24,16},{25,... | collective-permute-start | bytes 331784 | tf_op jit(solution)/shard_map/ppermute | solution.py:181
  105.1 2.3 %collective-permute-start.15 = (bf16[216,256]{1,0:T(8,128)(2,1)S(1)}, bf16[216,256]{1,0:T(8,128)(2,1)S(1)}, u32[]{:S(2)}, u32[]{:S(2)}) collective-permute-start(bf16[216,256]{1,0:T(8,128)(2,1)S(1)} %get-tuple-element.32), channel_id=1, source_target_pairs={{0,16},{1,17},{2,18},{3,19},{4,20},{5,21},{6,22},{7,23},{24,8},{25... | collective-permute-start | bytes 331784 | tf_op jit(solution)/shard_map/ppermute | solution.py:181
  107.4 0.1 fusion.4
  107.6 0.7 collective-permute-start.16
  108.3 1.3 %collective-permute-start.21 = (bf16[64,512]{1,0:T(8,128)(2,1)S(1)}, bf16[64,512]{1,0:T(8,128)(2,1)S(1)}, u32[]{:S(2)}, u32[]{:S(2)}) collective-permute-start(bf16[64,512]{1,0:T(8,128)(2,1)S(1)} %get-tuple-element.24), channel_id=1, source_target_pairs={{0,8},{1,9},{2,10},{3,11},{4,12},{5,13},{6,14},{7,15},{8,0},{9,1},... | collective-permute-start | bytes 196616 | tf_op jit(solution)/shard_map/ppermute | solution.py:181
  109.6 0.8 collective-permute-start.22
  110.4 2.4 %collective-permute-start.23 = (bf16[64,512]{1,0:T(8,128)(2,1)S(1)}, bf16[64,512]{1,0:T(8,128)(2,1)S(1)}, u32[]{:S(2)}, u32[]{:S(2)}) collective-permute-start(bf16[64,512]{1,0:T(8,128)(2,1)S(1)} %get-tuple-element.25), channel_id=1, source_target_pairs={{0,24},{1,25},{2,26},{3,27},{4,28},{5,29},{6,30},{7,31},{8,16},{9,... | collective-permute-start | bytes 196616 | tf_op jit(solution)/shard_map/ppermute | solution.py:181
  112.8 0.1 fusion.22
  112.9 0.8 copy.44
  113.7 4.2 %collective-permute-done.22 = bf16[64,512]{1,0:T(8,128)(2,1)S(1)} collective-permute-done((bf16[64,512]{1,0:T(8,128)(2,1)S(1)}, bf16[64,512]{1,0:T(8,128)(2,1)S(1)}, u32[]{:S(2)}, u32[]{:S(2)}) %collective-permute-start.22) | collective-permute-done | bytes 65568 | tf_op jit(solution)/shard_map/ppermute | solution.py:181
  117.9 0.7 fusion.27
  (61 shorter events, 0.6 us)
Async XLA Ops:
  0.6 3.8 %collective-permute-start = (bf16[128,512]{1,0:T(8,128)(2,1)}, bf16[128,512]{1,0:T(8,128)(2,1)S(1)}, u32[]{:S(2)}, u32[]{:S(2)}) collective-permute-start(bf16[128,512]{1,0:T(8,128)(2,1)} %cur.1), channel_id=1, source_target_pairs={{0,1},{1,2},{2,3},{3,4},{4,5},{5,6},{6,7},{7,8},{8,9},{9,10},{10,1... | collective-permute-start | bytes 393224 | tf_op jit(solution)/shard_map/ppermute | solution.py:181
  4.4 0.7 copy-start.15
  5.1 0.9 copy-start.6
  6.0 0.8 copy-start.9
  6.9 0.7 copy-start.10
  7.6 1.6 %copy-start.13 = (bf16[2048,512]{1,0:T(8,128)(2,1)S(1)}, bf16[2048,512]{1,0:T(8,128)(2,1)}, u32[]{:S(2)}) copy-start(bf16[2048,512]{1,0:T(8,128)(2,1)} %w.1) | copy-start | bytes 6291460
  9.1 0.9 copy-start.14
  10.1 0.9 copy-start.16
  11.0 9.7 %copy-start.18 = (bf16[512,256]{1,0:T(8,128)(2,1)S(1)}, bf16[512,256]{1,0:T(8,128)(2,1)}, u32[]{:S(2)}) copy-start(bf16[512,256]{1,0:T(8,128)(2,1)} %param.10) | copy-start | bytes 786436
  11.0 10.5 %copy-start.19 = (s32[1,27,8,128]{3,2,1,0:T(8,128)S(1)}, s32[1,27,8,128]{3,2,1,0:T(8,128)}, u32[]{:S(2)}) copy-start(s32[1,27,8,128]{3,2,1,0:T(8,128)} %param.17) | copy-start | bytes 331780
  11.0 11.3 %copy-start.20 = (s32[1,27,8]{1,2,0:T(8,128)S(1)}, s32[1,27,8]{1,2,0:T(8,128)}, u32[]{:S(2)}) copy-start(s32[1,27,8]{1,2,0:T(8,128)} %param.16) | copy-start | bytes 2596
  11.0 11.4 %copy-start.21 = (s32[1,27,8]{1,2,0:T(8,128)S(1)}, s32[1,27,8]{1,2,0:T(8,128)}, u32[]{:S(2)}) copy-start(s32[1,27,8]{1,2,0:T(8,128)} %param.15) | copy-start | bytes 2596
  12.4 0.7 copy-start.3
  12.4 12.1 %copy-start.4 = (bf16[1024,512]{1,0:T(8,128)(2,1)}, bf16[1024,512]{1,0:T(8,128)(2,1)S(1)}, u32[]{:S(2)}) copy-start(bf16[1024,512]{1,0:T(8,128)(2,1)S(1)} %get-tuple-element.14.gath) | copy-start | bytes 3145732
  13.1 9.5 %collective-permute-start.1 = (bf16[256,256]{1,0:T(8,128)(2,1)S(1)}, bf16[256,256]{1,0:T(8,128)(2,1)S(1)}, u32[]{:S(2)}, u32[]{:S(2)}) collective-permute-start(bf16[256,256]{1,0:T(8,128)(2,1)S(1)} %get-tuple-element.33), channel_id=1, source_target_pairs={{0,1},{1,2},{2,3},{3,4},{4,5},{5,6},{6,7},{7,8},{8,9},{9,10},{10,1... | collective-permute-start | bytes 393224 | tf_op jit(solution)/shard_map/ppermute | solution.py:181
  18.5 5.1 %collective-permute-start.2 = (bf16[256,256]{1,0:T(8,128)(2,1)S(1)}, bf16[256,256]{1,0:T(8,128)(2,1)S(1)}, u32[]{:S(2)}, u32[]{:S(2)}) collective-permute-start(bf16[256,256]{1,0:T(8,128)(2,1)S(1)} %get-tuple-element.34), channel_id=1, source_target_pairs={{1,0},{2,1},{3,2},{4,3},{5,4},{6,5},{7,6},{8,7},{9,8},{10,9},{11,1... | collective-permute-start | bytes 393224 | tf_op jit(solution)/shard_map/ppermute | solution.py:181
  24.5 1.0 copy-start.7
  25.5 0.9 copy-start.8
  26.4 2.0 %copy-start.12 = (bf16[6912,256]{1,0:T(8,128)(2,1)S(1)}, bf16[6912,256]{1,0:T(8,128)(2,1)}, u32[]{:S(2)}) copy-start(bf16[6912,256]{1,0:T(8,128)(2,1)} %refs_5_.3) | copy-start | bytes 10616836
  38.3 4.6 %copy-start.2 = (f32[3456,256]{1,0:T(8,128)}, f32[3456,256]{1,0:T(8,128)S(1)}, u32[]{:S(2)}) copy-start(f32[3456,256]{1,0:T(8,128)S(1)} %get-tuple-element.12) | copy-start | bytes 10616836
  39.4 22.6 %collective-permute-start.3 = (bf16[8,216,256]{2,1,0:T(8,128)(2,1)}, bf16[8,216,256]{2,1,0:T(8,128)(2,1)}, u32[]{:S(2)}, u32[]{:S(2)}) collective-permute-start(bf16[8,216,256]{2,1,0:T(8,128)(2,1)} %fusion.1), channel_id=1, source_target_pairs={{0,1},{1,0},{2,3},{3,2},{4,5},{5,4},{6,7},{7,6},{8,9},{9,8},{10,11... | collective-permute-start | bytes 2654216 | tf_op jit(solution)/shard_map/ppermute | solution.py:181
  43.0 13.6 %copy-start.17 = (bf16[512,256]{0,1:T(8,128)(2,1)S(1)}, bf16[512,256]{0,1:T(8,128)(2,1)}, u32[]{:S(2)}) copy-start(bf16[512,256]{0,1:T(8,128)(2,1)} %copy.32) | copy-start | bytes 786436
  54.6 2.0 %copy-start.5 = (bf16[1024,512]{1,0:T(8,128)(2,1)S(1)}, bf16[1024,512]{1,0:T(8,128)(2,1)}, u32[]{:S(2)}) copy-start(bf16[1024,512]{1,0:T(8,128)(2,1)} %copy-done.4) | copy-start | bytes 3145732
  54.6 2.0 %copy-start.11 = (s32[1,8,128]{2,1,0:T(8,128)S(1)}, s32[1,8,128]{2,1,0:T(8,128)}, u32[]{:S(2)}) copy-start(s32[1,8,128]{2,1,0:T(8,128)} %param.18) | copy-start | bytes 12292
  55.6 15.1 %collective-permute-start.10 = (bf16[8,216,256]{2,1,0:T(8,128)(2,1)}, bf16[8,216,256]{2,1,0:T(8,128)(2,1)}, u32[]{:S(2)}, u32[]{:S(2)}) collective-permute-start(bf16[8,216,256]{2,1,0:T(8,128)(2,1)} %fusion.2), channel_id=1, source_target_pairs={{0,1},{1,0},{2,3},{3,2},{4,5},{5,4},{6,7},{7,6},{8,9},{9,8},{10,11... | collective-permute-start | bytes 2654216 | tf_op jit(solution)/shard_map/ppermute | solution.py:181
  58.5 2.0 %copy-start = (f32[2048,512]{1,0:T(8,128)}, f32[2048,512]{1,0:T(8,128)S(1)}, u32[]{:S(2)}) copy-start(f32[2048,512]{1,0:T(8,128)S(1)} %down_weight.1) | copy-start | bytes 12582916
  61.6 12.2 %collective-permute-start.17 = (bf16[16,64,512]{2,1,0:T(8,128)(2,1)}, bf16[16,64,512]{2,1,0:T(8,128)(2,1)}, u32[]{:S(2)}, u32[]{:S(2)}) collective-permute-start(bf16[16,64,512]{2,1,0:T(8,128)(2,1)} %fusion), channel_id=1, source_target_pairs={{0,1},{1,0},{2,3},{3,2},{4,5},{5,4},{6,7},{7,6},{8,9},{9,8},{10,11... | collective-permute-start | bytes 3145736 | tf_op jit(solution)/shard_map/ppermute | solution.py:181
  64.1 13.4 %collective-permute-start.4 = (bf16[2,216,256]{2,1,0:T(8,128)(2,1)S(1)}, bf16[2,216,256]{2,1,0:T(8,128)(2,1)S(1)}, u32[]{:S(2)}, u32[]{:S(2)}) collective-permute-start(bf16[2,216,256]{2,1,0:T(8,128)(2,1)S(1)} %get-tuple-element.18), channel_id=1, source_target_pairs={{0,2},{1,3},{2,0},{3,1},{4,6},{5,7},{6,4},{7,5},{8,10},{9,11},{10,... | collective-permute-start | bytes 663560 | tf_op jit(solution)/shard_map/ppermute | solution.py:181
  67.5 13.9 %collective-permute-start.5 = (bf16[2,216,256]{2,1,0:T(8,128)(2,1)S(1)}, bf16[2,216,256]{2,1,0:T(8,128)(2,1)S(1)}, u32[]{:S(2)}, u32[]{:S(2)}) collective-permute-start(bf16[2,216,256]{2,1,0:T(8,128)(2,1)S(1)} %get-tuple-element.19), channel_id=1, source_target_pairs={{0,4},{1,5},{2,6},{3,7},{4,0},{5,1},{6,2},{7,3},{8,12},{9,13},{10,... | collective-permute-start | bytes 663560 | tf_op jit(solution)/shard_map/ppermute | solution.py:181
  70.8 5.0 %copy-start.1 = (f32[2048,512]{1,0:T(8,128)S(1)}, f32[2048,512]{1,0:T(8,128)}, u32[]{:S(2)}) copy-start(f32[2048,512]{1,0:T(8,128)} %copy-done) | copy-start | bytes 12582916
  70.8 10.7 %collective-permute-start.6 = (bf16[2,216,256]{2,1,0:T(8,128)(2,1)S(1)}, bf16[2,216,256]{2,1,0:T(8,128)(2,1)S(1)}, u32[]{:S(2)}, u32[]{:S(2)}) collective-permute-start(bf16[2,216,256]{2,1,0:T(8,128)(2,1)S(1)} %get-tuple-element.20), channel_id=1, source_target_pairs={{0,6},{1,7},{2,4},{3,5},{4,2},{5,3},{6,0},{7,1},{8,14},{9,15},{10,... | collective-permute-start | bytes 663560 | tf_op jit(solution)/shard_map/ppermute | solution.py:181
  72.4 11.8 %collective-permute-start.11 = (bf16[2,216,256]{2,1,0:T(8,128)(2,1)S(1)}, bf16[2,216,256]{2,1,0:T(8,128)(2,1)S(1)}, u32[]{:S(2)}, u32[]{:S(2)}) collective-permute-start(bf16[2,216,256]{2,1,0:T(8,128)(2,1)S(1)} %get-tuple-element.21), channel_id=1, source_target_pairs={{0,2},{1,3},{2,0},{3,1},{4,6},{5,7},{6,4},{7,5},{8,10},{9,11},{10,... | collective-permute-start | bytes 663560 | tf_op jit(solution)/shard_map/ppermute | solution.py:181
  73.8 17.1 %collective-permute-start.12 = (bf16[2,216,256]{2,1,0:T(8,128)(2,1)S(1)}, bf16[2,216,256]{2,1,0:T(8,128)(2,1)S(1)}, u32[]{:S(2)}, u32[]{:S(2)}) collective-permute-start(bf16[2,216,256]{2,1,0:T(8,128)(2,1)S(1)} %get-tuple-element.23), channel_id=1, source_target_pairs={{0,4},{1,5},{2,6},{3,7},{4,0},{5,1},{6,2},{7,3},{8,12},{9,13},{10,... | collective-permute-start | bytes 663560 | tf_op jit(solution)/shard_map/ppermute | solution.py:181
  77.5 14.7 %collective-permute-start.13 = (bf16[2,216,256]{2,1,0:T(8,128)(2,1)S(1)}, bf16[2,216,256]{2,1,0:T(8,128)(2,1)S(1)}, u32[]{:S(2)}, u32[]{:S(2)}) collective-permute-start(bf16[2,216,256]{2,1,0:T(8,128)(2,1)S(1)} %get-tuple-element.22), channel_id=1, source_target_pairs={{0,6},{1,7},{2,4},{3,5},{4,2},{5,3},{6,0},{7,1},{8,14},{9,15},{10,... | collective-permute-start | bytes 663560 | tf_op jit(solution)/shard_map/ppermute | solution.py:181
  81.4 12.3 %collective-permute-start.18 = (bf16[4,64,512]{2,1,0:T(8,128)(2,1)S(1)}, bf16[4,64,512]{2,1,0:T(8,128)(2,1)S(1)}, u32[]{:S(2)}, u32[]{:S(2)}) collective-permute-start(bf16[4,64,512]{2,1,0:T(8,128)(2,1)S(1)} %get-tuple-element.15), channel_id=1, source_target_pairs={{0,2},{1,3},{2,0},{3,1},{4,6},{5,7},{6,4},{7,5},{8,10},{9,11},{10,... | collective-permute-start | bytes 786440 | tf_op jit(solution)/shard_map/ppermute | solution.py:181
  81.4 20.2 %collective-permute-start.19 = (bf16[4,64,512]{2,1,0:T(8,128)(2,1)S(1)}, bf16[4,64,512]{2,1,0:T(8,128)(2,1)S(1)}, u32[]{:S(2)}, u32[]{:S(2)}) collective-permute-start(bf16[4,64,512]{2,1,0:T(8,128)(2,1)S(1)} %get-tuple-element.17), channel_id=1, source_target_pairs={{0,4},{1,5},{2,6},{3,7},{4,0},{5,1},{6,2},{7,3},{8,12},{9,13},{10,... | collective-permute-start | bytes 786440 | tf_op jit(solution)/shard_map/ppermute | solution.py:181
  84.2 20.9 %collective-permute-start.20 = (bf16[4,64,512]{2,1,0:T(8,128)(2,1)S(1)}, bf16[4,64,512]{2,1,0:T(8,128)(2,1)S(1)}, u32[]{:S(2)}, u32[]{:S(2)}) collective-permute-start(bf16[4,64,512]{2,1,0:T(8,128)(2,1)S(1)} %get-tuple-element.16), channel_id=1, source_target_pairs={{0,6},{1,7},{2,4},{3,5},{4,2},{5,3},{6,0},{7,1},{8,14},{9,15},{10,... | collective-permute-start | bytes 786440 | tf_op jit(solution)/shard_map/ppermute | solution.py:181
  90.9 16.7 %collective-permute-start.7 = (bf16[216,256]{1,0:T(8,128)(2,1)S(1)}, bf16[216,256]{1,0:T(8,128)(2,1)S(1)}, u32[]{:S(2)}, u32[]{:S(2)}) collective-permute-start(bf16[216,256]{1,0:T(8,128)(2,1)S(1)} %get-tuple-element.27), channel_id=1, source_target_pairs={{8,0},{9,1},{10,2},{11,3},{12,4},{13,5},{14,6},{15,7},{16,24},{17,... | collective-permute-start | bytes 331784 | tf_op jit(solution)/shard_map/ppermute | solution.py:181
  92.2 16.1 %collective-permute-start.8 = (bf16[216,256]{1,0:T(8,128)(2,1)S(1)}, bf16[216,256]{1,0:T(8,128)(2,1)S(1)}, u32[]{:S(2)}, u32[]{:S(2)}) collective-permute-start(bf16[216,256]{1,0:T(8,128)(2,1)S(1)} %get-tuple-element.29), channel_id=1, source_target_pairs={{8,24},{9,25},{10,26},{11,27},{12,28},{13,29},{14,30},{15,31},{16,... | collective-permute-start | bytes 331784 | tf_op jit(solution)/shard_map/ppermute | solution.py:181
  93.7 15.8 %collective-permute-start.9 = (bf16[216,256]{1,0:T(8,128)(2,1)S(1)}, bf16[216,256]{1,0:T(8,128)(2,1)S(1)}, u32[]{:S(2)}, u32[]{:S(2)}) collective-permute-start(bf16[216,256]{1,0:T(8,128)(2,1)S(1)} %get-tuple-element.28), channel_id=1, source_target_pairs={{0,24},{1,25},{2,26},{3,27},{4,28},{5,29},{6,30},{7,31},{24,0},{25... | collective-permute-start | bytes 331784 | tf_op jit(solution)/shard_map/ppermute | solution.py:181
  101.6 8.8 %collective-permute-start.14 = (bf16[216,256]{1,0:T(8,128)(2,1)S(1)}, bf16[216,256]{1,0:T(8,128)(2,1)S(1)}, u32[]{:S(2)}, u32[]{:S(2)}) collective-permute-start(bf16[216,256]{1,0:T(8,128)(2,1)S(1)} %get-tuple-element.30), channel_id=1, source_target_pairs={{0,8},{1,9},{2,10},{3,11},{4,12},{5,13},{6,14},{7,15},{24,16},{25,... | collective-permute-start | bytes 331784 | tf_op jit(solution)/shard_map/ppermute | solution.py:181
  105.1 7.7 %collective-permute-start.15 = (bf16[216,256]{1,0:T(8,128)(2,1)S(1)}, bf16[216,256]{1,0:T(8,128)(2,1)S(1)}, u32[]{:S(2)}, u32[]{:S(2)}) collective-permute-start(bf16[216,256]{1,0:T(8,128)(2,1)S(1)} %get-tuple-element.32), channel_id=1, source_target_pairs={{0,16},{1,17},{2,18},{3,19},{4,20},{5,21},{6,22},{7,23},{24,8},{25... | collective-permute-start | bytes 331784 | tf_op jit(solution)/shard_map/ppermute | solution.py:181
  107.6 5.2 %collective-permute-start.16 = (bf16[216,256]{1,0:T(8,128)(2,1)S(1)}, bf16[216,256]{1,0:T(8,128)(2,1)S(1)}, u32[]{:S(2)}, u32[]{:S(2)}) collective-permute-start(bf16[216,256]{1,0:T(8,128)(2,1)S(1)} %get-tuple-element.31), channel_id=1, source_target_pairs={{8,16},{9,17},{10,18},{11,19},{12,20},{13,21},{14,22},{15,23},{16,... | collective-permute-start | bytes 331784 | tf_op jit(solution)/shard_map/ppermute | solution.py:181
  108.3 5.4 %collective-permute-start.21 = (bf16[64,512]{1,0:T(8,128)(2,1)S(1)}, bf16[64,512]{1,0:T(8,128)(2,1)S(1)}, u32[]{:S(2)}, u32[]{:S(2)}) collective-permute-start(bf16[64,512]{1,0:T(8,128)(2,1)S(1)} %get-tuple-element.24), channel_id=1, source_target_pairs={{0,8},{1,9},{2,10},{3,11},{4,12},{5,13},{6,14},{7,15},{8,0},{9,1},... | collective-permute-start | bytes 196616 | tf_op jit(solution)/shard_map/ppermute | solution.py:181
  109.6 8.3 %collective-permute-start.22 = (bf16[64,512]{1,0:T(8,128)(2,1)S(1)}, bf16[64,512]{1,0:T(8,128)(2,1)S(1)}, u32[]{:S(2)}, u32[]{:S(2)}) collective-permute-start(bf16[64,512]{1,0:T(8,128)(2,1)S(1)} %get-tuple-element.26), channel_id=1, source_target_pairs={{0,16},{1,17},{2,18},{3,19},{4,20},{5,21},{6,22},{7,23},{8,24},{9,... | collective-permute-start | bytes 196616 | tf_op jit(solution)/shard_map/ppermute | solution.py:181
  110.4 7.5 %collective-permute-start.23 = (bf16[64,512]{1,0:T(8,128)(2,1)S(1)}, bf16[64,512]{1,0:T(8,128)(2,1)S(1)}, u32[]{:S(2)}, u32[]{:S(2)}) collective-permute-start(bf16[64,512]{1,0:T(8,128)(2,1)S(1)} %get-tuple-element.25), channel_id=1, source_target_pairs={{0,24},{1,25},{2,26},{3,27},{4,28},{5,29},{6,30},{7,31},{8,16},{9,... | collective-permute-start | bytes 196616 | tf_op jit(solution)/shard_map/ppermute | solution.py:181

commit v2 on v1

v2 whole, which is shorter than its diff:
```python
import functools
import math

import jax
import jax.numpy as jnp
from jax import lax
from jax.experimental import pallas as pl
from jax.experimental.pallas import tpu as pltpu
from jax.sharding import PartitionSpec as P

HB = 2
BF = jnp.bfloat16
F32 = jnp.float32


def dot(a, b):
    return lax.dot_general(a, b, (((1,), (0,)), ((), ())), preferred_element_type=F32)


def dot_nt(a, b):
    return lax.dot_general(a, b, (((1,), (1,)), ((), ())), preferred_element_type=F32)


def one_hot(index, shape, axis):
    return jnp.where(index == lax.broadcasted_iota(jnp.int32, shape, axis), 1.0, 0.0).astype(BF)


def cost(flops, nbytes):
    return pl.CostEstimate(flops=flops, bytes_accessed=nbytes, transcendentals=0)


def fetch(pairs, sems):
    copies = [pltpu.make_async_copy(a, b, sems.at[i]) for i, (a, b) in enumerate(pairs)]
    for copy in copies:
        copy.start()
    return copies


def down_grad_kernel(
    prev, cur, par_t, rows_in, pre_in, w_in, gpre, gath, ext, rows, pre, w, contrib, pick, sems
):
    children, slots = rows.shape
    count, channels = pre.shape
    coarse = prev.shape[0]
    pieces = [
        (rows_in, rows),
        (cur, ext.at[pl.ds(coarse, cur.shape[0]), :]),
        (prev, ext.at[pl.ds(0, coarse), :]),
        (pre_in, pre),
    ]
    own = [pl.ds(c * channels, channels) for c in range(children)]
    copies = fetch(pieces + [(w_in.at[at, :], w.at[at, :]) for at in own], sems)
    copies[0].wait()
    for c in range(children):
        pick[:, pl.ds(c * slots, slots)] = one_hot(rows[c : c + 1, :], (count, slots), 0)
    copies[1].wait()
    copies[2].wait()
    for c in range(children):
        mine = pl.ds(c * slots, slots)
        parents = one_hot(par_t[:, c : c + 1], (slots, ext.shape[0]), 1)
        got = dot(parents, ext[...]).astype(BF)
        gath[mine, :] = got
        copies[4 + c].wait()
        contrib[mine, :] = dot_nt(got, w[own[c], :]).astype(BF)
    grad = dot(pick[...], contrib[...])
    copies[3].wait()
    gpre[...] = jnp.where(pre[...].astype(F32) > 0, grad, 0.0).astype(BF)


def down_grad(prev, cur, par_t, rows, pre, w):
    children, slots = rows.shape
    count, channels = pre.shape
    width = cur.shape[1]
    anywhere = pl.BlockSpec(memory_space=pl.ANY)
    vmem = pl.BlockSpec(memory_space=pltpu.VMEM)
    return pl.pallas_call(
        down_grad_kernel,
        out_shape=(
            jax.ShapeDtypeStruct((count, channels), BF),
            jax.ShapeDtypeStruct((children * slots, width), BF),
        ),
        in_specs=[anywhere, anywhere, vmem, anywhere, anywhere, anywhere],
        out_specs=(vmem, vmem),
        scratch_shapes=[
            pltpu.VMEM((prev.shape[0] + cur.shape[0], width), BF),
            pltpu.VMEM(rows.shape, jnp.int32),
            pltpu.VMEM(pre.shape, BF),
            pltpu.VMEM(w.shape, BF),
            pltpu.VMEM((children * slots, channels), BF),
            pltpu.VMEM((count, children * slots), BF),
            pltpu.SemaphoreType.DMA((4 + children,)),
        ],
        compiler_params=pltpu.CompilerParams(vmem_limit_bytes=48 << 20),
        cost_estimate=cost(1 << 30, 4 << 20),
        name="down_grad",
    )(prev, cur, par_t, rows, pre, w)


def down_weight_kernel(act_t, rows_in, gath, out, rows, total, sems):
    children, slots = rows.shape
    channels, count = act_t.shape
    fetch([(rows_in, rows)], sems.at[pl.ds(children, 1)])[0].wait()
    copies = []
    for c in range(children):
        mine = pl.ds(c * channels, channels)
        pick = one_hot(rows[c : c + 1, :], (count, slots), 0)
        chosen = dot(act_t[...], pick).astype(BF)
        total[mine, :] = dot(chosen, gath[pl.ds(c * slots, slots), :])
        copies += fetch([(total.at[mine, :], out.at[mine, :])], sems.at[pl.ds(c, 1)])
    for copy in copies:
        copy.wait()


def down_weight(act_t, rows, gath):
    channels = act_t.shape[0]
    children = rows.shape[0]
    width = gath.shape[1]
    anywhere = pl.BlockSpec(memory_space=pl.ANY)
    vmem = pl.BlockSpec(memory_space=pltpu.VMEM)
    return pl.pallas_call(
        down_weight_kernel,
        out_shape=jax.ShapeDtypeStruct((children * channels, width), F32),
        in_specs=[vmem, anywhere, vmem],
        out_specs=anywhere,
        scratch_shapes=[
            pltpu.VMEM(rows.shape, jnp.int32),
            pltpu.VMEM((children * channels, width), F32),
            pltpu.SemaphoreType.DMA((children + 1,)),
        ],
        compiler_params=pltpu.CompilerParams(vmem_limit_bytes=48 << 20),
        cost_estimate=cost(1 << 30, 6 << 20),
        name="down_weight",
    )(act_t, rows, gath)


GROUP = 4


def conv_plan(kernel, channels, quarters):
    quarter = kernel * channels // 4
    plan, out = [], 0
    for q in quarters:
        row = q * quarter
        while row < (q + 1) * quarter:
            k, first = divmod(row, channels)
            last = min(channels, (q + 1) * quarter - k * channels)
            plan.append((k, first, last, out))
            out += last - first
            row += last - first
    return plan


def conv_kernel(plan, blocks, final, *refs):
    tab_in, before, own, after, feats_in, w, *rest = refs
    if final:
        partial_in, *rest = rest
    grad, sub, tab, ext, feats_t, wbuf, acc, total, cols, spare, pick0, pick1, sems = rest
    picks = (pick0, pick1)
    rows = tab.shape[0]
    channels, count = feats_t.shape
    halo = before.shape[0]
    pieces = [
        (tab_in, tab),
        (own, ext.at[pl.ds(halo, count), :]),
        (before, ext.at[pl.ds(0, halo), :]),
        (after, ext.at[pl.ds(halo + count, halo), :]),
        (feats_in, feats_t),
    ]
    if final:
        pieces.append((partial_in, acc))
    whole = [k for k, first, last, out in plan if first == 0]
    for at, k in enumerate(whole):
        pieces.append(
            (
                w.at[pl.ds(k * channels, channels), :],
                wbuf.at[:, pl.ds(at * channels, channels)],
            )
        )
    copies = fetch(pieces, sems)
    loads = copies[len(copies) - len(whole) :]
    lanes = lax.broadcasted_iota(jnp.int32, (rows, rows), 1).astype(jnp.int16)
    one, zero = jnp.ones((), BF), jnp.zeros((), BF)

    def build(k, pick):
        for b in range(blocks):
            at = k * blocks + b
            index = jnp.broadcast_to(tab[:, at : at + 1], (rows, rows)).astype(jnp.int16)
            for e in range(ext.shape[0] // rows):
                hit = index == lanes + jnp.int16(e * rows)
                pick[pl.ds(b * rows, rows), pl.ds(e * rows, rows)] = jnp.where(hit, one, zero)

    copies[0].wait()
    build(plan[0][0], picks[0])
    for copy in copies[1 : len(copies) - len(whole)]:
        copy.wait()
    if not final:
        acc[...] = jnp.zeros_like(acc)
    done, added, outs = 0, 0, []
    for at, (k, first, last, out) in enumerate(plan):
        column = dot(picks[at % 2][...], ext[...]).astype(BF)
        if at + 1 < len(plan):
            build(plan[at + 1][0], picks[(at + 1) % 2])
        if first == 0:
            col = cols.at[:, pl.ds(done * channels, channels)]
            done += 1
        else:
            col = spare
        col[...] = column
        mine = pl.ds(out, last - first)
        total[mine, :] = dot(feats_t[pl.ds(first, last - first), :], col[...])
        outs += fetch([(total.at[mine, :], sub.at[mine, :])], sems.at[pl.ds(len(pieces) + at, 1)])
        if first == 0 and (done - added == GROUP or done == len(whole)):
            for load in loads[added:done]:
                load.wait()
            span = pl.ds(added * channels, (done - added) * channels)
            acc[...] += dot_nt(cols[:, span], wbuf[:, span])
            added = done
    grad[...] = acc[...].astype(grad.dtype)
    for copy in outs:
        copy.wait()


def conv(tab, before, own, after, feats_t, w, quarters, partial=None):
    channels, count = feats_t.shape
    kernel = w.shape[0] // channels
    rows = tab.shape[0]
    blocks = count // rows
    plan = conv_plan(kernel, channels, quarters)
    whole = sum(first == 0 for k, first, last, out in plan)
    final = partial is not None
    anywhere = pl.BlockSpec(memory_space=pl.ANY)
    vmem = pl.BlockSpec(memory_space=pltpu.VMEM)
    total = (len(quarters) * kernel * channels // 4, channels)
    ext_rows = count + before.shape[0] + after.shape[0]
    return pl.pallas_call(
        functools.partial(conv_kernel, plan, blocks, final),
        out_shape=(
            jax.ShapeDtypeStruct((count, channels), BF if final else F32),
            jax.ShapeDtypeStruct(total, F32),
        ),
        in_specs=[anywhere] * (6 + final),
        out_specs=(vmem, anywhere),
        scratch_shapes=[
            pltpu.VMEM(tab.shape, jnp.int32),
            pltpu.VMEM((ext_rows, channels), BF),
            pltpu.VMEM((channels, count), BF),
            pltpu.VMEM((channels, whole * channels), BF),
            pltpu.VMEM((count, channels), F32),
            pltpu.VMEM(total, F32),
            pltpu.VMEM((count, whole * channels), BF),
            pltpu.VMEM((count, channels), BF),
            pltpu.VMEM((count, ext_rows), BF),
            pltpu.VMEM((count, ext_rows), BF),
            pltpu.SemaphoreType.DMA((6 + whole + len(plan),)),
        ],
        compiler_params=pltpu.CompilerParams(vmem_limit_bytes=48 << 20),
        cost_estimate=cost(8 << 30, 8 << 20),
        name="conv",
    )(tab, before, own, after, feats_t, w, *([partial] if final else []))


def moved(x, peers, to):
    pairs = [(i, to(i)) for i in range(peers)]
    return lax.ppermute(x, "space", [(i, j) for i, j in pairs if j is not None and 0 <= j < peers])


def taken(x, axis, digit):
    return lax.dynamic_index_in_dim(x, digit, axis=axis, keepdims=False)


def fold_core(x, kept, me, peers):
    core = me % 2
    axis = x.ndim - 3
    got = moved(taken(x, axis, 1 - core).astype(BF), peers, lambda i: i ^ 1)
    return taken(kept, axis, core), got


def low_steps(bits):
    left = [list(range(bits - 1, -1, -1)) for core in range(2)]
    steps = []
    for j in range(bits):
        by = (j, (j + bits // 2) % bits)
        steps.append((by, [left[core].index(by[core]) for core in range(2)]))
        for core in range(2):
            left[core].remove(by[core])
    return steps


def fold_low(keep, got, me, peers, step):
    core = me % 2
    by, axes = step
    bit = jnp.where(core == 0, me >> (1 + by[0]), me >> (1 + by[1])) % 2

    def half(x, digit):
        if axes[0] == axes[1]:
            return taken(x, 1 + axes[0], digit)
        return jnp.where(core == 0, taken(x, 1 + axes[0], digit), taken(x, 1 + axes[1], digit))

    def piece(digit):
        return half(keep, digit) + half(got, digit).astype(F32)

    sent = piece(1 - bit).astype(BF)
    return piece(bit), moved(sent, peers, lambda i: i ^ (2 << by[i % 2]))


def fold_bit(keep, got, me, peers, stride, first):
    bit = me // stride % 2
    axis = keep.ndim - 3

    def piece(digit):
        return taken(keep, axis, digit) + taken(got, axis, digit).astype(F32)

    mine = bit ^ first
    sent = piece(1 - mine).astype(BF)
    return piece(mine), moved(sent, peers, lambda i: i ^ stride)


def per_device(
    feats,
    pre_act,
    coarse_grad,
    w_sub,
    w_down,
    pair_src,
    pair_tgt,
    pair_rows,
    down_rows,
    down_parent,
):
    peers = lax.axis_size("space")
    me = lax.axis_index("space")
    row_count, channels = feats.shape
    block_rows = pair_rows.shape[-1]
    blocks = row_count // block_rows
    out_width = coarse_grad.shape[1]
    kernel = pair_src.shape[1]
    children = down_rows.shape[1]
    scale = 1.0 / math.sqrt(peers * row_count)
    bits = (peers // 8).bit_length() - 1
    steps = low_steps(bits)
    near, far = peers // 4, peers // 2

    previous = moved(coarse_grad[-block_rows:], peers, lambda i: i + 1)
    grad_pre, gathered = down_grad(
        previous, coarse_grad, down_parent[0].T, down_rows[0], pre_act, w_down
    )
    halo = HB * block_rows
    before = moved(grad_pre[-halo:], peers, lambda i: i + 1)
    after = moved(grad_pre[:halo], peers, lambda i: i - 1)

    feats_t = feats.T
    act_t = jnp.maximum(pre_act, 0).T
    owned = pair_src[0][:, None, :, None] == jnp.arange(blocks)[None, :, None, None]
    there = (pair_rows[0] < block_rows)[:, None]
    spot = (pair_tgt[0][:, :, None] * block_rows + pair_rows[0] + 1)[:, None]
    merged = jnp.sum(jnp.where(owned & there, spot, 0), axis=2) - 1
    tab = merged.reshape(kernel * blocks, block_rows).T

    down_term = down_weight(act_t, down_rows[0], gathered)
    own, down_tied = lax.optimization_barrier((grad_pre, down_term))

    down_shards = (4,) + (2,) * (bits + 1) + (children * channels // peers, out_width)
    down_keep, down_got = fold_core(
        down_term.reshape(down_shards), down_tied.reshape(down_shards), me, peers
    )

    def sub_shards(x):
        return x.reshape((2,) + (2,) * (bits + 1) + (kernel * channels // peers, channels))

    partial, outer = conv(tab, before, own, after, feats_t, w_sub, (0, 3))
    outer = sub_shards(outer)
    outer_keep, outer_got = fold_core(outer, outer, me, peers)
    partial, down_got = lax.optimization_barrier((partial, down_got))
    grad_in, inner = conv(tab, before, own, after, feats_t, w_sub, (1, 2), partial)
    inner = sub_shards(inner)
    inner_keep, inner_got = fold_core(inner, inner, me, peers)

    for step in steps:
        down_keep, down_got = fold_low(down_keep, down_got, me, peers, step)
        outer_keep, outer_got = fold_low(outer_keep, outer_got, me, peers, step)
        inner_keep, inner_got = fold_low(inner_keep, inner_got, me, peers, step)

    down_keep = down_keep.reshape((2, 2) + down_keep.shape[-2:])
    down_got = down_got.reshape((2, 2) + down_got.shape[-2:])
    down_keep, down_got = fold_bit(down_keep, down_got, me, peers, near, 0)
    outer_keep, outer_got = fold_bit(outer_keep, outer_got, me, peers, near, 0)
    inner_keep, inner_got = fold_bit(inner_keep, inner_got, me, peers, near, 1)
    down_keep, down_got = fold_bit(down_keep, down_got, me, peers, far, 0)
    down_sum = down_keep + down_got.astype(F32)

    digit = me // near
    is_outer = (digit == 0) | (digit == 3)
    outer_sum = outer_keep + outer_got.astype(F32)
    inner_sum = inner_keep + inner_got.astype(F32)
    sent = jnp.where(is_outer, inner_sum, outer_sum).astype(BF)
    sub_sum = jnp.where(is_outer, outer_sum, inner_sum)
    sub_sum = sub_sum + moved(sent, peers, lambda i: i ^ far).astype(F32)
    return (grad_in, sub_sum.reshape(-1) * scale, down_sum * scale)


def solution(mesh):
    rows = ("scene", "space")
    placed = (
        P(rows, None),
        P(rows, None),
        P(rows, None),
        P(),
        P(),
        P(rows, None, None),
        P(rows, None, None),
        P(rows, None, None, None),
        P(rows, None, None),
        P(rows, None, None),
    )
    return jax.shard_map(
        per_device,
        mesh=mesh,
        in_specs=placed,
        out_specs=(P(rows, None), P(rows), P(rows, None)),
        check_vma=False,
    )
```

time: 119 us -> 119 us (level)
  starting transfers between devices: 51.2 us -> 29.1 us
  Pallas kernels: 24.8 us -> 38.5 us
  waiting for transfers between devices: 12.5 us -> 18.3 us
  local copies, waits for them, and re-layouts: 21.8 us -> 23.1 us
    ppermute x24 -> x17, starting transfers between devices: 51.2 us -> 29.1 us  [moved(): lax.ppermute(x, 'space', [(i, j) for i, j in pairs if j is not None and 0...]
    pallas_call x2, Pallas kernels: 21.5 us -> 31.3 us  [conv(): pl.pallas_call(functools.partial(conv_kernel, plan, blocks, final), out_s...]
    ppermute x24 -> x17, waiting for transfers between devices: 12.5 us -> 18.3 us  [moved(): lax.ppermute(x, 'space', [(i, j) for i, j in pairs if j is not None and 0...]
    dynamic_slice x0 -> x4, local copies, waits for them, and re-layouts: none -> 4.72 us  [taken(): return lax.dynamic_index_in_dim(x, digit, axis=axis, keepdims=False)]
    unnamed x50, local copies, waits for them, and re-layouts: 17.2 us -> 12.9 us
    add x6 -> x4, other arithmetic: 5.36 us -> 2.6 us  [the longest x3 1.61 us: piece(): return half(keep, digit) + half(got, digit).astype(F32)]
    convert_element_type x0 -> x11, other arithmetic: none -> 2.72 us  [the longest x6 2.48 us: fold_low(): sent = piece(1 - bit).astype(BF)]
    pallas_call x1, Pallas kernels: 1.42 us -> 3.82 us  [down_grad(): pl.pallas_call(down_grad_kernel, out_shape=(jax.ShapeDtypeStruct((count,...]
  transfers between devices with their start and end apart: 24 -> 17, of which waited for: 5 -> 6; matrix products, arithmetic and copies ran while one was open for 11% -> 17% of each run, Pallas kernels for 11% -> 17%
where the time goes in v2:
time: 119 us; the launch traced here: 118 us
  Pallas kernels  38.5 us (32%)
  starting transfers between devices  29.1 us (24%)
  local copies, waits for them, and re-layouts  23.1 us (19%)
  waiting for transfers between devices  18.3 us (15%)
  other arithmetic  8.02 us (7%)
    pallas_call x2, Pallas kernels, conv(): pl.pallas_call(functools.partial(conv_kernel, plan, blocks, final), out_s...  31.3 us
    ppermute x17, starting transfers between devices, moved(): lax.ppermute(x, 'space', [(i, j) for i, j in pairs if j is not None and 0...  29.1 us
    ppermute x17, waiting for transfers between devices, moved(): lax.ppermute(x, 'space', [(i, j) for i, j in pairs if j is not None and 0...  18.3 us
    unnamed x50, local copies, waits for them, and re-layouts  12.9 us
    dynamic_slice x4, local copies, waits for them, and re-layouts, taken(): return lax.dynamic_index_in_dim(x, digit, axis=axis, keepdims=False)  4.72 us
    pallas_call x1, Pallas kernels, down_grad(): pl.pallas_call(down_grad_kernel, out_shape=(jax.ShapeDtypeStruct((count,...  3.82 us
    pallas_call x1, Pallas kernels, down_weight(): pl.pallas_call(down_weight_kernel, out_shape=jax.ShapeDtypeStruct((childr...  3.37 us
    convert_element_type x6, other arithmetic, fold_low(): sent = piece(1 - bit).astype(BF)  2.48 us
  transfers between devices with their start and end apart: 17, of which 6 were waited for; matrix products, arithmetic and copies ran while one was open for 17% of the time, Pallas kernels for 17%

profile of v2, /device:TPU:0, one launch (start us, length us, event | category | flops | bytes accessed | tf_op | source)
XLA Modules:
  0.0 118.1 jit_solution(17296950235956933581)
XLA Ops:
  0.6 2.5 %collective-permute-start = (bf16[128,512]{1,0:T(8,128)(2,1)}, bf16[128,512]{1,0:T(8,128)(2,1)S(1)}, u32[]{:S(2)}, u32[]{:S(2)}) collective-permute-start(bf16[128,512]{1,0:T(8,128)(2,1)} %cur.1), channel_id=1, source_target_pairs={{0,1},{1,2},{2,3},{3,4},{4,5},{5,6},{6,7},{7,8},{8,9},{9,10},{10,1... | collective-permute-start | bytes 393224 | tf_op jit(solution)/shard_map/ppermute | solution.py:264
  3.1 0.7 multiply_bitcast_fusion.1
  3.9 0.8 copy.66
  4.7 0.9 bitcast_compare_fusion
  5.7 0.8 copy.69
  6.4 1.0 fusion.24
  7.4 1.1 copy.70
  8.6 0.2 select_reduce_fusion
  8.8 0.9 copy-done.2
  9.8 0.7 copy-done.10
  10.5 1.6 %copy-done.12 = bf16[2048,512]{1,0:T(8,128)(2,1)S(1)} copy-done((bf16[2048,512]{1,0:T(8,128)(2,1)S(1)}, bf16[2048,512]{1,0:T(8,128)(2,1)}, u32[]{:S(2)}) %copy-start.12) | copy-done | bytes 2097176
  12.1 0.9 copy-done.13
  13.0 3.8 %down_grad.1 = (bf16[512,256]{1,0:T(8,128)(2,1)S(1)}, bf16[1024,512]{1,0:T(8,128)(2,1)S(1)}) custom-call(bf16[128,512]{1,0:T(8,128)(2,1)S(1)} %collective-permute-done.prev, bf16[128,512]{1,0:T(8,128)(2,1)S(1)} %copy-done.13, s32[128,8]{1,0:T(8,128)S(1)} %bitcast.202, s32[8,128]{1,0:T(8,128)S(1)} %bitcast.205, bf16[512,256]{1,0:T(8,128)(2,1)S(1)} %copy-done.2, ...), custom_call_target="tpu_custom_call" | custom-call | flops 1073741824 | bytes 4194304 | tf_op jit(solution)/shard_map/down_grad/pallas_call | solution.py:76
  16.8 0.7 copy-done.3
  17.5 1.3 %collective-permute-start.2 = (bf16[256,256]{1,0:T(8,128)(2,1)S(1)}, bf16[256,256]{1,0:T(8,128)(2,1)S(1)}, u32[]{:S(2)}, u32[]{:S(2)}) collective-permute-start(bf16[256,256]{1,0:T(8,128)(2,1)S(1)} %get-tuple-element.47), channel_id=1, source_target_pairs={{1,0},{2,1},{3,2},{4,3},{5,4},{6,5},{7,6},{8,7},{9,8},{10,9},{11,1... | collective-permute-start | bytes 393224 | tf_op jit(solution)/shard_map/ppermute | solution.py:264
  18.8 5.1 %collective-permute-start.1 = (bf16[256,256]{1,0:T(8,128)(2,1)S(1)}, bf16[256,256]{1,0:T(8,128)(2,1)S(1)}, u32[]{:S(2)}, u32[]{:S(2)}) collective-permute-start(bf16[256,256]{1,0:T(8,128)(2,1)S(1)} %get-tuple-element.48), channel_id=1, source_target_pairs={{0,1},{1,2},{2,3},{3,4},{4,5},{5,6},{6,7},{7,8},{8,9},{9,10},{10,1... | collective-permute-start | bytes 393224 | tf_op jit(solution)/shard_map/ppermute | solution.py:264
  24.0 0.7 copy.68
  24.8 0.8 copy.71
  25.6 3.4 %down_weight.1 = f32[2048,512]{1,0:T(8,128)S(1)} custom-call(bf16[256,512]{1,0:T(8,128)(2,1)S(1)} %maximum_bitcast_fusion.act_t, s32[8,128]{1,0:T(8,128)S(1)} %bitcast.206, bf16[1024,512]{1,0:T(8,128)(2,1)S(1)} %get-tuple-element.14.gath), custom_call_target="tpu_custom_call" | custom-call | flops 1073741824 | bytes 6291456 | tf_op jit(solution)/shard_map/down_weight/pallas_call | solution.py:120
  29.0 0.7 copy-done.14
  29.7 1.1 copy-done.17
  30.9 0.9 copy-done.15
  31.8 0.9 copy-done.18
  32.7 14.0 %conv.2 = (f32[512,256]{1,0:T(8,128)S(1)}, f32[3456,256]{1,0:T(8,128)S(1)}) custom-call(s32[128,108]{1,0:T(8,128)S(1)} %bitcast.203, bf16[256,256]{1,0:T(8,128)(2,1)S(1)} %copy-done.18, bf16[512,256]{1,0:T(8,128)(2,1)S(1)} %copy-done.4, bf16[256,256]{1,0:T(8,128)(2,1)S(1)} %copy-done.15, bf16[256,512]{1,0:T(8,128)(2,1)S(1)} %bitcast.200, ...), custom_call_target="tpu_custom_call" | custom-call | flops 8589934592 | bytes 8388608 | tf_op jit(solution)/shard_map/conv/pallas_call | solution.py:235
  46.7 1.1 fusion.4
  47.8 1.7 %collective-permute-start.4 = (bf16[2,2,2,216,256]{4,3,1,0,2:T(8,128)(2,1)}, bf16[2,2,2,216,256]{4,3,1,0,2:T(8,128)(2,1)}, u32[]{:S(2)}, u32[]{:S(2)}) collective-permute-start(bf16[2,2,2,216,256]{4,3,1,0,2:T(8,128)(2,1)} %fusion.4), channel_id=1, source_target_pairs={{0,1},{1,0},{2,3},{3,2},{4,5},{5,4},{6,7},{7,6},{8,9},{9,8},{10,11... | collective-permute-start | bytes 2654216 | tf_op jit(solution)/shard_map/ppermute | solution.py:264
  49.6 1.1 fusion
  50.7 1.9 %constant_dynamic-slice_fusion.3 = (f32[4,2,1,1,64,512]{5,4,3,2,1,0:T(8,128)S(1)}, f32[4,2,1,1,64,512]{5,4,3,2,1,0:T(8,128)S(1)}) fusion(f32[4,2,2,2,64,512]{5,4,3,2,1,0:T(8,128)} %bitcast.192, s32[]{:T(128)S(6)} %select_n.273, s32[]{:T(128)S(6)} %select_n.266, s32[]{:T(128)S(6)} %select_n.264), kind=kLoop, calls=%fused_computation.79 | loop fusion | bytes 4194316 | tf_op jit(solution)/shard_map/jit(dynamic_index_in_dim)/dynamic_slice | solution.py:268
  52.6 0.9 copy-done.1
  53.5 0.2 constant_dynamic-slice_fusion.2
  53.8 1.2 %dynamic-slice_bitcast_fusion.8 = (bf16[2,2,216,256]{3,2,1,0:T(8,128)(2,1)S(1)}, bf16[2,2,216,256]{3,2,1,0:T(8,128)(2,1)S(1)}) fusion(bf16[2,2,2,216,256]{4,3,1,0,2:T(8,128)(2,1)} %collective-permute-done.4, s32[]{:T(128)S(6)} %select_n.272, s32[]{:T(128)S(6)} %select_n.263), kind=kLoop, calls=%fused_computation.43 | loop fusion | bytes 1769480 | tf_op jit(solution)/shard_map/jit(dynamic_index_in_dim)/squeeze | solution.py:268
  55.0 1.3 %fusion.11 = bf16[2,2,216,256]{3,2,0,1:T(8,128)(2,1)S(1)} fusion(bf16[2,2,216,256]{3,2,1,0:T(8,128)(2,1)S(1)} %get-tuple-element.43, bf16[2,2,2,216,256]{4,3,1,0,2:T(8,128)(2,1)} %collective-permute-done.4, s32[]{:T(128)S(6)} %select_n.272, pred[]{:T(512)S(6)} %eq.72, f32[2,2,2,2,216,256]{5,4,3,2,1,0:T(8,128)S(1)} %bitcast.195, s32[]{:T(128)S(6)} %select_n.273, ...), kind=kLoop, calls=%fused_computation.20 | loop fusion | flops 1105920 | bytes 3099648 | tf_op jit(solution)/shard_map/convert_element_type | solution.py:302
  56.3 2.5 %collective-permute-start.5 = (bf16[2,2,216,256]{3,2,0,1:T(8,128)(2,1)S(1)}, bf16[2,2,216,256]{3,2,0,1:T(8,128)(2,1)S(1)}, u32[]{:S(2)}, u32[]{:S(2)}) collective-permute-start(bf16[2,2,216,256]{3,2,0,1:T(8,128)(2,1)S(1)} %fusion.11), channel_id=1, source_target_pairs={{0,2},{1,5},{2,0},{3,7},{4,6},{5,1},{6,4},{7,3},{8,10},{9,13},{10,... | collective-permute-start | bytes 1327112 | tf_op jit(solution)/shard_map/ppermute | solution.py:264
  58.8 1.2 %fusion.6 = f32[2,2,216,256]{3,2,1,0:T(8,128)S(1)} fusion(f32[2,2,2,2,216,256]{5,4,3,2,1,0:T(8,128)S(1)} %bitcast.196, s32[]{:T(128)S(6)} %select_n.264, s32[]{:T(128)S(6)} %select_n.266, pred[]{:T(512)S(6)} %eq.72, bf16[2,2,216,256]{3,2,1,0:T(8,128)(2,1)S(1)} %get-tuple-element.44, bf16[2,2,2,216,256]{4,3,1,0,2:T(8,128)(2,1)} %collective-permute-done.4, ...), kind=kLoop, calls=%fused_computation.12 | loop fusion | flops 884736 | bytes 3541504 | tf_op jit(solution)/shard_map/add | solution.py:300
  60.1 17.2 %conv.3 = (bf16[512,256]{1,0:T(8,128)(2,1)}, f32[3456,256]{1,0:T(8,128)S(1)}) custom-call(s32[128,108]{1,0:T(8,128)S(1)} %bitcast.204, bf16[256,256]{1,0:T(8,128)(2,1)S(1)} %copy-done.19, bf16[512,256]{1,0:T(8,128)(2,1)S(1)} %copy-done.5, bf16[256,256]{1,0:T(8,128)(2,1)S(1)} %copy-done.16, bf16[256,512]{1,0:T(8,128)(2,1)S(1)} %bitcast.201, ...), custom_call_target="tpu_custom_call" | custom-call | flops 8589934592 | bytes 8388608 | tf_op jit(solution)/shard_map/conv/pallas_call | solution.py:235
  77.3 0.1 fusion.5
  77.5 1.3 %constant_dynamic-slice_fusion.1 = (bf16[4,2,1,64,512]{4,3,2,1,0:T(8,128)(2,1)S(1)}, bf16[4,2,1,64,512]{4,3,2,1,0:T(8,128)(2,1)S(1)}) fusion(bf16[4,2,2,64,512]{4,3,2,1,0:T(8,128)(2,1)} %collective-permute-done.3, s32[]{:T(128)S(6)} %select_n.272, s32[]{:T(128)S(6)} %select_n.263), kind=kLoop, calls=%fused_computation.77 | loop fusion | bytes 2097160 | tf_op jit(solution)/shard_map/jit(dynamic_index_in_dim)/dynamic_slice | solution.py:268
  78.8 1.3 %constant_dynamic-slice_fusion = (bf16[4,1,2,64,512]{4,3,2,1,0:T(8,128)(2,1)S(1)}, bf16[4,1,2,64,512]{4,3,2,1,0:T(8,128)(2,1)S(1)}) fusion(bf16[4,2,2,64,512]{4,3,2,1,0:T(8,128)(2,1)} %collective-permute-done.3, s32[]{:T(128)S(6)} %select_n.272, s32[]{:T(128)S(6)} %select_n.263), kind=kLoop, calls=%fused_computation.76 | loop fusion | bytes 2097160 | tf_op jit(solution)/shard_map/jit(dynamic_index_in_dim)/dynamic_slice | solution.py:268
  80.1 0.4 fusion.2
  80.5 2.8 %collective-permute-start.13 = (bf16[4,2,64,512]{3,2,0,1:T(8,128)(2,1)S(1)}, bf16[4,2,64,512]{3,2,0,1:T(8,128)(2,1)S(1)}, u32[]{:S(2)}, u32[]{:S(2)}) collective-permute-start(bf16[4,2,64,512]{3,2,0,1:T(8,128)(2,1)S(1)} %fusion.2), channel_id=1, source_target_pairs={{0,2},{1,5},{2,0},{3,7},{4,6},{5,1},{6,4},{7,3},{8,10},{9,13},{10,... | collective-permute-start | bytes 1572872 | tf_op jit(solution)/shard_map/ppermute | solution.py:264
  83.3 0.1 dynamic-slice_bitcast_fusion
  83.4 0.1 dynamic-slice_bitcast_fusion.1
  83.6 0.4 fusion.8
  84.2 0.4 fusion.3
  84.6 5.9 %collective-permute-done.13 = bf16[4,2,64,512]{3,2,0,1:T(8,128)(2,1)S(1)} collective-permute-done((bf16[4,2,64,512]{3,2,0,1:T(8,128)(2,1)S(1)}, bf16[4,2,64,512]{3,2,0,1:T(8,128)(2,1)S(1)}, u32[]{:S(2)}, u32[]{:S(2)}) %collective-permute-start.13) | collective-permute-done | bytes 524320 | tf_op jit(solution)/shard_map/ppermute | solution.py:264
  90.4 0.2 fusion.14
  90.6 1.8 %collective-permute-start.14 = (bf16[4,64,512]{2,1,0:T(8,128)(2,1)S(1)}, bf16[4,64,512]{2,1,0:T(8,128)(2,1)S(1)}, u32[]{:S(2)}, u32[]{:S(2)}) collective-permute-start(bf16[4,64,512]{2,1,0:T(8,128)(2,1)S(1)} %get-tuple-element.31), channel_id=1, source_target_pairs={{0,4},{1,3},{2,6},{3,1},{4,0},{5,7},{6,2},{7,5},{8,12},{9,11},{10,... | collective-permute-start | bytes 786440 | tf_op jit(solution)/shard_map/ppermute | solution.py:264
  92.4 0.4 collective-permute-start.6
  92.8 4.6 %collective-permute-done.9 = bf16[2,2,216,256]{3,2,0,1:T(8,128)(2,1)S(1)} collective-permute-done((bf16[2,2,216,256]{3,2,0,1:T(8,128)(2,1)S(1)}, bf16[2,2,216,256]{3,2,0,1:T(8,128)(2,1)S(1)}, u32[]{:S(2)}, u32[]{:S(2)}) %collective-permute-start.9) | collective-permute-done | bytes 442400 | tf_op jit(solution)/shard_map/ppermute | solution.py:264
  97.4 0.1 fusion.15
  97.5 1.8 %collective-permute-start.10 = (bf16[2,216,256]{2,1,0:T(8,128)(2,1)S(1)}, bf16[2,216,256]{2,1,0:T(8,128)(2,1)S(1)}, u32[]{:S(2)}, u32[]{:S(2)}) collective-permute-start(bf16[2,216,256]{2,1,0:T(8,128)(2,1)S(1)} %get-tuple-element.33), channel_id=1, source_target_pairs={{0,4},{1,3},{2,6},{3,1},{4,0},{5,7},{6,2},{7,5},{8,12},{9,11},{10,... | collective-permute-start | bytes 663560 | tf_op jit(solution)/shard_map/ppermute | solution.py:264
  99.4 1.6 %collective-permute-start.15 = (bf16[2,64,512]{2,1,0:T(8,128)(2,1)S(1)}, bf16[2,64,512]{2,1,0:T(8,128)(2,1)S(1)}, u32[]{:S(2)}, u32[]{:S(2)}) collective-permute-start(bf16[2,64,512]{2,1,0:T(8,128)(2,1)S(1)} %get-tuple-element.45), channel_id=1, source_target_pairs={{0,8},{1,9},{2,10},{3,11},{4,12},{5,13},{6,14},{7,15},{8,0},{9,1},... | collective-permute-start | bytes 393224 | tf_op jit(solution)/shard_map/ppermute | solution.py:264
  101.1 0.5 collective-permute-start.7
  101.6 2.0 %collective-permute-done.10 = bf16[2,216,256]{2,1,0:T(8,128)(2,1)S(1)} collective-permute-done((bf16[2,216,256]{2,1,0:T(8,128)(2,1)S(1)}, bf16[2,216,256]{2,1,0:T(8,128)(2,1)S(1)}, u32[]{:S(2)}, u32[]{:S(2)}) %collective-permute-start.10) | collective-permute-done | bytes 221216 | tf_op jit(solution)/shard_map/ppermute | solution.py:264
  103.5 1.6 %collective-permute-start.11 = (bf16[216,256]{1,0:T(8,128)(2,1)S(1)}, bf16[216,256]{1,0:T(8,128)(2,1)S(1)}, u32[]{:S(2)}, u32[]{:S(2)}) collective-permute-start(bf16[216,256]{1,0:T(8,128)(2,1)S(1)} %fusion.23), channel_id=1, source_target_pairs={{0,8},{1,9},{2,10},{3,11},{4,12},{5,13},{6,14},{7,15},{8,0},{9,1},... | collective-permute-start | bytes 331784 | tf_op jit(solution)/shard_map/ppermute | solution.py:264
  105.2 0.3 collective-permute-done.15
  105.5 2.6 %collective-permute-start.16 = (bf16[64,512]{1,0:T(8,128)(2,1)S(1)}, bf16[64,512]{1,0:T(8,128)(2,1)S(1)}, u32[]{:S(2)}, u32[]{:S(2)}) collective-permute-start(bf16[64,512]{1,0:T(8,128)(2,1)S(1)} %fusion.25), channel_id=1, source_target_pairs={{0,16},{1,17},{2,18},{3,19},{4,20},{5,21},{6,22},{7,23},{8,24},{9,... | collective-permute-start | bytes 196616 | tf_op jit(solution)/shard_map/ppermute | solution.py:264
  108.1 1.6 %collective-permute-done.11 = bf16[216,256]{1,0:T(8,128)(2,1)S(1)} collective-permute-done((bf16[216,256]{1,0:T(8,128)(2,1)S(1)}, bf16[216,256]{1,0:T(8,128)(2,1)S(1)}, u32[]{:S(2)}, u32[]{:S(2)}) %collective-permute-start.11) | collective-permute-done | bytes 110624 | tf_op jit(solution)/shard_map/ppermute | solution.py:264
  109.7 0.1 select_convert_fusion
  109.8 2.6 %collective-permute-start.12 = (bf16[216,256]{1,0:T(8,128)(2,1)S(1)}, bf16[216,256]{1,0:T(8,128)(2,1)S(1)}, u32[]{:S(2)}, u32[]{:S(2)}) collective-permute-start(bf16[216,256]{1,0:T(8,128)(2,1)S(1)} %select_convert_fusion), channel_id=1, source_target_pairs={{0,16},{1,17},{2,18},{3,19},{4,20},{5,21},{6,22},{7,23},{8,24},{9,... | collective-permute-start | bytes 331784 | tf_op jit(solution)/shard_map/ppermute | solution.py:264
  112.5 0.7 fusion.21
  113.1 4.0 %collective-permute-done.12 = bf16[216,256]{1,0:T(8,128)(2,1)S(1)} collective-permute-done((bf16[216,256]{1,0:T(8,128)(2,1)S(1)}, bf16[216,256]{1,0:T(8,128)(2,1)S(1)}, u32[]{:S(2)}, u32[]{:S(2)}) %collective-permute-start.12) | collective-permute-done | bytes 110624 | tf_op jit(solution)/shard_map/ppermute | solution.py:264
  117.2 0.1 multiply_bitcast_fusion
  117.3 0.8 copy.129
  (63 shorter events, 0.8 us)
Async XLA Ops:
  0.6 24.1 %copy-start.22 = (bf16[512,256]{1,0:T(8,128)(2,1)S(1)}, bf16[512,256]{1,0:T(8,128)(2,1)}, u32[]{:S(2)}) copy-start(bf16[512,256]{1,0:T(8,128)(2,1)} %param.10) | copy-start | bytes 786436
  0.6 8.2 %collective-permute-start = (bf16[128,512]{1,0:T(8,128)(2,1)}, bf16[128,512]{1,0:T(8,128)(2,1)S(1)}, u32[]{:S(2)}, u32[]{:S(2)}) collective-permute-start(bf16[128,512]{1,0:T(8,128)(2,1)} %cur.1), channel_id=1, source_target_pairs={{0,1},{1,2},{2,3},{3,4},{4,5},{5,6},{6,7},{7,8},{8,9},{9,10},{10,1... | collective-permute-start | bytes 393224 | tf_op jit(solution)/shard_map/ppermute | solution.py:264
  4.7 20.9 %copy-start.11 = (s32[1,8,128]{2,1,0:T(8,128)S(1)}, s32[1,8,128]{2,1,0:T(8,128)}, u32[]{:S(2)}) copy-start(s32[1,8,128]{2,1,0:T(8,128)} %param.18) | copy-start | bytes 12292
  8.8 1.0 copy-start.2
  9.8 0.7 copy-start.10
  10.5 1.6 %copy-start.12 = (bf16[2048,512]{1,0:T(8,128)(2,1)S(1)}, bf16[2048,512]{1,0:T(8,128)(2,1)}, u32[]{:S(2)}) copy-start(bf16[2048,512]{1,0:T(8,128)(2,1)} %w_in.1) | copy-start | bytes 6291460
  12.0 0.9 copy-start.13
  16.8 0.7 copy-start.3
  17.5 11.5 %collective-permute-start.2 = (bf16[256,256]{1,0:T(8,128)(2,1)S(1)}, bf16[256,256]{1,0:T(8,128)(2,1)S(1)}, u32[]{:S(2)}, u32[]{:S(2)}) collective-permute-start(bf16[256,256]{1,0:T(8,128)(2,1)S(1)} %get-tuple-element.47), channel_id=1, source_target_pairs={{1,0},{2,1},{3,2},{4,3},{5,4},{6,5},{7,6},{8,7},{9,8},{10,9},{11,1... | collective-permute-start | bytes 393224 | tf_op jit(solution)/shard_map/ppermute | solution.py:264
  18.8 10.9 %collective-permute-start.1 = (bf16[256,256]{1,0:T(8,128)(2,1)S(1)}, bf16[256,256]{1,0:T(8,128)(2,1)S(1)}, u32[]{:S(2)}, u32[]{:S(2)}) collective-permute-start(bf16[256,256]{1,0:T(8,128)(2,1)S(1)} %get-tuple-element.48), channel_id=1, source_target_pairs={{0,1},{1,2},{2,3},{3,4},{4,5},{5,6},{6,7},{7,8},{8,9},{9,10},{10,1... | collective-permute-start | bytes 393224 | tf_op jit(solution)/shard_map/ppermute | solution.py:264
  25.6 5.3 %copy-start.4 = (bf16[512,256]{1,0:T(8,128)(2,1)S(1)}, bf16[512,256]{1,0:T(8,128)(2,1)}, u32[]{:S(2)}) copy-start(bf16[512,256]{1,0:T(8,128)(2,1)} %copy-done.3) | copy-start | bytes 786436
  25.6 5.3 %copy-start.6 = (bf16[512,256]{0,1:T(8,128)(2,1)S(1)}, bf16[512,256]{0,1:T(8,128)(2,1)}, u32[]{:S(2)}) copy-start(bf16[512,256]{0,1:T(8,128)(2,1)} %copy.71) | copy-start | bytes 786436
  25.6 5.3 %copy-start.8 = (s32[108,128]{0,1:T(8,128)S(1)}, s32[108,128]{0,1:T(8,128)}, u32[]{:S(2)}) copy-start(s32[108,128]{0,1:T(8,128)} %copy.68) | copy-start | bytes 165892
  29.0 20.6 %copy-start = (f32[2048,512]{1,0:T(8,128)}, f32[2048,512]{1,0:T(8,128)S(1)}, u32[]{:S(2)}) copy-start(f32[2048,512]{1,0:T(8,128)S(1)} %down_weight.1) | copy-start | bytes 12582916
  29.0 0.7 copy-start.14
  29.7 1.1 copy-start.17
  30.9 0.9 copy-start.15
  31.8 0.9 copy-start.18
  46.7 4.0 %copy-start.20 = (f32[512,256]{1,0:T(8,128)}, f32[512,256]{1,0:T(8,128)S(1)}, u32[]{:S(2)}) copy-start(f32[512,256]{1,0:T(8,128)S(1)} %get-tuple-element.17.refs_6_) | copy-start | bytes 1572868
  47.8 5.9 %collective-permute-start.4 = (bf16[2,2,2,216,256]{4,3,1,0,2:T(8,128)(2,1)}, bf16[2,2,2,216,256]{4,3,1,0,2:T(8,128)(2,1)}, u32[]{:S(2)}, u32[]{:S(2)}) collective-permute-start(bf16[2,2,2,216,256]{4,3,1,0,2:T(8,128)(2,1)} %fusion.4), channel_id=1, source_target_pairs={{0,1},{1,0},{2,3},{3,2},{4,5},{5,4},{6,7},{7,6},{8,9},{9,8},{10,11... | collective-permute-start | bytes 2654216 | tf_op jit(solution)/shard_map/ppermute | solution.py:264
  50.7 9.3 %collective-permute-start.3 = (bf16[4,2,2,64,512]{4,3,2,1,0:T(8,128)(2,1)}, bf16[4,2,2,64,512]{4,3,2,1,0:T(8,128)(2,1)}, u32[]{:S(2)}, u32[]{:S(2)}) collective-permute-start(bf16[4,2,2,64,512]{4,3,2,1,0:T(8,128)(2,1)} %fusion), channel_id=1, source_target_pairs={{0,1},{1,0},{2,3},{3,2},{4,5},{5,4},{6,7},{7,6},{8,9},{9,8},{10,11... | collective-permute-start | bytes 3145736 | tf_op jit(solution)/shard_map/ppermute | solution.py:264
  50.7 2.8 %copy-start.1 = (f32[2048,512]{1,0:T(8,128)S(1)}, f32[2048,512]{1,0:T(8,128)}, u32[]{:S(2)}) copy-start(f32[2048,512]{1,0:T(8,128)} %copy-done) | copy-start | bytes 12582916
  55.0 5.0 %copy-start.5 = (bf16[512,256]{1,0:T(8,128)(2,1)S(1)}, bf16[512,256]{1,0:T(8,128)(2,1)}, u32[]{:S(2)}) copy-start(bf16[512,256]{1,0:T(8,128)(2,1)} %copy-done.3) | copy-start | bytes 786436
  55.0 5.0 %copy-start.7 = (bf16[512,256]{0,1:T(8,128)(2,1)S(1)}, bf16[512,256]{0,1:T(8,128)(2,1)}, u32[]{:S(2)}) copy-start(bf16[512,256]{0,1:T(8,128)(2,1)} %copy.71) | copy-start | bytes 786436
  55.0 5.0 %copy-start.9 = (s32[108,128]{0,1:T(8,128)S(1)}, s32[108,128]{0,1:T(8,128)}, u32[]{:S(2)}) copy-start(s32[108,128]{0,1:T(8,128)} %copy.68) | copy-start | bytes 165892
  55.0 5.0 %copy-start.16 = (bf16[256,256]{1,0:T(8,128)(2,1)S(1)}, bf16[256,256]{1,0:T(8,128)(2,1)}, u32[]{:S(2)}) copy-start(bf16[256,256]{1,0:T(8,128)(2,1)} %copy-done.14) | copy-start | bytes 393220
  55.0 5.0 %copy-start.19 = (bf16[256,256]{1,0:T(8,128)(2,1)S(1)}, bf16[256,256]{1,0:T(8,128)(2,1)}, u32[]{:S(2)}) copy-start(bf16[256,256]{1,0:T(8,128)(2,1)} %copy-done.17) | copy-start | bytes 393220
  55.0 5.0 %copy-start.21 = (f32[512,256]{1,0:T(8,128)S(1)}, f32[512,256]{1,0:T(8,128)}, u32[]{:S(2)}) copy-start(f32[512,256]{1,0:T(8,128)} %copy-done.20) | copy-start | bytes 1572868
  56.3 36.0 %collective-permute-start.5 = (bf16[2,2,216,256]{3,2,0,1:T(8,128)(2,1)S(1)}, bf16[2,2,216,256]{3,2,0,1:T(8,128)(2,1)S(1)}, u32[]{:S(2)}, u32[]{:S(2)}) collective-permute-start(bf16[2,2,216,256]{3,2,0,1:T(8,128)(2,1)S(1)} %fusion.11), channel_id=1, source_target_pairs={{0,2},{1,5},{2,0},{3,7},{4,6},{5,1},{6,4},{7,3},{8,10},{9,13},{10,... | collective-permute-start | bytes 1327112 | tf_op jit(solution)/shard_map/ppermute | solution.py:264
  77.4 6.1 %collective-permute-start.8 = (bf16[2,2,2,216,256]{4,3,1,0,2:T(8,128)(2,1)S(1)}, bf16[2,2,2,216,256]{4,3,1,0,2:T(8,128)(2,1)S(1)}, u32[]{:S(2)}, u32[]{:S(2)}) collective-permute-start(bf16[2,2,2,216,256]{4,3,1,0,2:T(8,128)(2,1)S(1)} %fusion.5), channel_id=1, source_target_pairs={{0,1},{1,0},{2,3},{3,2},{4,5},{5,4},{6,7},{7,6},{8,9},{9,8},{10,11... | collective-permute-start | bytes 2654216 | tf_op jit(solution)/shard_map/ppermute | solution.py:264
  80.5 9.9 %collective-permute-start.13 = (bf16[4,2,64,512]{3,2,0,1:T(8,128)(2,1)S(1)}, bf16[4,2,64,512]{3,2,0,1:T(8,128)(2,1)S(1)}, u32[]{:S(2)}, u32[]{:S(2)}) collective-permute-start(bf16[4,2,64,512]{3,2,0,1:T(8,128)(2,1)S(1)} %fusion.2), channel_id=1, source_target_pairs={{0,2},{1,5},{2,0},{3,7},{4,6},{5,1},{6,4},{7,3},{8,10},{9,13},{10,... | collective-permute-start | bytes 1572872 | tf_op jit(solution)/shard_map/ppermute | solution.py:264
  84.1 13.3 %collective-permute-start.9 = (bf16[2,2,216,256]{3,2,0,1:T(8,128)(2,1)S(1)}, bf16[2,2,216,256]{3,2,0,1:T(8,128)(2,1)S(1)}, u32[]{:S(2)}, u32[]{:S(2)}) collective-permute-start(bf16[2,2,216,256]{3,2,0,1:T(8,128)(2,1)S(1)} %get-tuple-element.39), channel_id=1, source_target_pairs={{0,2},{1,5},{2,0},{3,7},{4,6},{5,1},{6,4},{7,3},{8,10},{9,13},{10,... | collective-permute-start | bytes 1327112 | tf_op jit(solution)/shard_map/ppermute | solution.py:264
  90.6 8.7 %collective-permute-start.14 = (bf16[4,64,512]{2,1,0:T(8,128)(2,1)S(1)}, bf16[4,64,512]{2,1,0:T(8,128)(2,1)S(1)}, u32[]{:S(2)}, u32[]{:S(2)}) collective-permute-start(bf16[4,64,512]{2,1,0:T(8,128)(2,1)S(1)} %get-tuple-element.31), channel_id=1, source_target_pairs={{0,4},{1,3},{2,6},{3,1},{4,0},{5,7},{6,2},{7,5},{8,12},{9,11},{10,... | collective-permute-start | bytes 786440 | tf_op jit(solution)/shard_map/ppermute | solution.py:264
  92.4 8.6 %collective-permute-start.6 = (bf16[2,216,256]{2,1,0:T(8,128)(2,1)S(1)}, bf16[2,216,256]{2,1,0:T(8,128)(2,1)S(1)}, u32[]{:S(2)}, u32[]{:S(2)}) collective-permute-start(bf16[2,216,256]{2,1,0:T(8,128)(2,1)S(1)} %fusion.16), channel_id=1, source_target_pairs={{0,4},{1,3},{2,6},{3,1},{4,0},{5,7},{6,2},{7,5},{8,12},{9,11},{10,... | collective-permute-start | bytes 663560 | tf_op jit(solution)/shard_map/ppermute | solution.py:264
  97.5 6.0 %collective-permute-start.10 = (bf16[2,216,256]{2,1,0:T(8,128)(2,1)S(1)}, bf16[2,216,256]{2,1,0:T(8,128)(2,1)S(1)}, u32[]{:S(2)}, u32[]{:S(2)}) collective-permute-start(bf16[2,216,256]{2,1,0:T(8,128)(2,1)S(1)} %get-tuple-element.33), channel_id=1, source_target_pairs={{0,4},{1,3},{2,6},{3,1},{4,0},{5,7},{6,2},{7,5},{8,12},{9,11},{10,... | collective-permute-start | bytes 663560 | tf_op jit(solution)/shard_map/ppermute | solution.py:264
  99.4 6.1 %collective-permute-start.15 = (bf16[2,64,512]{2,1,0:T(8,128)(2,1)S(1)}, bf16[2,64,512]{2,1,0:T(8,128)(2,1)S(1)}, u32[]{:S(2)}, u32[]{:S(2)}) collective-permute-start(bf16[2,64,512]{2,1,0:T(8,128)(2,1)S(1)} %get-tuple-element.45), channel_id=1, source_target_pairs={{0,8},{1,9},{2,10},{3,11},{4,12},{5,13},{6,14},{7,15},{8,0},{9,1},... | collective-permute-start | bytes 393224 | tf_op jit(solution)/shard_map/ppermute | solution.py:264
  101.1 7.1 %collective-permute-start.7 = (bf16[216,256]{1,0:T(8,128)(2,1)S(1)}, bf16[216,256]{1,0:T(8,128)(2,1)S(1)}, u32[]{:S(2)}, u32[]{:S(2)}) collective-permute-start(bf16[216,256]{1,0:T(8,128)(2,1)S(1)} %fusion.22), channel_id=1, source_target_pairs={{0,8},{1,9},{2,10},{3,11},{4,12},{5,13},{6,14},{7,15},{8,0},{9,1},... | collective-permute-start | bytes 331784 | tf_op jit(solution)/shard_map/ppermute | solution.py:264
  103.5 6.1 %collective-permute-start.11 = (bf16[216,256]{1,0:T(8,128)(2,1)S(1)}, bf16[216,256]{1,0:T(8,128)(2,1)S(1)}, u32[]{:S(2)}, u32[]{:S(2)}) collective-permute-start(bf16[216,256]{1,0:T(8,128)(2,1)S(1)} %fusion.23), channel_id=1, source_target_pairs={{0,8},{1,9},{2,10},{3,11},{4,12},{5,13},{6,14},{7,15},{8,0},{9,1},... | collective-permute-start | bytes 331784 | tf_op jit(solution)/shard_map/ppermute | solution.py:264
  105.5 7.0 %collective-permute-start.16 = (bf16[64,512]{1,0:T(8,128)(2,1)S(1)}, bf16[64,512]{1,0:T(8,128)(2,1)S(1)}, u32[]{:S(2)}, u32[]{:S(2)}) collective-permute-start(bf16[64,512]{1,0:T(8,128)(2,1)S(1)} %fusion.25), channel_id=1, source_target_pairs={{0,16},{1,17},{2,18},{3,19},{4,20},{5,21},{6,22},{7,23},{8,24},{9,... | collective-permute-start | bytes 196616 | tf_op jit(solution)/shard_map/ppermute | solution.py:264
  109.8 7.4 %collective-permute-start.12 = (bf16[216,256]{1,0:T(8,128)(2,1)S(1)}, bf16[216,256]{1,0:T(8,128)(2,1)S(1)}, u32[]{:S(2)}, u32[]{:S(2)}) collective-permute-start(bf16[216,256]{1,0:T(8,128)(2,1)S(1)} %select_convert_fusion), channel_id=1, source_target_pairs={{0,16},{1,17},{2,18},{3,19},{4,20},{5,21},{6,22},{7,23},{8,24},{9,... | collective-permute-start | bytes 331784 | tf_op jit(solution)/shard_map/ppermute | solution.py:264

commit v3 on v2

v3 whole, which is shorter than its diff:
```python
import functools
import math

import jax
import jax.numpy as jnp
from jax import lax
from jax.experimental import pallas as pl
from jax.experimental.pallas import tpu as pltpu
from jax.sharding import PartitionSpec as P

HB = 2
BF = jnp.bfloat16
F32 = jnp.float32


def dot(a, b):
    return lax.dot_general(a, b, (((1,), (0,)), ((), ())), preferred_element_type=F32)


def dot_nt(a, b):
    return lax.dot_general(a, b, (((1,), (1,)), ((), ())), preferred_element_type=F32)


def one_hot(index, shape, axis):
    return jnp.where(index == lax.broadcasted_iota(jnp.int32, shape, axis), 1.0, 0.0).astype(BF)


def split(total, keep, send, core):
    pairs, rows = keep.shape[:2]
    for j in range(pairs):
        mine = pl.multiple_of((2 * j + core) * rows, 8)
        other = pl.multiple_of((2 * j + 1 - core) * rows, 8)
        keep[j] = total[pl.ds(mine, rows), :]
        send[j] = total[pl.ds(other, rows), :].astype(BF)


def halves(total, rows):
    shape = (total[0] // (2 * rows), rows, total[1])
    return (jax.ShapeDtypeStruct(shape, F32), jax.ShapeDtypeStruct(shape, BF))


def split_outside(total, rows, core):
    pairs = total.reshape(-1, 2, rows, total.shape[1])
    return taken(pairs, 1, core), taken(pairs, 1, 1 - core).astype(BF)


def cost(flops, nbytes):
    return pl.CostEstimate(flops=flops, bytes_accessed=nbytes, transcendentals=0)


def fetch(pairs, sems):
    copies = [pltpu.make_async_copy(a, b, sems.at[i]) for i, (a, b) in enumerate(pairs)]
    for copy in copies:
        copy.start()
    return copies


def down_grad_kernel(
    prev, cur, par_t, rows_in, pre_in, w_in, gpre, gath, ext, rows, pre, w, contrib, pick, sems
):
    children, slots = rows.shape
    count, channels = pre.shape
    coarse = prev.shape[0]
    pieces = [
        (rows_in, rows),
        (cur, ext.at[pl.ds(coarse, cur.shape[0]), :]),
        (prev, ext.at[pl.ds(0, coarse), :]),
        (pre_in, pre),
    ]
    own = [pl.ds(c * channels, channels) for c in range(children)]
    copies = fetch(pieces + [(w_in.at[at, :], w.at[at, :]) for at in own], sems)
    copies[0].wait()
    for c in range(children):
        pick[:, pl.ds(c * slots, slots)] = one_hot(rows[c : c + 1, :], (count, slots), 0)
    copies[1].wait()
    copies[2].wait()
    for c in range(children):
        mine = pl.ds(c * slots, slots)
        parents = one_hot(par_t[:, c : c + 1], (slots, ext.shape[0]), 1)
        got = dot(parents, ext[...]).astype(BF)
        gath[mine, :] = got
        copies[4 + c].wait()
        contrib[mine, :] = dot_nt(got, w[own[c], :]).astype(BF)
    grad = dot(pick[...], contrib[...])
    copies[3].wait()
    gpre[...] = jnp.where(pre[...].astype(F32) > 0, grad, 0.0).astype(BF)


def down_grad(prev, cur, par_t, rows, pre, w):
    children, slots = rows.shape
    count, channels = pre.shape
    width = cur.shape[1]
    anywhere = pl.BlockSpec(memory_space=pl.ANY)
    hbm = pl.BlockSpec(memory_space=pltpu.HBM)
    vmem = pl.BlockSpec(memory_space=pltpu.VMEM)
    return pl.pallas_call(
        down_grad_kernel,
        out_shape=(
            jax.ShapeDtypeStruct((count, channels), BF),
            jax.ShapeDtypeStruct((children * slots, width), BF),
        ),
        in_specs=[anywhere, hbm, vmem, hbm, hbm, hbm],
        out_specs=(vmem, vmem),
        scratch_shapes=[
            pltpu.VMEM((prev.shape[0] + cur.shape[0], width), BF),
            pltpu.VMEM(rows.shape, jnp.int32),
            pltpu.VMEM(pre.shape, BF),
            pltpu.VMEM(w.shape, BF),
            pltpu.VMEM((children * slots, channels), BF),
            pltpu.VMEM((count, children * slots), BF),
            pltpu.SemaphoreType.DMA((4 + children,)),
        ],
        compiler_params=pltpu.CompilerParams(vmem_limit_bytes=62 << 20),
        cost_estimate=cost(1 << 30, 4 << 20),
        name="down_grad",
    )(prev, cur, par_t, rows, pre, w)


def down_weight_kernel(core, act_t, rows_in, gath, *refs):
    *outs, total, rows, sems = refs
    children, slots = rows.shape
    channels, count = act_t.shape
    fetch([(rows_in, rows)], sems)[0].wait()
    for c in range(children):
        pick = one_hot(rows[c : c + 1, :], (count, slots), 0)
        chosen = dot(act_t[...], pick).astype(BF)
        total[pl.ds(c * channels, channels), :] = dot(chosen, gath[pl.ds(c * slots, slots), :])
    if outs:
        split(total, *outs, core[0])


def down_weight(core, act_t, rows, gath, shard):
    channels = act_t.shape[0]
    children = rows.shape[0]
    total = (children * channels, gath.shape[1])
    hbm = pl.BlockSpec(memory_space=pltpu.HBM)
    vmem = pl.BlockSpec(memory_space=pltpu.VMEM)
    inside = shard % 8 == 0
    out = pl.pallas_call(
        down_weight_kernel,
        out_shape=halves(total, shard) if inside else jax.ShapeDtypeStruct(total, F32),
        in_specs=[pl.BlockSpec(memory_space=pltpu.SMEM), vmem, hbm, vmem],
        out_specs=(vmem, vmem) if inside else vmem,
        scratch_shapes=[pltpu.VMEM(total, F32)] * inside
        + [
            pltpu.VMEM(rows.shape, jnp.int32),
            pltpu.SemaphoreType.DMA((1,)),
        ],
        compiler_params=pltpu.CompilerParams(vmem_limit_bytes=56 << 20),
        cost_estimate=cost(1 << 30, 6 << 20),
        name="down_weight",
    )(core, act_t, rows, gath)
    return out if inside else split_outside(out, shard, core[0])


def conv_plan(kernel, channels, quarters):
    quarter = kernel * channels // 4
    plan, out = [], 0
    for q in quarters:
        row = q * quarter
        while row < (q + 1) * quarter:
            k, first = divmod(row, channels)
            last = min(channels, (q + 1) * quarter - k * channels)
            plan.append((k, first, last, out))
            out += last - first
            row += last - first
    return plan


def conv_kernel(plan, slots, final, inside, *refs):
    core, src, tgt, tab_in, before, own, after, feats_in, w, *rest = refs
    if final:
        partial_in, *rest = rest
    grad, *rest = rest
    if inside:
        keep, send, *rest = rest
    total, tab, ext, feats_t, wbuf, acc, col0, col1, sems = rest
    cols = (col0, col1)
    rows = tab.shape[0]
    blocks = col0.shape[0]
    channels, count = feats_t.shape
    halo = before.shape[0]
    side = halo // rows
    pieces = [(tab_in, tab)]
    pieces += [(own.at[pl.ds(b * rows, rows), :], ext.at[side + b]) for b in range(blocks)]
    pieces += [(before.at[pl.ds(b * rows, rows), :], ext.at[b]) for b in range(side)]
    pieces += [
        (after.at[pl.ds(b * rows, rows), :], ext.at[side + blocks + b]) for b in range(side)
    ]
    pieces.append((feats_in, feats_t))
    if final:
        pieces.append((partial_in, acc))
    early = len(pieces)
    for at, (k, first, last, out) in enumerate(plan):
        pieces.append((w.at[pl.ds(k * channels, channels), :], wbuf.at[at]))
    copies = fetch(pieces, sems)
    lanes = lax.broadcasted_iota(jnp.int32, (rows, rows), 1).astype(jnp.int16)
    one, zero = jnp.ones((), BF), jnp.zeros((), BF)

    def gather(k, col):
        col[...] = jnp.zeros_like(col)
        for p in range(slots):
            q = k * slots + p
            index = jnp.broadcast_to(tab[:, q : q + 1], (rows, rows)).astype(jnp.int16)
            pick = jnp.where(index == lanes, one, zero)
            piece = dot(pick, ext[tgt[q]]).astype(BF)
            owner = src[q]
            col[owner] = col[owner] + piece

    for copy in copies[:early]:
        copy.wait()
    if not final:
        acc[...] = jnp.zeros_like(acc)
    gather(plan[0][0], cols[0])
    for at, (k, first, last, out) in enumerate(plan):
        if at + 1 < len(plan):
            gather(plan[at + 1][0], cols[(at + 1) % 2])
        column = cols[at % 2][...].reshape(count, channels)
        total[pl.ds(out, last - first), :] = dot(feats_t[pl.ds(first, last - first), :], column)
        copies[early + at].wait()
        if first == 0:
            acc[...] += dot_nt(column, wbuf[at])
    grad[...] = acc[...].astype(grad.dtype)
    if inside:
        split(total, keep, send, core[0])


def conv(core, src, tgt, tab, before, own, after, feats_t, w, quarters, shard, partial=None):
    channels, count = feats_t.shape
    kernel = w.shape[0] // channels
    rows = tab.shape[0]
    slots = tab.shape[1] // kernel
    plan = conv_plan(kernel, channels, quarters)
    final = partial is not None
    inside = shard % 8 == 0
    anywhere = pl.BlockSpec(memory_space=pl.ANY)
    hbm = pl.BlockSpec(memory_space=pltpu.HBM)
    vmem = pl.BlockSpec(memory_space=pltpu.VMEM)
    smem = pl.BlockSpec(memory_space=pltpu.SMEM)
    total = (len(quarters) * kernel * channels // 4, channels)
    ext_rows = count + before.shape[0] + after.shape[0]
    block = (rows, channels)
    grad = jax.ShapeDtypeStruct((count, channels), BF if final else F32)
    weight = halves(total, shard) if inside else (jax.ShapeDtypeStruct(total, F32),)
    out = pl.pallas_call(
        functools.partial(conv_kernel, plan, slots, final, inside),
        out_shape=(grad,) + weight,
        in_specs=[smem] * 3 + [anywhere] * 5 + [hbm] + [anywhere] * final,
        out_specs=(vmem,) * (1 + len(weight)),
        scratch_shapes=[pltpu.VMEM(total, F32)] * inside
        + [
            pltpu.VMEM(tab.shape, jnp.int32),
            pltpu.VMEM((ext_rows // rows,) + block, BF),
            pltpu.VMEM((channels, count), BF),
            pltpu.VMEM((len(plan), channels, channels), BF),
            pltpu.VMEM((count, channels), F32),
            pltpu.VMEM((count // rows,) + block, BF),
            pltpu.VMEM((count // rows,) + block, BF),
            pltpu.SemaphoreType.DMA((3 + ext_rows // rows + len(plan),)),
        ],
        compiler_params=pltpu.CompilerParams(vmem_limit_bytes=56 << 20),
        cost_estimate=cost(12 << 30, 8 << 20),
        name="conv",
    )(core, src, tgt, tab, before, own, after, feats_t, w, *([partial] if final else []))
    return out if inside else (out[0],) + split_outside(out[1], shard, core[0])


def moved(x, peers, to):
    pairs = [(i, to(i)) for i in range(peers)]
    return lax.ppermute(x, "space", [(i, j) for i, j in pairs if j is not None and 0 <= j < peers])


def taken(x, axis, digit):
    return lax.dynamic_index_in_dim(x, digit, axis=axis, keepdims=False)


def low_steps(bits):
    left = [list(range(bits - 1, -1, -1)) for core in range(2)]
    steps = []
    for j in range(bits):
        by = (j, (j + bits // 2) % bits)
        steps.append((by, [left[core].index(by[core]) for core in range(2)]))
        for core in range(2):
            left[core].remove(by[core])
    return steps


def fold_low(keep, got, me, step):
    core = me % 2
    by, axes = step
    bit = jnp.where(core == 0, me >> (1 + by[0]), me >> (1 + by[1])) % 2

    def half(x, digit):
        if axes[0] == axes[1]:
            return taken(x, 1 + axes[0], digit)
        return jnp.where(core == 0, taken(x, 1 + axes[0], digit), taken(x, 1 + axes[1], digit))

    def piece(digit):
        return half(keep, digit) + half(got, digit).astype(F32)

    return piece(bit), piece(1 - bit).astype(BF), lambda i: i ^ (2 << by[i % 2])


def fold_bit(keep, got, me, peers, stride, first):
    bit = me // stride % 2
    axis = keep.ndim - 3

    def piece(digit):
        return taken(keep, axis, digit) + taken(got, axis, digit).astype(F32)

    mine = bit ^ first
    sent = piece(1 - mine).astype(BF)
    return piece(mine), moved(sent, peers, lambda i: i ^ stride)


def per_device(
    feats,
    pre_act,
    coarse_grad,
    w_sub,
    w_down,
    pair_src,
    pair_tgt,
    pair_rows,
    down_rows,
    down_parent,
):
    peers = lax.axis_size("space")
    me = lax.axis_index("space")
    row_count, channels = feats.shape
    block_rows = pair_rows.shape[-1]
    out_width = coarse_grad.shape[1]
    kernel = pair_src.shape[1]
    children = down_rows.shape[1]
    scale = 1.0 / math.sqrt(peers * row_count)
    bits = (peers // 8).bit_length() - 1
    steps = low_steps(bits)
    near, far = peers // 4, peers // 2

    previous = moved(coarse_grad[-block_rows:], peers, lambda i: i + 1)
    grad_pre, gathered = down_grad(
        previous, coarse_grad, down_parent[0].T, down_rows[0], pre_act, w_down
    )
    halo = HB * block_rows
    before = moved(grad_pre[-halo:], peers, lambda i: i + 1)
    after = moved(grad_pre[:halo], peers, lambda i: i - 1)

    feats_t = feats.T
    act_t = jnp.maximum(pre_act, 0).T
    src = pair_src[0].reshape(-1)
    tgt = pair_tgt[0].reshape(-1)
    tab = pair_rows[0].reshape(-1, block_rows).T
    core = (me % 2).reshape(1)

    def across(x):
        return moved(x, peers, lambda i: i ^ 1)

    def spread(x, high):
        return x.reshape((high,) + (2,) * bits + x.shape[-2:])

    down_keep, down_send = down_weight(
        core, act_t, down_rows[0], gathered, children * channels // peers
    )
    shard = kernel * channels // peers
    common = (core, src, tgt, tab, before, grad_pre, after, feats_t, w_sub)
    pinned = lax.optimization_barrier

    down_got = across(down_send)
    partial, outer_keep, outer_send = conv(*common, (0, 3), shard)
    partial, outer_keep, outer_send, down_got = pinned(
        (partial, outer_keep, outer_send, down_got)
    )
    down_keep, down_got = spread(down_keep, 4), spread(down_got, 4)
    down_keep, down_send, to = fold_low(down_keep, down_got, me, steps[0])
    down_got = moved(down_send, peers, to)
    outer_got = across(outer_send)
    grad_in, inner_keep, inner_send = conv(*common, (1, 2), shard, partial)
    grad_in, inner_keep, inner_send, down_got, outer_got = pinned(
        (grad_in, inner_keep, inner_send, down_got, outer_got)
    )
    inner_got = across(inner_send)
    outer_keep, outer_got = spread(outer_keep, 2), spread(outer_got, 2)
    inner_keep, inner_got = spread(inner_keep, 2), spread(inner_got, 2)

    for at, step in enumerate(steps):
        if at > 0:
            down_keep, down_send, to = fold_low(down_keep, down_got, me, step)
            down_got = moved(down_send, peers, to)
        outer_keep, outer_send, to = fold_low(outer_keep, outer_got, me, step)
        outer_got = moved(outer_send, peers, to)
        inner_keep, inner_send, to = fold_low(inner_keep, inner_got, me, step)
        inner_got = moved(inner_send, peers, to)

    down_keep = down_keep.reshape((2, 2) + down_keep.shape[-2:])
    down_got = down_got.reshape((2, 2) + down_got.shape[-2:])
    down_keep, down_got = fold_bit(down_keep, down_got, me, peers, near, 0)
    outer_keep, outer_got = fold_bit(outer_keep, outer_got, me, peers, near, 0)
    inner_keep, inner_got = fold_bit(inner_keep, inner_got, me, peers, near, 1)
    down_keep, down_got = fold_bit(down_keep, down_got, me, peers, far, 0)
    down_sum = down_keep + down_got.astype(F32)

    digit = me // near
    is_outer = (digit == 0) | (digit == 3)
    outer_sum = outer_keep + outer_got.astype(F32)
    inner_sum = inner_keep + inner_got.astype(F32)
    sent = jnp.where(is_outer, inner_sum, outer_sum).astype(BF)
    sub_sum = jnp.where(is_outer, outer_sum, inner_sum)
    sub_sum = sub_sum + moved(sent, peers, lambda i: i ^ far).astype(F32)
    return (grad_in, sub_sum.reshape(-1) * scale, down_sum * scale)


def solution(mesh):
    rows = ("scene", "space")
    placed = (
        P(rows, None),
        P(rows, None),
        P(rows, None),
        P(),
        P(),
        P(rows, None, None),
        P(rows, None, None),
        P(rows, None, None, None),
        P(rows, None, None),
        P(rows, None, None),
    )
    return jax.shard_map(
        per_device,
        mesh=mesh,
        in_specs=placed,
        out_specs=(P(rows, None), P(rows), P(rows, None)),
        check_vma=False,
    )
```

time: 119 us -> 105 us (0.88)
  local copies, waits for them, and re-layouts: 23.1 us -> 17.2 us
  other arithmetic: 8.02 us -> 3.7 us
  starting transfers between devices: 29.1 us -> 33.2 us
  waiting for transfers between devices: 18.3 us -> 14.3 us
  Pallas kernels: 38.5 us -> 34.9 us
    pallas_call x3, Pallas kernels: 34.7 us -> 29 us  [the longest x2 23.4 us: conv(): pl.pallas_call(functools.partial(conv_kernel, plan, slots, final, inside)...]
    ppermute x17, starting transfers between devices: 29.1 us -> 33.2 us  [moved(): lax.ppermute(x, 'space', [(i, j) for i, j in pairs if j is not None and 0...]
    ppermute x17, waiting for transfers between devices: 18.3 us -> 14.3 us  [moved(): lax.ppermute(x, 'space', [(i, j) for i, j in pairs if j is not None and 0...]
    another operation x0 -> x3, local copies, waits for them, and re-layouts: none -> 2.98 us  [the longest x1 1.65 us: per_device(): tab = pair_rows[0].reshape(-1, block_rows).T]
    unnamed x50 -> x22, local copies, waits for them, and re-layouts: 12.9 us -> 10.3 us
    dynamic_slice x4, local copies, waits for them, and re-layouts: 4.72 us -> 2.3 us  [taken(): return lax.dynamic_index_in_dim(x, digit, axis=axis, keepdims=False)]
    convert_element_type x3 -> x0, local copies, waits for them, and re-layouts: 2.31 us -> none  [fold_core(): got = moved(taken(x, axis, 1 - core).astype(BF), peers, lambda i: i ^ 1)]
    pallas_call x1, Pallas kernels: 3.82 us -> 5.87 us  [down_grad(): pl.pallas_call(down_grad_kernel, out_shape=(jax.ShapeDtypeStruct((count,...]
  transfers between devices with their start and end apart: 17 -> 17, of which waited for: 6 -> 6; matrix products, arithmetic and copies ran while one was open for 17% -> 14% of each run, Pallas kernels for 17% -> 28%
where the time goes in v3:
time: 105 us; the launch traced here: 104 us
  Pallas kernels  34.9 us (33%)
  starting transfers between devices  33.2 us (32%)
  local copies, waits for them, and re-layouts  17.2 us (16%)
  waiting for transfers between devices  14.3 us (14%)
  other arithmetic  3.7 us (4%)
  between operations  1.14 us (1%)
    ppermute x17, starting transfers between devices, moved(): lax.ppermute(x, 'space', [(i, j) for i, j in pairs if j is not None and 0...  33.2 us
    pallas_call x2, Pallas kernels, conv(): pl.pallas_call(functools.partial(conv_kernel, plan, slots, final, inside)...  23.4 us
    ppermute x17, waiting for transfers between devices, moved(): lax.ppermute(x, 'space', [(i, j) for i, j in pairs if j is not None and 0...  14.3 us
    unnamed x22, local copies, waits for them, and re-layouts  10.3 us
    pallas_call x1, Pallas kernels, down_grad(): pl.pallas_call(down_grad_kernel, out_shape=(jax.ShapeDtypeStruct((count,...  5.87 us
    pallas_call x1, Pallas kernels, down_weight(): pl.pallas_call(down_weight_kernel, out_shape=halves(total, shard) if insi...  5.69 us
    dynamic_slice x4, local copies, waits for them, and re-layouts, taken(): return lax.dynamic_index_in_dim(x, digit, axis=axis, keepdims=False)  2.3 us
  transfers between devices with their start and end apart: 17, of which 6 were waited for; matrix products, arithmetic and copies ran while one was open for 14% of the time, Pallas kernels for 28%

profile of v3, /device:TPU:0, one launch (start us, length us, event | category | flops | bytes accessed | tf_op | source)
XLA Modules:
  0.0 104.4 jit_solution(11527276479304501043)
XLA Ops:
  0.6 2.4 %collective-permute-start = (bf16[128,512]{1,0:T(8,128)(2,1)}, bf16[128,512]{1,0:T(8,128)(2,1)S(1)}, u32[]{:S(2)}, u32[]{:S(2)}) collective-permute-start(bf16[128,512]{1,0:T(8,128)(2,1)} %cur.1), channel_id=1, source_target_pairs={{0,1},{1,2},{2,3},{3,4},{4,5},{5,6},{6,7},{7,8},{8,9},{9,10},{10,1... | collective-permute-start | bytes 393224 | tf_op jit(solution)/shard_map/ppermute | solution.py:270
  3.1 0.8 copy.19
  3.9 0.7 reshape_squeeze.9.refs_1_
  4.6 0.8 copy.20
  5.3 0.7 reshape_squeeze.10.refs_2_
  6.0 1.4 %copy.22 = s32[1,8,128]{1,2,0:T(8,128)} copy(s32[1,8,128]{2,1,0:T(8,128)} %param.19) | data formatting | bytes 8192 | tf_op args[9]
  7.4 1.7 %copy.21 = s32[216,128]{0,1:T(8,128)} copy(s32[216,128]{1,0:T(8,128)} %bitcast.207) | data formatting | bytes 221184 | tf_op jit(solution)/shard_map/reshape;squeeze | solution.py:352
  9.1 1.8 %copy.23 = bf16[512,256]{0,1:T(8,128)(2,1)} copy(bf16[512,256]{1,0:T(8,128)(2,1)} %param.10) | data formatting | bytes 524288 | tf_op args[0]
  10.9 1.1 %copy.24 = bf16[512,256]{0,1:T(8,128)(2,1)S(1)} copy(bf16[512,256]{1,0:T(8,128)(2,1)} %pre_in.1) | data formatting | bytes 524288 | tf_op args[1]
  12.0 0.7 maximum_bitcast_fusion.act_t
  12.8 0.7 copy-done.5
  13.4 5.9 %down_grad.1 = (bf16[512,256]{1,0:T(8,128)(2,1)}, bf16[1024,512]{1,0:T(8,128)(2,1)}) custom-call(bf16[128,512]{1,0:T(8,128)(2,1)} %copy-done.5, bf16[128,512]{1,0:T(8,128)(2,1)} %cur.1, s32[128,8]{1,0:T(8,128)} %bitcast.208, s32[8,128]{1,0:T(8,128)} %bitcast.209, bf16[512,256]{1,0:T(8,128)(2,1)} %pre_in.1, bf16[2048,512]{1,0:T(8,128)(2,1)} %w_in.1), custom_call_target="tpu_custom_call" | custom-call | flops 1073741824 | bytes 4194304 | tf_op jit(solution)/shard_map/down_grad/pallas_call | solution.py:96
  19.3 1.0 fusion.22
  20.3 1.3 %collective-permute-start.2 = (bf16[256,256]{1,0:T(8,128)(2,1)S(1)}, bf16[256,256]{1,0:T(8,128)(2,1)S(1)}, u32[]{:S(2)}, u32[]{:S(2)}) collective-permute-start(bf16[256,256]{1,0:T(8,128)(2,1)S(1)} %get-tuple-element.67), channel_id=1, source_target_pairs={{1,0},{2,1},{3,2},{4,3},{5,4},{6,5},{7,6},{8,7},{9,8},{10,9},{11,1... | collective-permute-start | bytes 393224 | tf_op jit(solution)/shard_map/ppermute | solution.py:270
  21.6 5.3 %collective-permute-start.1 = (bf16[256,256]{1,0:T(8,128)(2,1)S(1)}, bf16[256,256]{1,0:T(8,128)(2,1)S(1)}, u32[]{:S(2)}, u32[]{:S(2)}) collective-permute-start(bf16[256,256]{1,0:T(8,128)(2,1)S(1)} %get-tuple-element.68), channel_id=1, source_target_pairs={{0,1},{1,2},{2,3},{3,4},{4,5},{5,6},{6,7},{7,8},{8,9},{9,10},{10,1... | collective-permute-start | bytes 393224 | tf_op jit(solution)/shard_map/ppermute | solution.py:270
  26.9 5.7 %down_weight.1 = (f32[16,64,512]{2,1,0:T(8,128)}, bf16[16,64,512]{2,1,0:T(8,128)(2,1)}) custom-call(s32[1]{0:T(128)} %bitcast.refs_0_.core, bf16[256,512]{1,0:T(8,128)(2,1)} %maximum_bitcast_fusion.act_t, s32[8,128]{1,0:T(8,128)} %bitcast.210, bf16[1024,512]{1,0:T(8,128)(2,1)} %get-tuple-element.26.gath), custom_call_target="tpu_custom_call" | custom-call | flops 1073741824 | bytes 6291456 | tf_op jit(solution)/shard_map/down_weight/pallas_call | solution.py:139
  32.6 1.8 %collective-permute-start.3 = (bf16[16,64,512]{2,1,0:T(8,128)(2,1)}, bf16[16,64,512]{2,1,0:T(8,128)(2,1)S(1)}, u32[]{:S(2)}, u32[]{:S(2)}) collective-permute-start(bf16[16,64,512]{2,1,0:T(8,128)(2,1)} %get-tuple-element.27), channel_id=1, source_target_pairs={{0,1},{1,0},{2,3},{3,2},{4,5},{5,4},{6,7},{7,6},{8,9},{9,8},{10,11... | collective-permute-start | bytes 3145736 | tf_op jit(solution)/shard_map/ppermute | solution.py:270
  34.4 1.9 %constant_dynamic-slice_fusion.3 = (f32[4,2,1,64,512]{4,3,2,1,0:T(8,128)S(1)}, f32[4,2,1,64,512]{4,3,2,1,0:T(8,128)S(1)}) fusion(f32[4,2,2,64,512]{4,3,2,1,0:T(8,128)} %bitcast.188, s32[]{:T(128)S(6)} %select_n.239, s32[]{:T(128)S(6)} %select_n.233), kind=kLoop, calls=%fused_computation.71 | loop fusion | bytes 4194312 | tf_op jit(solution)/shard_map/jit(dynamic_index_in_dim)/dynamic_slice | solution.py:274
  36.3 0.3 copy-done
  36.6 0.2 constant_dynamic-slice_fusion.2
  36.9 0.6 copy-done.6
  37.6 11.2 %conv.2 = (f32[512,256]{1,0:T(8,128)}, f32[8,216,256]{2,1,0:T(8,128)}, bf16[8,216,256]{2,1,0:T(8,128)(2,1)}) custom-call(s32[1]{0:T(128)} %bitcast.refs_0_.core, s32[216]{0:T(256)} %reshape_squeeze.9.refs_1_, s32[216]{0:T(256)} %reshape_squeeze.10.refs_2_, s32[128,216]{1,0:T(8,128)} %bitcast.205, bf16[256,256]{1,0:T(8,128)(2,1)} %copy-done.7, ...), custom_call_target="tpu_custom_call" | custom-call | flops 12884901888 | bytes 8388608 | tf_op jit(solution)/shard_map/conv/pallas_call | solution.py:245
  48.8 0.1 constant_dynamic-slice_fusion.1
  48.9 0.1 constant_dynamic-slice_fusion
  49.0 1.0 copy-done.4
  50.0 0.4 fusion.2
  50.4 2.4 %collective-permute-start.4 = (bf16[4,2,64,512]{3,2,0,1:T(8,128)(2,1)S(1)}, bf16[4,2,64,512]{3,2,0,1:T(8,128)(2,1)S(1)}, u32[]{:S(2)}, u32[]{:S(2)}) collective-permute-start(bf16[4,2,64,512]{3,2,0,1:T(8,128)(2,1)S(1)} %fusion.2), channel_id=1, source_target_pairs={{0,2},{1,5},{2,0},{3,7},{4,6},{5,1},{6,4},{7,3},{8,10},{9,13},{10,... | collective-permute-start | bytes 1572872 | tf_op jit(solution)/shard_map/ppermute | solution.py:270
  52.8 12.2 %conv.3 = (bf16[512,256]{1,0:T(8,128)(2,1)}, f32[8,216,256]{2,1,0:T(8,128)}, bf16[8,216,256]{2,1,0:T(8,128)(2,1)}) custom-call(s32[1]{0:T(128)} %bitcast.refs_0_.core, s32[216]{0:T(256)} %reshape_squeeze.9.refs_1_, s32[216]{0:T(256)} %reshape_squeeze.10.refs_2_, s32[128,216]{1,0:T(8,128)} %bitcast.206, bf16[256,256]{1,0:T(8,128)(2,1)} %copy-done.7, ...), custom_call_target="tpu_custom_call" | custom-call | flops 12884901888 | bytes 8388608 | tf_op jit(solution)/shard_map/conv/pallas_call | solution.py:245
  65.0 0.3 fusion
  65.3 0.1 dynamic-slice_bitcast_fusion.10
  65.4 0.1 dynamic-slice_bitcast_fusion.11
  65.5 1.0 copy-done.3
  66.5 0.2 fusion.11
  66.7 2.5 %collective-permute-start.14 = (bf16[4,64,512]{2,1,0:T(8,128)(2,1)S(1)}, bf16[4,64,512]{2,1,0:T(8,128)(2,1)S(1)}, u32[]{:S(2)}, u32[]{:S(2)}) collective-permute-start(bf16[4,64,512]{2,1,0:T(8,128)(2,1)S(1)} %get-tuple-element.49), channel_id=1, source_target_pairs={{0,4},{1,3},{2,6},{3,1},{4,0},{5,7},{6,2},{7,5},{8,12},{9,11},{10,... | collective-permute-start | bytes 786440 | tf_op jit(solution)/shard_map/ppermute | solution.py:270
  69.2 0.3 fusion.8
  69.5 0.5 collective-permute-start.6
  70.0 0.1 dynamic-slice_bitcast_fusion
  70.1 0.2 dynamic-slice_bitcast_fusion.1
  70.3 0.2 fusion.3
  70.5 0.1 dynamic-slice_bitcast_fusion.6
  70.6 0.1 dynamic-slice_bitcast_fusion.7
  70.7 0.2 fusion.5
  70.9 1.7 %collective-permute-start.10 = (bf16[2,2,216,256]{3,2,0,1:T(8,128)(2,1)S(1)}, bf16[2,2,216,256]{3,2,0,1:T(8,128)(2,1)S(1)}, u32[]{:S(2)}, u32[]{:S(2)}) collective-permute-start(bf16[2,2,216,256]{3,2,0,1:T(8,128)(2,1)S(1)} %fusion.5), channel_id=1, source_target_pairs={{0,2},{1,5},{2,0},{3,7},{4,6},{5,1},{6,4},{7,3},{8,10},{9,13},{10,... | collective-permute-start | bytes 1327112 | tf_op jit(solution)/shard_map/ppermute | solution.py:270
  72.6 3.3 %collective-permute-done.14 = bf16[4,64,512]{2,1,0:T(8,128)(2,1)S(1)} collective-permute-done((bf16[4,64,512]{2,1,0:T(8,128)(2,1)S(1)}, bf16[4,64,512]{2,1,0:T(8,128)(2,1)S(1)}, u32[]{:S(2)}, u32[]{:S(2)}) %collective-permute-start.14) | collective-permute-done | bytes 262176 | tf_op jit(solution)/shard_map/ppermute | solution.py:270
  75.9 0.1 fusion.16
  76.0 1.6 %collective-permute-start.15 = (bf16[2,64,512]{2,1,0:T(8,128)(2,1)S(1)}, bf16[2,64,512]{2,1,0:T(8,128)(2,1)S(1)}, u32[]{:S(2)}, u32[]{:S(2)}) collective-permute-start(bf16[2,64,512]{2,1,0:T(8,128)(2,1)S(1)} %get-tuple-element.65), channel_id=1, source_target_pairs={{0,8},{1,9},{2,10},{3,11},{4,12},{5,13},{6,14},{7,15},{8,0},{9,1},... | collective-permute-start | bytes 393224 | tf_op jit(solution)/shard_map/ppermute | solution.py:270
  77.6 0.3 collective-permute-done.6
  77.8 0.1 fusion.13
  77.9 2.3 %collective-permute-start.7 = (bf16[2,216,256]{2,1,0:T(8,128)(2,1)S(1)}, bf16[2,216,256]{2,1,0:T(8,128)(2,1)S(1)}, u32[]{:S(2)}, u32[]{:S(2)}) collective-permute-start(bf16[2,216,256]{2,1,0:T(8,128)(2,1)S(1)} %fusion.13), channel_id=1, source_target_pairs={{0,4},{1,3},{2,6},{3,1},{4,0},{5,7},{6,2},{7,5},{8,12},{9,11},{10,... | collective-permute-start | bytes 663560 | tf_op jit(solution)/shard_map/ppermute | solution.py:270
  80.2 0.2 fusion.6
  80.4 3.4 %collective-permute-done.10 = bf16[2,2,216,256]{3,2,0,1:T(8,128)(2,1)S(1)} collective-permute-done((bf16[2,2,216,256]{3,2,0,1:T(8,128)(2,1)S(1)}, bf16[2,2,216,256]{3,2,0,1:T(8,128)(2,1)S(1)}, u32[]{:S(2)}, u32[]{:S(2)}) %collective-permute-start.10) | collective-permute-done | bytes 442400 | tf_op jit(solution)/shard_map/ppermute | solution.py:270
  83.8 0.1 fusion.12
  83.9 2.4 %collective-permute-start.11 = (bf16[2,216,256]{2,1,0:T(8,128)(2,1)S(1)}, bf16[2,216,256]{2,1,0:T(8,128)(2,1)S(1)}, u32[]{:S(2)}, u32[]{:S(2)}) collective-permute-start(bf16[2,216,256]{2,1,0:T(8,128)(2,1)S(1)} %get-tuple-element.51), channel_id=1, source_target_pairs={{0,4},{1,3},{2,6},{3,1},{4,0},{5,7},{6,2},{7,5},{8,12},{9,11},{10,... | collective-permute-start | bytes 663560 | tf_op jit(solution)/shard_map/ppermute | solution.py:270
  86.4 1.6 %collective-permute-start.8 = (bf16[216,256]{1,0:T(8,128)(2,1)S(1)}, bf16[216,256]{1,0:T(8,128)(2,1)S(1)}, u32[]{:S(2)}, u32[]{:S(2)}) collective-permute-start(bf16[216,256]{1,0:T(8,128)(2,1)S(1)} %fusion.19), channel_id=1, source_target_pairs={{0,8},{1,9},{2,10},{3,11},{4,12},{5,13},{6,14},{7,15},{8,0},{9,1},... | collective-permute-start | bytes 331784 | tf_op jit(solution)/shard_map/ppermute | solution.py:270
  88.0 2.2 %collective-permute-done.11 = bf16[2,216,256]{2,1,0:T(8,128)(2,1)S(1)} collective-permute-done((bf16[2,216,256]{2,1,0:T(8,128)(2,1)S(1)}, bf16[2,216,256]{2,1,0:T(8,128)(2,1)S(1)}, u32[]{:S(2)}, u32[]{:S(2)}) %collective-permute-start.11) | collective-permute-done | bytes 221216 | tf_op jit(solution)/shard_map/ppermute | solution.py:270
  90.3 1.6 %collective-permute-start.12 = (bf16[216,256]{1,0:T(8,128)(2,1)S(1)}, bf16[216,256]{1,0:T(8,128)(2,1)S(1)}, u32[]{:S(2)}, u32[]{:S(2)}) collective-permute-start(bf16[216,256]{1,0:T(8,128)(2,1)S(1)} %fusion.20), channel_id=1, source_target_pairs={{0,8},{1,9},{2,10},{3,11},{4,12},{5,13},{6,14},{7,15},{8,0},{9,1},... | collective-permute-start | bytes 331784 | tf_op jit(solution)/shard_map/ppermute | solution.py:270
  91.9 2.1 %collective-permute-start.16 = (bf16[64,512]{1,0:T(8,128)(2,1)S(1)}, bf16[64,512]{1,0:T(8,128)(2,1)S(1)}, u32[]{:S(2)}, u32[]{:S(2)}) collective-permute-start(bf16[64,512]{1,0:T(8,128)(2,1)S(1)} %fusion.21), channel_id=1, source_target_pairs={{0,16},{1,17},{2,18},{3,19},{4,20},{5,21},{6,22},{7,23},{8,24},{9,... | collective-permute-start | bytes 196616 | tf_op jit(solution)/shard_map/ppermute | solution.py:270
  94.1 1.1 %collective-permute-done.12 = bf16[216,256]{1,0:T(8,128)(2,1)S(1)} collective-permute-done((bf16[216,256]{1,0:T(8,128)(2,1)S(1)}, bf16[216,256]{1,0:T(8,128)(2,1)S(1)}, u32[]{:S(2)}, u32[]{:S(2)}) %collective-permute-start.12) | collective-permute-done | bytes 110624 | tf_op jit(solution)/shard_map/ppermute | solution.py:270
  95.1 0.1 select_convert_fusion
  95.3 3.5 %collective-permute-start.13 = (bf16[216,256]{1,0:T(8,128)(2,1)S(1)}, bf16[216,256]{1,0:T(8,128)(2,1)S(1)}, u32[]{:S(2)}, u32[]{:S(2)}) collective-permute-start(bf16[216,256]{1,0:T(8,128)(2,1)S(1)} %select_convert_fusion), channel_id=1, source_target_pairs={{0,16},{1,17},{2,18},{3,19},{4,20},{5,21},{6,22},{7,23},{8,24},{9,... | collective-permute-start | bytes 331784 | tf_op jit(solution)/shard_map/ppermute | solution.py:270
  98.8 0.7 fusion.18
  99.5 4.0 %collective-permute-done.13 = bf16[216,256]{1,0:T(8,128)(2,1)S(1)} collective-permute-done((bf16[216,256]{1,0:T(8,128)(2,1)S(1)}, bf16[216,256]{1,0:T(8,128)(2,1)S(1)}, u32[]{:S(2)}, u32[]{:S(2)}) %collective-permute-start.13) | collective-permute-done | bytes 110624 | tf_op jit(solution)/shard_map/ppermute | solution.py:270
  103.5 0.1 multiply_bitcast_fusion
  103.6 0.8 copy.86
  (28 shorter events, 0.2 us)
Async XLA Ops:
  0.6 12.1 %collective-permute-start = (bf16[128,512]{1,0:T(8,128)(2,1)}, bf16[128,512]{1,0:T(8,128)(2,1)S(1)}, u32[]{:S(2)}, u32[]{:S(2)}) collective-permute-start(bf16[128,512]{1,0:T(8,128)(2,1)} %cur.1), channel_id=1, source_target_pairs={{0,1},{1,2},{2,3},{3,4},{4,5},{5,6},{6,7},{7,8},{8,9},{9,10},{10,1... | collective-permute-start | bytes 393224 | tf_op jit(solution)/shard_map/ppermute | solution.py:270
  12.8 0.7 copy-start.5
  20.3 16.6 %collective-permute-start.2 = (bf16[256,256]{1,0:T(8,128)(2,1)S(1)}, bf16[256,256]{1,0:T(8,128)(2,1)S(1)}, u32[]{:S(2)}, u32[]{:S(2)}) collective-permute-start(bf16[256,256]{1,0:T(8,128)(2,1)S(1)} %get-tuple-element.67), channel_id=1, source_target_pairs={{1,0},{2,1},{3,2},{4,3},{5,4},{6,5},{7,6},{8,7},{9,8},{10,9},{11,1... | collective-permute-start | bytes 393224 | tf_op jit(solution)/shard_map/ppermute | solution.py:270
  21.6 15.3 %collective-permute-start.1 = (bf16[256,256]{1,0:T(8,128)(2,1)S(1)}, bf16[256,256]{1,0:T(8,128)(2,1)S(1)}, u32[]{:S(2)}, u32[]{:S(2)}) collective-permute-start(bf16[256,256]{1,0:T(8,128)(2,1)S(1)} %get-tuple-element.68), channel_id=1, source_target_pairs={{0,1},{1,2},{2,3},{3,4},{4,5},{5,6},{6,7},{7,8},{8,9},{9,10},{10,1... | collective-permute-start | bytes 393224 | tf_op jit(solution)/shard_map/ppermute | solution.py:270
  32.6 16.2 %collective-permute-start.3 = (bf16[16,64,512]{2,1,0:T(8,128)(2,1)}, bf16[16,64,512]{2,1,0:T(8,128)(2,1)S(1)}, u32[]{:S(2)}, u32[]{:S(2)}) collective-permute-start(bf16[16,64,512]{2,1,0:T(8,128)(2,1)} %get-tuple-element.27), channel_id=1, source_target_pairs={{0,1},{1,0},{2,3},{3,2},{4,5},{5,4},{6,7},{7,6},{8,9},{9,8},{10,11... | collective-permute-start | bytes 3145736 | tf_op jit(solution)/shard_map/ppermute | solution.py:270
  34.4 2.2 %copy-start = (f32[16,64,512]{2,1,0:T(8,128)S(1)}, f32[16,64,512]{2,1,0:T(8,128)}, u32[]{:S(2)}) copy-start(f32[16,64,512]{2,1,0:T(8,128)} %get-tuple-element.32) | copy-start | bytes 6291460
  36.9 0.7 copy-start.6
  36.9 0.7 copy-start.7
  48.8 1.2 %copy-start.4 = (bf16[8,216,256]{2,1,0:T(8,128)(2,1)S(1)}, bf16[8,216,256]{2,1,0:T(8,128)(2,1)}, u32[]{:S(2)}) copy-start(bf16[8,216,256]{2,1,0:T(8,128)(2,1)} %get-tuple-element.34) | copy-start | bytes 2654212
  49.9 15.4 %collective-permute-start.5 = (bf16[8,216,256]{2,1,0:T(8,128)(2,1)S(1)}, bf16[8,216,256]{2,1,0:T(8,128)(2,1)S(1)}, u32[]{:S(2)}, u32[]{:S(2)}) collective-permute-start(bf16[8,216,256]{2,1,0:T(8,128)(2,1)S(1)} %copy-done.4), channel_id=1, source_target_pairs={{0,1},{1,0},{2,3},{3,2},{4,5},{5,4},{6,7},{7,6},{8,9},{9,8},{10,11... | collective-permute-start | bytes 2654216 | tf_op jit(solution)/shard_map/ppermute | solution.py:270
  50.4 14.9 %collective-permute-start.4 = (bf16[4,2,64,512]{3,2,0,1:T(8,128)(2,1)S(1)}, bf16[4,2,64,512]{3,2,0,1:T(8,128)(2,1)S(1)}, u32[]{:S(2)}, u32[]{:S(2)}) collective-permute-start(bf16[4,2,64,512]{3,2,0,1:T(8,128)(2,1)S(1)} %fusion.2), channel_id=1, source_target_pairs={{0,2},{1,5},{2,0},{3,7},{4,6},{5,1},{6,4},{7,3},{8,10},{9,13},{10,... | collective-permute-start | bytes 1572872 | tf_op jit(solution)/shard_map/ppermute | solution.py:270
  65.3 1.2 %copy-start.3 = (bf16[8,216,256]{2,1,0:T(8,128)(2,1)S(1)}, bf16[8,216,256]{2,1,0:T(8,128)(2,1)}, u32[]{:S(2)}) copy-start(bf16[8,216,256]{2,1,0:T(8,128)(2,1)} %get-tuple-element.39) | copy-start | bytes 2654212
  65.4 3.8 %copy-start.1 = (f32[8,216,256]{2,1,0:T(8,128)S(1)}, f32[8,216,256]{2,1,0:T(8,128)}, u32[]{:S(2)}) copy-start(f32[8,216,256]{2,1,0:T(8,128)} %get-tuple-element.36) | copy-start | bytes 5308420
  66.5 4.0 %collective-permute-start.9 = (bf16[8,216,256]{2,1,0:T(8,128)(2,1)S(1)}, bf16[8,216,256]{2,1,0:T(8,128)(2,1)S(1)}, u32[]{:S(2)}, u32[]{:S(2)}) collective-permute-start(bf16[8,216,256]{2,1,0:T(8,128)(2,1)S(1)} %copy-done.3), channel_id=1, source_target_pairs={{0,1},{1,0},{2,3},{3,2},{4,5},{5,4},{6,7},{7,6},{8,9},{9,8},{10,11... | collective-permute-start | bytes 2654216 | tf_op jit(solution)/shard_map/ppermute | solution.py:270
  66.7 3.3 %copy-start.2 = (f32[8,216,256]{2,1,0:T(8,128)S(1)}, f32[8,216,256]{2,1,0:T(8,128)}, u32[]{:S(2)}) copy-start(f32[8,216,256]{2,1,0:T(8,128)} %get-tuple-element.38) | copy-start | bytes 5308420
  66.7 9.2 %collective-permute-start.14 = (bf16[4,64,512]{2,1,0:T(8,128)(2,1)S(1)}, bf16[4,64,512]{2,1,0:T(8,128)(2,1)S(1)}, u32[]{:S(2)}, u32[]{:S(2)}) collective-permute-start(bf16[4,64,512]{2,1,0:T(8,128)(2,1)S(1)} %get-tuple-element.49), channel_id=1, source_target_pairs={{0,4},{1,3},{2,6},{3,1},{4,0},{5,7},{6,2},{7,5},{8,12},{9,11},{10,... | collective-permute-start | bytes 786440 | tf_op jit(solution)/shard_map/ppermute | solution.py:270
  69.5 8.4 %collective-permute-start.6 = (bf16[2,2,216,256]{3,2,0,1:T(8,128)(2,1)S(1)}, bf16[2,2,216,256]{3,2,0,1:T(8,128)(2,1)S(1)}, u32[]{:S(2)}, u32[]{:S(2)}) collective-permute-start(bf16[2,2,216,256]{3,2,0,1:T(8,128)(2,1)S(1)} %fusion.8), channel_id=1, source_target_pairs={{0,2},{1,5},{2,0},{3,7},{4,6},{5,1},{6,4},{7,3},{8,10},{9,13},{10,... | collective-permute-start | bytes 1327112 | tf_op jit(solution)/shard_map/ppermute | solution.py:270
  70.9 12.9 %collective-permute-start.10 = (bf16[2,2,216,256]{3,2,0,1:T(8,128)(2,1)S(1)}, bf16[2,2,216,256]{3,2,0,1:T(8,128)(2,1)S(1)}, u32[]{:S(2)}, u32[]{:S(2)}) collective-permute-start(bf16[2,2,216,256]{3,2,0,1:T(8,128)(2,1)S(1)} %fusion.5), channel_id=1, source_target_pairs={{0,2},{1,5},{2,0},{3,7},{4,6},{5,1},{6,4},{7,3},{8,10},{9,13},{10,... | collective-permute-start | bytes 1327112 | tf_op jit(solution)/shard_map/ppermute | solution.py:270
  76.0 15.9 %collective-permute-start.15 = (bf16[2,64,512]{2,1,0:T(8,128)(2,1)S(1)}, bf16[2,64,512]{2,1,0:T(8,128)(2,1)S(1)}, u32[]{:S(2)}, u32[]{:S(2)}) collective-permute-start(bf16[2,64,512]{2,1,0:T(8,128)(2,1)S(1)} %get-tuple-element.65), channel_id=1, source_target_pairs={{0,8},{1,9},{2,10},{3,11},{4,12},{5,13},{6,14},{7,15},{8,0},{9,1},... | collective-permute-start | bytes 393224 | tf_op jit(solution)/shard_map/ppermute | solution.py:270
  77.9 8.5 %collective-permute-start.7 = (bf16[2,216,256]{2,1,0:T(8,128)(2,1)S(1)}, bf16[2,216,256]{2,1,0:T(8,128)(2,1)S(1)}, u32[]{:S(2)}, u32[]{:S(2)}) collective-permute-start(bf16[2,216,256]{2,1,0:T(8,128)(2,1)S(1)} %fusion.13), channel_id=1, source_target_pairs={{0,4},{1,3},{2,6},{3,1},{4,0},{5,7},{6,2},{7,5},{8,12},{9,11},{10,... | collective-permute-start | bytes 663560 | tf_op jit(solution)/shard_map/ppermute | solution.py:270
  83.9 6.3 %collective-permute-start.11 = (bf16[2,216,256]{2,1,0:T(8,128)(2,1)S(1)}, bf16[2,216,256]{2,1,0:T(8,128)(2,1)S(1)}, u32[]{:S(2)}, u32[]{:S(2)}) collective-permute-start(bf16[2,216,256]{2,1,0:T(8,128)(2,1)S(1)} %get-tuple-element.51), channel_id=1, source_target_pairs={{0,4},{1,3},{2,6},{3,1},{4,0},{5,7},{6,2},{7,5},{8,12},{9,11},{10,... | collective-permute-start | bytes 663560 | tf_op jit(solution)/shard_map/ppermute | solution.py:270
  86.4 7.6 %collective-permute-start.8 = (bf16[216,256]{1,0:T(8,128)(2,1)S(1)}, bf16[216,256]{1,0:T(8,128)(2,1)S(1)}, u32[]{:S(2)}, u32[]{:S(2)}) collective-permute-start(bf16[216,256]{1,0:T(8,128)(2,1)S(1)} %fusion.19), channel_id=1, source_target_pairs={{0,8},{1,9},{2,10},{3,11},{4,12},{5,13},{6,14},{7,15},{8,0},{9,1},... | collective-permute-start | bytes 331784 | tf_op jit(solution)/shard_map/ppermute | solution.py:270
  90.3 4.9 %collective-permute-start.12 = (bf16[216,256]{1,0:T(8,128)(2,1)S(1)}, bf16[216,256]{1,0:T(8,128)(2,1)S(1)}, u32[]{:S(2)}, u32[]{:S(2)}) collective-permute-start(bf16[216,256]{1,0:T(8,128)(2,1)S(1)} %fusion.20), channel_id=1, source_target_pairs={{0,8},{1,9},{2,10},{3,11},{4,12},{5,13},{6,14},{7,15},{8,0},{9,1},... | collective-permute-start | bytes 331784 | tf_op jit(solution)/shard_map/ppermute | solution.py:270
  91.9 6.9 %collective-permute-start.16 = (bf16[64,512]{1,0:T(8,128)(2,1)S(1)}, bf16[64,512]{1,0:T(8,128)(2,1)S(1)}, u32[]{:S(2)}, u32[]{:S(2)}) collective-permute-start(bf16[64,512]{1,0:T(8,128)(2,1)S(1)} %fusion.21), channel_id=1, source_target_pairs={{0,16},{1,17},{2,18},{3,19},{4,20},{5,21},{6,22},{7,23},{8,24},{9,... | collective-permute-start | bytes 196616 | tf_op jit(solution)/shard_map/ppermute | solution.py:270
  95.3 8.2 %collective-permute-start.13 = (bf16[216,256]{1,0:T(8,128)(2,1)S(1)}, bf16[216,256]{1,0:T(8,128)(2,1)S(1)}, u32[]{:S(2)}, u32[]{:S(2)}) collective-permute-start(bf16[216,256]{1,0:T(8,128)(2,1)S(1)} %select_convert_fusion), channel_id=1, source_target_pairs={{0,16},{1,17},{2,18},{3,19},{4,20},{5,21},{6,22},{7,23},{8,24},{9,... | collective-permute-start | bytes 331784 | tf_op jit(solution)/shard_map/ppermute | solution.py:270

commit v4 on v0

v4 whole, which is shorter than its diff:
```python
import functools
import math

import jax
import jax.numpy as jnp
from jax import lax
from jax.experimental import pallas as pl
from jax.experimental.pallas import tpu as pltpu
from jax.sharding import PartitionSpec as P

HB = 2
BF = jnp.bfloat16
F32 = jnp.float32


def dot(a, b):
    return lax.dot_general(a, b, (((1,), (0,)), ((), ())), preferred_element_type=F32)


def dot_nt(a, b):
    return lax.dot_general(a, b, (((1,), (1,)), ((), ())), preferred_element_type=F32)


def one_hot(index, shape, axis):
    return jnp.where(index == lax.broadcasted_iota(jnp.int32, shape, axis), 1.0, 0.0).astype(BF)


def segments(first, count, shard):
    row, cuts = first, []
    while row < first + count:
        number, inside = divmod(row, shard)
        rows = min(shard - inside, first + count - row)
        cuts.append((row - first, number, inside, rows))
        row += rows
    return cuts


def place(both, value, first, core):
    for at, number, inside, rows in segments(first, value.shape[0], both.shape[2]):
        both[(number % 2) ^ core, number // 2, pl.ds(inside, rows), :] = value[at : at + rows]


def halves(total, shard):
    pairs = total[0] // (2 * shard)
    return (
        jax.ShapeDtypeStruct((2, pairs, shard, total[1]), F32),
        jax.ShapeDtypeStruct((pairs, shard, total[1]), BF),
    )


VMEM = pl.BlockSpec(memory_space=pltpu.VMEM)
SMEM = pl.BlockSpec(memory_space=pltpu.SMEM)


def cost(flops, nbytes):
    return pl.CostEstimate(flops=flops, bytes_accessed=nbytes, transcendentals=0)


def prep_kernel(feats, pre, pairs, rows, parents, feats_t, act, tab, pick, parent_pick, chosen):
    children, slots = rows.shape
    count, channels = feats.shape
    square = (channels, channels)
    wide = one_hot(lax.broadcasted_iota(jnp.int32, square, 0), square, 1)
    eye = wide[:slots, :slots]
    for c in range(children):
        pick[:, pl.ds(c * slots, slots)] = one_hot(rows[c : c + 1, :], (count, slots), 0)
    columns = dot_nt(eye, parents[...].astype(F32).astype(BF)).astype(jnp.int32)
    for c in range(children):
        parent_pick[pl.ds(c * slots, slots), :] = one_hot(
            columns[:, c : c + 1], (slots, parent_pick.shape[1]), 1
        )
    act[...] = jnp.maximum(pre[...], jnp.zeros((), BF))
    chosen[...] = dot(dot_nt(wide, act[...]).astype(BF), pick[...]).astype(BF)
    tab[...] = dot_nt(eye, pairs[...].astype(F32).astype(BF)).astype(jnp.int32)
    feats_t[...] = dot_nt(wide, feats[...]).astype(BF)


def prep(feats, pre, pairs, rows, parents, parent_rows):
    count, channels = feats.shape
    children, slots = rows.shape
    shapes = (
        ((channels, count), BF),
        ((count, channels), BF),
        ((pairs.shape[1], pairs.shape[0]), jnp.int32),
        ((count, children * slots), BF),
        ((children * slots, parent_rows), BF),
        ((channels, children * slots), BF),
    )
    return pl.pallas_call(
        prep_kernel,
        out_shape=tuple(jax.ShapeDtypeStruct(*shape) for shape in shapes),
        in_specs=[VMEM] * 5,
        out_specs=(VMEM,) * len(shapes),
        compiler_params=pltpu.CompilerParams(vmem_limit_bytes=16 << 20),
        cost_estimate=cost(1 << 30, 3 << 20),
        name="prep",
    )(feats, pre, pairs, rows, parents)


def down_grad_kernel(prev, cur, act, w, pick, parent_pick, gpre, head, tail, gath, contrib):
    count, channels = act.shape
    children = w.shape[0] // channels
    slots = gath.shape[0] // children
    ext = jnp.concatenate([prev[...], cur[...]], 0)
    for c in range(children):
        mine = pl.ds(c * slots, slots)
        got = dot(parent_pick[mine, :], ext).astype(BF)
        gath[mine, :] = got
        contrib[mine, :] = dot_nt(got, w[pl.ds(c * channels, channels), :]).astype(BF)
    grad = dot(pick[...], contrib[...])
    masked = jnp.where(act[...].astype(F32) > 0, grad, 0.0).astype(BF)
    gpre[...] = masked
    halo = head.shape[0]
    head[...] = masked[:halo]
    tail[...] = masked[count - halo :]


def down_grad(prev, cur, act, w, pick, parent_pick, halo):
    count, channels = act.shape
    listed = parent_pick.shape[0]
    shapes = ((count, channels), (halo, channels), (halo, channels), (listed, cur.shape[1]))
    return pl.pallas_call(
        down_grad_kernel,
        out_shape=tuple(jax.ShapeDtypeStruct(shape, BF) for shape in shapes),
        in_specs=[VMEM] * 6,
        out_specs=(VMEM,) * 4,
        scratch_shapes=[pltpu.VMEM((listed, channels), BF)],
        compiler_params=pltpu.CompilerParams(vmem_limit_bytes=16 << 20),
        cost_estimate=cost(1 << 30, 4 << 20),
        name="down_grad",
    )(prev, cur, act, w, pick, parent_pick)


def down_weight_kernel(core, chosen, gath, ahead, both, send):
    channels, listed = chosen.shape
    pairs, shard = send.shape[:2]
    children = 2 * pairs * shard // channels
    slots = listed // children
    for c in range(children):
        mine = pl.ds(c * slots, slots)
        place(both, dot(chosen[:, mine], gath[mine, :]), c * channels, core[0])
    send[...] = both[1].astype(BF)


def down_weight(core, chosen, gath, ahead, shard, total):
    return pl.pallas_call(
        down_weight_kernel,
        out_shape=halves(total, shard),
        in_specs=[SMEM, VMEM, VMEM, VMEM],
        out_specs=(VMEM, VMEM),
        compiler_params=pltpu.CompilerParams(vmem_limit_bytes=16 << 20),
        cost_estimate=cost(1 << 30, 6 << 20),
        name="down_weight",
    )(core, chosen, gath, ahead)


def conv_plan(kernel, channels, quarter):
    size = kernel * channels // 4
    plan, row = [], quarter * size
    while row < (quarter + 1) * size:
        k, first = divmod(row, channels)
        last = min(channels, (quarter + 1) * size - k * channels)
        plan.append((k, first, last, row - quarter * size))
        row += last - first
    return plan


def conv_kernel(plan, begun, *refs):
    core, src, tgt, tab, before, own, after, feats_t, w, *rest = refs
    if begun:
        partial, *rest = rest
    grad, both, send, ext, acc, col0, col1 = rest
    cols = (col0, col1)
    slots = src.shape[0]
    blocks, rows, channels = col0.shape
    count = feats_t.shape[1]
    at = 0
    for piece in (before, own, after):
        for b in range(piece.shape[0] // rows):
            ext[at] = piece[pl.ds(b * rows, rows), :]
            at += 1
    acc[...] = partial[...] if begun else jnp.zeros_like(acc)
    lanes = lax.broadcasted_iota(jnp.int32, (rows, rows), 1).astype(jnp.int16)
    one, zero = jnp.ones((), BF), jnp.zeros((), BF)

    def gather(k, col):
        col[...] = jnp.zeros_like(col)
        for p in range(slots):
            q = k * slots + p
            index = jnp.broadcast_to(tab[:, q : q + 1], (rows, rows)).astype(jnp.int16)
            pick = jnp.where(index == lanes, one, zero)
            piece = dot(pick, ext[tgt[p, k]]).astype(BF)
            owner = src[p, k]
            col[owner] = col[owner] + piece

    gather(plan[0][0], cols[0])
    for at, (k, first, last, out) in enumerate(plan):
        if at + 1 < len(plan):
            gather(plan[at + 1][0], cols[(at + 1) % 2])
        column = cols[at % 2][...].reshape(count, channels)
        place(both, dot(feats_t[pl.ds(first, last - first), :], column), out, core[0])
        if first == 0:
            acc[...] += dot_nt(column, w[pl.ds(k * channels, channels), :])
    grad[...] = acc[...].astype(grad.dtype)
    send[...] = both[1].astype(BF)


def conv(core, src, tgt, tab, before, own, after, feats_t, w, quarter, shard, partial, final):
    channels, count = feats_t.shape
    kernel = w.shape[0] // channels
    rows = tab.shape[0]
    begun = partial is not None
    total = (kernel * channels // 4, channels)
    ext_rows = count + before.shape[0] + after.shape[0]
    block = (rows, channels)
    grad = jax.ShapeDtypeStruct((count, channels), BF if final else F32)
    return pl.pallas_call(
        functools.partial(conv_kernel, conv_plan(kernel, channels, quarter), begun),
        out_shape=(grad,) + halves(total, shard),
        in_specs=[SMEM] * 3 + [VMEM] * (6 + begun),
        out_specs=(VMEM,) * 3,
        scratch_shapes=[
            pltpu.VMEM((ext_rows // rows,) + block, BF),
            pltpu.VMEM((count, channels), F32),
            pltpu.VMEM((count // rows,) + block, BF),
            pltpu.VMEM((count // rows,) + block, BF),
        ],
        compiler_params=pltpu.CompilerParams(vmem_limit_bytes=16 << 20),
        cost_estimate=cost(6 << 30, 5 << 20),
        name="conv",
    )(core, src, tgt, tab, before, own, after, feats_t, w, *([partial] if begun else []))


def moved(x, peers, to):
    pairs = [(i, to(i)) for i in range(peers)]
    return lax.ppermute(x, "space", [(i, j) for i, j in pairs if j is not None and 0 <= j < peers])


def taken(x, axis, digit):
    return lax.dynamic_index_in_dim(x, digit, axis=axis, keepdims=False)


def low_steps(bits):
    left = [list(range(bits - 1, -1, -1)) for core in range(2)]
    steps = []
    for j in range(bits):
        by = (j, (j + bits // 2) % bits)
        steps.append((by, [left[core].index(by[core]) for core in range(2)]))
        for core in range(2):
            left[core].remove(by[core])
    return steps


def fold_low(parts, me, step):
    core = me % 2
    by, axes = step
    bit = jnp.where(core == 0, me >> (1 + by[0]), me >> (1 + by[1])) % 2

    def half(x, digit):
        if axes[0] == axes[1]:
            return taken(x, 1 + axes[0], digit)
        return jnp.where(core == 0, taken(x, 1 + axes[0], digit), taken(x, 1 + axes[1], digit))

    def piece(digit):
        pieces = [half(kept, digit) + half(got, digit).astype(F32) for kept, got in parts]
        return jnp.concatenate(pieces, 0) if len(pieces) > 1 else pieces[0]

    return piece(bit), piece(1 - bit).astype(BF), lambda i: i ^ (2 << by[i % 2])


def fold_bit(keep, got, me, peers, stride, first):
    bit = me // stride % 2
    axis = keep.ndim - 3

    def piece(digit):
        return taken(keep, axis, digit) + taken(got, axis, digit).astype(F32)

    mine = bit ^ first
    sent = piece(1 - mine).astype(BF)
    return piece(mine), moved(sent, peers, lambda i: i ^ stride)


def per_device(
    feats,
    pre_act,
    coarse_grad,
    w_sub,
    w_down,
    pair_src,
    pair_tgt,
    pair_rows,
    down_rows,
    down_parent,
):
    peers = lax.axis_size("space")
    me = lax.axis_index("space")
    row_count, channels = feats.shape
    block_rows = pair_rows.shape[-1]
    out_width = coarse_grad.shape[1]
    kernel = pair_src.shape[1]
    children = down_rows.shape[1]
    scale = 1.0 / math.sqrt(peers * row_count)
    bits = (peers // 8).bit_length() - 1
    steps = low_steps(bits)
    near, far = peers // 4, peers // 2

    previous = moved(coarse_grad[-block_rows:], peers, lambda i: i + 1)
    feats_t, act, tab, pick, parent_pick, chosen = prep(
        feats,
        pre_act,
        pair_rows[0].reshape(-1, block_rows),
        down_rows[0],
        down_parent[0],
        block_rows + coarse_grad.shape[0],
    )
    grad_pre, head, tail, gathered = down_grad(
        previous, coarse_grad, act, w_down, pick, parent_pick, HB * block_rows
    )
    before = moved(tail, peers, lambda i: i + 1)
    after = moved(head, peers, lambda i: i - 1)
    src = pair_src[0].T
    tgt = pair_tgt[0].T
    core = (me % 2).reshape(1)
    pinned = lax.optimization_barrier

    def across(x):
        return moved(x, peers, lambda i: i ^ 1)

    def spread(both, got, high):
        shape = (high,) + (2,) * bits + got.shape[-2:]
        return both[0].reshape(shape), got.reshape(shape)

    def quarter(number, partial=None, final=False):
        return conv(
            core, src, tgt, tab, before, grad_pre, after, feats_t, w_sub,
            number, kernel * channels // peers, partial, final,
        )

    down, down_send = down_weight(
        core,
        chosen,
        gathered,
        w_sub,
        children * channels // peers,
        (children * channels, out_width),
    )
    before, after, down_send = pinned((before, after, down_send))
    down_got = across(down_send)
    partial, sub0, send0 = quarter(0)
    partial, sub0, send0, down_got = pinned((partial, sub0, send0, down_got))

    got0 = across(send0)
    down, down_send, to = fold_low([spread(down, down_got, 4)], me, steps[0])
    down_got = moved(down_send, peers, to)
    partial, sub3, send3 = quarter(3, partial)
    partial, sub3, send3, got0, down, down_got = pinned(
        (partial, sub3, send3, got0, down, down_got)
    )

    got3 = across(send3)
    for step in steps[1:]:
        down, down_send, to = fold_low([(down, down_got)], me, step)
        down_got = moved(down_send, peers, to)
    partial, sub1, send1 = quarter(1, partial)
    partial, sub1, send1, got3, down, down_got = pinned(
        (partial, sub1, send1, got3, down, down_got)
    )

    got1 = across(send1)
    outer, outer_send, to = fold_low([spread(sub0, got0, 1), spread(sub3, got3, 1)], me, steps[0])
    outer_got = moved(outer_send, peers, to)
    down, down_got = (x.reshape((2, 2) + x.shape[-2:]) for x in (down, down_got))
    down, down_got = fold_bit(down, down_got, me, peers, near, 0)
    grad_in, sub2, send2 = quarter(2, partial, True)
    grad_in, sub2, send2, got1, outer, outer_got, down, down_got = pinned(
        (grad_in, sub2, send2, got1, outer, outer_got, down, down_got)
    )

    got2 = across(send2)
    for step in steps[1:]:
        outer, outer_send, to = fold_low([(outer, outer_got)], me, step)
        outer_got = moved(outer_send, peers, to)
    down, down_got = fold_bit(down, down_got, me, peers, far, 0)
    got2, outer, outer_got, down, down_got = pinned((got2, outer, outer_got, down, down_got))

    inner, inner_send, to = fold_low([spread(sub1, got1, 1), spread(sub2, got2, 1)], me, steps[0])
    inner_got = moved(inner_send, peers, to)
    outer, outer_got = fold_bit(outer, outer_got, me, peers, near, 0)
    down_sum = (down + down_got.astype(F32)) * scale
    inner, inner_got, outer, outer_got, down_sum = pinned(
        (inner, inner_got, outer, outer_got, down_sum)
    )

    for step in steps[1:]:
        inner, inner_send, to = fold_low([(inner, inner_got)], me, step)
        inner_got = moved(inner_send, peers, to)
    inner, inner_got = fold_bit(inner, inner_got, me, peers, near, 1)

    digit = me // near
    is_outer = (digit == 0) | (digit == 3)
    outer_sum = outer + outer_got.astype(F32)
    inner_sum = inner + inner_got.astype(F32)
    sent = jnp.where(is_outer, inner_sum, outer_sum).astype(BF)
    sub_sum = jnp.where(is_outer, outer_sum, inner_sum)
    sub_sum = sub_sum + moved(sent, peers, lambda i: i ^ far).astype(F32)
    return (grad_in, sub_sum.reshape(-1) * scale, down_sum)


def solution(mesh):
    rows = ("scene", "space")
    placed = (
        P(rows, None),
        P(rows, None),
        P(rows, None),
        P(),
        P(),
        P(rows, None, None),
        P(rows, None, None),
        P(rows, None, None, None),
        P(rows, None, None),
        P(rows, None, None),
    )
    return jax.shard_map(
        per_device,
        mesh=mesh,
        in_specs=placed,
        out_specs=(P(rows, None), P(rows), P(rows, None)),
        check_vma=False,
    )
```

time: 518 us -> 105 us (0.20)
  waiting for transfers between devices: 305 us -> 28.9 us
  matrix products: 104 us -> 0 us
  local copies, waits for them, and re-layouts: 78.3 us -> 21 us
  Pallas kernels: 0 us -> 20.3 us
  starting transfers between devices: 8.79 us -> 24 us
  between operations: 14.1 us -> 1.09 us
  other arithmetic: 3.86 us -> 9.22 us
    unnamed x3 -> x0, waiting for transfers between devices: 159 us -> none
    reduce_scatter x1 -> x0, waiting for transfers between devices: 142 us -> none  [per_device(): lax.psum_scatter(down_term, 'space', scatter_dimension=0, tiled=True)]
    dot_general x86 -> x0, matrix products: 104 us -> none  [the longest x27 37.5 us: slot_pieces(): jnp.einsum('pe,erc->prc', block_pick, ext_blocks, preferred_element_type=...]
    eq x55 -> x0, local copies, waits for them, and re-layouts: 38 us -> none  [the longest x27 18.7 us: slot_pieces(): targets[:, None] == jnp.arange(block_count)[None, :]]
    ppermute x3 -> x19, waiting for transfers between devices: 3.27 us -> 28.9 us  [moved(): lax.ppermute(x, 'space', [(i, j) for i, j in pairs if j is not None and 0...]
    pallas_call x0 -> x7, Pallas kernels: none -> 20.3 us  [the longest x4 15.6 us: conv(): pl.pallas_call(functools.partial(conv_kernel, conv_plan(kernel, channels,...]
    dynamic_update_slice x27 -> x0, local copies, waits for them, and re-layouts: 19.6 us -> none  [per_device(): columns = lax.map(offset_sum, (pair_tgt[0], pair_rows[0], owners))]
    ppermute x3 -> x19, starting transfers between devices: 8.53 us -> 24 us  [moved(): lax.ppermute(x, 'space', [(i, j) for i, j in pairs if j is not None and 0...]
  transfers between devices with their start and end apart: 5 -> 19, of which waited for: 3 -> 8; matrix products, arithmetic and copies ran while one was open for 3% -> 9% of each run, Pallas kernels for 0% -> 18%
where the time goes in v4:
time: 105 us
  waiting for transfers between devices  28.9 us (28%)
  starting transfers between devices  24 us (23%)
  local copies, waits for them, and re-layouts  21 us (20%)
  Pallas kernels  20.3 us (19%)
  other arithmetic  9.22 us (9%)
  between operations  1.09 us (1%)
    ppermute x19, waiting for transfers between devices, moved(): lax.ppermute(x, 'space', [(i, j) for i, j in pairs if j is not None and 0...  28.9 us
    ppermute x19, starting transfers between devices, moved(): lax.ppermute(x, 'space', [(i, j) for i, j in pairs if j is not None and 0...  24 us
    unnamed x61, local copies, waits for them, and re-layouts  15.9 us
    pallas_call x4, Pallas kernels, conv(): pl.pallas_call(functools.partial(conv_kernel, conv_plan(kernel, channels,...  15.6 us
    dynamic_slice x4, local copies, waits for them, and re-layouts, taken(): return lax.dynamic_index_in_dim(x, digit, axis=axis, keepdims=False)  3.07 us
    another operation x3, other arithmetic  2.35 us
    convert_element_type x4, other arithmetic, fold_bit(): sent = piece(1 - mine).astype(BF)  2.15 us
  transfers between devices with their start and end apart: 19, of which 8 were waited for; matrix products, arithmetic and copies ran while one was open for 9% of the time, Pallas kernels for 18%

profile of v4, /device:TPU:0, one launch (start us, length us, event | category | flops | bytes accessed | tf_op | source)
XLA Modules:
  0.0 104.6 jit_solution(4166140756815710865)
XLA Ops:
  0.7 2.5 %collective-permute-start = (bf16[128,512]{1,0:T(8,128)(2,1)}, bf16[128,512]{1,0:T(8,128)(2,1)S(1)}, u32[]{:S(2)}, u32[]{:S(2)}) collective-permute-start(bf16[128,512]{1,0:T(8,128)(2,1)} %cur.1), channel_id=1, source_target_pairs={{0,1},{1,2},{2,3},{3,4},{4,5},{5,6},{6,7},{7,8},{8,9},{9,10},{10,1... | collective-permute-start | bytes 393224 | tf_op jit(solution)/shard_map/ppermute | solution.py:236
  3.2 0.9 copy-done.12
  4.1 0.9 copy-done.13
  5.1 0.9 copy-done.16
  6.0 0.7 copy-done.17
  6.6 0.7 copy-done.18
  7.3 0.9 prep.1
  8.3 0.8 copy-done.5
  9.1 0.7 copy-done.21
  9.8 0.7 copy-done.23
  10.4 2.0 %down_grad.1 = (bf16[512,256]{1,0:T(8,128)(2,1)S(1)}, bf16[256,256]{1,0:T(8,128)(2,1)}, bf16[256,256]{1,0:T(8,128)(2,1)}, bf16[1024,512]{1,0:T(8,128)(2,1)S(1)}) custom-call(bf16[128,512]{1,0:T(8,128)(2,1)S(1)} %collective-permute-done.prev, bf16[128,512]{1,0:T(8,128)(2,1)S(1)} %copy-done.11, bf16[512,256]{1,0:T(8,128)(2,1)S(1)} %get-tuple-element.65.act, ...), custom_call_target="tpu_custom_call" | custom-call | flops 1073741824 | bytes 4194304 | tf_op jit(solution)/shard_map/down_grad/pallas_call | solution.py:122
  12.5 1.0 copy-done.3
  13.5 0.7 copy-done.14
  14.2 5.1 %collective-permute-start.1 = (bf16[256,256]{1,0:T(8,128)(2,1)}, bf16[256,256]{1,0:T(8,128)(2,1)}, u32[]{:S(2)}, u32[]{:S(2)}) collective-permute-start(bf16[256,256]{1,0:T(8,128)(2,1)} %get-tuple-element.68), channel_id=1, source_target_pairs={{0,1},{1,2},{2,3},{3,4},{4,5},{5,6},{6,7},{7,8},{8,9},{9,10},{10,1... | collective-permute-start | bytes 393224 | tf_op jit(solution)/shard_map/ppermute | solution.py:236
  19.3 1.5 %collective-permute-start.2 = (bf16[256,256]{1,0:T(8,128)(2,1)}, bf16[256,256]{1,0:T(8,128)(2,1)}, u32[]{:S(2)}, u32[]{:S(2)}) collective-permute-start(bf16[256,256]{1,0:T(8,128)(2,1)} %get-tuple-element.69), channel_id=1, source_target_pairs={{1,0},{2,1},{3,2},{4,3},{5,4},{6,5},{7,6},{8,7},{9,8},{10,9},{11,1... | collective-permute-start | bytes 393224 | tf_op jit(solution)/shard_map/ppermute | solution.py:236
  20.8 1.2 %copy-done.4 = bf16[1024,512]{1,0:T(8,128)(2,1)S(1)} copy-done((bf16[1024,512]{1,0:T(8,128)(2,1)S(1)}, bf16[1024,512]{1,0:T(8,128)(2,1)}, u32[]{:S(2)}) %copy-start.4) | copy-done | bytes 1048600
  22.0 1.0 copy-done.6
  23.1 1.8 %down_weight.1 = (f32[2,16,64,512]{3,2,1,0:T(8,128)S(1)}, bf16[16,64,512]{2,1,0:T(8,128)(2,1)}) custom-call(s32[1]{0:T(128)} %bitcast.core.refs_0_, bf16[256,1024]{1,0:T(8,128)(2,1)S(1)} %copy-done.6, bf16[1024,512]{1,0:T(8,128)(2,1)S(1)} %copy-done.4, bf16[6912,256]{1,0:T(8,128)(2,1)S(1)} %copy-done), custom_call_target="tpu_custom_call" | custom-call | flops 1073741824 | bytes 6291456 | tf_op jit(solution)/shard_map/down_weight/pallas_call | solution.py:146
  24.9 2.0 %copy-done.2 = f32[2,16,64,512]{3,2,1,0:T(8,128)} copy-done((f32[2,16,64,512]{3,2,1,0:T(8,128)}, f32[2,16,64,512]{3,2,1,0:T(8,128)S(1)}, u32[]{:S(2)}) %copy-start.2) | copy-done | bytes 4194328
  26.9 1.1 %collective-permute-start.3 = (bf16[16,64,512]{2,1,0:T(8,128)(2,1)}, bf16[16,64,512]{2,1,0:T(8,128)(2,1)}, u32[]{:S(2)}, u32[]{:S(2)}) collective-permute-start(bf16[16,64,512]{2,1,0:T(8,128)(2,1)} %get-tuple-element.80), channel_id=1, source_target_pairs={{0,1},{1,0},{2,3},{3,2},{4,5},{5,4},{6,7},{7,6},{8,9},{9,8},{10,11... | collective-permute-start | bytes 3145736 | tf_op jit(solution)/shard_map/ppermute | solution.py:236
  28.0 1.8 %slice.15 = f32[1,16,64,512]{3,2,1,0:T(8,128)S(1)} slice(f32[2,16,64,512]{3,2,1,0:T(8,128)} %copy-done.2), slice={[0:1], [0:16], [0:64], [0:512]} | slice | bytes 4194304 | tf_op jit(solution)/shard_map/slice | solution.py:331
  29.8 0.3 constant_dynamic-slice_fusion.3
  30.1 0.3 constant_dynamic-slice_fusion.2
  30.4 0.6 copy-done.15
  31.0 0.1 copy-done.22
  31.2 3.5 %conv.4 = (f32[512,256]{1,0:T(8,128)S(1)}, f32[2,4,216,256]{3,2,1,0:T(8,128)S(1)}, bf16[4,216,256]{2,1,0:T(8,128)(2,1)S(1)}) custom-call(s32[1]{0:T(128)} %bitcast.core.refs_0_, s32[8,27]{1,0:T(8,128)S(1)} %bitcast.214, s32[8,27]{1,0:T(8,128)S(1)} %bitcast.218, s32[128,216]{1,0:T(8,128)S(1)} %copy-done.24, bf16[256,256]{1,0:T(8,128)(2,1)} %collective-permute-done.1.refs_4_, ...), custom_call_target="tpu_custom_call" | custom-call | flops 6442450944 | bytes 5242880 | tf_op jit(solution)/shard_map/conv/pallas_call | solution.py:217
  34.7 1.3 %constant_dynamic-slice_fusion.1 = (bf16[4,2,1,64,512]{4,3,2,1,0:T(8,128)(2,1)S(1)}, bf16[4,2,1,64,512]{4,3,2,1,0:T(8,128)(2,1)S(1)}) fusion(bf16[4,2,2,64,512]{4,3,2,1,0:T(8,128)(2,1)} %bitcast.13, s32[]{:T(128)S(6)} %select_n.412, s32[]{:T(128)S(6)} %select_n.409), kind=kLoop, calls=%fused_computation.69 | loop fusion | bytes 2097160 | tf_op jit(solution)/shard_map/jit(dynamic_index_in_dim)/dynamic_slice | solution.py:240
  36.0 1.3 %constant_dynamic-slice_fusion = (bf16[4,1,2,64,512]{4,3,2,1,0:T(8,128)(2,1)S(1)}, bf16[4,1,2,64,512]{4,3,2,1,0:T(8,128)(2,1)S(1)}) fusion(bf16[4,2,2,64,512]{4,3,2,1,0:T(8,128)(2,1)} %bitcast.13, s32[]{:T(128)S(6)} %select_n.412, s32[]{:T(128)S(6)} %select_n.409), kind=kLoop, calls=%fused_computation.68 | loop fusion | bytes 2097160 | tf_op jit(solution)/shard_map/jit(dynamic_index_in_dim)/dynamic_slice | solution.py:240
  37.3 0.2 collective-permute-start.4
  37.5 0.3 fusion.1
  37.8 1.0 collective-permute-start.5
  38.8 3.5 %conv.5 = (f32[512,256]{1,0:T(8,128)S(1)}, f32[2,4,216,256]{3,2,1,0:T(8,128)S(1)}, bf16[4,216,256]{2,1,0:T(8,128)(2,1)S(1)}) custom-call(s32[1]{0:T(128)} %bitcast.core.refs_0_, s32[8,27]{1,0:T(8,128)S(1)} %bitcast.215, s32[8,27]{1,0:T(8,128)S(1)} %bitcast.219, s32[128,216]{1,0:T(8,128)S(1)} %copy-done.24, bf16[256,256]{1,0:T(8,128)(2,1)} %collective-permute-done.1.refs_4_, ...), custom_call_target="tpu_custom_call" | custom-call | flops 6442450944 | bytes 5242880 | tf_op jit(solution)/shard_map/conv/pallas_call | solution.py:217
  42.3 0.4 fusion.2
  42.7 4.3 %collective-permute-done.5 = bf16[4,2,64,512]{3,2,0,1:T(8,128)(2,1)S(1)} collective-permute-done((bf16[4,2,64,512]{3,2,0,1:T(8,128)(2,1)S(1)}, bf16[4,2,64,512]{3,2,0,1:T(8,128)(2,1)S(1)}, u32[]{:S(2)}, u32[]{:S(2)}) %collective-permute-start.5) | collective-permute-done | bytes 524320 | tf_op jit(solution)/shard_map/ppermute | solution.py:236
  47.1 0.1 fusion.16
  47.2 1.9 %collective-permute-start.7 = (bf16[4,64,512]{2,1,0:T(8,128)(2,1)S(1)}, bf16[4,64,512]{2,1,0:T(8,128)(2,1)S(1)}, u32[]{:S(2)}, u32[]{:S(2)}) collective-permute-start(bf16[4,64,512]{2,1,0:T(8,128)(2,1)S(1)} %get-tuple-element.129), channel_id=1, source_target_pairs={{0,4},{1,3},{2,6},{3,1},{4,0},{5,7},{6,2},{7,5},{8,12},{9,11},{10,... | collective-permute-start | bytes 786440 | tf_op jit(solution)/shard_map/ppermute | solution.py:236
  49.1 3.8 %conv.6 = (f32[512,256]{1,0:T(8,128)S(1)}, f32[2,4,216,256]{3,2,1,0:T(8,128)S(1)}, bf16[4,216,256]{2,1,0:T(8,128)(2,1)S(1)}) custom-call(s32[1]{0:T(128)} %bitcast.core.refs_0_, s32[8,27]{1,0:T(8,128)S(1)} %bitcast.216, s32[8,27]{1,0:T(8,128)S(1)} %bitcast.220, s32[128,216]{1,0:T(8,128)S(1)} %copy-done.24, bf16[256,256]{1,0:T(8,128)(2,1)} %collective-permute-done.1.refs_4_, ...), custom_call_target="tpu_custom_call" | custom-call | flops 6442450944 | bytes 5242880 | tf_op jit(solution)/shard_map/conv/pallas_call | solution.py:217
  52.9 1.2 %copy-done.7 = f32[2,4,216,256]{3,2,1,0:T(8,128)} copy-done((f32[2,4,216,256]{3,2,1,0:T(8,128)}, f32[2,4,216,256]{3,2,1,0:T(8,128)S(1)}, u32[]{:S(2)}) %copy-start.7) | copy-done | bytes 1769496
  54.2 0.3 fusion.13
  54.5 2.0 %collective-permute-start.10 = (bf16[2,64,512]{2,1,0:T(8,128)(2,1)S(1)}, bf16[2,64,512]{2,1,0:T(8,128)(2,1)S(1)}, u32[]{:S(2)}, u32[]{:S(2)}) collective-permute-start(bf16[2,64,512]{2,1,0:T(8,128)(2,1)S(1)} %fusion.21), channel_id=1, source_target_pairs={{0,8},{1,9},{2,10},{3,11},{4,12},{5,13},{6,14},{7,15},{8,0},{9,1},... | collective-permute-start | bytes 393224 | tf_op jit(solution)/shard_map/ppermute | solution.py:236
  56.5 0.3 fusion.11
  56.9 1.0 collective-permute-start.9
  57.9 4.8 %conv.7 = (bf16[512,256]{1,0:T(8,128)(2,1)}, f32[2,4,216,256]{3,2,1,0:T(8,128)S(1)}, bf16[4,216,256]{2,1,0:T(8,128)(2,1)}) custom-call(s32[1]{0:T(128)} %bitcast.core.refs_0_, s32[8,27]{1,0:T(8,128)S(1)} %bitcast.217, s32[8,27]{1,0:T(8,128)S(1)} %bitcast.221, s32[128,216]{1,0:T(8,128)S(1)} %copy-done.24, bf16[256,256]{1,0:T(8,128)(2,1)} %collective-permute-done.1.refs_4_, ...), custom_call_target="tpu_custom_call" | custom-call | flops 6442450944 | bytes 5242880 | tf_op jit(solution)/shard_map/conv/pallas_call | solution.py:217
  62.7 0.8 fusion.17
  63.6 1.6 %collective-permute-done.9 = bf16[2,2,216,256]{3,2,0,1:T(8,128)(2,1)S(1)} collective-permute-done((bf16[2,2,216,256]{3,2,0,1:T(8,128)(2,1)S(1)}, bf16[2,2,216,256]{3,2,0,1:T(8,128)(2,1)S(1)}, u32[]{:S(2)}, u32[]{:S(2)}) %collective-permute-start.9) | collective-permute-done | bytes 442400 | tf_op jit(solution)/shard_map/ppermute | solution.py:236
  65.2 0.9 fusion.18
  66.2 1.1 %collective-permute-start.12 = (bf16[2,216,256]{2,1,0:T(8,128)(2,1)}, bf16[2,216,256]{2,1,0:T(8,128)(2,1)}, u32[]{:S(2)}, u32[]{:S(2)}) collective-permute-start(bf16[2,216,256]{2,1,0:T(8,128)(2,1)} %get-tuple-element.135), channel_id=1, source_target_pairs={{0,4},{1,3},{2,6},{3,1},{4,0},{5,7},{6,2},{7,5},{8,12},{9,11},{10,... | collective-permute-start | bytes 663560 | tf_op jit(solution)/shard_map/ppermute | solution.py:236
  67.3 1.1 %fusion.24 = (bf16[64,512]{1,0:T(8,128)(2,1)S(1)}, f32[64,512]{1,0:T(8,128)S(1)}) fusion(f32[2,64,512]{2,1,0:T(8,128)} %fusion.17, s32[]{:T(128)S(6)} %select_n.439, bf16[2,64,512]{2,1,0:T(8,128)(2,1)} %copy-done.29, s32[]{:T(128)S(6)} %select_n.438), kind=kLoop, calls=%fused_computation.67 | loop fusion | flops 163840 | bytes 589832 | tf_op jit(solution)/shard_map/convert_element_type | solution.py:279
  68.4 2.7 %collective-permute-start.13 = (bf16[64,512]{1,0:T(8,128)(2,1)S(1)}, bf16[64,512]{1,0:T(8,128)(2,1)S(1)}, u32[]{:S(2)}, u32[]{:S(2)}) collective-permute-start(bf16[64,512]{1,0:T(8,128)(2,1)S(1)} %get-tuple-element.147), channel_id=1, source_target_pairs={{0,16},{1,17},{2,18},{3,19},{4,20},{5,21},{6,22},{7,23},{8,24},{9,... | collective-permute-start | bytes 196616 | tf_op jit(solution)/shard_map/ppermute | solution.py:236
  71.1 3.6 %collective-permute-done.13 = bf16[64,512]{1,0:T(8,128)(2,1)S(1)} collective-permute-done((bf16[64,512]{1,0:T(8,128)(2,1)S(1)}, bf16[64,512]{1,0:T(8,128)(2,1)S(1)}, u32[]{:S(2)}, u32[]{:S(2)}) %collective-permute-start.13) | collective-permute-done | bytes 65568 | tf_op jit(solution)/shard_map/ppermute | solution.py:236
  74.7 1.8 %fusion.5 = (bf16[1,2,216,256]{3,2,0,1:T(8,128)(2,1)S(1)}, f32[1,2,216,256]{3,2,0,1:T(8,128)S(1)}, f32[1,2,216,256]{3,2,0,1:T(8,128)S(1)}, bf16[1,2,216,256]{3,2,0,1:T(8,128)(2,1)S(1)}) fusion(f32[1,2,2,216,256]{4,3,2,1,0:T(8,128)S(1)} %bitcast.225, s32[]{:T(128)S(6)} %select_n.412, bf16[1,2,2,216,256]{4,3,2,1,0:T(8,128)(2,1)} %bitcast.59, pred[]{:T(512)S(6)} %eq.24, ...), kind=kLoop, calls=%fused_computation.17 | loop fusion | flops 1990656 | bytes 6635529 | tf_op jit(solution)/shard_map/convert.1
  76.6 1.2 %collective-permute-start.14 = (bf16[2,2,216,256]{3,2,0,1:T(8,128)(2,1)S(1)}, bf16[2,2,216,256]{3,2,0,1:T(8,128)(2,1)S(1)}, u32[]{:S(2)}, u32[]{:S(2)}) collective-permute-start(bf16[2,2,216,256]{3,2,0,1:T(8,128)(2,1)S(1)} %pad_maximum_fusion.3), channel_id=1, source_target_pairs={{0,2},{1,5},{2,0},{3,7},{4,6},{5,1},{6,4},{7,3},{8,10},{9,13},{10,... | collective-permute-start | bytes 1327112 | tf_op jit(solution)/shard_map/ppermute | solution.py:236
  77.8 1.0 fusion.22
  78.9 0.7 add_multiply_fusion
  79.6 4.0 %collective-permute-done.15 = bf16[216,256]{1,0:T(8,128)(2,1)S(1)} collective-permute-done((bf16[216,256]{1,0:T(8,128)(2,1)S(1)}, bf16[216,256]{1,0:T(8,128)(2,1)S(1)}, u32[]{:S(2)}, u32[]{:S(2)}) %collective-permute-start.15) | collective-permute-done | bytes 110624 | tf_op jit(solution)/shard_map/ppermute | solution.py:236
  83.6 1.4 %collective-permute-done.14 = bf16[2,2,216,256]{3,2,0,1:T(8,128)(2,1)S(1)} collective-permute-done((bf16[2,2,216,256]{3,2,0,1:T(8,128)(2,1)S(1)}, bf16[2,2,216,256]{3,2,0,1:T(8,128)(2,1)S(1)}, u32[]{:S(2)}, u32[]{:S(2)}) %collective-permute-start.14) | collective-permute-done | bytes 442400 | tf_op jit(solution)/shard_map/ppermute | solution.py:236
  85.0 0.8 copy-done.28
  85.8 0.8 collective-permute-start.16
  86.6 1.0 convert_add_fusion
  87.6 4.2 %collective-permute-done.16 = bf16[2,216,256]{2,1,0:T(8,128)(2,1)S(1)} collective-permute-done((bf16[2,216,256]{2,1,0:T(8,128)(2,1)S(1)}, bf16[2,216,256]{2,1,0:T(8,128)(2,1)S(1)}, u32[]{:S(2)}, u32[]{:S(2)}) %collective-permute-start.16) | collective-permute-done | bytes 221216 | tf_op jit(solution)/shard_map/ppermute | solution.py:236
  92.0 4.7 %collective-permute-done.17 = bf16[216,256]{1,0:T(8,128)(2,1)S(1)} collective-permute-done((bf16[216,256]{1,0:T(8,128)(2,1)S(1)}, bf16[216,256]{1,0:T(8,128)(2,1)S(1)}, u32[]{:S(2)}, u32[]{:S(2)}) %collective-permute-start.17) | collective-permute-done | bytes 110624 | tf_op jit(solution)/shard_map/ppermute | solution.py:236
  96.8 1.9 %collective-permute-start.18 = (bf16[216,256]{1,0:T(8,128)(2,1)S(1)}, bf16[216,256]{1,0:T(8,128)(2,1)S(1)}, u32[]{:S(2)}, u32[]{:S(2)}) collective-permute-start(bf16[216,256]{1,0:T(8,128)(2,1)S(1)} %select_convert_fusion), channel_id=1, source_target_pairs={{0,16},{1,17},{2,18},{3,19},{4,20},{5,21},{6,22},{7,23},{8,24},{9,... | collective-permute-start | bytes 331784 | tf_op jit(solution)/shard_map/ppermute | solution.py:236
  98.7 5.0 %collective-permute-done.18 = bf16[216,256]{1,0:T(8,128)(2,1)S(1)} collective-permute-done((bf16[216,256]{1,0:T(8,128)(2,1)S(1)}, bf16[216,256]{1,0:T(8,128)(2,1)S(1)}, u32[]{:S(2)}, u32[]{:S(2)}) %collective-permute-start.18) | collective-permute-done | bytes 110624 | tf_op jit(solution)/shard_map/ppermute | solution.py:236
  103.8 0.8 copy.29
  (72 shorter events, 1.1 us)
Async XLA Ops:
  0.6 9.8 %copy-start.11 = (bf16[128,512]{1,0:T(8,128)(2,1)S(1)}, bf16[128,512]{1,0:T(8,128)(2,1)}, u32[]{:S(2)}) copy-start(bf16[128,512]{1,0:T(8,128)(2,1)} %cur.1) | copy-start | bytes 393220
  0.6 9.8 %copy-start.1 = (bf16[2048,512]{1,0:T(8,128)(2,1)S(1)}, bf16[2048,512]{1,0:T(8,128)(2,1)}, u32[]{:S(2)}) copy-start(bf16[2048,512]{1,0:T(8,128)(2,1)} %w.1) | copy-start | bytes 6291460
  0.7 9.8 %collective-permute-start = (bf16[128,512]{1,0:T(8,128)(2,1)}, bf16[128,512]{1,0:T(8,128)(2,1)S(1)}, u32[]{:S(2)}, u32[]{:S(2)}) collective-permute-start(bf16[128,512]{1,0:T(8,128)(2,1)} %cur.1), channel_id=1, source_target_pairs={{0,1},{1,2},{2,3},{3,4},{4,5},{5,6},{6,7},{7,8},{8,9},{9,10},{10,1... | collective-permute-start | bytes 393224 | tf_op jit(solution)/shard_map/ppermute | solution.py:236
  3.2 1.0 copy-start.12
  4.1 0.9 copy-start.13
  5.1 0.9 copy-start.16
  6.0 0.7 copy-start.17
  6.6 0.7 copy-start.18
  8.3 0.8 copy-start.5
  9.1 0.7 copy-start.21
  9.8 0.7 copy-start.23
  10.4 10.4 %copy-start = (bf16[6912,256]{1,0:T(8,128)(2,1)S(1)}, bf16[6912,256]{1,0:T(8,128)(2,1)}, u32[]{:S(2)}) copy-start(bf16[6912,256]{1,0:T(8,128)(2,1)} %refs_8_.7) | copy-start | bytes 10616836
  12.5 1.0 copy-start.3
  13.5 0.7 copy-start.14
  14.2 12.7 %collective-permute-start.1 = (bf16[256,256]{1,0:T(8,128)(2,1)}, bf16[256,256]{1,0:T(8,128)(2,1)}, u32[]{:S(2)}, u32[]{:S(2)}) collective-permute-start(bf16[256,256]{1,0:T(8,128)(2,1)} %get-tuple-element.68), channel_id=1, source_target_pairs={{0,1},{1,2},{2,3},{3,4},{4,5},{5,6},{6,7},{7,8},{8,9},{9,10},{10,1... | collective-permute-start | bytes 393224 | tf_op jit(solution)/shard_map/ppermute | solution.py:236
  19.3 7.5 %collective-permute-start.2 = (bf16[256,256]{1,0:T(8,128)(2,1)}, bf16[256,256]{1,0:T(8,128)(2,1)}, u32[]{:S(2)}, u32[]{:S(2)}) collective-permute-start(bf16[256,256]{1,0:T(8,128)(2,1)} %get-tuple-element.69), channel_id=1, source_target_pairs={{1,0},{2,1},{3,2},{4,3},{5,4},{6,5},{7,6},{8,7},{9,8},{10,9},{11,1... | collective-permute-start | bytes 393224 | tf_op jit(solution)/shard_map/ppermute | solution.py:236
  20.8 1.2 %copy-start.4 = (bf16[1024,512]{1,0:T(8,128)(2,1)S(1)}, bf16[1024,512]{1,0:T(8,128)(2,1)}, u32[]{:S(2)}) copy-start(bf16[1024,512]{1,0:T(8,128)(2,1)} %copy-done.3) | copy-start | bytes 3145732
  22.0 1.0 copy-start.6
  24.9 2.0 %copy-start.2 = (f32[2,16,64,512]{3,2,1,0:T(8,128)}, f32[2,16,64,512]{3,2,1,0:T(8,128)S(1)}, u32[]{:S(2)}) copy-start(f32[2,16,64,512]{3,2,1,0:T(8,128)S(1)} %get-tuple-element.86) | copy-start | bytes 12582916
  26.9 7.9 %collective-permute-start.3 = (bf16[16,64,512]{2,1,0:T(8,128)(2,1)}, bf16[16,64,512]{2,1,0:T(8,128)(2,1)}, u32[]{:S(2)}, u32[]{:S(2)}) collective-permute-start(bf16[16,64,512]{2,1,0:T(8,128)(2,1)} %get-tuple-element.80), channel_id=1, source_target_pairs={{0,1},{1,0},{2,3},{3,2},{4,5},{5,4},{6,7},{7,6},{8,9},{9,8},{10,11... | collective-permute-start | bytes 3145736 | tf_op jit(solution)/shard_map/ppermute | solution.py:236
  30.1 1.0 copy-start.15
  30.1 0.9 copy-start.19
  30.1 0.9 copy-start.20
  30.1 1.0 copy-start.22
  30.1 1.1 %copy-start.24 = (s32[128,216]{1,0:T(8,128)S(1)}, s32[128,216]{1,0:T(8,128)}, u32[]{:S(2)}) copy-start(s32[128,216]{1,0:T(8,128)} %copy-done.23) | copy-start | bytes 331780
  37.3 5.4 %collective-permute-start.4 = (bf16[4,216,256]{2,1,0:T(8,128)(2,1)S(1)}, bf16[4,216,256]{2,1,0:T(8,128)(2,1)S(1)}, u32[]{:S(2)}, u32[]{:S(2)}) collective-permute-start(bf16[4,216,256]{2,1,0:T(8,128)(2,1)S(1)} %get-tuple-element.85), channel_id=1, source_target_pairs={{0,1},{1,0},{2,3},{3,2},{4,5},{5,4},{6,7},{7,6},{8,9},{9,8},{10,11... | collective-permute-start | bytes 1327112 | tf_op jit(solution)/shard_map/ppermute | solution.py:236
  37.8 9.2 %collective-permute-start.5 = (bf16[4,2,64,512]{3,2,0,1:T(8,128)(2,1)S(1)}, bf16[4,2,64,512]{3,2,0,1:T(8,128)(2,1)S(1)}, u32[]{:S(2)}, u32[]{:S(2)}) collective-permute-start(bf16[4,2,64,512]{3,2,0,1:T(8,128)(2,1)S(1)} %fusion.1), channel_id=1, source_target_pairs={{0,2},{1,5},{2,0},{3,7},{4,6},{5,1},{6,4},{7,3},{8,10},{9,13},{10,... | collective-permute-start | bytes 1572872 | tf_op jit(solution)/shard_map/ppermute | solution.py:236
  47.1 7.4 %collective-permute-start.6 = (bf16[4,216,256]{2,1,0:T(8,128)(2,1)S(1)}, bf16[4,216,256]{2,1,0:T(8,128)(2,1)S(1)}, u32[]{:S(2)}, u32[]{:S(2)}) collective-permute-start(bf16[4,216,256]{2,1,0:T(8,128)(2,1)S(1)} %get-tuple-element.92), channel_id=1, source_target_pairs={{0,1},{1,0},{2,3},{3,2},{4,5},{5,4},{6,7},{7,6},{8,9},{9,8},{10,11... | collective-permute-start | bytes 1327112 | tf_op jit(solution)/shard_map/ppermute | solution.py:236
  47.2 7.2 %collective-permute-start.7 = (bf16[4,64,512]{2,1,0:T(8,128)(2,1)S(1)}, bf16[4,64,512]{2,1,0:T(8,128)(2,1)S(1)}, u32[]{:S(2)}, u32[]{:S(2)}) collective-permute-start(bf16[4,64,512]{2,1,0:T(8,128)(2,1)S(1)} %get-tuple-element.129), channel_id=1, source_target_pairs={{0,4},{1,3},{2,6},{3,1},{4,0},{5,7},{6,2},{7,5},{8,12},{9,11},{10,... | collective-permute-start | bytes 786440 | tf_op jit(solution)/shard_map/ppermute | solution.py:236
  52.9 1.2 %copy-start.7 = (f32[2,4,216,256]{3,2,1,0:T(8,128)}, f32[2,4,216,256]{3,2,1,0:T(8,128)S(1)}, u32[]{:S(2)}) copy-start(f32[2,4,216,256]{3,2,1,0:T(8,128)S(1)} %get-tuple-element.107) | copy-start | bytes 5308420
  54.5 9.0 %collective-permute-start.10 = (bf16[2,64,512]{2,1,0:T(8,128)(2,1)S(1)}, bf16[2,64,512]{2,1,0:T(8,128)(2,1)S(1)}, u32[]{:S(2)}, u32[]{:S(2)}) collective-permute-start(bf16[2,64,512]{2,1,0:T(8,128)(2,1)S(1)} %fusion.21), channel_id=1, source_target_pairs={{0,8},{1,9},{2,10},{3,11},{4,12},{5,13},{6,14},{7,15},{8,0},{9,1},... | collective-permute-start | bytes 393224 | tf_op jit(solution)/shard_map/ppermute | solution.py:236
  56.5 7.0 %collective-permute-start.8 = (bf16[4,216,256]{2,1,0:T(8,128)(2,1)S(1)}, bf16[4,216,256]{2,1,0:T(8,128)(2,1)S(1)}, u32[]{:S(2)}, u32[]{:S(2)}) collective-permute-start(bf16[4,216,256]{2,1,0:T(8,128)(2,1)S(1)} %get-tuple-element.99), channel_id=1, source_target_pairs={{0,1},{1,0},{2,3},{3,2},{4,5},{5,4},{6,7},{7,6},{8,9},{9,8},{10,11... | collective-permute-start | bytes 1327112 | tf_op jit(solution)/shard_map/ppermute | solution.py:236
  56.9 8.4 %collective-permute-start.9 = (bf16[2,2,216,256]{3,2,0,1:T(8,128)(2,1)S(1)}, bf16[2,2,216,256]{3,2,0,1:T(8,128)(2,1)S(1)}, u32[]{:S(2)}, u32[]{:S(2)}) collective-permute-start(bf16[2,2,216,256]{3,2,0,1:T(8,128)(2,1)S(1)} %pad_maximum_fusion.2), channel_id=1, source_target_pairs={{0,2},{1,5},{2,0},{3,7},{4,6},{5,1},{6,4},{7,3},{8,10},{9,13},{10,... | collective-permute-start | bytes 1327112 | tf_op jit(solution)/shard_map/ppermute | solution.py:236
  62.7 3.5 %copy-start.9 = (f32[2,4,216,256]{3,2,1,0:T(8,128)}, f32[2,4,216,256]{3,2,1,0:T(8,128)S(1)}, u32[]{:S(2)}) copy-start(f32[2,4,216,256]{3,2,1,0:T(8,128)S(1)} %get-tuple-element.109) | copy-start | bytes 5308420
  63.5 7.5 %copy-start.8 = (f32[2,4,216,256]{3,2,1,0:T(8,128)S(1)}, f32[2,4,216,256]{3,2,1,0:T(8,128)}, u32[]{:S(2)}) copy-start(f32[2,4,216,256]{3,2,1,0:T(8,128)} %copy-done.7) | copy-start | bytes 5308420
  63.6 2.6 %copy-start.29 = (bf16[2,64,512]{2,1,0:T(8,128)(2,1)}, bf16[2,64,512]{2,1,0:T(8,128)(2,1)S(1)}, u32[]{:S(2)}) copy-start(bf16[2,64,512]{2,1,0:T(8,128)(2,1)S(1)} %collective-permute-done.10) | copy-start | bytes 393220
  63.6 2.6 %copy-start.26 = (bf16[4,216,256]{2,1,0:T(8,128)(2,1)}, bf16[4,216,256]{2,1,0:T(8,128)(2,1)S(1)}, u32[]{:S(2)}) copy-start(bf16[4,216,256]{2,1,0:T(8,128)(2,1)S(1)} %collective-permute-done.8) | copy-start | bytes 1327108
  65.2 9.5 %collective-permute-start.11 = (bf16[4,216,256]{2,1,0:T(8,128)(2,1)}, bf16[4,216,256]{2,1,0:T(8,128)(2,1)}, u32[]{:S(2)}, u32[]{:S(2)}) collective-permute-start(bf16[4,216,256]{2,1,0:T(8,128)(2,1)} %get-tuple-element.110), channel_id=1, source_target_pairs={{0,1},{1,0},{2,3},{3,2},{4,5},{5,4},{6,7},{7,6},{8,9},{9,8},{10,11... | collective-permute-start | bytes 1327112 | tf_op jit(solution)/shard_map/ppermute | solution.py:236
  66.2 4.9 %copy-start.10 = (f32[2,4,216,256]{3,2,1,0:T(8,128)S(1)}, f32[2,4,216,256]{3,2,1,0:T(8,128)}, u32[]{:S(2)}) copy-start(f32[2,4,216,256]{3,2,1,0:T(8,128)} %copy-done.9) | copy-start | bytes 5308420
  66.2 8.5 %collective-permute-start.12 = (bf16[2,216,256]{2,1,0:T(8,128)(2,1)}, bf16[2,216,256]{2,1,0:T(8,128)(2,1)}, u32[]{:S(2)}, u32[]{:S(2)}) collective-permute-start(bf16[2,216,256]{2,1,0:T(8,128)(2,1)} %get-tuple-element.135), channel_id=1, source_target_pairs={{0,4},{1,3},{2,6},{3,1},{4,0},{5,7},{6,2},{7,5},{8,12},{9,11},{10,... | collective-permute-start | bytes 663560 | tf_op jit(solution)/shard_map/ppermute | solution.py:236
  67.3 7.5 %copy-start.27 = (bf16[4,216,256]{2,1,0:T(8,128)(2,1)S(1)}, bf16[4,216,256]{2,1,0:T(8,128)(2,1)}, u32[]{:S(2)}) copy-start(bf16[4,216,256]{2,1,0:T(8,128)(2,1)} %copy-done.26) | copy-start | bytes 1327108
  68.4 6.4 %collective-permute-start.13 = (bf16[64,512]{1,0:T(8,128)(2,1)S(1)}, bf16[64,512]{1,0:T(8,128)(2,1)S(1)}, u32[]{:S(2)}, u32[]{:S(2)}) collective-permute-start(bf16[64,512]{1,0:T(8,128)(2,1)S(1)} %get-tuple-element.147), channel_id=1, source_target_pairs={{0,16},{1,17},{2,18},{3,19},{4,20},{5,21},{6,22},{7,23},{8,24},{9,... | collective-permute-start | bytes 196616 | tf_op jit(solution)/shard_map/ppermute | solution.py:236
  74.7 3.1 %copy-start.25 = (f32[2,216,256]{2,1,0:T(8,128)S(1)}, f32[2,216,256]{2,1,0:T(8,128)}, u32[]{:S(2)}) copy-start(f32[2,216,256]{2,1,0:T(8,128)} %get-tuple-element.116) | copy-start | bytes 1327108
  76.6 8.4 %collective-permute-start.14 = (bf16[2,2,216,256]{3,2,0,1:T(8,128)(2,1)S(1)}, bf16[2,2,216,256]{3,2,0,1:T(8,128)(2,1)S(1)}, u32[]{:S(2)}, u32[]{:S(2)}) collective-permute-start(bf16[2,2,216,256]{3,2,0,1:T(8,128)(2,1)S(1)} %pad_maximum_fusion.3), channel_id=1, source_target_pairs={{0,2},{1,5},{2,0},{3,7},{4,6},{5,1},{6,4},{7,3},{8,10},{9,13},{10,... | collective-permute-start | bytes 1327112 | tf_op jit(solution)/shard_map/ppermute | solution.py:236
  78.8 4.8 %collective-permute-start.15 = (bf16[216,256]{1,0:T(8,128)(2,1)S(1)}, bf16[216,256]{1,0:T(8,128)(2,1)S(1)}, u32[]{:S(2)}, u32[]{:S(2)}) collective-permute-start(bf16[216,256]{1,0:T(8,128)(2,1)S(1)} %get-tuple-element.145), channel_id=1, source_target_pairs={{0,8},{1,9},{2,10},{3,11},{4,12},{5,13},{6,14},{7,15},{8,0},{9,1},... | collective-permute-start | bytes 331784 | tf_op jit(solution)/shard_map/ppermute | solution.py:236
  85.0 0.8 copy-start.28
  85.8 6.0 %collective-permute-start.16 = (bf16[2,216,256]{2,1,0:T(8,128)(2,1)S(1)}, bf16[2,216,256]{2,1,0:T(8,128)(2,1)S(1)}, u32[]{:S(2)}, u32[]{:S(2)}) collective-permute-start(bf16[2,216,256]{2,1,0:T(8,128)(2,1)S(1)} %fusion.19), channel_id=1, source_target_pairs={{0,4},{1,3},{2,6},{3,1},{4,0},{5,7},{6,2},{7,5},{8,12},{9,11},{10,... | collective-permute-start | bytes 663560 | tf_op jit(solution)/shard_map/ppermute | solution.py:236
  91.9 4.8 %collective-permute-start.17 = (bf16[216,256]{1,0:T(8,128)(2,1)S(1)}, bf16[216,256]{1,0:T(8,128)(2,1)S(1)}, u32[]{:S(2)}, u32[]{:S(2)}) collective-permute-start(bf16[216,256]{1,0:T(8,128)(2,1)S(1)} %fusion.23), channel_id=1, source_target_pairs={{0,8},{1,9},{2,10},{3,11},{4,12},{5,13},{6,14},{7,15},{8,0},{9,1},... | collective-permute-start | bytes 331784 | tf_op jit(solution)/shard_map/ppermute | solution.py:236
  96.8 6.9 %collective-permute-start.18 = (bf16[216,256]{1,0:T(8,128)(2,1)S(1)}, bf16[216,256]{1,0:T(8,128)(2,1)S(1)}, u32[]{:S(2)}, u32[]{:S(2)}) collective-permute-start(bf16[216,256]{1,0:T(8,128)(2,1)S(1)} %select_convert_fusion), channel_id=1, source_target_pairs={{0,16},{1,17},{2,18},{3,19},{4,20},{5,21},{6,22},{7,23},{8,24},{9,... | collective-permute-start | bytes 331784 | tf_op jit(solution)/shard_map/ppermute | solution.py:236

commit v5 on v4

--- a/solution.py
+++ b/solution.py
@@ -41,60 +41,65 @@
 
 
 def halves(total, shard):
-    pairs = total[0] // (2 * shard)
-    return (
-        jax.ShapeDtypeStruct((2, pairs, shard, total[1]), F32),
-        jax.ShapeDtypeStruct((pairs, shard, total[1]), BF),
-    )
+    shape = (total[0] // (2 * shard), shard, total[1])
+    kinds = (jax.ShapeDtypeStruct(shape, F32), jax.ShapeDtypeStruct(shape, BF))
+    return kinds, pltpu.VMEM((2,) + shape, F32)
+
+
+def part(both, keep, send):
+    keep[...] = both[0]
+    send[...] = both[1].astype(BF)
+
+
+def identity(size):
+    return one_hot(lax.broadcasted_iota(jnp.int32, (size, size), 0), (size, size), 1)
+
+
+def turned(table):
+    values = table.astype(F32).astype(BF)
+    return dot_nt(identity(table.shape[1]), values).astype(jnp.int32)
 
 
 VMEM = pl.BlockSpec(memory_space=pltpu.VMEM)
 SMEM = pl.BlockSpec(memory_space=pltpu.SMEM)
 
 
-def cost(flops, nbytes):
-    return pl.CostEstimate(flops=flops, bytes_accessed=nbytes, transcendentals=0)
-
-
-def prep_kernel(feats, pre, pairs, rows, parents, feats_t, act, tab, pick, parent_pick, chosen):
+SMALL = pl.CostEstimate(flops=1 << 20, bytes_accessed=1 << 10, transcendentals=0)
+
+
+def prep_kernel(pre, rows, parents, w, cur, act, pick, parent_pick, chosen):
     children, slots = rows.shape
-    count, channels = feats.shape
-    square = (channels, channels)
-    wide = one_hot(lax.broadcasted_iota(jnp.int32, square, 0), square, 1)
-    eye = wide[:slots, :slots]
+    count, channels = pre.shape
     for c in range(children):
         pick[:, pl.ds(c * slots, slots)] = one_hot(rows[c : c + 1, :], (count, slots), 0)
-    columns = dot_nt(eye, parents[...].astype(F32).astype(BF)).astype(jnp.int32)
+    columns = turned(parents[...])
     for c in range(children):
         parent_pick[pl.ds(c * slots, slots), :] = one_hot(
             columns[:, c : c + 1], (slots, parent_pick.shape[1]), 1
         )
     act[...] = jnp.maximum(pre[...], jnp.zeros((), BF))
-    chosen[...] = dot(dot_nt(wide, act[...]).astype(BF), pick[...]).astype(BF)
-    tab[...] = dot_nt(eye, pairs[...].astype(F32).astype(BF)).astype(jnp.int32)
-    feats_t[...] = dot_nt(wide, feats[...]).astype(BF)
-
-
-def prep(feats, pre, pairs, rows, parents, parent_rows):
-    count, channels = feats.shape
+    act_t = dot_nt(identity(channels), act[...]).astype(BF)
+    chosen[...] = dot(act_t, pick[...]).astype(BF)
+
+
+def prep(pre, rows, parents, w, cur, parent_rows):
+    count, channels = pre.shape
     children, slots = rows.shape
     shapes = (
-        ((channels, count), BF),
-        ((count, channels), BF),
-        ((pairs.shape[1], pairs.shape[0]), jnp.int32),
-        ((count, children * slots), BF),
-        ((children * slots, parent_rows), BF),
-        ((channels, children * slots), BF),
+        (count, channels),
+        (count, children * slots),
+        (children * slots, parent_rows),
+        (channels, children * slots),
     )
     return pl.pallas_call(
         prep_kernel,
-        out_shape=tuple(jax.ShapeDtypeStruct(*shape) for shape in shapes),
+        out_shape=tuple(jax.ShapeDtypeStruct(shape, BF) for shape in shapes),
         in_specs=[VMEM] * 5,
         out_specs=(VMEM,) * len(shapes),
         compiler_params=pltpu.CompilerParams(vmem_limit_bytes=16 << 20),
-        cost_estimate=cost(1 << 30, 3 << 20),
+        cost_estimate=SMALL,
         name="prep",
-    )(feats, pre, pairs, rows, parents)
+    )(pre, rows, parents, w, cur)
 
 
 def down_grad_kernel(prev, cur, act, w, pick, parent_pick, gpre, head, tail, gath, contrib):
@@ -126,12 +131,12 @@
         out_specs=(VMEM,) * 4,
         scratch_shapes=[pltpu.VMEM((listed, channels), BF)],
         compiler_params=pltpu.CompilerParams(vmem_limit_bytes=16 << 20),
-        cost_estimate=cost(1 << 30, 4 << 20),
+        cost_estimate=SMALL,
         name="down_grad",
     )(prev, cur, act, w, pick, parent_pick)
 
 
-def down_weight_kernel(core, chosen, gath, ahead, both, send):
+def down_weight_kernel(core, chosen, gath, ahead, keep, send, both):
     channels, listed = chosen.shape
     pairs, shard = send.shape[:2]
     children = 2 * pairs * shard // channels
@@ -139,46 +144,53 @@
     for c in range(children):
         mine = pl.ds(c * slots, slots)
         place(both, dot(chosen[:, mine], gath[mine, :]), c * channels, core[0])
-    send[...] = both[1].astype(BF)
+    part(both, keep, send)
 
 
 def down_weight(core, chosen, gath, ahead, shard, total):
+    kinds, both = halves(total, shard)
     return pl.pallas_call(
         down_weight_kernel,
-        out_shape=halves(total, shard),
+        out_shape=kinds,
         in_specs=[SMEM, VMEM, VMEM, VMEM],
         out_specs=(VMEM, VMEM),
+        scratch_shapes=[both],
         compiler_params=pltpu.CompilerParams(vmem_limit_bytes=16 << 20),
-        cost_estimate=cost(1 << 30, 6 << 20),
+        cost_estimate=SMALL,
         name="down_weight",
     )(core, chosen, gath, ahead)
 
 
-def conv_plan(kernel, channels, quarter):
+def conv_plan(kernel, channels, quarters):
     size = kernel * channels // 4
-    plan, row = [], quarter * size
-    while row < (quarter + 1) * size:
-        k, first = divmod(row, channels)
-        last = min(channels, (quarter + 1) * size - k * channels)
-        plan.append((k, first, last, row - quarter * size))
-        row += last - first
+    plan, out = [], 0
+    for quarter in quarters:
+        row = quarter * size
+        while row < (quarter + 1) * size:
+            k, first = divmod(row, channels)
+            last = min(channels, (quarter + 1) * size - k * channels)
+            plan.append((k, first, last, out))
+            out += last - first
+            row += last - first
     return plan
 
 
 def conv_kernel(plan, begun, *refs):
-    core, src, tgt, tab, before, own, after, feats_t, w, *rest = refs
+    core, src, tgt, pairs, before, own, after, feats, w, *rest = refs
     if begun:
         partial, *rest = rest
-    grad, both, send, ext, acc, col0, col1 = rest
+    grad, keep, send, both, ext, acc, col0, col1, feats_t, tab = rest
     cols = (col0, col1)
     slots = src.shape[0]
     blocks, rows, channels = col0.shape
-    count = feats_t.shape[1]
+    count = feats.shape[0]
     at = 0
     for piece in (before, own, after):
         for b in range(piece.shape[0] // rows):
             ext[at] = piece[pl.ds(b * rows, rows), :]
             at += 1
+    tab[...] = turned(pairs[...])
+    feats_t[...] = dot_nt(identity(channels), feats[...]).astype(BF)
     acc[...] = partial[...] if begun else jnp.zeros_like(acc)
     lanes = lax.broadcasted_iota(jnp.int32, (rows, rows), 1).astype(jnp.int16)
     one, zero = jnp.ones((), BF), jnp.zeros((), BF)
@@ -202,33 +214,36 @@
         if first == 0:
             acc[...] += dot_nt(column, w[pl.ds(k * channels, channels), :])
     grad[...] = acc[...].astype(grad.dtype)
-    send[...] = both[1].astype(BF)
-
-
-def conv(core, src, tgt, tab, before, own, after, feats_t, w, quarter, shard, partial, final):
-    channels, count = feats_t.shape
+    part(both, keep, send)
+
+
+def conv(core, src, tgt, pairs, before, own, after, feats, w, quarters, shard, partial, final):
+    count, channels = feats.shape
     kernel = w.shape[0] // channels
-    rows = tab.shape[0]
+    rows = pairs.shape[1]
     begun = partial is not None
-    total = (kernel * channels // 4, channels)
+    kinds, both = halves((len(quarters) * kernel * channels // 4, channels), shard)
     ext_rows = count + before.shape[0] + after.shape[0]
     block = (rows, channels)
     grad = jax.ShapeDtypeStruct((count, channels), BF if final else F32)
     return pl.pallas_call(
-        functools.partial(conv_kernel, conv_plan(kernel, channels, quarter), begun),
-        out_shape=(grad,) + halves(total, shard),
+        functools.partial(conv_kernel, conv_plan(kernel, channels, quarters), begun),
+        out_shape=(grad,) + kinds,
         in_specs=[SMEM] * 3 + [VMEM] * (6 + begun),
         out_specs=(VMEM,) * 3,
         scratch_shapes=[
+            both,
             pltpu.VMEM((ext_rows // rows,) + block, BF),
             pltpu.VMEM((count, channels), F32),
             pltpu.VMEM((count // rows,) + block, BF),
             pltpu.VMEM((count // rows,) + block, BF),
+            pltpu.VMEM((channels, count), BF),
+            pltpu.VMEM((rows, pairs.shape[0]), jnp.int32),
         ],
-        compiler_params=pltpu.CompilerParams(vmem_limit_bytes=16 << 20),
-        cost_estimate=cost(6 << 30, 5 << 20),
+        compiler_params=pltpu.CompilerParams(vmem_limit_bytes=20 << 20),
+        cost_estimate=SMALL,
         name="conv",
-    )(core, src, tgt, tab, before, own, after, feats_t, w, *([partial] if begun else []))
+    )(core, src, tgt, pairs, before, own, after, feats, w, *([partial] if begun else []))
 
 
 def moved(x, peers, to):
@@ -305,12 +320,12 @@
     near, far = peers // 4, peers // 2
 
     previous = moved(coarse_grad[-block_rows:], peers, lambda i: i + 1)
-    feats_t, act, tab, pick, parent_pick, chosen = prep(
-        feats,
+    act, pick, parent_pick, chosen = prep(
         pre_act,
-        pair_rows[0].reshape(-1, block_rows),
         down_rows[0],
         down_parent[0],
+        w_down,
+        coarse_grad,
         block_rows + coarse_grad.shape[0],
     )
     grad_pre, head, tail, gathered = down_grad(
@@ -326,14 +341,17 @@
     def across(x):
         return moved(x, peers, lambda i: i ^ 1)
 
-    def spread(both, got, high):
+    def spread(kept, got, high):
         shape = (high,) + (2,) * bits + got.shape[-2:]
-        return both[0].reshape(shape), got.reshape(shape)
-
-    def quarter(number, partial=None, final=False):
+        return kept.reshape(shape), got.reshape(shape)
+
+    pairs = pair_rows[0].reshape(-1, block_rows)
+    shard = kernel * channels // peers
+
+    def quarters(numbers, partial=None, final=False):
         return conv(
-            core, src, tgt, tab, before, grad_pre, after, feats_t, w_sub,
-            number, kernel * channels // peers, partial, final,
+            core, src, tgt, pairs, before, grad_pre, after, feats, w_sub,
+            numbers, shard, partial, final,
         )
 
     down, down_send = down_weight(
@@ -346,32 +364,19 @@
     )
     before, after, down_send = pinned((before, after, down_send))
     down_got = across(down_send)
-    partial, sub0, send0 = quarter(0)
-    partial, sub0, send0, down_got = pinned((partial, sub0, send0, down_got))
-
-    got0 = across(send0)
+    partial, outer, outer_send = quarters((0, 3))
+    partial, outer, outer_send, down_got = pinned((partial, outer, outer_send, down_got))
+
+    outer_got = across(outer_send)
     down, down_send, to = fold_low([spread(down, down_got, 4)], me, steps[0])
     down_got = moved(down_send, peers, to)
-    partial, sub3, send3 = quarter(3, partial)
-    partial, sub3, send3, got0, down, down_got = pinned(
-        (partial, sub3, send3, got0, down, down_got)
-    )
-
-    got3 = across(send3)
-    for step in steps[1:]:
-        down, down_send, to = fold_low([(down, down_got)], me, step)
-        down_got = moved(down_send, peers, to)
-    partial, sub1, send1 = quarter(1, partial)
-    partial, sub1, send1, got3, down, down_got = pinned(
-        (partial, sub1, send1, got3, down, down_got)
-    )
+    partial, sub1, send1 = quarters((1,), partial)
+    partial, sub1, send1, outer_got = pinned((partial, sub1, send1, outer_got))
 
     got1 = across(send1)
-    outer, outer_send, to = fold_low([spread(sub0, got0, 1), spread(sub3, got3, 1)], me, steps[0])
+    outer, outer_send, to = fold_low([spread(outer, outer_got, 2)], me, steps[0])
     outer_got = moved(outer_send, peers, to)
-    down, down_got = (x.reshape((2, 2) + x.shape[-2:]) for x in (down, down_got))
-    down, down_got = fold_bit(down, down_got, me, peers, near, 0)
-    grad_in, sub2, send2 = quarter(2, partial, True)
+    grad_in, sub2, send2 = quarters((2,), partial, True)
     grad_in, sub2, send2, got1, outer, outer_got, down, down_got = pinned(
         (grad_in, sub2, send2, got1, outer, outer_got, down, down_got)
     )
@@ -380,30 +385,31 @@
     for step in steps[1:]:
         outer, outer_send, to = fold_low([(outer, outer_got)], me, step)
         outer_got = moved(outer_send, peers, to)
-    down, down_got = fold_bit(down, down_got, me, peers, far, 0)
-    got2, outer, outer_got, down, down_got = pinned((got2, outer, outer_got, down, down_got))
-
+        down, down_send, to = fold_low([(down, down_got)], me, step)
+        down_got = moved(down_send, peers, to)
     inner, inner_send, to = fold_low([spread(sub1, got1, 1), spread(sub2, got2, 1)], me, steps[0])
     inner_got = moved(inner_send, peers, to)
-    outer, outer_got = fold_bit(outer, outer_got, me, peers, near, 0)
-    down_sum = (down + down_got.astype(F32)) * scale
-    inner, inner_got, outer, outer_got, down_sum = pinned(
-        (inner, inner_got, outer, outer_got, down_sum)
-    )
-
     for step in steps[1:]:
         inner, inner_send, to = fold_low([(inner, inner_got)], me, step)
         inner_got = moved(inner_send, peers, to)
+    down, down_got = (x.reshape((2, 2) + x.shape[-2:]) for x in (down, down_got))
+    down, down_got = fold_bit(down, down_got, me, peers, near, 0)
+    outer, outer_got = fold_bit(outer, outer_got, me, peers, near, 0)
+    down, down_got = fold_bit(down, down_got, me, peers, far, 0)
     inner, inner_got = fold_bit(inner, inner_got, me, peers, near, 1)
+
+    def last_step(kept, got, wanted):
+        total = kept + got.astype(F32)
+        to = lambda i: i ^ far if (i ^ far) // near in wanted else None
+        return total + moved(total.astype(BF), peers, to).astype(F32)
 
     digit = me // near
     is_outer = (digit == 0) | (digit == 3)
-    outer_sum = outer + outer_got.astype(F32)
-    inner_sum = inner + inner_got.astype(F32)
-    sent = jnp.where(is_outer, inner_sum, outer_sum).astype(BF)
+    outer_sum = last_step(outer, outer_got, (0, 3))
+    inner_sum = last_step(inner, inner_got, (1, 2))
     sub_sum = jnp.where(is_outer, outer_sum, inner_sum)
-    sub_sum = sub_sum + moved(sent, peers, lambda i: i ^ far).astype(F32)
-    return (grad_in, sub_sum.reshape(-1) * scale, down_sum)
+    down_sum = down + down_got.astype(F32)
+    return (grad_in, sub_sum.reshape(-1) * scale, down_sum * scale)
 
 
 def solution(mesh):

time: 105 us -> 92.7 us (0.88)
  waiting for transfers between devices: 28.9 us -> 14.7 us
  starting transfers between devices: 24 us -> 29.8 us
  other arithmetic: 9.22 us -> 7.02 us
    ppermute x19, waiting for transfers between devices: 28.9 us -> 14.7 us  [moved(): lax.ppermute(x, 'space', [(i, j) for i, j in pairs if j is not None and 0...]
    ppermute x19, starting transfers between devices: 24 us -> 29.8 us  [moved(): lax.ppermute(x, 'space', [(i, j) for i, j in pairs if j is not None and 0...]
    convert_element_type x4 -> x5, other arithmetic: 1.5 us -> 4.12 us  [fold_low(): return (piece(bit), piece(1 - bit).astype(BF), lambda i: i ^ 2 << by[i % 2])]
    slice x5 -> x0, local copies, waits for them, and re-layouts: 2.03 us -> none  [spread(): return (both[0].reshape(shape), got.reshape(shape))]
    convert_element_type x4, other arithmetic: 2.15 us -> 0.13 us  [fold_bit(): sent = piece(1 - mine).astype(BF)]
    another operation x3 -> x2, other arithmetic: 2.35 us -> 0.51 us
    unnamed x61 -> x67, local copies, waits for them, and re-layouts: 15.9 us -> 17 us
    pallas_call x4 -> x3, Pallas kernels: 15.6 us -> 14.8 us  [conv(): pl.pallas_call(functools.partial(conv_kernel, conv_plan(kernel, channels,...]
  transfers between devices with their start and end apart: 19 -> 19, of which waited for: 8 -> 5; matrix products, arithmetic and copies ran while one was open for 9% -> 11% of each run, Pallas kernels for 18% -> 19%
where the time goes in v5:
time: 92.7 us; the launch traced here: 91.9 us
  starting transfers between devices  29.8 us (32%)
  local copies, waits for them, and re-layouts  20 us (22%)
  Pallas kernels  19.5 us (21%)
  waiting for transfers between devices  14.7 us (16%)
  other arithmetic  7.02 us (8%)
    ppermute x19, starting transfers between devices, moved(): lax.ppermute(x, 'space', [(i, j) for i, j in pairs if j is not None and 0...  29.8 us
    unnamed x67, local copies, waits for them, and re-layouts  17 us
    pallas_call x3, Pallas kernels, conv(): pl.pallas_call(functools.partial(conv_kernel, conv_plan(kernel, channels,...  14.8 us
    ppermute x19, waiting for transfers between devices, moved(): lax.ppermute(x, 'space', [(i, j) for i, j in pairs if j is not None and 0...  14.7 us
    convert_element_type x5, other arithmetic, fold_low(): return (piece(bit), piece(1 - bit).astype(BF), lambda i: i ^ 2 << by[i % 2])  4.12 us
    dynamic_slice x4, local copies, waits for them, and re-layouts, taken(): return lax.dynamic_index_in_dim(x, digit, axis=axis, keepdims=False)  2.97 us
    pallas_call x1, Pallas kernels, down_grad(): pl.pallas_call(down_grad_kernel, out_shape=tuple((jax.ShapeDtypeStruct(sh...  2.02 us
    pallas_call x1, Pallas kernels, down_weight(): pl.pallas_call(down_weight_kernel, out_shape=kinds, in_specs=[SMEM, VMEM,...  1.92 us
  transfers between devices with their start and end apart: 19, of which 5 were waited for; matrix products, arithmetic and copies ran while one was open for 11% of the time, Pallas kernels for 19%

profile of v5, /device:TPU:0, one launch (start us, length us, event | category | flops | bytes accessed | tf_op | source)
XLA Modules:
  0.0 91.9 jit_solution(15998262515331154770)
XLA Ops:
  0.6 2.4 %collective-permute-start = (bf16[128,512]{1,0:T(8,128)(2,1)}, bf16[128,512]{1,0:T(8,128)(2,1)S(1)}, u32[]{:S(2)}, u32[]{:S(2)}) collective-permute-start(bf16[128,512]{1,0:T(8,128)(2,1)} %cur.3), channel_id=1, source_target_pairs={{0,1},{1,2},{2,3},{3,4},{4,5},{5,6},{6,7},{7,8},{8,9},{9,10},{10,1... | collective-permute-start | bytes 393224 | tf_op jit(solution)/shard_map/ppermute | solution.py:251
  3.0 1.6 %copy-done.3 = bf16[2048,512]{1,0:T(8,128)(2,1)S(1)} copy-done((bf16[2048,512]{1,0:T(8,128)(2,1)S(1)}, bf16[2048,512]{1,0:T(8,128)(2,1)}, u32[]{:S(2)}) %copy-start.3) | copy-done | bytes 2097176
  4.6 0.9 copy-done.18
  5.5 0.9 %copy-done.22 = bf16[512,256]{1,0:T(8,128)(2,1)S(1)} copy-done((bf16[512,256]{1,0:T(8,128)(2,1)S(1)}, bf16[512,256]{1,0:T(8,128)(2,1)}, u32[]{:S(2)}) %copy-start.22) | copy-done | bytes 262168
  6.5 0.7 copy-done.25
  7.1 0.7 copy-done.26
  7.8 0.8 prep.1
  8.7 0.7 copy-done.4
  9.4 2.0 %down_grad.1 = (bf16[512,256]{1,0:T(8,128)(2,1)S(1)}, bf16[256,256]{1,0:T(8,128)(2,1)}, bf16[256,256]{1,0:T(8,128)(2,1)}, bf16[1024,512]{1,0:T(8,128)(2,1)S(1)}) custom-call(bf16[128,512]{1,0:T(8,128)(2,1)S(1)} %collective-permute-done.prev, bf16[128,512]{1,0:T(8,128)(2,1)S(1)} %copy-done.19, bf16[512,256]{1,0:T(8,128)(2,1)S(1)} %get-tuple-element.41.act, ...), custom_call_target="tpu_custom_call" | custom-call | flops 1048576 | bytes 1024 | tf_op jit(solution)/shard_map/down_grad/pallas_call | solution.py:127
  11.4 0.7 copy-done.11
  12.1 1.0 %copy-done.14 = bf16[1024,512]{1,0:T(8,128)(2,1)} copy-done((bf16[1024,512]{1,0:T(8,128)(2,1)}, bf16[1024,512]{1,0:T(8,128)(2,1)S(1)}, u32[]{:S(2)}) %copy-start.14) | copy-done | bytes 1048600
  13.2 5.2 %collective-permute-start.1 = (bf16[256,256]{1,0:T(8,128)(2,1)}, bf16[256,256]{1,0:T(8,128)(2,1)}, u32[]{:S(2)}, u32[]{:S(2)}) collective-permute-start(bf16[256,256]{1,0:T(8,128)(2,1)} %get-tuple-element.44), channel_id=1, source_target_pairs={{0,1},{1,2},{2,3},{3,4},{4,5},{5,6},{6,7},{7,8},{8,9},{9,10},{10,1... | collective-permute-start | bytes 393224 | tf_op jit(solution)/shard_map/ppermute | solution.py:251
  18.3 1.3 %collective-permute-start.2 = (bf16[256,256]{1,0:T(8,128)(2,1)}, bf16[256,256]{1,0:T(8,128)(2,1)}, u32[]{:S(2)}, u32[]{:S(2)}) collective-permute-start(bf16[256,256]{1,0:T(8,128)(2,1)} %get-tuple-element.45), channel_id=1, source_target_pairs={{1,0},{2,1},{3,2},{4,3},{5,4},{6,5},{7,6},{8,7},{9,8},{10,9},{11,1... | collective-permute-start | bytes 393224 | tf_op jit(solution)/shard_map/ppermute | solution.py:251
  19.6 1.2 %copy-done.15 = bf16[1024,512]{1,0:T(8,128)(2,1)S(1)} copy-done((bf16[1024,512]{1,0:T(8,128)(2,1)S(1)}, bf16[1024,512]{1,0:T(8,128)(2,1)}, u32[]{:S(2)}) %copy-start.15) | copy-done | bytes 1048600
  20.8 1.0 %copy-done.21 = bf16[256,1024]{1,0:T(8,128)(2,1)S(1)} copy-done((bf16[256,1024]{1,0:T(8,128)(2,1)S(1)}, bf16[256,1024]{1,0:T(8,128)(2,1)}, u32[]{:S(2)}) %copy-start.21) | copy-done | bytes 524312
  21.9 1.9 %down_weight.1 = (f32[16,64,512]{2,1,0:T(8,128)S(1)}, bf16[16,64,512]{2,1,0:T(8,128)(2,1)}) custom-call(s32[1]{0:T(128)} %bitcast.core.refs_0_, bf16[256,1024]{1,0:T(8,128)(2,1)S(1)} %copy-done.21, bf16[1024,512]{1,0:T(8,128)(2,1)S(1)} %copy-done.15, bf16[6912,256]{1,0:T(8,128)(2,1)S(1)} %copy-done), custom_call_target="tpu_custom_call" | custom-call | flops 1048576 | bytes 1024 | tf_op jit(solution)/shard_map/down_weight/pallas_call | solution.py:152
  23.8 1.3 %copy-done.1 = f32[16,64,512]{2,1,0:T(8,128)} copy-done((f32[16,64,512]{2,1,0:T(8,128)}, f32[16,64,512]{2,1,0:T(8,128)S(1)}, u32[]{:S(2)}) %copy-start.1) | copy-done | bytes 2097176
  25.1 1.1 %collective-permute-start.3 = (bf16[16,64,512]{2,1,0:T(8,128)(2,1)}, bf16[16,64,512]{2,1,0:T(8,128)(2,1)}, u32[]{:S(2)}, u32[]{:S(2)}) collective-permute-start(bf16[16,64,512]{2,1,0:T(8,128)(2,1)} %get-tuple-element.55), channel_id=1, source_target_pairs={{0,1},{1,0},{2,3},{3,2},{4,5},{5,4},{6,7},{7,6},{8,9},{9,8},{10,11... | collective-permute-start | bytes 3145736 | tf_op jit(solution)/shard_map/ppermute | solution.py:251
  26.3 0.9 %copy-done.9 = bf16[512,256]{1,0:T(8,128)(2,1)S(1)} copy-done((bf16[512,256]{1,0:T(8,128)(2,1)S(1)}, bf16[512,256]{1,0:T(8,128)(2,1)}, u32[]{:S(2)}) %copy-start.9) | copy-done | bytes 262168
  27.2 0.9 %copy-done.12 = bf16[512,256]{1,0:T(8,128)(2,1)S(1)} copy-done((bf16[512,256]{1,0:T(8,128)(2,1)S(1)}, bf16[512,256]{1,0:T(8,128)(2,1)}, u32[]{:S(2)}) %copy-start.12) | copy-done | bytes 262168
  28.2 0.9 copy-done.16
  29.1 5.8 %conv.3 = (f32[512,256]{1,0:T(8,128)S(1)}, f32[8,216,256]{2,1,0:T(8,128)S(1)}, bf16[8,216,256]{2,1,0:T(8,128)(2,1)S(1)}) custom-call(s32[1]{0:T(128)} %bitcast.core.refs_0_, s32[8,27]{1,0:T(8,128)S(1)} %bitcast.219, s32[8,27]{1,0:T(8,128)S(1)} %bitcast.222, s32[216,128]{1,0:T(8,128)S(1)} %bitcast.216, bf16[256,256]{1,0:T(8,128)(2,1)} %collective-permute-done.1.refs_4_, ...), custom_call_target="tpu_custom_call" | custom-call | flops 1048576 | bytes 1024 | tf_op jit(solution)/shard_map/conv/pallas_call | solution.py:229
  34.9 0.1 collective-permute-start.4
  35.0 0.2 constant_dynamic-slice_fusion.3
  35.2 0.2 constant_dynamic-slice_fusion.2
  35.5 1.3 %constant_dynamic-slice_fusion.1 = (bf16[4,2,1,64,512]{4,3,2,1,0:T(8,128)(2,1)S(1)}, bf16[4,2,1,64,512]{4,3,2,1,0:T(8,128)(2,1)S(1)}) fusion(bf16[4,2,2,64,512]{4,3,2,1,0:T(8,128)(2,1)} %bitcast.23, s32[]{:T(128)S(6)} %select_n.330, s32[]{:T(128)S(6)} %select_n.327), kind=kLoop, calls=%fused_computation.68 | loop fusion | bytes 2097160 | tf_op jit(solution)/shard_map/jit(dynamic_index_in_dim)/dynamic_slice | solution.py:255
  36.7 1.3 %constant_dynamic-slice_fusion = (bf16[4,1,2,64,512]{4,3,2,1,0:T(8,128)(2,1)S(1)}, bf16[4,1,2,64,512]{4,3,2,1,0:T(8,128)(2,1)S(1)}) fusion(bf16[4,2,2,64,512]{4,3,2,1,0:T(8,128)(2,1)} %bitcast.23, s32[]{:T(128)S(6)} %select_n.330, s32[]{:T(128)S(6)} %select_n.327), kind=kLoop, calls=%fused_computation.67 | loop fusion | bytes 2097160 | tf_op jit(solution)/shard_map/jit(dynamic_index_in_dim)/dynamic_slice | solution.py:255
  38.0 0.3 fusion.1
  38.4 1.0 %collective-permute-start.7 = (bf16[4,2,64,512]{3,2,0,1:T(8,128)(2,1)S(1)}, bf16[4,2,64,512]{3,2,0,1:T(8,128)(2,1)S(1)}, u32[]{:S(2)}, u32[]{:S(2)}) collective-permute-start(bf16[4,2,64,512]{3,2,0,1:T(8,128)(2,1)S(1)} %fusion.1), channel_id=1, source_target_pairs={{0,2},{1,5},{2,0},{3,7},{4,6},{5,1},{6,4},{7,3},{8,10},{9,13},{10,... | collective-permute-start | bytes 1572872 | tf_op jit(solution)/shard_map/ppermute | solution.py:251
  39.4 4.0 %conv.4 = (f32[512,256]{1,0:T(8,128)S(1)}, f32[4,216,256]{2,1,0:T(8,128)S(1)}, bf16[4,216,256]{2,1,0:T(8,128)(2,1)S(1)}) custom-call(s32[1]{0:T(128)} %bitcast.core.refs_0_, s32[8,27]{1,0:T(8,128)S(1)} %bitcast.220, s32[8,27]{1,0:T(8,128)S(1)} %bitcast.223, s32[216,128]{1,0:T(8,128)S(1)} %bitcast.217, bf16[256,256]{1,0:T(8,128)(2,1)} %collective-permute-done.1.refs_4_, ...), custom_call_target="tpu_custom_call" | custom-call | flops 1048576 | bytes 1024 | tf_op jit(solution)/shard_map/conv/pallas_call | solution.py:229
  43.4 0.8 collective-permute-start.5
  44.2 1.5 %fusion.4 = (bf16[2,2,216,256]{3,2,1,0:T(8,128)(2,1)S(1)}, f32[2,2,216,256]{3,2,1,0:T(8,128)}) fusion(f32[2,2,2,216,256]{4,3,2,1,0:T(8,128)S(1)} %bitcast.213, s32[]{:T(128)S(6)} %select_n.330, bf16[2,2,2,216,256]{4,3,2,1,0:T(8,128)(2,1)S(1)} %bitcast.227, pred[]{:T(512)S(6)} %eq.24, s32[]{:T(128)S(6)} %select_n.327), kind=kLoop, calls=%fused_computation.11 | loop fusion | flops 1990656 | bytes 6635529 | tf_op jit(solution)/shard_map/convert_element_type | solution.py:283
  45.6 1.3 %collective-permute-start.6 = (bf16[2,2,216,256]{3,2,1,0:T(8,128)(2,1)S(1)}, bf16[2,2,216,256]{3,2,1,0:T(8,128)(2,1)S(1)}, u32[]{:S(2)}, u32[]{:S(2)}) collective-permute-start(bf16[2,2,216,256]{3,2,1,0:T(8,128)(2,1)S(1)} %get-tuple-element.79), channel_id=1, source_target_pairs={{0,2},{1,5},{2,0},{3,7},{4,6},{5,1},{6,4},{7,3},{8,10},{9,13},{10,... | collective-permute-start | bytes 1327112 | tf_op jit(solution)/shard_map/ppermute | solution.py:251
  47.0 1.3 %fusion.2 = f32[4,2,64,512]{3,2,0,1:T(8,128)} fusion(f32[4,1,2,64,512]{4,3,2,1,0:T(8,128)S(1)} %get-tuple-element.84, f32[4,2,1,64,512]{4,3,2,1,0:T(8,128)S(1)} %get-tuple-element.82, bf16[4,1,2,64,512]{4,3,2,1,0:T(8,128)(2,1)S(1)} %get-tuple-element.98, bf16[4,2,1,64,512]{4,3,2,1,0:T(8,128)(2,1)S(1)} %get-tuple-element.96, pred[]{:T(512)S(6)} %eq.24), kind=kLoop, calls=%fused_computation.8 | loop fusion | flops 1048576 | bytes 4194305 | tf_op jit(solution)/shard_map/add | solution.py:280
  48.3 5.0 %conv.5 = (bf16[512,256]{1,0:T(8,128)(2,1)}, f32[4,216,256]{2,1,0:T(8,128)S(1)}, bf16[4,216,256]{2,1,0:T(8,128)(2,1)}) custom-call(s32[1]{0:T(128)} %bitcast.core.refs_0_, s32[8,27]{1,0:T(8,128)S(1)} %bitcast.221, s32[8,27]{1,0:T(8,128)S(1)} %bitcast.224, s32[216,128]{1,0:T(8,128)S(1)} %bitcast.218, bf16[256,256]{1,0:T(8,128)(2,1)} %collective-permute-done.1.refs_4_, ...), custom_call_target="tpu_custom_call" | custom-call | flops 1048576 | bytes 1024 | tf_op jit(solution)/shard_map/conv/pallas_call | solution.py:229
  53.3 0.9 copy-done.7
  54.2 0.8 copy-done.28
  55.0 0.1 copy-done.30
  55.2 0.6 copy-done.32
  55.8 0.0 collective-permute-start.11
  55.9 2.0 %fusion.18 = (bf16[2,216,256]{2,1,0:T(8,128)(2,1)}, f32[2,1,216,256]{3,2,1,0:T(8,128)S(1)}) fusion(f32[2,2,216,256]{3,2,1,0:T(8,128)} %get-tuple-element.71, s32[]{:T(128)S(6)} %select_n.345, bf16[2,2,216,256]{3,2,1,0:T(8,128)(2,1)} %copy-done.32, s32[]{:T(128)S(6)} %select_n.342), kind=kLoop, calls=%fused_computation.41 | loop fusion | flops 552960 | bytes 1990664 | tf_op jit(solution)/shard_map/convert_element_type | solution.py:283
  57.9 0.9 collective-permute-start.8
  58.8 0.3 fusion.14
  59.1 0.3 fusion.12
  59.4 1.1 %collective-permute-start.12 = (bf16[2,2,216,256]{3,2,0,1:T(8,128)(2,1)S(1)}, bf16[2,2,216,256]{3,2,0,1:T(8,128)(2,1)S(1)}, u32[]{:S(2)}, u32[]{:S(2)}) collective-permute-start(bf16[2,2,216,256]{3,2,0,1:T(8,128)(2,1)S(1)} %pad_maximum_fusion), channel_id=1, source_target_pairs={{0,2},{1,5},{2,0},{3,7},{4,6},{5,1},{6,4},{7,3},{8,10},{9,13},{10,... | collective-permute-start | bytes 1327112 | tf_op jit(solution)/shard_map/ppermute | solution.py:251
  60.5 0.2 fusion.17
  60.7 1.2 %collective-permute-start.16 = (bf16[4,64,512]{2,1,0:T(8,128)(2,1)S(1)}, bf16[4,64,512]{2,1,0:T(8,128)(2,1)S(1)}, u32[]{:S(2)}, u32[]{:S(2)}) collective-permute-start(bf16[4,64,512]{2,1,0:T(8,128)(2,1)S(1)} %get-tuple-element.85), channel_id=1, source_target_pairs={{0,4},{1,3},{2,6},{3,1},{4,0},{5,7},{6,2},{7,5},{8,12},{9,11},{10,... | collective-permute-start | bytes 786440 | tf_op jit(solution)/shard_map/ppermute | solution.py:251
  61.9 3.7 %collective-permute-done.8 = bf16[2,216,256]{2,1,0:T(8,128)(2,1)S(1)} collective-permute-done((bf16[2,216,256]{2,1,0:T(8,128)(2,1)}, bf16[2,216,256]{2,1,0:T(8,128)(2,1)S(1)}, u32[]{:S(2)}, u32[]{:S(2)}) %collective-permute-start.8) | collective-permute-done | bytes 221216 | tf_op jit(solution)/shard_map/ppermute | solution.py:251
  65.6 1.9 %collective-permute-start.9 = (bf16[216,256]{1,0:T(8,128)(2,1)S(1)}, bf16[216,256]{1,0:T(8,128)(2,1)S(1)}, u32[]{:S(2)}, u32[]{:S(2)}) collective-permute-start(bf16[216,256]{1,0:T(8,128)(2,1)S(1)} %fusion.25), channel_id=1, source_target_pairs={{0,8},{1,9},{2,10},{3,11},{4,12},{5,13},{6,14},{7,15},{8,0},{9,1},... | collective-permute-start | bytes 331784 | tf_op jit(solution)/shard_map/ppermute | solution.py:251
  67.5 3.7 %collective-permute-done.16 = bf16[4,64,512]{2,1,0:T(8,128)(2,1)S(1)} collective-permute-done((bf16[4,64,512]{2,1,0:T(8,128)(2,1)S(1)}, bf16[4,64,512]{2,1,0:T(8,128)(2,1)S(1)}, u32[]{:S(2)}, u32[]{:S(2)}) %collective-permute-start.16) | collective-permute-done | bytes 262176 | tf_op jit(solution)/shard_map/ppermute | solution.py:251
  71.2 0.1 fusion.22
  71.3 1.9 %collective-permute-start.17 = (bf16[2,64,512]{2,1,0:T(8,128)(2,1)S(1)}, bf16[2,64,512]{2,1,0:T(8,128)(2,1)S(1)}, u32[]{:S(2)}, u32[]{:S(2)}) collective-permute-start(bf16[2,64,512]{2,1,0:T(8,128)(2,1)S(1)} %get-tuple-element.99), channel_id=1, source_target_pairs={{0,8},{1,9},{2,10},{3,11},{4,12},{5,13},{6,14},{7,15},{8,0},{9,1},... | collective-permute-start | bytes 393224 | tf_op jit(solution)/shard_map/ppermute | solution.py:251
  73.2 0.1 fusion.19
  73.3 0.6 collective-permute-start.13
  74.0 1.3 %collective-permute-start.10 = (bf16[216,256]{1,0:T(8,128)(2,1)S(1)}, bf16[216,256]{1,0:T(8,128)(2,1)S(1)}, u32[]{:S(2)}, u32[]{:S(2)}) collective-permute-start(bf16[216,256]{1,0:T(8,128)(2,1)S(1)} %fusion.28), channel_id=1, source_target_pairs={{8,24},{9,25},{10,26},{11,27},{12,28},{13,29},{14,30},{15,31},{16,... | collective-permute-start | bytes 331784 | tf_op jit(solution)/shard_map/ppermute | solution.py:251
  75.3 4.0 %collective-permute-done.13 = bf16[2,216,256]{2,1,0:T(8,128)(2,1)S(1)} collective-permute-done((bf16[2,216,256]{2,1,0:T(8,128)(2,1)S(1)}, bf16[2,216,256]{2,1,0:T(8,128)(2,1)S(1)}, u32[]{:S(2)}, u32[]{:S(2)}) %collective-permute-start.13) | collective-permute-done | bytes 221216 | tf_op jit(solution)/shard_map/ppermute | solution.py:251
  79.3 0.3 collective-permute-start.14
  79.6 2.9 %collective-permute-start.18 = (bf16[64,512]{1,0:T(8,128)(2,1)S(1)}, bf16[64,512]{1,0:T(8,128)(2,1)S(1)}, u32[]{:S(2)}, u32[]{:S(2)}) collective-permute-start(bf16[64,512]{1,0:T(8,128)(2,1)S(1)} %fusion.27), channel_id=1, source_target_pairs={{0,16},{1,17},{2,18},{3,19},{4,20},{5,21},{6,22},{7,23},{8,24},{9,... | collective-permute-start | bytes 196616 | tf_op jit(solution)/shard_map/ppermute | solution.py:251
  82.5 1.6 %collective-permute-done.14 = bf16[216,256]{1,0:T(8,128)(2,1)S(1)} collective-permute-done((bf16[216,256]{1,0:T(8,128)(2,1)S(1)}, bf16[216,256]{1,0:T(8,128)(2,1)S(1)}, u32[]{:S(2)}, u32[]{:S(2)}) %collective-permute-start.14) | collective-permute-done | bytes 110624 | tf_op jit(solution)/shard_map/ppermute | solution.py:251
  84.2 4.5 %collective-permute-start.15 = (bf16[216,256]{1,0:T(8,128)(2,1)S(1)}, bf16[216,256]{1,0:T(8,128)(2,1)S(1)}, u32[]{:S(2)}, u32[]{:S(2)}) collective-permute-start(bf16[216,256]{1,0:T(8,128)(2,1)S(1)} %fusion.29), channel_id=1, source_target_pairs={{0,16},{1,17},{2,18},{3,19},{4,20},{5,21},{6,22},{7,23},{24,8},{25... | collective-permute-start | bytes 331784 | tf_op jit(solution)/shard_map/ppermute | solution.py:251
  88.7 0.7 fusion.24
  89.4 1.6 %collective-permute-done.15 = bf16[216,256]{1,0:T(8,128)(2,1)S(1)} collective-permute-done((bf16[216,256]{1,0:T(8,128)(2,1)S(1)}, bf16[216,256]{1,0:T(8,128)(2,1)S(1)}, u32[]{:S(2)}, u32[]{:S(2)}) %collective-permute-start.15) | collective-permute-done | bytes 110624 | tf_op jit(solution)/shard_map/ppermute | solution.py:251
  91.0 0.1 multiply_bitcast_fusion
  91.1 0.8 copy.37
  (68 shorter events, 0.3 us)
Async XLA Ops:
  0.6 8.0 %collective-permute-start = (bf16[128,512]{1,0:T(8,128)(2,1)}, bf16[128,512]{1,0:T(8,128)(2,1)S(1)}, u32[]{:S(2)}, u32[]{:S(2)}) collective-permute-start(bf16[128,512]{1,0:T(8,128)(2,1)} %cur.3), channel_id=1, source_target_pairs={{0,1},{1,2},{2,3},{3,4},{4,5},{5,6},{6,7},{7,8},{8,9},{9,10},{10,1... | collective-permute-start | bytes 393224 | tf_op jit(solution)/shard_map/ppermute | solution.py:251
  3.0 1.6 %copy-start.3 = (bf16[2048,512]{1,0:T(8,128)(2,1)S(1)}, bf16[2048,512]{1,0:T(8,128)(2,1)}, u32[]{:S(2)}) copy-start(bf16[2048,512]{1,0:T(8,128)(2,1)} %w.3) | copy-start | bytes 6291460
  4.6 0.9 copy-start.18
  5.5 0.9 %copy-start.22 = (bf16[512,256]{1,0:T(8,128)(2,1)S(1)}, bf16[512,256]{1,0:T(8,128)(2,1)}, u32[]{:S(2)}) copy-start(bf16[512,256]{1,0:T(8,128)(2,1)} %pre.1) | copy-start | bytes 786436
  6.5 0.7 copy-start.25
  7.1 0.7 copy-start.26
  7.8 1.6 %copy-start.4 = (bf16[2048,512]{1,0:T(8,128)(2,1)S(1)}, bf16[2048,512]{1,0:T(8,128)(2,1)}, u32[]{:S(2)}) copy-start(bf16[2048,512]{1,0:T(8,128)(2,1)} %w.3) | copy-start | bytes 6291460
  7.8 1.6 %copy-start.19 = (bf16[128,512]{1,0:T(8,128)(2,1)S(1)}, bf16[128,512]{1,0:T(8,128)(2,1)}, u32[]{:S(2)}) copy-start(bf16[128,512]{1,0:T(8,128)(2,1)} %cur.3) | copy-start | bytes 393220
  8.7 2.8 %copy-start.20 = (bf16[256,1024]{1,0:T(8,128)(2,1)}, bf16[256,1024]{1,0:T(8,128)(2,1)S(1)}, u32[]{:S(2)}) copy-start(bf16[256,1024]{1,0:T(8,128)(2,1)S(1)} %get-tuple-element.46.chosen) | copy-start | bytes 1572868
  9.4 10.2 %copy-start = (bf16[6912,256]{1,0:T(8,128)(2,1)S(1)}, bf16[6912,256]{1,0:T(8,128)(2,1)}, u32[]{:S(2)}) copy-start(bf16[6912,256]{1,0:T(8,128)(2,1)} %refs_8_.5) | copy-start | bytes 10616836
  11.4 0.7 copy-start.11
  12.1 1.0 %copy-start.14 = (bf16[1024,512]{1,0:T(8,128)(2,1)}, bf16[1024,512]{1,0:T(8,128)(2,1)S(1)}, u32[]{:S(2)}) copy-start(bf16[1024,512]{1,0:T(8,128)(2,1)S(1)} %get-tuple-element.47.gath) | copy-start | bytes 3145732
  13.2 12.0 %collective-permute-start.1 = (bf16[256,256]{1,0:T(8,128)(2,1)}, bf16[256,256]{1,0:T(8,128)(2,1)}, u32[]{:S(2)}, u32[]{:S(2)}) collective-permute-start(bf16[256,256]{1,0:T(8,128)(2,1)} %get-tuple-element.44), channel_id=1, source_target_pairs={{0,1},{1,2},{2,3},{3,4},{4,5},{5,6},{6,7},{7,8},{8,9},{9,10},{10,1... | collective-permute-start | bytes 393224 | tf_op jit(solution)/shard_map/ppermute | solution.py:251
  18.3 6.8 %collective-permute-start.2 = (bf16[256,256]{1,0:T(8,128)(2,1)}, bf16[256,256]{1,0:T(8,128)(2,1)}, u32[]{:S(2)}, u32[]{:S(2)}) collective-permute-start(bf16[256,256]{1,0:T(8,128)(2,1)} %get-tuple-element.45), channel_id=1, source_target_pairs={{1,0},{2,1},{3,2},{4,3},{5,4},{6,5},{7,6},{8,7},{9,8},{10,9},{11,1... | collective-permute-start | bytes 393224 | tf_op jit(solution)/shard_map/ppermute | solution.py:251
  19.6 1.2 %copy-start.15 = (bf16[1024,512]{1,0:T(8,128)(2,1)S(1)}, bf16[1024,512]{1,0:T(8,128)(2,1)}, u32[]{:S(2)}) copy-start(bf16[1024,512]{1,0:T(8,128)(2,1)} %copy-done.14) | copy-start | bytes 3145732
  20.8 1.0 %copy-start.21 = (bf16[256,1024]{1,0:T(8,128)(2,1)S(1)}, bf16[256,1024]{1,0:T(8,128)(2,1)}, u32[]{:S(2)}) copy-start(bf16[256,1024]{1,0:T(8,128)(2,1)} %copy-done.20) | copy-start | bytes 1572868
  21.9 4.4 %copy-start.23 = (s32[1,27,8]{1,2,0:T(8,128)S(1)}, s32[1,27,8]{1,2,0:T(8,128)}, u32[]{:S(2)}) copy-start(s32[1,27,8]{1,2,0:T(8,128)} %param.15) | copy-start | bytes 2596
  21.9 4.4 %copy-start.24 = (s32[1,27,8]{1,2,0:T(8,128)S(1)}, s32[1,27,8]{1,2,0:T(8,128)}, u32[]{:S(2)}) copy-start(s32[1,27,8]{1,2,0:T(8,128)} %param.16) | copy-start | bytes 2596
  23.8 1.3 %copy-start.1 = (f32[16,64,512]{2,1,0:T(8,128)}, f32[16,64,512]{2,1,0:T(8,128)S(1)}, u32[]{:S(2)}) copy-start(f32[16,64,512]{2,1,0:T(8,128)S(1)} %get-tuple-element.68) | copy-start | bytes 6291460
  25.1 9.8 %collective-permute-start.3 = (bf16[16,64,512]{2,1,0:T(8,128)(2,1)}, bf16[16,64,512]{2,1,0:T(8,128)(2,1)}, u32[]{:S(2)}, u32[]{:S(2)}) collective-permute-start(bf16[16,64,512]{2,1,0:T(8,128)(2,1)} %get-tuple-element.55), channel_id=1, source_target_pairs={{0,1},{1,0},{2,3},{3,2},{4,5},{5,4},{6,7},{7,6},{8,9},{9,8},{10,11... | collective-permute-start | bytes 3145736 | tf_op jit(solution)/shard_map/ppermute | solution.py:251
  26.3 1.0 %copy-start.9 = (bf16[512,256]{1,0:T(8,128)(2,1)S(1)}, bf16[512,256]{1,0:T(8,128)(2,1)}, u32[]{:S(2)}) copy-start(bf16[512,256]{1,0:T(8,128)(2,1)} %refs_7_.5) | copy-start | bytes 786436
  27.2 0.9 %copy-start.12 = (bf16[512,256]{1,0:T(8,128)(2,1)S(1)}, bf16[512,256]{1,0:T(8,128)(2,1)}, u32[]{:S(2)}) copy-start(bf16[512,256]{1,0:T(8,128)(2,1)} %copy-done.11) | copy-start | bytes 786436
  28.2 0.9 copy-start.16
  29.1 6.0 %copy-start.2 = (f32[16,64,512]{2,1,0:T(8,128)S(1)}, f32[16,64,512]{2,1,0:T(8,128)}, u32[]{:S(2)}) copy-start(f32[16,64,512]{2,1,0:T(8,128)} %copy-done.1) | copy-start | bytes 6291460
  34.9 8.5 %collective-permute-start.4 = (bf16[8,216,256]{2,1,0:T(8,128)(2,1)S(1)}, bf16[8,216,256]{2,1,0:T(8,128)(2,1)S(1)}, u32[]{:S(2)}, u32[]{:S(2)}) collective-permute-start(bf16[8,216,256]{2,1,0:T(8,128)(2,1)S(1)} %get-tuple-element.60), channel_id=1, source_target_pairs={{0,1},{1,0},{2,3},{3,2},{4,5},{5,4},{6,7},{7,6},{8,9},{9,8},{10,11... | collective-permute-start | bytes 2654216 | tf_op jit(solution)/shard_map/ppermute | solution.py:251
  38.4 15.8 %collective-permute-start.7 = (bf16[4,2,64,512]{3,2,0,1:T(8,128)(2,1)S(1)}, bf16[4,2,64,512]{3,2,0,1:T(8,128)(2,1)S(1)}, u32[]{:S(2)}, u32[]{:S(2)}) collective-permute-start(bf16[4,2,64,512]{3,2,0,1:T(8,128)(2,1)S(1)} %fusion.1), channel_id=1, source_target_pairs={{0,2},{1,5},{2,0},{3,7},{4,6},{5,1},{6,4},{7,3},{8,10},{9,13},{10,... | collective-permute-start | bytes 1572872 | tf_op jit(solution)/shard_map/ppermute | solution.py:251
  43.4 2.2 %copy-start.5 = (f32[4,216,256]{2,1,0:T(8,128)}, f32[4,216,256]{2,1,0:T(8,128)S(1)}, u32[]{:S(2)}) copy-start(f32[4,216,256]{2,1,0:T(8,128)S(1)} %get-tuple-element.73) | copy-start | bytes 2654212
  43.4 10.8 %collective-permute-start.5 = (bf16[4,216,256]{2,1,0:T(8,128)(2,1)S(1)}, bf16[4,216,256]{2,1,0:T(8,128)(2,1)S(1)}, u32[]{:S(2)}, u32[]{:S(2)}) collective-permute-start(bf16[4,216,256]{2,1,0:T(8,128)(2,1)S(1)} %get-tuple-element.65), channel_id=1, source_target_pairs={{0,1},{1,0},{2,3},{3,2},{4,5},{5,4},{6,7},{7,6},{8,9},{9,8},{10,11... | collective-permute-start | bytes 1327112 | tf_op jit(solution)/shard_map/ppermute | solution.py:251
  45.6 9.4 %collective-permute-start.6 = (bf16[2,2,216,256]{3,2,1,0:T(8,128)(2,1)S(1)}, bf16[2,2,216,256]{3,2,1,0:T(8,128)(2,1)S(1)}, u32[]{:S(2)}, u32[]{:S(2)}) collective-permute-start(bf16[2,2,216,256]{3,2,1,0:T(8,128)(2,1)S(1)} %get-tuple-element.79), channel_id=1, source_target_pairs={{0,2},{1,5},{2,0},{3,7},{4,6},{5,1},{6,4},{7,3},{8,10},{9,13},{10,... | collective-permute-start | bytes 1327112 | tf_op jit(solution)/shard_map/ppermute | solution.py:251
  47.0 1.3 %copy-start.10 = (bf16[512,256]{1,0:T(8,128)(2,1)S(1)}, bf16[512,256]{1,0:T(8,128)(2,1)}, u32[]{:S(2)}) copy-start(bf16[512,256]{1,0:T(8,128)(2,1)} %refs_7_.5) | copy-start | bytes 786436
  47.0 1.3 %copy-start.13 = (bf16[512,256]{1,0:T(8,128)(2,1)S(1)}, bf16[512,256]{1,0:T(8,128)(2,1)}, u32[]{:S(2)}) copy-start(bf16[512,256]{1,0:T(8,128)(2,1)} %copy-done.11) | copy-start | bytes 786436
  47.0 1.3 %copy-start.17 = (s32[1,27,8,128]{3,2,1,0:T(8,128)S(1)}, s32[1,27,8,128]{3,2,1,0:T(8,128)}, u32[]{:S(2)}) copy-start(s32[1,27,8,128]{3,2,1,0:T(8,128)} %param.17) | copy-start | bytes 331780
  53.3 0.9 copy-start.7
  54.2 4.6 %copy-start.6 = (f32[4,216,256]{2,1,0:T(8,128)S(1)}, f32[4,216,256]{2,1,0:T(8,128)}, u32[]{:S(2)}) copy-start(f32[4,216,256]{2,1,0:T(8,128)} %copy-done.5) | copy-start | bytes 2654212
  54.2 0.9 %copy-start.30 = (bf16[4,2,64,512]{3,2,0,1:T(8,128)(2,1)}, bf16[4,2,64,512]{3,2,0,1:T(8,128)(2,1)S(1)}, u32[]{:S(2)}) copy-start(bf16[4,2,64,512]{3,2,0,1:T(8,128)(2,1)S(1)} %collective-permute-done.7) | copy-start | bytes 1572868
  54.2 0.8 copy-start.28
  55.0 0.8 copy-start.32
  55.0 3.8 %copy-start.29 = (bf16[4,216,256]{2,1,0:T(8,128)(2,1)S(1)}, bf16[4,216,256]{2,1,0:T(8,128)(2,1)}, u32[]{:S(2)}) copy-start(bf16[4,216,256]{2,1,0:T(8,128)(2,1)} %copy-done.28) | copy-start | bytes 1327108
  55.8 3.2 %collective-permute-start.11 = (bf16[4,216,256]{2,1,0:T(8,128)(2,1)}, bf16[4,216,256]{2,1,0:T(8,128)(2,1)S(1)}, u32[]{:S(2)}, u32[]{:S(2)}) collective-permute-start(bf16[4,216,256]{2,1,0:T(8,128)(2,1)} %get-tuple-element.76), channel_id=1, source_target_pairs={{0,1},{1,0},{2,3},{3,2},{4,5},{5,4},{6,7},{7,6},{8,9},{9,8},{10,11... | collective-permute-start | bytes 1327112 | tf_op jit(solution)/shard_map/ppermute | solution.py:251
  57.9 1.2 %copy-start.8 = (f32[4,216,256]{2,1,0:T(8,128)S(1)}, f32[4,216,256]{2,1,0:T(8,128)}, u32[]{:S(2)}) copy-start(f32[4,216,256]{2,1,0:T(8,128)} %copy-done.7) | copy-start | bytes 2654212
  57.9 7.7 %collective-permute-start.8 = (bf16[2,216,256]{2,1,0:T(8,128)(2,1)}, bf16[2,216,256]{2,1,0:T(8,128)(2,1)S(1)}, u32[]{:S(2)}, u32[]{:S(2)}) collective-permute-start(bf16[2,216,256]{2,1,0:T(8,128)(2,1)} %get-tuple-element.87), channel_id=1, source_target_pairs={{0,4},{1,3},{2,6},{3,1},{4,0},{5,7},{6,2},{7,5},{8,12},{9,11},{10,... | collective-permute-start | bytes 663560 | tf_op jit(solution)/shard_map/ppermute | solution.py:251
  59.1 1.5 %copy-start.27 = (f32[4,2,64,512]{3,2,0,1:T(8,128)S(1)}, f32[4,2,64,512]{3,2,0,1:T(8,128)}, u32[]{:S(2)}) copy-start(f32[4,2,64,512]{3,2,0,1:T(8,128)} %fusion.2) | copy-start | bytes 3145732
  59.1 1.5 %copy-start.31 = (bf16[4,2,64,512]{3,2,0,1:T(8,128)(2,1)S(1)}, bf16[4,2,64,512]{3,2,0,1:T(8,128)(2,1)}, u32[]{:S(2)}) copy-start(bf16[4,2,64,512]{3,2,0,1:T(8,128)(2,1)} %copy-done.30) | copy-start | bytes 1572868
  59.4 13.8 %collective-permute-start.12 = (bf16[2,2,216,256]{3,2,0,1:T(8,128)(2,1)S(1)}, bf16[2,2,216,256]{3,2,0,1:T(8,128)(2,1)S(1)}, u32[]{:S(2)}, u32[]{:S(2)}) collective-permute-start(bf16[2,2,216,256]{3,2,0,1:T(8,128)(2,1)S(1)} %pad_maximum_fusion), channel_id=1, source_target_pairs={{0,2},{1,5},{2,0},{3,7},{4,6},{5,1},{6,4},{7,3},{8,10},{9,13},{10,... | collective-permute-start | bytes 1327112 | tf_op jit(solution)/shard_map/ppermute | solution.py:251
  60.7 10.5 %collective-permute-start.16 = (bf16[4,64,512]{2,1,0:T(8,128)(2,1)S(1)}, bf16[4,64,512]{2,1,0:T(8,128)(2,1)S(1)}, u32[]{:S(2)}, u32[]{:S(2)}) collective-permute-start(bf16[4,64,512]{2,1,0:T(8,128)(2,1)S(1)} %get-tuple-element.85), channel_id=1, source_target_pairs={{0,4},{1,3},{2,6},{3,1},{4,0},{5,7},{6,2},{7,5},{8,12},{9,11},{10,... | collective-permute-start | bytes 786440 | tf_op jit(solution)/shard_map/ppermute | solution.py:251
  65.6 8.3 %collective-permute-start.9 = (bf16[216,256]{1,0:T(8,128)(2,1)S(1)}, bf16[216,256]{1,0:T(8,128)(2,1)S(1)}, u32[]{:S(2)}, u32[]{:S(2)}) collective-permute-start(bf16[216,256]{1,0:T(8,128)(2,1)S(1)} %fusion.25), channel_id=1, source_target_pairs={{0,8},{1,9},{2,10},{3,11},{4,12},{5,13},{6,14},{7,15},{8,0},{9,1},... | collective-permute-start | bytes 331784 | tf_op jit(solution)/shard_map/ppermute | solution.py:251
  71.3 8.3 %collective-permute-start.17 = (bf16[2,64,512]{2,1,0:T(8,128)(2,1)S(1)}, bf16[2,64,512]{2,1,0:T(8,128)(2,1)S(1)}, u32[]{:S(2)}, u32[]{:S(2)}) collective-permute-start(bf16[2,64,512]{2,1,0:T(8,128)(2,1)S(1)} %get-tuple-element.99), channel_id=1, source_target_pairs={{0,8},{1,9},{2,10},{3,11},{4,12},{5,13},{6,14},{7,15},{8,0},{9,1},... | collective-permute-start | bytes 393224 | tf_op jit(solution)/shard_map/ppermute | solution.py:251
  73.3 6.0 %collective-permute-start.13 = (bf16[2,216,256]{2,1,0:T(8,128)(2,1)S(1)}, bf16[2,216,256]{2,1,0:T(8,128)(2,1)S(1)}, u32[]{:S(2)}, u32[]{:S(2)}) collective-permute-start(bf16[2,216,256]{2,1,0:T(8,128)(2,1)S(1)} %get-tuple-element.89), channel_id=1, source_target_pairs={{0,4},{1,3},{2,6},{3,1},{4,0},{5,7},{6,2},{7,5},{8,12},{9,11},{10,... | collective-permute-start | bytes 663560 | tf_op jit(solution)/shard_map/ppermute | solution.py:251
  74.0 15.4 %collective-permute-start.10 = (bf16[216,256]{1,0:T(8,128)(2,1)S(1)}, bf16[216,256]{1,0:T(8,128)(2,1)S(1)}, u32[]{:S(2)}, u32[]{:S(2)}) collective-permute-start(bf16[216,256]{1,0:T(8,128)(2,1)S(1)} %fusion.28), channel_id=1, source_target_pairs={{8,24},{9,25},{10,26},{11,27},{12,28},{13,29},{14,30},{15,31},{16,... | collective-permute-start | bytes 331784 | tf_op jit(solution)/shard_map/ppermute | solution.py:251
  79.3 4.8 %collective-permute-start.14 = (bf16[216,256]{1,0:T(8,128)(2,1)S(1)}, bf16[216,256]{1,0:T(8,128)(2,1)S(1)}, u32[]{:S(2)}, u32[]{:S(2)}) collective-permute-start(bf16[216,256]{1,0:T(8,128)(2,1)S(1)} %fusion.26), channel_id=1, source_target_pairs={{0,8},{1,9},{2,10},{3,11},{4,12},{5,13},{6,14},{7,15},{8,0},{9,1},... | collective-permute-start | bytes 331784 | tf_op jit(solution)/shard_map/ppermute | solution.py:251
  79.6 9.1 %collective-permute-start.18 = (bf16[64,512]{1,0:T(8,128)(2,1)S(1)}, bf16[64,512]{1,0:T(8,128)(2,1)S(1)}, u32[]{:S(2)}, u32[]{:S(2)}) collective-permute-start(bf16[64,512]{1,0:T(8,128)(2,1)S(1)} %fusion.27), channel_id=1, source_target_pairs={{0,16},{1,17},{2,18},{3,19},{4,20},{5,21},{6,22},{7,23},{8,24},{9,... | collective-permute-start | bytes 196616 | tf_op jit(solution)/shard_map/ppermute | solution.py:251
  84.2 6.8 %collective-permute-start.15 = (bf16[216,256]{1,0:T(8,128)(2,1)S(1)}, bf16[216,256]{1,0:T(8,128)(2,1)S(1)}, u32[]{:S(2)}, u32[]{:S(2)}) collective-permute-start(bf16[216,256]{1,0:T(8,128)(2,1)S(1)} %fusion.29), channel_id=1, source_target_pairs={{0,16},{1,17},{2,18},{3,19},{4,20},{5,21},{6,22},{7,23},{24,8},{25... | collective-permute-start | bytes 331784 | tf_op jit(solution)/shard_map/ppermute | solution.py:251

commit v6 on v5

v6 whole, which is shorter than its diff:
```python
import functools
import math

import jax
import jax.numpy as jnp
from jax import lax
from jax.experimental import pallas as pl
from jax.experimental.pallas import tpu as pltpu
from jax.sharding import PartitionSpec as P

HB = 2
BF = jnp.bfloat16
F32 = jnp.float32


def dot(a, b):
    return lax.dot_general(a, b, (((1,), (0,)), ((), ())), preferred_element_type=F32)


def dot_nt(a, b):
    return lax.dot_general(a, b, (((1,), (1,)), ((), ())), preferred_element_type=F32)


def one_hot(index, shape, axis):
    return jnp.where(index == lax.broadcasted_iota(jnp.int32, shape, axis), 1.0, 0.0).astype(BF)


def segments(first, count, shard):
    row, cuts = first, []
    while row < first + count:
        number, inside = divmod(row, shard)
        rows = min(shard - inside, first + count - row)
        cuts.append((row - first, number, inside, rows))
        row += rows
    return cuts


def place(both, value, first, core):
    for at, number, inside, rows in segments(first, value.shape[0], both.shape[2]):
        both[(number % 2) ^ core, number // 2, pl.ds(inside, rows), :] = value[at : at + rows]


def halves(total, shard):
    shape = (total[0] // (2 * shard), shard, total[1])
    return (jax.ShapeDtypeStruct(shape, BF),) * 2, pltpu.VMEM((2,) + shape, F32)


def part(both, keep, send):
    keep[...] = both[0].astype(BF)
    send[...] = both[1].astype(BF)


def identity(size):
    return one_hot(lax.broadcasted_iota(jnp.int32, (size, size), 0), (size, size), 1)


def turned(table):
    values = table.astype(F32).astype(BF)
    return dot_nt(identity(table.shape[1]), values).astype(jnp.int32)


VMEM = pl.BlockSpec(memory_space=pltpu.VMEM)
SMEM = pl.BlockSpec(memory_space=pltpu.SMEM)


SMALL = pl.CostEstimate(flops=1 << 20, bytes_accessed=1 << 10, transcendentals=0)


def prep_kernel(pre, rows, parents, w_in, cur_in, act, pick, parent_pick, chosen, w, cur):
    children, slots = rows.shape
    count, channels = pre.shape
    columns = turned(parents[...])
    for c in range(children):
        mine = pl.ds(c * slots, slots)
        pick[:, mine] = one_hot(rows[c : c + 1, :], (count, slots), 0)
        parent_pick[mine, :] = one_hot(columns[:, c : c + 1], (slots, parent_pick.shape[1]), 1)
    act[...] = jnp.maximum(pre[...], jnp.zeros((), BF))
    turned_act = dot_nt(identity(channels), act[...]).astype(BF)
    chosen[...] = dot(turned_act, pick[...]).astype(BF)
    w[...] = w_in[...]
    cur[...] = cur_in[...]


def prep(pre, rows, parents, w, cur, parent_rows):
    count, channels = pre.shape
    children, slots = rows.shape
    shapes = (
        (count, channels),
        (count, children * slots),
        (children * slots, parent_rows),
        (channels, children * slots),
        w.shape,
        cur.shape,
    )
    return pl.pallas_call(
        prep_kernel,
        out_shape=tuple(jax.ShapeDtypeStruct(shape, BF) for shape in shapes),
        in_specs=[VMEM] * 5,
        out_specs=(VMEM,) * len(shapes),
        compiler_params=pltpu.CompilerParams(vmem_limit_bytes=16 << 20),
        cost_estimate=SMALL,
        name="prep",
    )(pre, rows, parents, w, cur)


def down_kernel(
    core, prev, act, pick, parent_pick, chosen, w, cur, head, tail, keep, send, both, gath, contrib
):
    count, channels = act.shape
    children = w.shape[0] // channels
    slots = pick.shape[1] // children
    halo = head.shape[0]
    ext = jnp.concatenate([prev[...], cur[...]], 0)
    own = [pl.ds(c * slots, slots) for c in range(children)]
    for c in range(children):
        got = dot(parent_pick[own[c], :], ext).astype(BF)
        gath[own[c], :] = got
        contrib[own[c], :] = dot_nt(got, w[pl.ds(c * channels, channels), :]).astype(BF)
    grad = dot(pick[...], contrib[...])
    masked = jnp.where(act[...].astype(F32) > 0, grad, 0.0).astype(BF)
    head[...] = masked[:halo]
    tail[...] = masked[count - halo :]
    for c in range(children):
        place(both, dot(chosen[:, own[c]], gath[own[c], :]), c * channels, core[0])
    part(both, keep, send)


def down(core, prev, prepared, halo, shard):
    act, pick, parent_pick, chosen, w, cur = prepared
    channels = act.shape[1]
    listed, width = pick.shape[1], cur.shape[1]
    kinds, both = halves(w.shape, shard)
    side = jax.ShapeDtypeStruct((halo, channels), BF)
    return pl.pallas_call(
        down_kernel,
        out_shape=(side, side) + kinds,
        in_specs=[SMEM] + [VMEM] * 7,
        out_specs=(VMEM,) * 4,
        scratch_shapes=[
            both,
            pltpu.VMEM((listed, width), BF),
            pltpu.VMEM((listed, channels), BF),
        ],
        compiler_params=pltpu.CompilerParams(vmem_limit_bytes=20 << 20),
        cost_estimate=SMALL,
        name="down",
    )(core, prev, *prepared)


def conv_plan(kernel, channels, quarters):
    size = kernel * channels // 4
    plan, out = [], 0
    for quarter in quarters:
        row = quarter * size
        while row < (quarter + 1) * size:
            k, first = divmod(row, channels)
            last = min(channels, (quarter + 1) * size - k * channels)
            plan.append((k, first, last, out))
            out += last - first
            row += last - first
    return plan


def turn_kernel(pairs, feats, w, tab, feats_t):
    tab[...] = turned(pairs[...])
    feats_t[...] = dot_nt(identity(feats.shape[1]), feats[...]).astype(BF)


def turn(pairs, feats, w):
    return pl.pallas_call(
        turn_kernel,
        out_shape=(
            jax.ShapeDtypeStruct(pairs.shape[::-1], jnp.int32),
            jax.ShapeDtypeStruct(feats.shape[::-1], BF),
        ),
        in_specs=[VMEM] * 3,
        out_specs=(VMEM,) * 2,
        compiler_params=pltpu.CompilerParams(vmem_limit_bytes=20 << 20),
        cost_estimate=SMALL,
        name="turn",
    )(pairs, feats, w)


def conv_kernel(plan, begun, *refs):
    core, src, tgt, before, head, tail, after, w, *rest = refs
    if begun:
        pairs, feats, partial, grad, keep, send, both, ext, acc, col0, col1, tab, feats_t = rest
        turn_kernel(pairs, feats, w, tab, feats_t)
    else:
        tab, feats_t, grad, keep, send, both, ext, acc, col0, col1 = rest
    cols = (col0, col1)
    slots = src.shape[0]
    blocks, rows, channels = col0.shape
    count = feats_t.shape[1]
    at = 0
    for piece in (before, head, tail, after):
        for b in range(piece.shape[0] // rows):
            ext[at] = piece[pl.ds(b * rows, rows), :]
            at += 1
    acc[...] = partial[...] if begun else jnp.zeros_like(acc)
    lanes = lax.broadcasted_iota(jnp.int32, (rows, rows), 1).astype(jnp.int16)
    one, zero = jnp.ones((), BF), jnp.zeros((), BF)

    def gather(k, col):
        col[...] = jnp.zeros_like(col)
        for p in range(slots):
            q = k * slots + p
            index = jnp.broadcast_to(tab[:, q : q + 1], (rows, rows)).astype(jnp.int16)
            pick = jnp.where(index == lanes, one, zero)
            piece = dot(pick, ext[tgt[p, k]]).astype(BF)
            owner = src[p, k]
            col[owner] = col[owner] + piece

    gather(plan[0][0], cols[0])
    for at, (k, first, last, out) in enumerate(plan):
        if at + 1 < len(plan):
            gather(plan[at + 1][0], cols[(at + 1) % 2])
        column = cols[at % 2][...].reshape(count, channels)
        place(both, dot(feats_t[pl.ds(first, last - first), :], column), out, core[0])
        if first == 0:
            acc[...] += dot_nt(column, w[pl.ds(k * channels, channels), :])
    grad[...] = acc[...].astype(grad.dtype)
    part(both, keep, send)


def conv(core, src, tgt, sides, w, tables, quarters, shard, partial):
    begun = partial is not None
    shapes = [x.shape if begun else x.shape[::-1] for x in tables]
    (listed, rows), (count, channels) = shapes
    kernel = w.shape[0] // channels
    kinds, both = halves((len(quarters) * kernel * channels // 4, channels), shard)
    ext_rows = sum(side.shape[0] for side in sides)
    block = (rows, channels)
    grad = jax.ShapeDtypeStruct((count, channels), BF if begun else F32)
    operands = (core, src, tgt, *sides, w, *tables) + ((partial,) if begun else ())
    return pl.pallas_call(
        functools.partial(conv_kernel, conv_plan(kernel, channels, quarters), begun),
        out_shape=(grad,) + kinds,
        in_specs=[SMEM] * 3 + [VMEM] * (len(operands) - 3),
        out_specs=(VMEM,) * 3,
        scratch_shapes=[
            both,
            pltpu.VMEM((ext_rows // rows,) + block, BF),
            pltpu.VMEM((count, channels), F32),
            pltpu.VMEM((count // rows,) + block, BF),
            pltpu.VMEM((count // rows,) + block, BF),
        ]
        + [
            pltpu.VMEM((rows, listed), jnp.int32),
            pltpu.VMEM((channels, count), BF),
        ]
        * begun,
        compiler_params=pltpu.CompilerParams(vmem_limit_bytes=24 << 20),
        cost_estimate=SMALL,
        name="conv",
    )(*operands)


def moved(x, peers, to):
    pairs = [(i, to(i)) for i in range(peers)]
    return lax.ppermute(x, "space", [(i, j) for i, j in pairs if j is not None and 0 <= j < peers])


def moved_together(x, to_x, y, to_y, peers):
    if any(to_x(i) != to_y(i) for i in range(peers)):
        return moved(x, peers, to_x), moved(y, peers, to_y)
    rows = x.shape[-2:]
    flat = [z.reshape((-1,) + rows) for z in (x, y)]
    got = moved(jnp.concatenate(flat, 0), peers, to_x)
    cut = flat[0].shape[0]
    return got[:cut].reshape(x.shape), got[cut:].reshape(y.shape)


def taken(x, axis, digit):
    return lax.dynamic_index_in_dim(x, digit, axis=axis, keepdims=False)


def low_steps(bits):
    left = [list(range(bits - 1, -1, -1)) for core in range(2)]
    steps = []
    for j in range(bits):
        by = (j, (j + bits // 2) % bits)
        steps.append((by, [left[core].index(by[core]) for core in range(2)]))
        for core in range(2):
            left[core].remove(by[core])
    return steps


def fold_low(parts, me, step):
    core = me % 2
    by, axes = step
    bit = jnp.where(core == 0, me >> (1 + by[0]), me >> (1 + by[1])) % 2

    def half(x, digit):
        if axes[0] == axes[1]:
            return taken(x, 1 + axes[0], digit)
        return jnp.where(core == 0, taken(x, 1 + axes[0], digit), taken(x, 1 + axes[1], digit))

    def piece(digit):
        pieces = [half(kept, digit).astype(F32) + half(got, digit).astype(F32) for kept, got in parts]
        return jnp.concatenate(pieces, 0) if len(pieces) > 1 else pieces[0]

    return piece(bit), piece(1 - bit).astype(BF), lambda i: i ^ (2 << by[i % 2])


def fold_bit(keep, got, me, peers, stride, first):
    bit = me // stride % 2
    axis = keep.ndim - 3

    def piece(digit):
        return taken(keep, axis, digit) + taken(got, axis, digit).astype(F32)

    mine = bit ^ first
    sent = piece(1 - mine).astype(BF)
    return piece(mine), moved(sent, peers, lambda i: i ^ stride)


def per_device(
    feats,
    pre_act,
    coarse_grad,
    w_sub,
    w_down,
    pair_src,
    pair_tgt,
    pair_rows,
    down_rows,
    down_parent,
):
    peers = lax.axis_size("space")
    me = lax.axis_index("space")
    row_count, channels = feats.shape
    block_rows = pair_rows.shape[-1]
    out_width = coarse_grad.shape[1]
    kernel = pair_src.shape[1]
    children = down_rows.shape[1]
    scale = 1.0 / math.sqrt(peers * row_count)
    bits = (peers // 8).bit_length() - 1
    steps = low_steps(bits)
    near, far = peers // 4, peers // 2

    halo = HB * block_rows
    core = (me % 2).reshape(1)
    pinned = lax.optimization_barrier
    other_way = [((b, a), [y, x]) for (a, b), (x, y) in steps]

    def across(x):
        return moved(x, peers, lambda i: i ^ 1)

    def spread(kept, got, high):
        shape = (high,) + (2,) * bits + got.shape[-2:]
        return kept.reshape(shape), got.reshape(shape)

    previous = moved(coarse_grad[-block_rows:], peers, lambda i: i + 1)
    prepared = prep(
        pre_act,
        down_rows[0],
        down_parent[0],
        w_down,
        coarse_grad,
        block_rows + coarse_grad.shape[0],
    )
    head, tail, low, low_send = down(
        core, previous, prepared, halo, children * channels // peers
    )

    before = moved(tail, peers, lambda i: i + 1)
    after = moved(head, peers, lambda i: i - 1)
    low_got = across(low_send)
    pairs = pair_rows[0].reshape(-1, block_rows)
    tables = turn(pairs, feats, w_sub)
    before, after, tables, low, low_got = pinned((before, after, tables, low, low_got))
    sides = (before, head, tail, after)
    shard = kernel * channels // peers

    def quarters(numbers, tables, partial=None):
        src, tgt = pair_src[0].T, pair_tgt[0].T
        return conv(core, src, tgt, sides, w_sub, tables, numbers, shard, partial)

    low, low_send, to = fold_low([spread(low, low_got, 4)], me, steps[0])
    low_got = moved(low_send, peers, to)
    partial, outer, outer_send = quarters((0, 3), tables)
    partial, outer, outer_send, low, low_got = pinned((partial, outer, outer_send, low, low_got))

    outer_got = across(outer_send)
    for step in steps[1:]:
        low, low_send, to = fold_low([(low, low_got)], me, step)
        low_got = moved(low_send, peers, to)
    grad_in, inner, inner_send = quarters((1, 2), (pairs, feats), partial)
    grad_in, inner, inner_send, outer, outer_got, low, low_got = pinned(
        (grad_in, inner, inner_send, outer, outer_got, low, low_got)
    )

    inner_got = across(inner_send)
    outer, outer_send, outer_to = fold_low([spread(outer, outer_got, 2)], me, other_way[0])
    for step in other_way[1:]:
        outer_got = moved(outer_send, peers, outer_to)
        outer, outer_send, outer_to = fold_low([(outer, outer_got)], me, step)
    low, low_got = (x.reshape((2, 2) + x.shape[-2:]) for x in (low, low_got))
    low, low_got = fold_bit(low, low_got, me, peers, near, 0)

    inner, inner_send, inner_to = fold_low([spread(inner, inner_got, 2)], me, steps[0])
    outer_got, inner_got = moved_together(outer_send, outer_to, inner_send, inner_to, peers)
    low, low_got = fold_bit(low, low_got, me, peers, far, 0)

    for step in steps[1:]:
        inner, inner_send, to = fold_low([(inner, inner_got)], me, step)
        inner_got = moved(inner_send, peers, to)
    outer, outer_got = fold_bit(outer, outer_got, me, peers, near, 0)
    inner, inner_got = fold_bit(inner, inner_got, me, peers, near, 1)

    def last_step(kept, got, wanted):
        total = kept + got.astype(F32)
        to = lambda i: i ^ far if (i ^ far) // near in wanted else None
        return total + moved(total.astype(BF), peers, to).astype(F32)

    digit = me // near
    is_outer = (digit == 0) | (digit == 3)
    outer_sum = last_step(outer, outer_got, (0, 3))
    inner_sum = last_step(inner, inner_got, (1, 2))
    sub_sum = jnp.where(is_outer, outer_sum, inner_sum)
    low_sum = low + low_got.astype(F32)
    return (grad_in, sub_sum.reshape(-1) * scale, low_sum * scale)


def solution(mesh):
    rows = ("scene", "space")
    placed = (
        P(rows, None),
        P(rows, None),
        P(rows, None),
        P(),
        P(),
        P(rows, None, None),
        P(rows, None, None),
        P(rows, None, None, None),
        P(rows, None, None),
        P(rows, None, None),
    )
    return jax.shard_map(
        per_device,
        mesh=mesh,
        in_specs=placed,
        out_specs=(P(rows, None), P(rows), P(rows, None)),
        check_vma=False,
    )
```

time: 92.7 us -> 96.3 us (1.039)
  waiting for transfers between devices: 14.7 us -> 20.1 us
  local copies, waits for them, and re-layouts: 20 us -> 14.8 us
  other arithmetic: 7.02 us -> 9.72 us
  starting transfers between devices: 29.8 us -> 32.1 us
  Pallas kernels: 19.5 us -> 18 us
    ppermute x19 -> x17, waiting for transfers between devices: 14.7 us -> 20.1 us  [moved(): lax.ppermute(x, 'space', [(i, j) for i, j in pairs if j is not None and 0...]
    unnamed x67 -> x49, local copies, waits for them, and re-layouts: 17 us -> 11.8 us
    ppermute x19 -> x17, starting transfers between devices: 29.8 us -> 32.1 us  [moved(): lax.ppermute(x, 'space', [(i, j) for i, j in pairs if j is not None and 0...]
    pallas_call x3 -> x2, Pallas kernels: 14.8 us -> 13.6 us  [conv(): pl.pallas_call(functools.partial(conv_kernel, conv_plan(kernel, channels,...]
    convert_element_type x5, other arithmetic: 4.12 us -> 5.22 us  [fold_low(): return (piece(bit), piece(1 - bit).astype(BF), lambda i: i ^ 2 << by[i % 2])]
    convert_element_type x4, other arithmetic: 0.13 us -> 1.11 us  [fold_bit(): sent = piece(1 - mine).astype(BF)]
    dynamic_slice x4 -> x6, local copies, waits for them, and re-layouts: 2.97 us -> 2.9 us  [taken(): return lax.dynamic_index_in_dim(x, digit, axis=axis, keepdims=False)]
  transfers between devices with their start and end apart: 19 -> 17, of which waited for: 5 -> 8; matrix products, arithmetic and copies ran while one was open for 11% -> 9% of each run, Pallas kernels for 19% -> 15%
where the time goes in v6:
time: 96.3 us; the launch traced here: 95.7 us
  starting transfers between devices  32.1 us (33%)
  waiting for transfers between devices  20.1 us (21%)
  Pallas kernels  18 us (19%)
  local copies, waits for them, and re-layouts  14.8 us (15%)
  other arithmetic  9.72 us (10%)
  between operations  0.98 us (1%)
    ppermute x17, starting transfers between devices, moved(): lax.ppermute(x, 'space', [(i, j) for i, j in pairs if j is not None and 0...  32.1 us
    ppermute x17, waiting for transfers between devices, moved(): lax.ppermute(x, 'space', [(i, j) for i, j in pairs if j is not None and 0...  20.1 us
    pallas_call x2, Pallas kernels, conv(): pl.pallas_call(functools.partial(conv_kernel, conv_plan(kernel, channels,...  13.6 us
    unnamed x49, local copies, waits for them, and re-layouts  11.8 us
    convert_element_type x5, other arithmetic, fold_low(): return (piece(bit), piece(1 - bit).astype(BF), lambda i: i ^ 2 << by[i % 2])  5.22 us
    pallas_call x1, Pallas kernels, down(): pl.pallas_call(down_kernel, out_shape=(side, side) + kinds, in_specs=[SME...  3.21 us
    dynamic_slice x6, local copies, waits for them, and re-layouts, taken(): return lax.dynamic_index_in_dim(x, digit, axis=axis, keepdims=False)  2.9 us
  transfers between devices with their start and end apart: 17, of which 8 were waited for; matrix products, arithmetic and copies ran while one was open for 9% of the time, Pallas kernels for 15%

profile of v6, /device:TPU:0, one launch (start us, length us, event | category | flops | bytes accessed | tf_op | source)
XLA Modules:
  0.0 95.7 jit_solution(16945295170686781190)
XLA Ops:
  0.6 2.4 %collective-permute-start = (bf16[128,512]{1,0:T(8,128)(2,1)}, bf16[128,512]{1,0:T(8,128)(2,1)S(1)}, u32[]{:S(2)}, u32[]{:S(2)}) collective-permute-start(bf16[128,512]{1,0:T(8,128)(2,1)} %cur_in.1), channel_id=1, source_target_pairs={{0,1},{1,2},{2,3},{3,4},{4,5},{5,6},{6,7},{7,8},{8,9},{9,10},{10,1... | collective-permute-start | bytes 393224 | tf_op jit(solution)/shard_map/ppermute | solution.py:261
  3.0 1.6 %copy-done.7 = bf16[2048,512]{1,0:T(8,128)(2,1)S(1)} copy-done((bf16[2048,512]{1,0:T(8,128)(2,1)S(1)}, bf16[2048,512]{1,0:T(8,128)(2,1)}, u32[]{:S(2)}) %copy-start.7) | copy-done | bytes 2097176
  4.6 0.9 copy-done.14
  5.6 0.9 copy-done.15
  6.5 0.7 copy-done.20
  7.2 0.7 copy-done.21
  7.8 0.9 prep.1
  8.7 0.0 collective-permute-done.prev
  8.8 0.0 copy-start.16
  8.8 0.6 copy-done.16
  9.4 0.9 copy-done.17
  10.3 3.2 %down.1 = (bf16[256,256]{1,0:T(8,128)(2,1)}, bf16[256,256]{1,0:T(8,128)(2,1)}, bf16[16,64,512]{2,1,0:T(8,128)(2,1)S(1)}, bf16[16,64,512]{2,1,0:T(8,128)(2,1)}) custom-call(s32[1]{0:T(128)} %bitcast.core.refs_0_, bf16[128,512]{1,0:T(8,128)(2,1)S(1)} %copy-done.17, bf16[512,256]{1,0:T(8,128)(2,1)S(1)} %get-tuple-element.39.act, ...), custom_call_target="tpu_custom_call" | custom-call | flops 1048576 | bytes 1024 | tf_op jit(solution)/shard_map/down/pallas_call | solution.py:134
  13.5 1.0 %copy-done.1 = bf16[16,64,512]{2,1,0:T(8,128)(2,1)} copy-done((bf16[16,64,512]{2,1,0:T(8,128)(2,1)}, bf16[16,64,512]{2,1,0:T(8,128)(2,1)S(1)}, u32[]{:S(2)}) %copy-start.1) | copy-done | bytes 1048600
  14.5 2.6 %collective-permute-start.3 = (bf16[16,64,512]{2,1,0:T(8,128)(2,1)}, bf16[16,64,512]{2,1,0:T(8,128)(2,1)}, u32[]{:S(2)}, u32[]{:S(2)}) collective-permute-start(bf16[16,64,512]{2,1,0:T(8,128)(2,1)} %get-tuple-element.50), channel_id=1, source_target_pairs={{0,1},{1,0},{2,3},{3,2},{4,5},{5,4},{6,7},{7,6},{8,9},{9,8},{10,11... | collective-permute-start | bytes 3145736 | tf_op jit(solution)/shard_map/ppermute | solution.py:261
  17.1 2.6 %collective-permute-start.1 = (bf16[256,256]{1,0:T(8,128)(2,1)}, bf16[256,256]{1,0:T(8,128)(2,1)}, u32[]{:S(2)}, u32[]{:S(2)}) collective-permute-start(bf16[256,256]{1,0:T(8,128)(2,1)} %get-tuple-element.45.refs_5_), channel_id=1, source_target_pairs={{0,1},{1,2},{2,3},{3,4},{4,5},{5,6},{6,7},{7,8},{8,9},{9,10},{10,1... | collective-permute-start | bytes 393224 | tf_op jit(solution)/shard_map/ppermute | solution.py:261
  19.7 1.5 %collective-permute-start.2 = (bf16[256,256]{1,0:T(8,128)(2,1)}, bf16[256,256]{1,0:T(8,128)(2,1)}, u32[]{:S(2)}, u32[]{:S(2)}) collective-permute-start(bf16[256,256]{1,0:T(8,128)(2,1)} %get-tuple-element.46.refs_4_), channel_id=1, source_target_pairs={{1,0},{2,1},{3,2},{4,3},{5,4},{6,5},{7,6},{8,7},{9,8},{10,9},{11,1... | collective-permute-start | bytes 393224 | tf_op jit(solution)/shard_map/ppermute | solution.py:261
  21.2 0.0 copy-start.8
  21.2 1.0 %copy-done.8 = bf16[512,256]{1,0:T(8,128)(2,1)S(1)} copy-done((bf16[512,256]{1,0:T(8,128)(2,1)S(1)}, bf16[512,256]{1,0:T(8,128)(2,1)}, u32[]{:S(2)}) %copy-start.8) | copy-done | bytes 262168
  22.2 0.9 copy-done.12
  23.1 0.3 turn.1
  23.4 0.3 collective-permute-done.2.refs_6_
  23.7 0.0 collective-permute-done.3
  23.7 1.4 %constant_dynamic-slice_fusion.5 = (bf16[4,2,1,64,512]{4,3,2,1,0:T(8,128)(2,1)S(1)}, bf16[4,2,1,64,512]{4,3,2,1,0:T(8,128)(2,1)S(1)}, bf16[4,2,1,64,512]{4,3,2,1,0:T(8,128)(2,1)S(1)}, bf16[4,2,1,64,512]{4,3,2,1,0:T(8,128)(2,1)S(1)}) fusion(bf16[4,2,2,64,512]{4,3,2,1,0:T(8,128)(2,1)} %bitcast.13, s32[]{:T(128)S(6)} %select_n.228, s32[]{:T(128)S(6)} %select_n.225, ...), kind=kLoop, calls=%fused_computation.55 | loop fusion | bytes 4194312 | tf_op jit(solution)/shard_map/jit(dynamic_index_in_dim)/dynamic_slice | solution.py:275
  25.1 1.4 %constant_dynamic-slice_fusion.4 = (bf16[4,1,2,64,512]{4,3,2,1,0:T(8,128)(2,1)S(1)}, bf16[4,1,2,64,512]{4,3,2,1,0:T(8,128)(2,1)S(1)}, bf16[4,1,2,64,512]{4,3,2,1,0:T(8,128)(2,1)S(1)}, bf16[4,1,2,64,512]{4,3,2,1,0:T(8,128)(2,1)S(1)}) fusion(bf16[4,2,2,64,512]{4,3,2,1,0:T(8,128)(2,1)} %bitcast.13, s32[]{:T(128)S(6)} %select_n.228, s32[]{:T(128)S(6)} %select_n.225, ...), kind=kLoop, calls=%fused_computation.54 | loop fusion | bytes 4194312 | tf_op jit(solution)/shard_map/jit(dynamic_index_in_dim)/dynamic_slice | solution.py:275
  26.5 0.0 copy-start.18
  26.5 0.0 copy-start.19
  26.5 0.3 add_convert_fusion
  26.8 3.3 %collective-permute-start.4 = (bf16[4,2,64,512]{3,2,0,1:T(8,128)(2,1)S(1)}, bf16[4,2,64,512]{3,2,0,1:T(8,128)(2,1)}, u32[]{:S(2)}, u32[]{:S(2)}) collective-permute-start(bf16[4,2,64,512]{3,2,0,1:T(8,128)(2,1)S(1)} %add_convert_fusion), channel_id=1, source_target_pairs={{0,2},{1,5},{2,0},{3,7},{4,6},{5,1},{6,4},{7,3},{8,10},{9,13},{10,... | collective-permute-start | bytes 1572872 | tf_op jit(solution)/shard_map/ppermute | solution.py:261
  30.2 6.5 %conv.2 = (f32[512,256]{1,0:T(8,128)S(1)}, bf16[8,216,256]{2,1,0:T(8,128)(2,1)S(1)}, bf16[8,216,256]{2,1,0:T(8,128)(2,1)}) custom-call(s32[1]{0:T(128)} %bitcast.core.refs_0_, s32[8,27]{1,0:T(8,128)S(1)} %bitcast.192, s32[8,27]{1,0:T(8,128)S(1)} %bitcast.194, bf16[256,256]{1,0:T(8,128)(2,1)} %collective-permute-done.1.refs_3_, ...), custom_call_target="tpu_custom_call" | custom-call | flops 1048576 | bytes 1024 | tf_op jit(solution)/shard_map/conv/pallas_call | solution.py:236
  36.7 0.9 copy-done.5
  37.6 0.8 copy-done.10
  38.4 1.3 %convert_add_fusion = f32[4,2,64,512]{3,2,0,1:T(8,128)} fusion(bf16[4,1,2,64,512]{4,3,2,1,0:T(8,128)(2,1)S(1)} %get-tuple-element.90, bf16[4,2,1,64,512]{4,3,2,1,0:T(8,128)(2,1)S(1)} %get-tuple-element.88, bf16[4,1,2,64,512]{4,3,2,1,0:T(8,128)(2,1)S(1)} %get-tuple-element.93, bf16[4,2,1,64,512]{4,3,2,1,0:T(8,128)(2,1)S(1)} %get-tuple-element.95, pred[]{:T(512)S(6)} %eq.44), kind=kLoop, calls=%fused_computation.1 | loop fusion | flops 1310720 | bytes 3145729 | tf_op jit(solution)/shard_map/add | solution.py:300
  39.7 0.0 collective-permute-done.4
  39.7 1.5 %collective-permute-start.5 = (bf16[8,216,256]{2,1,0:T(8,128)(2,1)}, bf16[8,216,256]{2,1,0:T(8,128)(2,1)}, u32[]{:S(2)}, u32[]{:S(2)}) collective-permute-start(bf16[8,216,256]{2,1,0:T(8,128)(2,1)} %get-tuple-element.65), channel_id=1, source_target_pairs={{0,1},{1,0},{2,3},{3,2},{4,5},{5,4},{6,7},{7,6},{8,9},{9,8},{10,11... | collective-permute-start | bytes 2654216 | tf_op jit(solution)/shard_map/ppermute | solution.py:261
  41.2 2.4 %fusion = (bf16[4,64,512]{2,1,0:T(8,128)(2,1)S(1)}, f32[4,64,512]{2,1,0:T(8,128)}) fusion(f32[4,2,64,512]{3,2,0,1:T(8,128)} %convert_add_fusion, s32[]{:T(128)S(6)} %select_n.234, bf16[4,2,64,512]{3,2,0,1:T(8,128)(2,1)} %collective-permute-done.4, s32[]{:T(128)S(6)} %select_n.233), kind=kLoop, calls=%fused_computation.25 | loop fusion | flops 655360 | bytes 2359304 | tf_op jit(solution)/shard_map/convert_element_type | solution.py:303
  43.6 0.6 collective-permute-start.6
  44.1 7.1 %conv.3 = (bf16[512,256]{1,0:T(8,128)(2,1)}, bf16[8,216,256]{2,1,0:T(8,128)(2,1)S(1)}, bf16[8,216,256]{2,1,0:T(8,128)(2,1)S(1)}) custom-call(s32[1]{0:T(128)} %bitcast.core.refs_0_, s32[8,27]{1,0:T(8,128)S(1)} %bitcast.193, s32[8,27]{1,0:T(8,128)S(1)} %bitcast.195, bf16[256,256]{1,0:T(8,128)(2,1)} %collective-permute-done.1.refs_3_, ...), custom_call_target="tpu_custom_call" | custom-call | flops 1048576 | bytes 1024 | tf_op jit(solution)/shard_map/conv/pallas_call | solution.py:236
  51.3 2.5 %collective-permute-start.8 = (bf16[8,216,256]{2,1,0:T(8,128)(2,1)S(1)}, bf16[8,216,256]{2,1,0:T(8,128)(2,1)S(1)}, u32[]{:S(2)}, u32[]{:S(2)}) collective-permute-start(bf16[8,216,256]{2,1,0:T(8,128)(2,1)S(1)} %get-tuple-element.72), channel_id=1, source_target_pairs={{0,1},{1,0},{2,3},{3,2},{4,5},{5,4},{6,7},{7,6},{8,9},{9,8},{10,11... | collective-permute-start | bytes 2654216 | tf_op jit(solution)/shard_map/ppermute | solution.py:261
  53.8 2.1 %add_convert_fusion.2 = (bf16[2,2,216,256]{3,2,1,0:T(8,128)(2,1)S(1)}, f32[2,2,216,256]{3,2,1,0:T(8,128)S(1)}) fusion(bf16[2,2,2,216,256]{4,3,2,1,0:T(8,128)(2,1)} %bitcast.25, s32[]{:T(128)S(6)} %select_n.234, bf16[2,2,2,216,256]{4,3,2,1,0:T(8,128)(2,1)S(1)} %bitcast.189, pred[]{:T(512)S(6)} %eq.44, s32[]{:T(128)S(6)} %select_n.233), kind=kLoop, calls=%fused_computation.4 | loop fusion | flops 2433024 | bytes 4866057 | tf_op jit(solution)/shard_map/convert_element_type | solution.py:303
  55.9 0.7 collective-permute-start.7
  56.6 7.6 %collective-permute-done.7 = bf16[2,2,216,256]{3,2,1,0:T(8,128)(2,1)S(1)} collective-permute-done((bf16[2,2,216,256]{3,2,1,0:T(8,128)(2,1)S(1)}, bf16[2,2,216,256]{3,2,1,0:T(8,128)(2,1)S(1)}, u32[]{:S(2)}, u32[]{:S(2)}) %collective-permute-start.7) | collective-permute-done | bytes 442400 | tf_op jit(solution)/shard_map/ppermute | solution.py:261
  64.3 0.1 convert_add_fusion.4
  64.5 0.3 add_convert_fusion.1
  64.8 0.9 pad_maximum_fusion
  65.7 1.2 %collective-permute-start.9 = (bf16[6,216,256]{2,1,0:T(8,128)(2,1)}, bf16[6,216,256]{2,1,0:T(8,128)(2,1)S(1)}, u32[]{:S(2)}, u32[]{:S(2)}) collective-permute-start(bf16[6,216,256]{2,1,0:T(8,128)(2,1)} %pad_maximum_fusion), channel_id=1, source_target_pairs={{0,2},{1,5},{2,0},{3,7},{4,6},{5,1},{6,4},{7,3},{8,10},{9,13},{10,... | collective-permute-start | bytes 1990664 | tf_op jit(solution)/shard_map/ppermute | solution.py:261
  66.9 1.0 %fusion.5 = (bf16[2,64,512]{2,1,0:T(8,128)(2,1)S(1)}, f32[2,1,64,512]{3,2,1,0:T(8,128)S(1)}) fusion(f32[2,2,64,512]{3,2,1,0:T(8,128)S(1)} %bitcast.201, s32[]{:T(128)S(6)} %select_n.247, bf16[2,2,64,512]{3,2,1,0:T(8,128)(2,1)} %bitcast.203, s32[]{:T(128)S(6)} %select_n.243), kind=kLoop, calls=%fused_computation.39 | loop fusion | flops 327680 | bytes 1179656 | tf_op jit(solution)/shard_map/convert_element_type | solution.py:314
  68.0 1.6 %collective-permute-start.15 = (bf16[2,64,512]{2,1,0:T(8,128)(2,1)S(1)}, bf16[2,64,512]{2,1,0:T(8,128)(2,1)S(1)}, u32[]{:S(2)}, u32[]{:S(2)}) collective-permute-start(bf16[2,64,512]{2,1,0:T(8,128)(2,1)S(1)} %get-tuple-element.91), channel_id=1, source_target_pairs={{0,8},{1,9},{2,10},{3,11},{4,12},{5,13},{6,14},{7,15},{8,0},{9,1},... | collective-permute-start | bytes 393224 | tf_op jit(solution)/shard_map/ppermute | solution.py:261
  69.6 0.2 convert_add_fusion.1
  69.8 6.8 %collective-permute-done.9 = bf16[6,216,256]{2,1,0:T(8,128)(2,1)S(1)} collective-permute-done((bf16[6,216,256]{2,1,0:T(8,128)(2,1)}, bf16[6,216,256]{2,1,0:T(8,128)(2,1)S(1)}, u32[]{:S(2)}, u32[]{:S(2)}) %collective-permute-start.9) | collective-permute-done | bytes 663584 | tf_op jit(solution)/shard_map/ppermute | solution.py:261
  76.7 0.1 fusion.2
  76.8 0.7 collective-permute-start.12
  77.5 2.6 %collective-permute-start.16 = (bf16[64,512]{1,0:T(8,128)(2,1)S(1)}, bf16[64,512]{1,0:T(8,128)(2,1)S(1)}, u32[]{:S(2)}, u32[]{:S(2)}) collective-permute-start(bf16[64,512]{1,0:T(8,128)(2,1)S(1)} %fusion.10), channel_id=1, source_target_pairs={{0,16},{1,17},{2,18},{3,19},{4,20},{5,21},{6,22},{7,23},{8,24},{9,... | collective-permute-start | bytes 196616 | tf_op jit(solution)/shard_map/ppermute | solution.py:261
  80.2 0.7 collective-permute-start.10
  80.8 2.0 %collective-permute-done.12 = bf16[2,216,256]{2,1,0:T(8,128)(2,1)S(1)} collective-permute-done((bf16[2,216,256]{2,1,0:T(8,128)(2,1)S(1)}, bf16[2,216,256]{2,1,0:T(8,128)(2,1)S(1)}, u32[]{:S(2)}, u32[]{:S(2)}) %collective-permute-start.12) | collective-permute-done | bytes 221216 | tf_op jit(solution)/shard_map/ppermute | solution.py:261
  82.8 1.6 %collective-permute-start.13 = (bf16[216,256]{1,0:T(8,128)(2,1)S(1)}, bf16[216,256]{1,0:T(8,128)(2,1)S(1)}, u32[]{:S(2)}, u32[]{:S(2)}) collective-permute-start(bf16[216,256]{1,0:T(8,128)(2,1)S(1)} %fusion.9), channel_id=1, source_target_pairs={{0,8},{1,9},{2,10},{3,11},{4,12},{5,13},{6,14},{7,15},{8,0},{9,1},... | collective-permute-start | bytes 331784 | tf_op jit(solution)/shard_map/ppermute | solution.py:261
  84.4 1.2 %collective-permute-done.10 = bf16[216,256]{1,0:T(8,128)(2,1)S(1)} collective-permute-done((bf16[216,256]{1,0:T(8,128)(2,1)S(1)}, bf16[216,256]{1,0:T(8,128)(2,1)S(1)}, u32[]{:S(2)}, u32[]{:S(2)}) %collective-permute-start.10) | collective-permute-done | bytes 110624 | tf_op jit(solution)/shard_map/ppermute | solution.py:261
  85.7 1.3 %collective-permute-start.11 = (bf16[216,256]{1,0:T(8,128)(2,1)S(1)}, bf16[216,256]{1,0:T(8,128)(2,1)S(1)}, u32[]{:S(2)}, u32[]{:S(2)}) collective-permute-start(bf16[216,256]{1,0:T(8,128)(2,1)S(1)} %fusion.11), channel_id=1, source_target_pairs={{8,24},{9,25},{10,26},{11,27},{12,28},{13,29},{14,30},{15,31},{16,... | collective-permute-start | bytes 331784 | tf_op jit(solution)/shard_map/ppermute | solution.py:261
  87.0 0.7 collective-permute-done.13
  87.7 4.8 %collective-permute-start.14 = (bf16[216,256]{1,0:T(8,128)(2,1)S(1)}, bf16[216,256]{1,0:T(8,128)(2,1)S(1)}, u32[]{:S(2)}, u32[]{:S(2)}) collective-permute-start(bf16[216,256]{1,0:T(8,128)(2,1)S(1)} %fusion.12), channel_id=1, source_target_pairs={{0,16},{1,17},{2,18},{3,19},{4,20},{5,21},{6,22},{7,23},{24,8},{25... | collective-permute-start | bytes 331784 | tf_op jit(solution)/shard_map/ppermute | solution.py:261
  92.5 0.7 fusion.7
  93.2 0.7 collective-permute-done.11
  93.9 0.9 collective-permute-done.14
  94.8 0.1 multiply_bitcast_fusion
  94.9 0.8 copy.43
  (49 shorter events, 0.4 us)
Async XLA Ops:
  0.6 8.1 %collective-permute-start = (bf16[128,512]{1,0:T(8,128)(2,1)}, bf16[128,512]{1,0:T(8,128)(2,1)S(1)}, u32[]{:S(2)}, u32[]{:S(2)}) collective-permute-start(bf16[128,512]{1,0:T(8,128)(2,1)} %cur_in.1), channel_id=1, source_target_pairs={{0,1},{1,2},{2,3},{3,4},{4,5},{5,6},{6,7},{7,8},{8,9},{9,10},{10,1... | collective-permute-start | bytes 393224 | tf_op jit(solution)/shard_map/ppermute | solution.py:261
  3.0 1.6 %copy-start.7 = (bf16[2048,512]{1,0:T(8,128)(2,1)S(1)}, bf16[2048,512]{1,0:T(8,128)(2,1)}, u32[]{:S(2)}) copy-start(bf16[2048,512]{1,0:T(8,128)(2,1)} %w_in.1) | copy-start | bytes 6291460
  4.6 0.9 copy-start.14
  5.6 0.9 copy-start.15
  6.5 0.7 copy-start.20
  7.2 0.7 copy-start.21
  8.8 0.7 copy-start.16
  9.4 0.9 copy-start.17
  10.3 10.9 %copy-start = (bf16[6912,256]{1,0:T(8,128)(2,1)S(1)}, bf16[6912,256]{1,0:T(8,128)(2,1)}, u32[]{:S(2)}) copy-start(bf16[6912,256]{1,0:T(8,128)(2,1)} %refs_7_.3) | copy-start | bytes 10616836
  13.5 1.0 %copy-start.1 = (bf16[16,64,512]{2,1,0:T(8,128)(2,1)}, bf16[16,64,512]{2,1,0:T(8,128)(2,1)S(1)}, u32[]{:S(2)}) copy-start(bf16[16,64,512]{2,1,0:T(8,128)(2,1)S(1)} %get-tuple-element.58) | copy-start | bytes 3145732
  14.5 9.2 %collective-permute-start.3 = (bf16[16,64,512]{2,1,0:T(8,128)(2,1)}, bf16[16,64,512]{2,1,0:T(8,128)(2,1)}, u32[]{:S(2)}, u32[]{:S(2)}) collective-permute-start(bf16[16,64,512]{2,1,0:T(8,128)(2,1)} %get-tuple-element.50), channel_id=1, source_target_pairs={{0,1},{1,0},{2,3},{3,2},{4,5},{5,4},{6,7},{7,6},{8,9},{9,8},{10,11... | collective-permute-start | bytes 3145736 | tf_op jit(solution)/shard_map/ppermute | solution.py:261
  17.1 6.3 %collective-permute-start.1 = (bf16[256,256]{1,0:T(8,128)(2,1)}, bf16[256,256]{1,0:T(8,128)(2,1)}, u32[]{:S(2)}, u32[]{:S(2)}) collective-permute-start(bf16[256,256]{1,0:T(8,128)(2,1)} %get-tuple-element.45.refs_5_), channel_id=1, source_target_pairs={{0,1},{1,2},{2,3},{3,4},{4,5},{5,6},{6,7},{7,8},{8,9},{9,10},{10,1... | collective-permute-start | bytes 393224 | tf_op jit(solution)/shard_map/ppermute | solution.py:261
  19.7 4.0 %collective-permute-start.2 = (bf16[256,256]{1,0:T(8,128)(2,1)}, bf16[256,256]{1,0:T(8,128)(2,1)}, u32[]{:S(2)}, u32[]{:S(2)}) collective-permute-start(bf16[256,256]{1,0:T(8,128)(2,1)} %get-tuple-element.46.refs_4_), channel_id=1, source_target_pairs={{1,0},{2,1},{3,2},{4,3},{5,4},{6,5},{7,6},{8,7},{9,8},{10,9},{11,1... | collective-permute-start | bytes 393224 | tf_op jit(solution)/shard_map/ppermute | solution.py:261
  21.2 2.5 %copy-start.2 = (bf16[16,64,512]{2,1,0:T(8,128)(2,1)S(1)}, bf16[16,64,512]{2,1,0:T(8,128)(2,1)}, u32[]{:S(2)}) copy-start(bf16[16,64,512]{2,1,0:T(8,128)(2,1)} %copy-done.1) | copy-start | bytes 3145732
  21.2 1.0 %copy-start.8 = (bf16[512,256]{1,0:T(8,128)(2,1)S(1)}, bf16[512,256]{1,0:T(8,128)(2,1)}, u32[]{:S(2)}) copy-start(bf16[512,256]{1,0:T(8,128)(2,1)} %refs_9_.1) | copy-start | bytes 786436
  22.2 0.9 copy-start.12
  26.5 3.7 %copy-start.18 = (s32[1,27,8]{1,2,0:T(8,128)S(1)}, s32[1,27,8]{1,2,0:T(8,128)}, u32[]{:S(2)}) copy-start(s32[1,27,8]{1,2,0:T(8,128)} %param.15) | copy-start | bytes 2596
  26.5 3.7 %copy-start.19 = (s32[1,27,8]{1,2,0:T(8,128)S(1)}, s32[1,27,8]{1,2,0:T(8,128)}, u32[]{:S(2)}) copy-start(s32[1,27,8]{1,2,0:T(8,128)} %param.16) | copy-start | bytes 2596
  26.8 12.9 %collective-permute-start.4 = (bf16[4,2,64,512]{3,2,0,1:T(8,128)(2,1)S(1)}, bf16[4,2,64,512]{3,2,0,1:T(8,128)(2,1)}, u32[]{:S(2)}, u32[]{:S(2)}) collective-permute-start(bf16[4,2,64,512]{3,2,0,1:T(8,128)(2,1)S(1)} %add_convert_fusion), channel_id=1, source_target_pairs={{0,2},{1,5},{2,0},{3,7},{4,6},{5,1},{6,4},{7,3},{8,10},{9,13},{10,... | collective-permute-start | bytes 1572872 | tf_op jit(solution)/shard_map/ppermute | solution.py:261
  36.7 0.9 copy-start.5
  37.6 0.8 copy-start.10
  39.7 11.6 %collective-permute-start.5 = (bf16[8,216,256]{2,1,0:T(8,128)(2,1)}, bf16[8,216,256]{2,1,0:T(8,128)(2,1)}, u32[]{:S(2)}, u32[]{:S(2)}) collective-permute-start(bf16[8,216,256]{2,1,0:T(8,128)(2,1)} %get-tuple-element.65), channel_id=1, source_target_pairs={{0,1},{1,0},{2,3},{3,2},{4,5},{5,4},{6,7},{7,6},{8,9},{9,8},{10,11... | collective-permute-start | bytes 2654216 | tf_op jit(solution)/shard_map/ppermute | solution.py:261
  41.2 3.0 %copy-start.9 = (bf16[512,256]{1,0:T(8,128)(2,1)S(1)}, bf16[512,256]{1,0:T(8,128)(2,1)}, u32[]{:S(2)}) copy-start(bf16[512,256]{1,0:T(8,128)(2,1)} %refs_9_.1) | copy-start | bytes 786436
  41.2 3.0 %copy-start.11 = (f32[512,256]{1,0:T(8,128)S(1)}, f32[512,256]{1,0:T(8,128)}, u32[]{:S(2)}) copy-start(f32[512,256]{1,0:T(8,128)} %copy-done.10) | copy-start | bytes 1572868
  41.2 3.0 %copy-start.13 = (s32[1,27,8,128]{3,2,1,0:T(8,128)S(1)}, s32[1,27,8,128]{3,2,1,0:T(8,128)}, u32[]{:S(2)}) copy-start(s32[1,27,8,128]{3,2,1,0:T(8,128)} %param.17) | copy-start | bytes 331780
  43.5 10.3 %copy-start.6 = (bf16[8,216,256]{2,1,0:T(8,128)(2,1)S(1)}, bf16[8,216,256]{2,1,0:T(8,128)(2,1)}, u32[]{:S(2)}) copy-start(bf16[8,216,256]{2,1,0:T(8,128)(2,1)} %copy-done.5) | copy-start | bytes 2654212
  43.6 7.7 %collective-permute-start.6 = (bf16[4,64,512]{2,1,0:T(8,128)(2,1)S(1)}, bf16[4,64,512]{2,1,0:T(8,128)(2,1)S(1)}, u32[]{:S(2)}, u32[]{:S(2)}) collective-permute-start(bf16[4,64,512]{2,1,0:T(8,128)(2,1)S(1)} %get-tuple-element.77), channel_id=1, source_target_pairs={{0,4},{1,3},{2,6},{3,1},{4,0},{5,7},{6,2},{7,5},{8,12},{9,11},{10,... | collective-permute-start | bytes 786440 | tf_op jit(solution)/shard_map/ppermute | solution.py:261
  51.3 5.3 %copy-start.3 = (bf16[8,216,256]{2,1,0:T(8,128)(2,1)}, bf16[8,216,256]{2,1,0:T(8,128)(2,1)S(1)}, u32[]{:S(2)}) copy-start(bf16[8,216,256]{2,1,0:T(8,128)(2,1)S(1)} %get-tuple-element.71) | copy-start | bytes 2654212
  51.3 4.6 %copy-start.23 = (bf16[4,64,512]{2,1,0:T(8,128)(2,1)}, bf16[4,64,512]{2,1,0:T(8,128)(2,1)S(1)}, u32[]{:S(2)}) copy-start(bf16[4,64,512]{2,1,0:T(8,128)(2,1)S(1)} %collective-permute-done.6) | copy-start | bytes 786436
  51.3 13.1 %collective-permute-start.8 = (bf16[8,216,256]{2,1,0:T(8,128)(2,1)S(1)}, bf16[8,216,256]{2,1,0:T(8,128)(2,1)S(1)}, u32[]{:S(2)}, u32[]{:S(2)}) collective-permute-start(bf16[8,216,256]{2,1,0:T(8,128)(2,1)S(1)} %get-tuple-element.72), channel_id=1, source_target_pairs={{0,1},{1,0},{2,3},{3,2},{4,5},{5,4},{6,7},{7,6},{8,9},{9,8},{10,11... | collective-permute-start | bytes 2654216 | tf_op jit(solution)/shard_map/ppermute | solution.py:261
  55.9 8.4 %collective-permute-start.7 = (bf16[2,2,216,256]{3,2,1,0:T(8,128)(2,1)S(1)}, bf16[2,2,216,256]{3,2,1,0:T(8,128)(2,1)S(1)}, u32[]{:S(2)}, u32[]{:S(2)}) collective-permute-start(bf16[2,2,216,256]{3,2,1,0:T(8,128)(2,1)S(1)} %get-tuple-element.75), channel_id=1, source_target_pairs={{0,4},{1,3},{2,6},{3,1},{4,0},{5,7},{6,2},{7,5},{8,12},{9,11},{10,... | collective-permute-start | bytes 1327112 | tf_op jit(solution)/shard_map/ppermute | solution.py:261
  64.4 2.5 %copy-start.22 = (f32[4,64,512]{2,1,0:T(8,128)S(1)}, f32[4,64,512]{2,1,0:T(8,128)}, u32[]{:S(2)}) copy-start(f32[4,64,512]{2,1,0:T(8,128)} %get-tuple-element.73) | copy-start | bytes 1572868
  64.5 5.1 %copy-start.4 = (bf16[8,216,256]{2,1,0:T(8,128)(2,1)S(1)}, bf16[8,216,256]{2,1,0:T(8,128)(2,1)}, u32[]{:S(2)}) copy-start(bf16[8,216,256]{2,1,0:T(8,128)(2,1)} %copy-done.3) | copy-start | bytes 2654212
  65.7 10.9 %collective-permute-start.9 = (bf16[6,216,256]{2,1,0:T(8,128)(2,1)}, bf16[6,216,256]{2,1,0:T(8,128)(2,1)S(1)}, u32[]{:S(2)}, u32[]{:S(2)}) collective-permute-start(bf16[6,216,256]{2,1,0:T(8,128)(2,1)} %pad_maximum_fusion), channel_id=1, source_target_pairs={{0,2},{1,5},{2,0},{3,7},{4,6},{5,1},{6,4},{7,3},{8,10},{9,13},{10,... | collective-permute-start | bytes 1990664 | tf_op jit(solution)/shard_map/ppermute | solution.py:261
  68.0 9.5 %collective-permute-start.15 = (bf16[2,64,512]{2,1,0:T(8,128)(2,1)S(1)}, bf16[2,64,512]{2,1,0:T(8,128)(2,1)S(1)}, u32[]{:S(2)}, u32[]{:S(2)}) collective-permute-start(bf16[2,64,512]{2,1,0:T(8,128)(2,1)S(1)} %get-tuple-element.91), channel_id=1, source_target_pairs={{0,8},{1,9},{2,10},{3,11},{4,12},{5,13},{6,14},{7,15},{8,0},{9,1},... | collective-permute-start | bytes 393224 | tf_op jit(solution)/shard_map/ppermute | solution.py:261
  76.8 6.0 %collective-permute-start.12 = (bf16[2,216,256]{2,1,0:T(8,128)(2,1)S(1)}, bf16[2,216,256]{2,1,0:T(8,128)(2,1)S(1)}, u32[]{:S(2)}, u32[]{:S(2)}) collective-permute-start(bf16[2,216,256]{2,1,0:T(8,128)(2,1)S(1)} %get-tuple-element.81), channel_id=1, source_target_pairs={{0,4},{1,3},{2,6},{3,1},{4,0},{5,7},{6,2},{7,5},{8,12},{9,11},{10,... | collective-permute-start | bytes 663560 | tf_op jit(solution)/shard_map/ppermute | solution.py:261
  77.5 15.0 %collective-permute-start.16 = (bf16[64,512]{1,0:T(8,128)(2,1)S(1)}, bf16[64,512]{1,0:T(8,128)(2,1)S(1)}, u32[]{:S(2)}, u32[]{:S(2)}) collective-permute-start(bf16[64,512]{1,0:T(8,128)(2,1)S(1)} %fusion.10), channel_id=1, source_target_pairs={{0,16},{1,17},{2,18},{3,19},{4,20},{5,21},{6,22},{7,23},{8,24},{9,... | collective-permute-start | bytes 196616 | tf_op jit(solution)/shard_map/ppermute | solution.py:261
  80.2 5.5 %collective-permute-start.10 = (bf16[216,256]{1,0:T(8,128)(2,1)S(1)}, bf16[216,256]{1,0:T(8,128)(2,1)S(1)}, u32[]{:S(2)}, u32[]{:S(2)}) collective-permute-start(bf16[216,256]{1,0:T(8,128)(2,1)S(1)} %fusion.8), channel_id=1, source_target_pairs={{0,8},{1,9},{2,10},{3,11},{4,12},{5,13},{6,14},{7,15},{8,0},{9,1},... | collective-permute-start | bytes 331784 | tf_op jit(solution)/shard_map/ppermute | solution.py:261
  82.8 4.8 %collective-permute-start.13 = (bf16[216,256]{1,0:T(8,128)(2,1)S(1)}, bf16[216,256]{1,0:T(8,128)(2,1)S(1)}, u32[]{:S(2)}, u32[]{:S(2)}) collective-permute-start(bf16[216,256]{1,0:T(8,128)(2,1)S(1)} %fusion.9), channel_id=1, source_target_pairs={{0,8},{1,9},{2,10},{3,11},{4,12},{5,13},{6,14},{7,15},{8,0},{9,1},... | collective-permute-start | bytes 331784 | tf_op jit(solution)/shard_map/ppermute | solution.py:261
  85.7 8.2 %collective-permute-start.11 = (bf16[216,256]{1,0:T(8,128)(2,1)S(1)}, bf16[216,256]{1,0:T(8,128)(2,1)S(1)}, u32[]{:S(2)}, u32[]{:S(2)}) collective-permute-start(bf16[216,256]{1,0:T(8,128)(2,1)S(1)} %fusion.11), channel_id=1, source_target_pairs={{8,24},{9,25},{10,26},{11,27},{12,28},{13,29},{14,30},{15,31},{16,... | collective-permute-start | bytes 331784 | tf_op jit(solution)/shard_map/ppermute | solution.py:261
  87.7 7.1 %collective-permute-start.14 = (bf16[216,256]{1,0:T(8,128)(2,1)S(1)}, bf16[216,256]{1,0:T(8,128)(2,1)S(1)}, u32[]{:S(2)}, u32[]{:S(2)}) collective-permute-start(bf16[216,256]{1,0:T(8,128)(2,1)S(1)} %fusion.12), channel_id=1, source_target_pairs={{0,16},{1,17},{2,18},{3,19},{4,20},{5,21},{6,22},{7,23},{24,8},{25... | collective-permute-start | bytes 331784 | tf_op jit(solution)/shard_map/ppermute | solution.py:261

commit v7 on v6

--- a/solution.py
+++ b/solution.py
@@ -35,19 +35,38 @@
     return cuts
 
 
-def place(both, value, first, core):
-    for at, number, inside, rows in segments(first, value.shape[0], both.shape[2]):
-        both[(number % 2) ^ core, number // 2, pl.ds(inside, rows), :] = value[at : at + rows]
+def low_order(bits):
+    return [[(j + core * (bits // 2)) % bits for j in range(bits)] for core in range(2)]
+
+
+def position(number, me, bits, quarters):
+    part, low = divmod(number, 2 << bits)
+    core = low % 2
+    at = core ^ (me & 1)
+    for bit in low_order(bits)[core]:
+        at = at * 2 + ((low >> (1 + bit) & 1) ^ (me >> (1 + bit) & 1))
+    z = me >> (1 + bits)
+    if len(quarters) == 4:
+        at = at * 2 + ((part & 1) ^ (z & 1))
+        return at * 2 + ((part >> 1) ^ (z >> 1))
+    return at * 2 + (part ^ (z & 1) ^ (quarters[0] & 1))
+
+
+def place(both, value, first, me, bits, quarters):
+    for at, number, inside, rows in segments(first, value.shape[0], both.shape[1]):
+        both[position(number, me, bits, quarters), pl.ds(inside, rows), :] = value[at : at + rows]
 
 
 def halves(total, shard):
-    shape = (total[0] // (2 * shard), shard, total[1])
-    return (jax.ShapeDtypeStruct(shape, BF),) * 2, pltpu.VMEM((2,) + shape, F32)
+    count = total[0] // shard
+    half = jax.ShapeDtypeStruct((count // 2, shard, total[1]), BF)
+    return (half, half), pltpu.VMEM((count, shard, total[1]), F32)
 
 
 def part(both, keep, send):
-    keep[...] = both[0].astype(BF)
-    send[...] = both[1].astype(BF)
+    half = keep.shape[0]
+    keep[...] = both[:half].astype(BF)
+    send[...] = both[half:].astype(BF)
 
 
 def identity(size):
@@ -104,7 +123,7 @@
 
 
 def down_kernel(
-    core, prev, act, pick, parent_pick, chosen, w, cur, head, tail, keep, send, both, gath, contrib
+    bits, me, prev, act, pick, parent_pick, chosen, w, cur, head, tail, keep, send, both, gath, contrib
 ):
     count, channels = act.shape
     children = w.shape[0] // channels
@@ -121,18 +140,19 @@
     head[...] = masked[:halo]
     tail[...] = masked[count - halo :]
     for c in range(children):
-        place(both, dot(chosen[:, own[c]], gath[own[c], :]), c * channels, core[0])
+        value = dot(chosen[:, own[c]], gath[own[c], :])
+        place(both, value, c * channels, me[0], bits, range(4))
     part(both, keep, send)
 
 
-def down(core, prev, prepared, halo, shard):
+def down(bits, me, prev, prepared, halo, shard):
     act, pick, parent_pick, chosen, w, cur = prepared
     channels = act.shape[1]
     listed, width = pick.shape[1], cur.shape[1]
     kinds, both = halves(w.shape, shard)
     side = jax.ShapeDtypeStruct((halo, channels), BF)
     return pl.pallas_call(
-        down_kernel,
+        functools.partial(down_kernel, bits),
         out_shape=(side, side) + kinds,
         in_specs=[SMEM] + [VMEM] * 7,
         out_specs=(VMEM,) * 4,
@@ -144,7 +164,7 @@
         compiler_params=pltpu.CompilerParams(vmem_limit_bytes=20 << 20),
         cost_estimate=SMALL,
         name="down",
-    )(core, prev, *prepared)
+    )(me, prev, *prepared)
 
 
 def conv_plan(kernel, channels, quarters):
@@ -181,8 +201,8 @@
     )(pairs, feats, w)
 
 
-def conv_kernel(plan, begun, *refs):
-    core, src, tgt, before, head, tail, after, w, *rest = refs
+def conv_kernel(plan, bits, quarters, begun, *refs):
+    me, src, tgt, before, head, tail, after, w, *rest = refs
     if begun:
         pairs, feats, partial, grad, keep, send, both, ext, acc, col0, col1, tab, feats_t = rest
         turn_kernel(pairs, feats, w, tab, feats_t)
@@ -216,14 +236,15 @@
         if at + 1 < len(plan):
             gather(plan[at + 1][0], cols[(at + 1) % 2])
         column = cols[at % 2][...].reshape(count, channels)
-        place(both, dot(feats_t[pl.ds(first, last - first), :], column), out, core[0])
+        value = dot(feats_t[pl.ds(first, last - first), :], column)
+        place(both, value, out, me[0], bits, quarters)
         if first == 0:
             acc[...] += dot_nt(column, w[pl.ds(k * channels, channels), :])
     grad[...] = acc[...].astype(grad.dtype)
     part(both, keep, send)
 
 
-def conv(core, src, tgt, sides, w, tables, quarters, shard, partial):
+def conv(bits, me, src, tgt, sides, w, tables, quarters, shard, partial):
     begun = partial is not None
     shapes = [x.shape if begun else x.shape[::-1] for x in tables]
     (listed, rows), (count, channels) = shapes
@@ -232,9 +253,11 @@
     ext_rows = sum(side.shape[0] for side in sides)
     block = (rows, channels)
     grad = jax.ShapeDtypeStruct((count, channels), BF if begun else F32)
-    operands = (core, src, tgt, *sides, w, *tables) + ((partial,) if begun else ())
+    operands = (me, src, tgt, *sides, w, *tables) + ((partial,) if begun else ())
     return pl.pallas_call(
-        functools.partial(conv_kernel, conv_plan(kernel, channels, quarters), begun),
+        functools.partial(
+            conv_kernel, conv_plan(kernel, channels, quarters), bits, quarters, begun
+        ),
         out_shape=(grad,) + kinds,
         in_specs=[SMEM] * 3 + [VMEM] * (len(operands) - 3),
         out_specs=(VMEM,) * 3,
@@ -261,58 +284,10 @@
     return lax.ppermute(x, "space", [(i, j) for i, j in pairs if j is not None and 0 <= j < peers])
 
 
-def moved_together(x, to_x, y, to_y, peers):
-    if any(to_x(i) != to_y(i) for i in range(peers)):
-        return moved(x, peers, to_x), moved(y, peers, to_y)
-    rows = x.shape[-2:]
-    flat = [z.reshape((-1,) + rows) for z in (x, y)]
-    got = moved(jnp.concatenate(flat, 0), peers, to_x)
-    cut = flat[0].shape[0]
-    return got[:cut].reshape(x.shape), got[cut:].reshape(y.shape)
-
-
-def taken(x, axis, digit):
-    return lax.dynamic_index_in_dim(x, digit, axis=axis, keepdims=False)
-
-
-def low_steps(bits):
-    left = [list(range(bits - 1, -1, -1)) for core in range(2)]
-    steps = []
-    for j in range(bits):
-        by = (j, (j + bits // 2) % bits)
-        steps.append((by, [left[core].index(by[core]) for core in range(2)]))
-        for core in range(2):
-            left[core].remove(by[core])
-    return steps
-
-
-def fold_low(parts, me, step):
-    core = me % 2
-    by, axes = step
-    bit = jnp.where(core == 0, me >> (1 + by[0]), me >> (1 + by[1])) % 2
-
-    def half(x, digit):
-        if axes[0] == axes[1]:
-            return taken(x, 1 + axes[0], digit)
-        return jnp.where(core == 0, taken(x, 1 + axes[0], digit), taken(x, 1 + axes[1], digit))
-
-    def piece(digit):
-        pieces = [half(kept, digit).astype(F32) + half(got, digit).astype(F32) for kept, got in parts]
-        return jnp.concatenate(pieces, 0) if len(pieces) > 1 else pieces[0]
-
-    return piece(bit), piece(1 - bit).astype(BF), lambda i: i ^ (2 << by[i % 2])
-
-
-def fold_bit(keep, got, me, peers, stride, first):
-    bit = me // stride % 2
-    axis = keep.ndim - 3
-
-    def piece(digit):
-        return taken(keep, axis, digit) + taken(got, axis, digit).astype(F32)
-
-    mine = bit ^ first
-    sent = piece(1 - mine).astype(BF)
-    return piece(mine), moved(sent, peers, lambda i: i ^ stride)
+def fold(kept, got):
+    half = kept.shape[0] // 2
+    total = kept.astype(F32) + got.astype(F32)
+    return total[:half], total[half:].astype(BF)
 
 
 def per_device(
@@ -336,20 +311,30 @@
     children = down_rows.shape[1]
     scale = 1.0 / math.sqrt(peers * row_count)
     bits = (peers // 8).bit_length() - 1
-    steps = low_steps(bits)
     near, far = peers // 4, peers // 2
 
     halo = HB * block_rows
-    core = (me % 2).reshape(1)
+    ident = me.reshape(1)
     pinned = lax.optimization_barrier
-    other_way = [((b, a), [y, x]) for (a, b), (x, y) in steps]
+    low_bits = list(zip(*low_order(bits)))
 
     def across(x):
         return moved(x, peers, lambda i: i ^ 1)
 
-    def spread(kept, got, high):
-        shape = (high,) + (2,) * bits + got.shape[-2:]
-        return kept.reshape(shape), got.reshape(shape)
+    def xy(x, step):
+        return moved(x, peers, lambda i: i ^ (2 << low_bits[step][i % 2]))
+
+    def z_near(x):
+        return moved(x, peers, lambda i: i ^ near)
+
+    def z_far(x, wanted=(0, 1, 2, 3)):
+        return moved(x, peers, lambda i: i ^ far if (i ^ far) // near in wanted else None)
+
+    def middle(kept, got):
+        kept, send = fold(kept, got)
+        for step in range(1, bits - 1):
+            kept, send = fold(kept, xy(send, step))
+        return kept, send
 
     previous = moved(coarse_grad[-block_rows:], peers, lambda i: i + 1)
     prepared = prep(
@@ -361,7 +346,7 @@
         block_rows + coarse_grad.shape[0],
     )
     head, tail, low, low_send = down(
-        core, previous, prepared, halo, children * channels // peers
+        bits, ident, previous, prepared, halo, children * channels // peers
     )
 
     before = moved(tail, peers, lambda i: i + 1)
@@ -375,51 +360,52 @@
 
     def quarters(numbers, tables, partial=None):
         src, tgt = pair_src[0].T, pair_tgt[0].T
-        return conv(core, src, tgt, sides, w_sub, tables, numbers, shard, partial)
-
-    low, low_send, to = fold_low([spread(low, low_got, 4)], me, steps[0])
-    low_got = moved(low_send, peers, to)
+        return conv(bits, ident, src, tgt, sides, w_sub, tables, numbers, shard, partial)
+
+    low, low_send = fold(low, low_got)
+    low_got = xy(low_send, 0)
     partial, outer, outer_send = quarters((0, 3), tables)
     partial, outer, outer_send, low, low_got = pinned((partial, outer, outer_send, low, low_got))
 
     outer_got = across(outer_send)
-    for step in steps[1:]:
-        low, low_send, to = fold_low([(low, low_got)], me, step)
-        low_got = moved(low_send, peers, to)
+    low, low_send = middle(low, low_got)
+    low_got = xy(low_send, bits - 1)
+    outer, outer_send = fold(outer, outer_got)
+    partial, outer_send = pinned((partial, outer_send))
+    outer_got = xy(outer_send, 0)
     grad_in, inner, inner_send = quarters((1, 2), (pairs, feats), partial)
     grad_in, inner, inner_send, outer, outer_got, low, low_got = pinned(
         (grad_in, inner, inner_send, outer, outer_got, low, low_got)
     )
 
     inner_got = across(inner_send)
-    outer, outer_send, outer_to = fold_low([spread(outer, outer_got, 2)], me, other_way[0])
-    for step in other_way[1:]:
-        outer_got = moved(outer_send, peers, outer_to)
-        outer, outer_send, outer_to = fold_low([(outer, outer_got)], me, step)
-    low, low_got = (x.reshape((2, 2) + x.shape[-2:]) for x in (low, low_got))
-    low, low_got = fold_bit(low, low_got, me, peers, near, 0)
-
-    inner, inner_send, inner_to = fold_low([spread(inner, inner_got, 2)], me, steps[0])
-    outer_got, inner_got = moved_together(outer_send, outer_to, inner_send, inner_to, peers)
-    low, low_got = fold_bit(low, low_got, me, peers, far, 0)
-
-    for step in steps[1:]:
-        inner, inner_send, to = fold_low([(inner, inner_got)], me, step)
-        inner_got = moved(inner_send, peers, to)
-    outer, outer_got = fold_bit(outer, outer_got, me, peers, near, 0)
-    inner, inner_got = fold_bit(inner, inner_got, me, peers, near, 1)
+    outer, outer_send = middle(outer, outer_got)
+    outer_got = xy(outer_send, bits - 1)
+    low, low_send = fold(low, low_got)
+    low_got = z_near(low_send)
+    inner, inner_send = fold(inner, inner_got)
+    inner_got = xy(inner_send, 0)
+
+    outer, outer_send = fold(outer, outer_got)
+    outer_got = z_near(outer_send)
+    low, low_send = fold(low, low_got)
+    low_got = z_far(low_send)
+    inner, inner_send = middle(inner, inner_got)
+    inner_got = xy(inner_send, bits - 1)
+
+    inner, inner_send = fold(inner, inner_got)
+    inner_got = z_near(inner_send)
 
     def last_step(kept, got, wanted):
         total = kept + got.astype(F32)
-        to = lambda i: i ^ far if (i ^ far) // near in wanted else None
-        return total + moved(total.astype(BF), peers, to).astype(F32)
+        return total + z_far(total.astype(BF), wanted).astype(F32)
 
     digit = me // near
     is_outer = (digit == 0) | (digit == 3)
     outer_sum = last_step(outer, outer_got, (0, 3))
     inner_sum = last_step(inner, inner_got, (1, 2))
     sub_sum = jnp.where(is_outer, outer_sum, inner_sum)
-    low_sum = low + low_got.astype(F32)
+    low_sum = (low + low_got.astype(F32)).reshape(-1, out_width)
     return (grad_in, sub_sum.reshape(-1) * scale, low_sum * scale)
 
 

time: 96.3 us -> 80.6 us (0.84)
  local copies, waits for them, and re-layouts: 14.8 us -> 7.65 us
  other arithmetic: 9.72 us -> 3.12 us
  Pallas kernels: 18 us -> 15.5 us
  starting transfers between devices: 32.1 us -> 33.4 us
    convert_element_type x11 -> x2, other arithmetic: 6.41 us -> 0.05 us  [last_step(): return total + z_far(total.astype(BF), wanted).astype(F32)]
    unnamed x49 -> x33, local copies, waits for them, and re-layouts: 11.8 us -> 6.52 us
    dynamic_slice x6 -> x0, local copies, waits for them, and re-layouts: 2.9 us -> none  [taken(): return lax.dynamic_index_in_dim(x, digit, axis=axis, keepdims=False)]
    pallas_call x2, Pallas kernels: 13.6 us -> 12.1 us  [conv(): pl.pallas_call(functools.partial(conv_kernel, conv_plan(kernel, channels,...]
    ppermute x17 -> x18, starting transfers between devices: 32.1 us -> 33.4 us  [moved(): lax.ppermute(x, 'space', [(i, j) for i, j in pairs if j is not None and 0...]
    slice x2 -> x15, local copies, waits for them, and re-layouts: 0.04 us -> 1.12 us  [fold(): return (total[:half], total[half:].astype(BF))]
    add x3 -> x10, other arithmetic: 1.59 us -> 2.3 us  [fold(): total = kept.astype(F32) + got.astype(F32)]
    ppermute x17 -> x18, waiting for transfers between devices: 20.1 us -> 19.6 us  [moved(): lax.ppermute(x, 'space', [(i, j) for i, j in pairs if j is not None and 0...]
  transfers between devices with their start and end apart: 17 -> 18, of which waited for: 8 -> 8; matrix products, arithmetic and copies ran while one was open for 9% -> 4% of each run, Pallas kernels for 15% -> 17%
where the time goes in v7:
time: 80.6 us; the launch traced here: 80.2 us
  starting transfers between devices  33.4 us (41%)
  waiting for transfers between devices  19.6 us (24%)
  Pallas kernels  15.5 us (19%)
  local copies, waits for them, and re-layouts  7.65 us (9%)
  other arithmetic  3.12 us (4%)
  between operations  1.01 us (1%)
    ppermute x18, starting transfers between devices, moved(): lax.ppermute(x, 'space', [(i, j) for i, j in pairs if j is not None and 0...  33.4 us
    ppermute x18, waiting for transfers between devices, moved(): lax.ppermute(x, 'space', [(i, j) for i, j in pairs if j is not None and 0...  19.6 us
    pallas_call x2, Pallas kernels, conv(): pl.pallas_call(functools.partial(conv_kernel, conv_plan(kernel, channels,...  12.1 us
    unnamed x33, local copies, waits for them, and re-layouts  6.52 us
    add x10, other arithmetic, fold(): total = kept.astype(F32) + got.astype(F32)  2.3 us
    pallas_call x1, Pallas kernels, down(): pl.pallas_call(functools.partial(down_kernel, bits), out_shape=(side, sid...  2.26 us
  transfers between devices with their start and end apart: 18, of which 8 were waited for; matrix products, arithmetic and copies ran while one was open for 4% of the time, Pallas kernels for 17%

profile of v7, /device:TPU:0, one launch (start us, length us, event | category | flops | bytes accessed | tf_op | source)
XLA Modules:
  0.0 80.2 jit_solution(14985741127921612359)
XLA Ops:
  0.6 2.4 %collective-permute-start = (bf16[128,512]{1,0:T(8,128)(2,1)}, bf16[128,512]{1,0:T(8,128)(2,1)S(1)}, u32[]{:S(2)}, u32[]{:S(2)}) collective-permute-start(bf16[128,512]{1,0:T(8,128)(2,1)} %cur_in.1), channel_id=1, source_target_pairs={{0,1},{1,2},{2,3},{3,4},{4,5},{5,6},{6,7},{7,8},{8,9},{9,10},{10,1... | collective-permute-start | bytes 393224 | tf_op jit(solution)/shard_map/ppermute | solution.py:284
  3.0 1.6 %copy-done.1 = bf16[2048,512]{1,0:T(8,128)(2,1)S(1)} copy-done((bf16[2048,512]{1,0:T(8,128)(2,1)S(1)}, bf16[2048,512]{1,0:T(8,128)(2,1)}, u32[]{:S(2)}) %copy-start.1) | copy-done | bytes 2097176
  4.6 0.9 %copy-done.4 = bf16[512,256]{1,0:T(8,128)(2,1)S(1)} copy-done((bf16[512,256]{1,0:T(8,128)(2,1)S(1)}, bf16[512,256]{1,0:T(8,128)(2,1)}, u32[]{:S(2)}) %copy-start.4) | copy-done | bytes 262168
  5.6 0.9 %copy-done.5 = bf16[128,512]{1,0:T(8,128)(2,1)S(1)} copy-done((bf16[128,512]{1,0:T(8,128)(2,1)S(1)}, bf16[128,512]{1,0:T(8,128)(2,1)}, u32[]{:S(2)}) %copy-start.5) | copy-done | bytes 131096
  6.5 0.7 copy-done.8
  7.1 0.7 copy-done.9
  7.8 0.9 %prep.1 = (bf16[512,256]{1,0:T(8,128)(2,1)S(1)}, bf16[512,1024]{1,0:T(8,128)(2,1)S(1)}, bf16[1024,256]{1,0:T(8,128)(2,1)S(1)}, bf16[256,1024]{1,0:T(8,128)(2,1)S...) custom-call(bf16[512,256]{1,0:T(8,128)(2,1)S(1)} %copy-done.4, s32[8,128]{1,0:T(8,128)S(1)} %bitcast.21, ...), custom_call_target="tpu_custom_call" | custom-call | flops 1048576 | bytes 1024 | tf_op jit(solution)/shard_map/prep/pallas_call | solution.py:114
  8.7 0.0 collective-permute-done.prev
  8.7 0.0 copy-start
  8.8 0.0 copy-start.2
  8.8 0.0 copy-start.3
  8.8 2.3 %down.1 = (bf16[256,256]{1,0:T(8,128)(2,1)S(1)}, bf16[256,256]{1,0:T(8,128)(2,1)S(1)}, bf16[16,64,512]{2,1,0:T(8,128)(2,1)S(1)}, bf16[16,64,512]{2,1,0:T(8,128)(2,1)S(1)}) custom-call(s32[1]{0:T(128)} %bitcast.me.refs_0_, bf16[128,512]{1,0:T(8,128)(2,1)S(1)} %collective-permute-done.prev, bf16[512,256]{1,0:T(8,128)(2,1)S(1)} %get-tuple-element.41.act, ...), custom_call_target="tpu_custom_call" | custom-call | flops 1048576 | bytes 1024 | tf_op jit(solution)/shard_map/down/pallas_call | solution.py:154
  11.1 2.7 %collective-permute-start.3 = (bf16[16,64,512]{2,1,0:T(8,128)(2,1)S(1)}, bf16[16,64,512]{2,1,0:T(8,128)(2,1)S(1)}, u32[]{:S(2)}, u32[]{:S(2)}) collective-permute-start(bf16[16,64,512]{2,1,0:T(8,128)(2,1)S(1)} %get-tuple-element.52), channel_id=1, source_target_pairs={{0,1},{1,0},{2,3},{3,2},{4,5},{5,4},{6,7},{7,6},{8,9},{9,8},{10,11... | collective-permute-start | bytes 3145736 | tf_op jit(solution)/shard_map/ppermute | solution.py:284
  13.7 1.9 %collective-permute-start.1 = (bf16[256,256]{1,0:T(8,128)(2,1)S(1)}, bf16[256,256]{1,0:T(8,128)(2,1)S(1)}, u32[]{:S(2)}, u32[]{:S(2)}) collective-permute-start(bf16[256,256]{1,0:T(8,128)(2,1)S(1)} %get-tuple-element.47.refs_5_), channel_id=1, source_target_pairs={{0,1},{1,2},{2,3},{3,4},{4,5},{5,6},{6,7},{7,8},{8,9},{9,10},{10,1... | collective-permute-start | bytes 393224 | tf_op jit(solution)/shard_map/ppermute | solution.py:284
  15.6 1.5 %collective-permute-start.2 = (bf16[256,256]{1,0:T(8,128)(2,1)S(1)}, bf16[256,256]{1,0:T(8,128)(2,1)S(1)}, u32[]{:S(2)}, u32[]{:S(2)}) collective-permute-start(bf16[256,256]{1,0:T(8,128)(2,1)S(1)} %get-tuple-element.48.refs_4_), channel_id=1, source_target_pairs={{1,0},{2,1},{3,2},{4,3},{5,4},{6,5},{7,6},{8,7},{9,8},{10,9},{11,1... | collective-permute-start | bytes 393224 | tf_op jit(solution)/shard_map/ppermute | solution.py:284
  17.2 0.3 turn.1
  17.5 2.5 %collective-permute-done.2.refs_6_ = bf16[256,256]{1,0:T(8,128)(2,1)S(1)} collective-permute-done((bf16[256,256]{1,0:T(8,128)(2,1)S(1)}, bf16[256,256]{1,0:T(8,128)(2,1)S(1)}, u32[]{:S(2)}, u32[]{:S(2)}) %collective-permute-start.2) | collective-permute-done | bytes 131104 | tf_op jit(solution)/shard_map/ppermute | solution.py:284
  20.0 0.0 collective-permute-done.3
  20.0 0.3 convert_add_fusion
  20.3 0.0 copy-start.6
  20.3 0.0 copy-start.7
  20.4 0.1 slice.139
  20.4 3.4 %collective-permute-start.4 = (bf16[8,64,512]{2,1,0:T(8,128)(2,1)S(1)}, bf16[8,64,512]{2,1,0:T(8,128)(2,1)S(1)}, u32[]{:S(2)}, u32[]{:S(2)}) collective-permute-start(bf16[8,64,512]{2,1,0:T(8,128)(2,1)S(1)} %slice.139), channel_id=1, source_target_pairs={{0,2},{1,5},{2,0},{3,7},{4,6},{5,1},{6,4},{7,3},{8,10},{9,13},{10,... | collective-permute-start | bytes 1572872 | tf_op jit(solution)/shard_map/ppermute | solution.py:284
  23.8 5.3 %conv.2 = (f32[512,256]{1,0:T(8,128)S(1)}, bf16[8,216,256]{2,1,0:T(8,128)(2,1)S(1)}, bf16[8,216,256]{2,1,0:T(8,128)(2,1)S(1)}) custom-call(s32[1]{0:T(128)} %bitcast.me.refs_0_, s32[8,27]{1,0:T(8,128)S(1)} %bitcast.17, s32[8,27]{1,0:T(8,128)S(1)} %bitcast.19, bf16[256,256]{1,0:T(8,128)(2,1)S(1)} %collective-permute-done.1.refs_3_, ...), custom_call_target="tpu_custom_call" | custom-call | flops 1048576 | bytes 1024 | tf_op jit(solution)/shard_map/conv/pallas_call | solution.py:257
  29.1 1.8 %collective-permute-done.4 = bf16[8,64,512]{2,1,0:T(8,128)(2,1)S(1)} collective-permute-done((bf16[8,64,512]{2,1,0:T(8,128)(2,1)S(1)}, bf16[8,64,512]{2,1,0:T(8,128)(2,1)S(1)}, u32[]{:S(2)}, u32[]{:S(2)}) %collective-permute-start.4) | collective-permute-done | bytes 524320 | tf_op jit(solution)/shard_map/ppermute | solution.py:284
  31.0 1.1 %collective-permute-start.5 = (bf16[8,216,256]{2,1,0:T(8,128)(2,1)S(1)}, bf16[8,216,256]{2,1,0:T(8,128)(2,1)S(1)}, u32[]{:S(2)}, u32[]{:S(2)}) collective-permute-start(bf16[8,216,256]{2,1,0:T(8,128)(2,1)S(1)} %get-tuple-element.64), channel_id=1, source_target_pairs={{0,1},{1,0},{2,3},{3,2},{4,5},{5,4},{6,7},{7,6},{8,9},{9,8},{10,11... | collective-permute-start | bytes 2654216 | tf_op jit(solution)/shard_map/ppermute | solution.py:284
  32.1 2.1 %collective-permute-done.5 = bf16[8,216,256]{2,1,0:T(8,128)(2,1)S(1)} collective-permute-done((bf16[8,216,256]{2,1,0:T(8,128)(2,1)S(1)}, bf16[8,216,256]{2,1,0:T(8,128)(2,1)S(1)}, u32[]{:S(2)}, u32[]{:S(2)}) %collective-permute-start.5) | collective-permute-done | bytes 884768 | tf_op jit(solution)/shard_map/ppermute | solution.py:284
  34.1 0.2 convert_add_fusion.2
  34.4 3.1 %collective-permute-start.6 = (bf16[4,216,256]{2,1,0:T(8,128)(2,1)S(1)}, bf16[4,216,256]{2,1,0:T(8,128)(2,1)S(1)}, u32[]{:S(2)}, u32[]{:S(2)}) collective-permute-start(bf16[4,216,256]{2,1,0:T(8,128)(2,1)S(1)} %slice.141), channel_id=1, source_target_pairs={{0,2},{1,5},{2,0},{3,7},{4,6},{5,1},{6,4},{7,3},{8,10},{9,13},{10,... | collective-permute-start | bytes 1327112 | tf_op jit(solution)/shard_map/ppermute | solution.py:284
  37.5 0.2 convert_add_fusion.3
  37.8 1.8 %collective-permute-start.7 = (bf16[4,64,512]{2,1,0:T(8,128)(2,1)S(1)}, bf16[4,64,512]{2,1,0:T(8,128)(2,1)S(1)}, u32[]{:S(2)}, u32[]{:S(2)}) collective-permute-start(bf16[4,64,512]{2,1,0:T(8,128)(2,1)S(1)} %slice.142), channel_id=1, source_target_pairs={{0,4},{1,3},{2,6},{3,1},{4,0},{5,7},{6,2},{7,5},{8,12},{9,11},{10,... | collective-permute-start | bytes 786440 | tf_op jit(solution)/shard_map/ppermute | solution.py:284
  39.6 0.8 %slice.94 = f32[4,64,512]{2,1,0:T(8,128)} slice(f32[8,64,512]{2,1,0:T(8,128)S(1)} %convert_add_fusion.3), slice={[0:4], [0:64], [0:512]} | slice | bytes 1048576 | tf_op jit(solution)/shard_map/slice | solution.py:290
  40.4 6.7 %conv.3 = (bf16[512,256]{1,0:T(8,128)(2,1)}, bf16[8,216,256]{2,1,0:T(8,128)(2,1)S(1)}, bf16[8,216,256]{2,1,0:T(8,128)(2,1)S(1)}) custom-call(s32[1]{0:T(128)} %bitcast.me.refs_0_, s32[8,27]{1,0:T(8,128)S(1)} %bitcast.18, s32[8,27]{1,0:T(8,128)S(1)} %bitcast.20, bf16[256,256]{1,0:T(8,128)(2,1)S(1)} %collective-permute-done.1.refs_3_, ...), custom_call_target="tpu_custom_call" | custom-call | flops 1048576 | bytes 1024 | tf_op jit(solution)/shard_map/conv/pallas_call | solution.py:257
  47.1 0.0 collective-permute-done.7
  47.1 0.0 collective-permute-done.6
  47.1 0.8 %copy-done.13 = bf16[4,216,256]{2,1,0:T(8,128)(2,1)} copy-done((bf16[4,216,256]{2,1,0:T(8,128)(2,1)}, bf16[4,216,256]{2,1,0:T(8,128)(2,1)S(1)}, u32[]{:S(2)}) %copy-start.13) | copy-done | bytes 442392
  47.9 0.1 copy-done.15
  48.0 1.0 %convert_add_fusion.5 = f32[4,64,512]{2,1,0:T(8,128)S(1)} fusion(f32[4,64,512]{2,1,0:T(8,128)S(1)} %copy-done.12, bf16[4,64,512]{2,1,0:T(8,128)(2,1)} %copy-done.15), kind=kLoop, calls=%fused_computation.10 | loop fusion | flops 262144 | bytes 1310720 | tf_op jit(solution)/shard_map/add | solution.py:289
  49.1 1.6 %collective-permute-start.16 = (bf16[2,64,512]{2,1,0:T(8,128)(2,1)S(1)}, bf16[2,64,512]{2,1,0:T(8,128)(2,1)S(1)}, u32[]{:S(2)}, u32[]{:S(2)}) collective-permute-start(bf16[2,64,512]{2,1,0:T(8,128)(2,1)S(1)} %slice.145), channel_id=1, source_target_pairs={{0,8},{1,9},{2,10},{3,11},{4,12},{5,13},{6,14},{7,15},{8,0},{9,1},... | collective-permute-start | bytes 393224 | tf_op jit(solution)/shard_map/ppermute | solution.py:284
  50.7 0.2 convert_add_fusion.1
  51.0 1.5 %collective-permute-start.12 = (bf16[4,216,256]{2,1,0:T(8,128)(2,1)S(1)}, bf16[4,216,256]{2,1,0:T(8,128)(2,1)S(1)}, u32[]{:S(2)}, u32[]{:S(2)}) collective-permute-start(bf16[4,216,256]{2,1,0:T(8,128)(2,1)S(1)} %slice.140), channel_id=1, source_target_pairs={{0,2},{1,5},{2,0},{3,7},{4,6},{5,1},{6,4},{7,3},{8,10},{9,13},{10,... | collective-permute-start | bytes 1327112 | tf_op jit(solution)/shard_map/ppermute | solution.py:284
  52.5 0.1 convert_add_fusion.4
  52.6 1.5 %collective-permute-start.8 = (bf16[2,216,256]{2,1,0:T(8,128)(2,1)S(1)}, bf16[2,216,256]{2,1,0:T(8,128)(2,1)S(1)}, u32[]{:S(2)}, u32[]{:S(2)}) collective-permute-start(bf16[2,216,256]{2,1,0:T(8,128)(2,1)S(1)} %slice.144), channel_id=1, source_target_pairs={{0,4},{1,3},{2,6},{3,1},{4,0},{5,7},{6,2},{7,5},{8,12},{9,11},{10,... | collective-permute-start | bytes 663560 | tf_op jit(solution)/shard_map/ppermute | solution.py:284
  54.1 0.9 %collective-permute-done.16 = bf16[2,64,512]{2,1,0:T(8,128)(2,1)S(1)} collective-permute-done((bf16[2,64,512]{2,1,0:T(8,128)(2,1)S(1)}, bf16[2,64,512]{2,1,0:T(8,128)(2,1)S(1)}, u32[]{:S(2)}, u32[]{:S(2)}) %collective-permute-start.16) | collective-permute-done | bytes 131104 | tf_op jit(solution)/shard_map/ppermute | solution.py:284
  55.1 2.7 %collective-permute-start.17 = (bf16[1,64,512]{2,1,0:T(8,128)(2,1)S(1)}, bf16[1,64,512]{2,1,0:T(8,128)(2,1)S(1)}, u32[]{:S(2)}, u32[]{:S(2)}) collective-permute-start(bf16[1,64,512]{2,1,0:T(8,128)(2,1)S(1)} %slice.148), channel_id=1, source_target_pairs={{0,16},{1,17},{2,18},{3,19},{4,20},{5,21},{6,22},{7,23},{8,24},{9,... | collective-permute-start | bytes 196616 | tf_op jit(solution)/shard_map/ppermute | solution.py:284
  57.8 3.9 %collective-permute-done.12 = bf16[4,216,256]{2,1,0:T(8,128)(2,1)S(1)} collective-permute-done((bf16[4,216,256]{2,1,0:T(8,128)(2,1)S(1)}, bf16[4,216,256]{2,1,0:T(8,128)(2,1)S(1)}, u32[]{:S(2)}, u32[]{:S(2)}) %collective-permute-start.12) | collective-permute-done | bytes 442400 | tf_op jit(solution)/shard_map/ppermute | solution.py:284
  61.7 0.1 slice_add_fusion
  61.9 1.2 %collective-permute-start.13 = (bf16[2,216,256]{2,1,0:T(8,128)(2,1)S(1)}, bf16[2,216,256]{2,1,0:T(8,128)(2,1)S(1)}, u32[]{:S(2)}, u32[]{:S(2)}) collective-permute-start(bf16[2,216,256]{2,1,0:T(8,128)(2,1)S(1)} %slice.143), channel_id=1, source_target_pairs={{0,4},{1,3},{2,6},{3,1},{4,0},{5,7},{6,2},{7,5},{8,12},{9,11},{10,... | collective-permute-start | bytes 663560 | tf_op jit(solution)/shard_map/ppermute | solution.py:284
  63.1 0.0 collective-permute-done.8
  63.1 0.1 slice_add_fusion.2
  63.2 1.3 %collective-permute-start.9 = (bf16[1,216,256]{2,1,0:T(8,128)(2,1)S(1)}, bf16[1,216,256]{2,1,0:T(8,128)(2,1)S(1)}, u32[]{:S(2)}, u32[]{:S(2)}) collective-permute-start(bf16[1,216,256]{2,1,0:T(8,128)(2,1)S(1)} %slice.147), channel_id=1, source_target_pairs={{0,8},{1,9},{2,10},{3,11},{4,12},{5,13},{6,14},{7,15},{8,0},{9,1},... | collective-permute-start | bytes 331784 | tf_op jit(solution)/shard_map/ppermute | solution.py:284
  64.5 3.4 %collective-permute-done.13 = bf16[2,216,256]{2,1,0:T(8,128)(2,1)S(1)} collective-permute-done((bf16[2,216,256]{2,1,0:T(8,128)(2,1)S(1)}, bf16[2,216,256]{2,1,0:T(8,128)(2,1)S(1)}, u32[]{:S(2)}, u32[]{:S(2)}) %collective-permute-start.13) | collective-permute-done | bytes 221216 | tf_op jit(solution)/shard_map/ppermute | solution.py:284
  67.8 0.1 slice_add_fusion.1
  67.9 1.3 %collective-permute-start.14 = (bf16[1,216,256]{2,1,0:T(8,128)(2,1)S(1)}, bf16[1,216,256]{2,1,0:T(8,128)(2,1)S(1)}, u32[]{:S(2)}, u32[]{:S(2)}) collective-permute-start(bf16[1,216,256]{2,1,0:T(8,128)(2,1)S(1)} %slice.146), channel_id=1, source_target_pairs={{0,8},{1,9},{2,10},{3,11},{4,12},{5,13},{6,14},{7,15},{8,0},{9,1},... | collective-permute-start | bytes 331784 | tf_op jit(solution)/shard_map/ppermute | solution.py:284
  69.3 0.0 collective-permute-done.9
  69.3 1.3 %collective-permute-start.10 = (bf16[1,216,256]{2,1,0:T(8,128)(2,1)S(1)}, bf16[1,216,256]{2,1,0:T(8,128)(2,1)S(1)}, u32[]{:S(2)}, u32[]{:S(2)}) collective-permute-start(bf16[1,216,256]{2,1,0:T(8,128)(2,1)S(1)} %fusion), channel_id=1, source_target_pairs={{8,24},{9,25},{10,26},{11,27},{12,28},{13,29},{14,30},{15,31},{16,... | collective-permute-start | bytes 331784 | tf_op jit(solution)/shard_map/ppermute | solution.py:284
  70.6 3.3 %collective-permute-done.14 = bf16[1,216,256]{2,1,0:T(8,128)(2,1)S(1)} collective-permute-done((bf16[1,216,256]{2,1,0:T(8,128)(2,1)S(1)}, bf16[1,216,256]{2,1,0:T(8,128)(2,1)S(1)}, u32[]{:S(2)}, u32[]{:S(2)}) %collective-permute-start.14) | collective-permute-done | bytes 110624 | tf_op jit(solution)/shard_map/ppermute | solution.py:284
  74.0 3.1 %collective-permute-start.15 = (bf16[1,216,256]{2,1,0:T(8,128)(2,1)S(1)}, bf16[1,216,256]{2,1,0:T(8,128)(2,1)S(1)}, u32[]{:S(2)}, u32[]{:S(2)}) collective-permute-start(bf16[1,216,256]{2,1,0:T(8,128)(2,1)S(1)} %fusion.1), channel_id=1, source_target_pairs={{0,16},{1,17},{2,18},{3,19},{4,20},{5,21},{6,22},{7,23},{24,8},{25... | collective-permute-start | bytes 331784 | tf_op jit(solution)/shard_map/ppermute | solution.py:284
  77.0 0.0 collective-permute-done.17
  77.0 0.7 fusion.3
  77.7 0.0 collective-permute-done.10
  77.7 1.6 %collective-permute-done.15 = bf16[1,216,256]{2,1,0:T(8,128)(2,1)S(1)} collective-permute-done((bf16[1,216,256]{2,1,0:T(8,128)(2,1)S(1)}, bf16[1,216,256]{2,1,0:T(8,128)(2,1)S(1)}, u32[]{:S(2)}, u32[]{:S(2)}) %collective-permute-start.15) | collective-permute-done | bytes 110624 | tf_op jit(solution)/shard_map/ppermute | solution.py:284
  79.3 0.1 multiply_bitcast_fusion
  79.4 0.8 copy.13
  (39 shorter events, 0.4 us)
Async XLA Ops:
  0.6 8.1 %collective-permute-start = (bf16[128,512]{1,0:T(8,128)(2,1)}, bf16[128,512]{1,0:T(8,128)(2,1)S(1)}, u32[]{:S(2)}, u32[]{:S(2)}) collective-permute-start(bf16[128,512]{1,0:T(8,128)(2,1)} %cur_in.1), channel_id=1, source_target_pairs={{0,1},{1,2},{2,3},{3,4},{4,5},{5,6},{6,7},{7,8},{8,9},{9,10},{10,1... | collective-permute-start | bytes 393224 | tf_op jit(solution)/shard_map/ppermute | solution.py:284
  3.0 1.6 %copy-start.1 = (bf16[2048,512]{1,0:T(8,128)(2,1)S(1)}, bf16[2048,512]{1,0:T(8,128)(2,1)}, u32[]{:S(2)}) copy-start(bf16[2048,512]{1,0:T(8,128)(2,1)} %w_in.1) | copy-start | bytes 6291460
  4.6 0.9 %copy-start.4 = (bf16[512,256]{1,0:T(8,128)(2,1)S(1)}, bf16[512,256]{1,0:T(8,128)(2,1)}, u32[]{:S(2)}) copy-start(bf16[512,256]{1,0:T(8,128)(2,1)} %pre.1) | copy-start | bytes 786436
  5.6 0.9 %copy-start.5 = (bf16[128,512]{1,0:T(8,128)(2,1)S(1)}, bf16[128,512]{1,0:T(8,128)(2,1)}, u32[]{:S(2)}) copy-start(bf16[128,512]{1,0:T(8,128)(2,1)} %cur_in.1) | copy-start | bytes 393220
  6.5 0.7 copy-start.8
  7.1 0.7 copy-start.9
  8.7 8.4 %copy-start = (bf16[6912,256]{1,0:T(8,128)(2,1)S(1)}, bf16[6912,256]{1,0:T(8,128)(2,1)}, u32[]{:S(2)}) copy-start(bf16[6912,256]{1,0:T(8,128)(2,1)} %refs_7_.3) | copy-start | bytes 10616836
  8.8 8.4 %copy-start.2 = (bf16[512,256]{1,0:T(8,128)(2,1)S(1)}, bf16[512,256]{1,0:T(8,128)(2,1)}, u32[]{:S(2)}) copy-start(bf16[512,256]{1,0:T(8,128)(2,1)} %refs_9_.1) | copy-start | bytes 786436
  8.8 8.4 %copy-start.3 = (s32[1,27,8,128]{3,2,1,0:T(8,128)S(1)}, s32[1,27,8,128]{3,2,1,0:T(8,128)}, u32[]{:S(2)}) copy-start(s32[1,27,8,128]{3,2,1,0:T(8,128)} %param.17) | copy-start | bytes 331780
  11.1 8.9 %collective-permute-start.3 = (bf16[16,64,512]{2,1,0:T(8,128)(2,1)S(1)}, bf16[16,64,512]{2,1,0:T(8,128)(2,1)S(1)}, u32[]{:S(2)}, u32[]{:S(2)}) collective-permute-start(bf16[16,64,512]{2,1,0:T(8,128)(2,1)S(1)} %get-tuple-element.52), channel_id=1, source_target_pairs={{0,1},{1,0},{2,3},{3,2},{4,5},{5,4},{6,7},{7,6},{8,9},{9,8},{10,11... | collective-permute-start | bytes 3145736 | tf_op jit(solution)/shard_map/ppermute | solution.py:284
  13.7 3.8 %collective-permute-start.1 = (bf16[256,256]{1,0:T(8,128)(2,1)S(1)}, bf16[256,256]{1,0:T(8,128)(2,1)S(1)}, u32[]{:S(2)}, u32[]{:S(2)}) collective-permute-start(bf16[256,256]{1,0:T(8,128)(2,1)S(1)} %get-tuple-element.47.refs_5_), channel_id=1, source_target_pairs={{0,1},{1,2},{2,3},{3,4},{4,5},{5,6},{6,7},{7,8},{8,9},{9,10},{10,1... | collective-permute-start | bytes 393224 | tf_op jit(solution)/shard_map/ppermute | solution.py:284
  15.6 4.3 %collective-permute-start.2 = (bf16[256,256]{1,0:T(8,128)(2,1)S(1)}, bf16[256,256]{1,0:T(8,128)(2,1)S(1)}, u32[]{:S(2)}, u32[]{:S(2)}) collective-permute-start(bf16[256,256]{1,0:T(8,128)(2,1)S(1)} %get-tuple-element.48.refs_4_), channel_id=1, source_target_pairs={{1,0},{2,1},{3,2},{4,3},{5,4},{6,5},{7,6},{8,7},{9,8},{10,9},{11,1... | collective-permute-start | bytes 393224 | tf_op jit(solution)/shard_map/ppermute | solution.py:284
  20.3 8.8 %copy-start.10 = (f32[16,64,512]{2,1,0:T(8,128)}, f32[16,64,512]{2,1,0:T(8,128)S(1)}, u32[]{:S(2)}) copy-start(f32[16,64,512]{2,1,0:T(8,128)S(1)} %convert_add_fusion) | copy-start | bytes 6291460
  20.3 3.5 %copy-start.6 = (s32[1,27,8]{1,2,0:T(8,128)S(1)}, s32[1,27,8]{1,2,0:T(8,128)}, u32[]{:S(2)}) copy-start(s32[1,27,8]{1,2,0:T(8,128)} %param.15) | copy-start | bytes 2596
  20.3 3.5 %copy-start.7 = (s32[1,27,8]{1,2,0:T(8,128)S(1)}, s32[1,27,8]{1,2,0:T(8,128)}, u32[]{:S(2)}) copy-start(s32[1,27,8]{1,2,0:T(8,128)} %param.16) | copy-start | bytes 2596
  20.4 10.5 %collective-permute-start.4 = (bf16[8,64,512]{2,1,0:T(8,128)(2,1)S(1)}, bf16[8,64,512]{2,1,0:T(8,128)(2,1)S(1)}, u32[]{:S(2)}, u32[]{:S(2)}) collective-permute-start(bf16[8,64,512]{2,1,0:T(8,128)(2,1)S(1)} %slice.139), channel_id=1, source_target_pairs={{0,2},{1,5},{2,0},{3,7},{4,6},{5,1},{6,4},{7,3},{8,10},{9,13},{10,... | collective-permute-start | bytes 1572872 | tf_op jit(solution)/shard_map/ppermute | solution.py:284
  31.0 6.6 %slice-start = ((f32[16,64,512]{2,1,0:T(8,128)}), f32[8,64,512]{2,1,0:T(8,128)S(1)}, s32[]{:S(2)}) async-start(f32[16,64,512]{2,1,0:T(8,128)} %copy-done.10), calls=%async_computation | async-start | bytes 2097152 | tf_op jit(solution)/shard_map/slice | solution.py:290
  31.0 3.2 %collective-permute-start.5 = (bf16[8,216,256]{2,1,0:T(8,128)(2,1)S(1)}, bf16[8,216,256]{2,1,0:T(8,128)(2,1)S(1)}, u32[]{:S(2)}, u32[]{:S(2)}) collective-permute-start(bf16[8,216,256]{2,1,0:T(8,128)(2,1)S(1)} %get-tuple-element.64), channel_id=1, source_target_pairs={{0,1},{1,0},{2,3},{3,2},{4,5},{5,4},{6,7},{7,6},{8,9},{9,8},{10,11... | collective-permute-start | bytes 2654216 | tf_op jit(solution)/shard_map/ppermute | solution.py:284
  34.4 6.0 %copy-start.11 = (f32[8,216,256]{2,1,0:T(8,128)}, f32[8,216,256]{2,1,0:T(8,128)S(1)}, u32[]{:S(2)}) copy-start(f32[8,216,256]{2,1,0:T(8,128)S(1)} %convert_add_fusion.2) | copy-start | bytes 5308420
  34.4 12.7 %collective-permute-start.6 = (bf16[4,216,256]{2,1,0:T(8,128)(2,1)S(1)}, bf16[4,216,256]{2,1,0:T(8,128)(2,1)S(1)}, u32[]{:S(2)}, u32[]{:S(2)}) collective-permute-start(bf16[4,216,256]{2,1,0:T(8,128)(2,1)S(1)} %slice.141), channel_id=1, source_target_pairs={{0,2},{1,5},{2,0},{3,7},{4,6},{5,1},{6,4},{7,3},{8,10},{9,13},{10,... | collective-permute-start | bytes 1327112 | tf_op jit(solution)/shard_map/ppermute | solution.py:284
  37.8 9.4 %collective-permute-start.7 = (bf16[4,64,512]{2,1,0:T(8,128)(2,1)S(1)}, bf16[4,64,512]{2,1,0:T(8,128)(2,1)S(1)}, u32[]{:S(2)}, u32[]{:S(2)}) collective-permute-start(bf16[4,64,512]{2,1,0:T(8,128)(2,1)S(1)} %slice.142), channel_id=1, source_target_pairs={{0,4},{1,3},{2,6},{3,1},{4,0},{5,7},{6,2},{7,5},{8,12},{9,11},{10,... | collective-permute-start | bytes 786440 | tf_op jit(solution)/shard_map/ppermute | solution.py:284
  40.4 7.6 %copy-start.12 = (f32[4,64,512]{2,1,0:T(8,128)S(1)}, f32[4,64,512]{2,1,0:T(8,128)}, u32[]{:S(2)}) copy-start(f32[4,64,512]{2,1,0:T(8,128)} %slice.94) | copy-start | bytes 1572868
  47.1 0.9 %copy-start.15 = (bf16[4,64,512]{2,1,0:T(8,128)(2,1)}, bf16[4,64,512]{2,1,0:T(8,128)(2,1)S(1)}, u32[]{:S(2)}) copy-start(bf16[4,64,512]{2,1,0:T(8,128)(2,1)S(1)} %collective-permute-done.7) | copy-start | bytes 786436
  47.1 0.8 %copy-start.13 = (bf16[4,216,256]{2,1,0:T(8,128)(2,1)}, bf16[4,216,256]{2,1,0:T(8,128)(2,1)S(1)}, u32[]{:S(2)}) copy-start(bf16[4,216,256]{2,1,0:T(8,128)(2,1)S(1)} %collective-permute-done.6) | copy-start | bytes 1327108
  48.0 2.7 %collective-permute-start.11 = (bf16[8,216,256]{2,1,0:T(8,128)(2,1)S(1)}, bf16[8,216,256]{2,1,0:T(8,128)(2,1)S(1)}, u32[]{:S(2)}, u32[]{:S(2)}) collective-permute-start(bf16[8,216,256]{2,1,0:T(8,128)(2,1)S(1)} %get-tuple-element.76), channel_id=1, source_target_pairs={{0,1},{1,0},{2,3},{3,2},{4,5},{5,4},{6,7},{7,6},{8,9},{9,8},{10,11... | collective-permute-start | bytes 2654216 | tf_op jit(solution)/shard_map/ppermute | solution.py:284
  49.1 3.4 %slice-start.1 = ((f32[8,216,256]{2,1,0:T(8,128)}), f32[4,216,256]{2,1,0:T(8,128)S(1)}, s32[]{:S(2)}) async-start(f32[8,216,256]{2,1,0:T(8,128)} %copy-done.11), calls=%async_computation.1 | async-start | bytes 1769472 | tf_op jit(solution)/shard_map/slice | solution.py:290
  49.1 3.4 %copy-start.14 = (bf16[4,216,256]{2,1,0:T(8,128)(2,1)S(1)}, bf16[4,216,256]{2,1,0:T(8,128)(2,1)}, u32[]{:S(2)}) copy-start(bf16[4,216,256]{2,1,0:T(8,128)(2,1)} %copy-done.13) | copy-start | bytes 1327108
  49.1 6.0 %collective-permute-start.16 = (bf16[2,64,512]{2,1,0:T(8,128)(2,1)S(1)}, bf16[2,64,512]{2,1,0:T(8,128)(2,1)S(1)}, u32[]{:S(2)}, u32[]{:S(2)}) collective-permute-start(bf16[2,64,512]{2,1,0:T(8,128)(2,1)S(1)} %slice.145), channel_id=1, source_target_pairs={{0,8},{1,9},{2,10},{3,11},{4,12},{5,13},{6,14},{7,15},{8,0},{9,1},... | collective-permute-start | bytes 393224 | tf_op jit(solution)/shard_map/ppermute | solution.py:284
  51.0 10.7 %collective-permute-start.12 = (bf16[4,216,256]{2,1,0:T(8,128)(2,1)S(1)}, bf16[4,216,256]{2,1,0:T(8,128)(2,1)S(1)}, u32[]{:S(2)}, u32[]{:S(2)}) collective-permute-start(bf16[4,216,256]{2,1,0:T(8,128)(2,1)S(1)} %slice.140), channel_id=1, source_target_pairs={{0,2},{1,5},{2,0},{3,7},{4,6},{5,1},{6,4},{7,3},{8,10},{9,13},{10,... | collective-permute-start | bytes 1327112 | tf_op jit(solution)/shard_map/ppermute | solution.py:284
  52.6 10.4 %collective-permute-start.8 = (bf16[2,216,256]{2,1,0:T(8,128)(2,1)S(1)}, bf16[2,216,256]{2,1,0:T(8,128)(2,1)S(1)}, u32[]{:S(2)}, u32[]{:S(2)}) collective-permute-start(bf16[2,216,256]{2,1,0:T(8,128)(2,1)S(1)} %slice.144), channel_id=1, source_target_pairs={{0,4},{1,3},{2,6},{3,1},{4,0},{5,7},{6,2},{7,5},{8,12},{9,11},{10,... | collective-permute-start | bytes 663560 | tf_op jit(solution)/shard_map/ppermute | solution.py:284
  55.1 21.9 %collective-permute-start.17 = (bf16[1,64,512]{2,1,0:T(8,128)(2,1)S(1)}, bf16[1,64,512]{2,1,0:T(8,128)(2,1)S(1)}, u32[]{:S(2)}, u32[]{:S(2)}) collective-permute-start(bf16[1,64,512]{2,1,0:T(8,128)(2,1)S(1)} %slice.148), channel_id=1, source_target_pairs={{0,16},{1,17},{2,18},{3,19},{4,20},{5,21},{6,22},{7,23},{8,24},{9,... | collective-permute-start | bytes 196616 | tf_op jit(solution)/shard_map/ppermute | solution.py:284
  61.9 6.0 %collective-permute-start.13 = (bf16[2,216,256]{2,1,0:T(8,128)(2,1)S(1)}, bf16[2,216,256]{2,1,0:T(8,128)(2,1)S(1)}, u32[]{:S(2)}, u32[]{:S(2)}) collective-permute-start(bf16[2,216,256]{2,1,0:T(8,128)(2,1)S(1)} %slice.143), channel_id=1, source_target_pairs={{0,4},{1,3},{2,6},{3,1},{4,0},{5,7},{6,2},{7,5},{8,12},{9,11},{10,... | collective-permute-start | bytes 663560 | tf_op jit(solution)/shard_map/ppermute | solution.py:284
  63.2 6.1 %collective-permute-start.9 = (bf16[1,216,256]{2,1,0:T(8,128)(2,1)S(1)}, bf16[1,216,256]{2,1,0:T(8,128)(2,1)S(1)}, u32[]{:S(2)}, u32[]{:S(2)}) collective-permute-start(bf16[1,216,256]{2,1,0:T(8,128)(2,1)S(1)} %slice.147), channel_id=1, source_target_pairs={{0,8},{1,9},{2,10},{3,11},{4,12},{5,13},{6,14},{7,15},{8,0},{9,1},... | collective-permute-start | bytes 331784 | tf_op jit(solution)/shard_map/ppermute | solution.py:284
  67.9 6.0 %collective-permute-start.14 = (bf16[1,216,256]{2,1,0:T(8,128)(2,1)S(1)}, bf16[1,216,256]{2,1,0:T(8,128)(2,1)S(1)}, u32[]{:S(2)}, u32[]{:S(2)}) collective-permute-start(bf16[1,216,256]{2,1,0:T(8,128)(2,1)S(1)} %slice.146), channel_id=1, source_target_pairs={{0,8},{1,9},{2,10},{3,11},{4,12},{5,13},{6,14},{7,15},{8,0},{9,1},... | collective-permute-start | bytes 331784 | tf_op jit(solution)/shard_map/ppermute | solution.py:284
  69.3 8.4 %collective-permute-start.10 = (bf16[1,216,256]{2,1,0:T(8,128)(2,1)S(1)}, bf16[1,216,256]{2,1,0:T(8,128)(2,1)S(1)}, u32[]{:S(2)}, u32[]{:S(2)}) collective-permute-start(bf16[1,216,256]{2,1,0:T(8,128)(2,1)S(1)} %fusion), channel_id=1, source_target_pairs={{8,24},{9,25},{10,26},{11,27},{12,28},{13,29},{14,30},{15,31},{16,... | collective-permute-start | bytes 331784 | tf_op jit(solution)/shard_map/ppermute | solution.py:284
  74.0 5.4 %collective-permute-start.15 = (bf16[1,216,256]{2,1,0:T(8,128)(2,1)S(1)}, bf16[1,216,256]{2,1,0:T(8,128)(2,1)S(1)}, u32[]{:S(2)}, u32[]{:S(2)}) collective-permute-start(bf16[1,216,256]{2,1,0:T(8,128)(2,1)S(1)} %fusion.1), channel_id=1, source_target_pairs={{0,16},{1,17},{2,18},{3,19},{4,20},{5,21},{6,22},{7,23},{24,8},{25... | collective-permute-start | bytes 331784 | tf_op jit(solution)/shard_map/ppermute | solution.py:284

commit v8 on v7

--- a/solution.py
+++ b/solution.py
@@ -290,6 +290,25 @@
     return total[:half], total[half:].astype(BF)
 
 
+def fold_kernel(kept, got, keep, send):
+    half = keep.shape[0]
+    keep[...] = kept[:half].astype(F32) + got[:half].astype(F32)
+    send[...] = (kept[half:].astype(F32) + got[half:].astype(F32)).astype(BF)
+
+
+def fold_long(kept, got):
+    shape = (kept.shape[0] // 2,) + kept.shape[1:]
+    return pl.pallas_call(
+        fold_kernel,
+        out_shape=(jax.ShapeDtypeStruct(shape, F32), jax.ShapeDtypeStruct(shape, BF)),
+        in_specs=[VMEM] * 2,
+        out_specs=(VMEM,) * 2,
+        compiler_params=pltpu.CompilerParams(vmem_limit_bytes=16 << 20),
+        cost_estimate=pl.CostEstimate(flops=12 << 30, bytes_accessed=1 << 10, transcendentals=0),
+        name="fold",
+    )(kept, got)
+
+
 def per_device(
     feats,
     pre_act,
@@ -331,7 +350,7 @@
         return moved(x, peers, lambda i: i ^ far if (i ^ far) // near in wanted else None)
 
     def middle(kept, got):
-        kept, send = fold(kept, got)
+        kept, send = fold_long(kept, got)
         for step in range(1, bits - 1):
             kept, send = fold(kept, xy(send, step))
         return kept, send
@@ -365,26 +384,26 @@
     low, low_send = fold(low, low_got)
     low_got = xy(low_send, 0)
     partial, outer, outer_send = quarters((0, 3), tables)
-    partial, outer, outer_send, low, low_got = pinned((partial, outer, outer_send, low, low_got))
+    partial, low, low_got = pinned((partial, low, low_got))
 
     outer_got = across(outer_send)
     low, low_send = middle(low, low_got)
+    outer_got, low, low_send = pinned((outer_got, low, low_send))
     low_got = xy(low_send, bits - 1)
     outer, outer_send = fold(outer, outer_got)
     partial, outer_send = pinned((partial, outer_send))
     outer_got = xy(outer_send, 0)
     grad_in, inner, inner_send = quarters((1, 2), (pairs, feats), partial)
-    grad_in, inner, inner_send, outer, outer_got, low, low_got = pinned(
-        (grad_in, inner, inner_send, outer, outer_got, low, low_got)
-    )
+    grad_in, outer, outer_got, low, low_got = pinned((grad_in, outer, outer_got, low, low_got))
 
     inner_got = across(inner_send)
     outer, outer_send = middle(outer, outer_got)
     outer_got = xy(outer_send, bits - 1)
+    inner, inner_send = fold(inner, inner_got)
+    inner_send, low, low_got = pinned((inner_send, low, low_got))
+    inner_got = xy(inner_send, 0)
     low, low_send = fold(low, low_got)
     low_got = z_near(low_send)
-    inner, inner_send = fold(inner, inner_got)
-    inner_got = xy(inner_send, 0)
 
     outer, outer_send = fold(outer, outer_got)
     outer_got = z_near(outer_send)

time: 80.6 us -> 82 us (1.017)
  the two profiles are of different devices: /device:TPU:0 before, /device:TPU:14 now
where the time goes in v8:
time: 82 us; the launch traced here: 81.6 us
  waiting for transfers between devices  31.3 us (38%)
  starting transfers between devices  24.3 us (30%)
  Pallas kernels  15.8 us (19%)
  local copies, waits for them, and re-layouts  7.46 us (9%)
  other arithmetic  1.79 us (2%)
  between operations  0.97 us (1%)
    ppermute x18, waiting for transfers between devices, moved(): lax.ppermute(x, 'space', [(i, j) for i, j in pairs if j is not None and 0...  31.3 us
    ppermute x18, starting transfers between devices, moved(): lax.ppermute(x, 'space', [(i, j) for i, j in pairs if j is not None and 0...  24.3 us
    pallas_call x2, Pallas kernels, conv(): pl.pallas_call(functools.partial(conv_kernel, conv_plan(kernel, channels,...  12.1 us
    unnamed x21, local copies, waits for them, and re-layouts  5.64 us
    pallas_call x1, Pallas kernels, down(): pl.pallas_call(functools.partial(down_kernel, bits), out_shape=(side, sid...  2.26 us
    slice x10, local copies, waits for them, and re-layouts, fold(): return (total[:half], total[half:].astype(BF))  1.82 us
  transfers between devices with their start and end apart: 18, of which 11 were waited for; matrix products, arithmetic and copies ran while one was open for 4% of the time, Pallas kernels for 17%

profile of v8, /device:TPU:14, one launch (start us, length us, event | category | flops | bytes accessed | tf_op | source)
XLA Modules:
  0.0 81.6 jit_solution(16140952896639413044)
XLA Ops:
  0.6 1.9 %collective-permute-start = (bf16[128,512]{1,0:T(8,128)(2,1)}, bf16[128,512]{1,0:T(8,128)(2,1)S(1)}, u32[]{:S(2)}, u32[]{:S(2)}) collective-permute-start(bf16[128,512]{1,0:T(8,128)(2,1)} %cur_in.1), channel_id=1, source_target_pairs={{0,1},{1,2},{2,3},{3,4},{4,5},{5,6},{6,7},{7,8},{8,9},{9,10},{10,1... | collective-permute-start | bytes 393224 | tf_op jit(solution)/shard_map/ppermute | solution.py:284
  2.6 1.6 %copy-done.1 = bf16[2048,512]{1,0:T(8,128)(2,1)S(1)} copy-done((bf16[2048,512]{1,0:T(8,128)(2,1)S(1)}, bf16[2048,512]{1,0:T(8,128)(2,1)}, u32[]{:S(2)}) %copy-start.1) | copy-done | bytes 2097176
  4.2 0.9 %copy-done.4 = bf16[512,256]{1,0:T(8,128)(2,1)S(1)} copy-done((bf16[512,256]{1,0:T(8,128)(2,1)S(1)}, bf16[512,256]{1,0:T(8,128)(2,1)}, u32[]{:S(2)}) %copy-start.4) | copy-done | bytes 262168
  5.1 0.9 %copy-done.5 = bf16[128,512]{1,0:T(8,128)(2,1)S(1)} copy-done((bf16[128,512]{1,0:T(8,128)(2,1)S(1)}, bf16[128,512]{1,0:T(8,128)(2,1)}, u32[]{:S(2)}) %copy-start.5) | copy-done | bytes 131096
  6.0 0.7 copy-done.8
  6.7 0.7 copy-done.9
  7.4 0.9 %prep.1 = (bf16[512,256]{1,0:T(8,128)(2,1)S(1)}, bf16[512,1024]{1,0:T(8,128)(2,1)S(1)}, bf16[1024,256]{1,0:T(8,128)(2,1)S(1)}, bf16[256,1024]{1,0:T(8,128)(2,1)S...) custom-call(bf16[512,256]{1,0:T(8,128)(2,1)S(1)} %copy-done.4, s32[8,128]{1,0:T(8,128)S(1)} %bitcast.21, ...), custom_call_target="tpu_custom_call" | custom-call | flops 1048576 | bytes 1024 | tf_op jit(solution)/shard_map/prep/pallas_call | solution.py:114
  8.3 0.0 collective-permute-done.prev
  8.3 0.0 copy-start
  8.3 0.0 copy-start.2
  8.3 0.0 copy-start.3
  8.3 2.3 %down.1 = (bf16[256,256]{1,0:T(8,128)(2,1)S(1)}, bf16[256,256]{1,0:T(8,128)(2,1)S(1)}, bf16[16,64,512]{2,1,0:T(8,128)(2,1)S(1)}, bf16[16,64,512]{2,1,0:T(8,128)(2,1)S(1)}) custom-call(s32[1]{0:T(128)} %bitcast.me.refs_0_, bf16[128,512]{1,0:T(8,128)(2,1)S(1)} %collective-permute-done.prev, bf16[512,256]{1,0:T(8,128)(2,1)S(1)} %get-tuple-element.49.act, ...), custom_call_target="tpu_custom_call" | custom-call | flops 1048576 | bytes 1024 | tf_op jit(solution)/shard_map/down/pallas_call | solution.py:154
  10.6 1.7 %collective-permute-start.3 = (bf16[16,64,512]{2,1,0:T(8,128)(2,1)S(1)}, bf16[16,64,512]{2,1,0:T(8,128)(2,1)S(1)}, u32[]{:S(2)}, u32[]{:S(2)}) collective-permute-start(bf16[16,64,512]{2,1,0:T(8,128)(2,1)S(1)} %get-tuple-element.60), channel_id=1, source_target_pairs={{0,1},{1,0},{2,3},{3,2},{4,5},{5,4},{6,7},{7,6},{8,9},{9,8},{10,11... | collective-permute-start | bytes 3145736 | tf_op jit(solution)/shard_map/ppermute | solution.py:284
  12.3 1.9 %collective-permute-start.1 = (bf16[256,256]{1,0:T(8,128)(2,1)S(1)}, bf16[256,256]{1,0:T(8,128)(2,1)S(1)}, u32[]{:S(2)}, u32[]{:S(2)}) collective-permute-start(bf16[256,256]{1,0:T(8,128)(2,1)S(1)} %get-tuple-element.55.refs_5_), channel_id=1, source_target_pairs={{0,1},{1,2},{2,3},{3,4},{4,5},{5,6},{6,7},{7,8},{8,9},{9,10},{10,1... | collective-permute-start | bytes 393224 | tf_op jit(solution)/shard_map/ppermute | solution.py:284
  14.2 3.8 %collective-permute-start.2 = (bf16[256,256]{1,0:T(8,128)(2,1)S(1)}, bf16[256,256]{1,0:T(8,128)(2,1)S(1)}, u32[]{:S(2)}, u32[]{:S(2)}) collective-permute-start(bf16[256,256]{1,0:T(8,128)(2,1)S(1)} %get-tuple-element.56.refs_4_), channel_id=1, source_target_pairs={{1,0},{2,1},{3,2},{4,3},{5,4},{6,5},{7,6},{8,7},{9,8},{10,9},{11,1... | collective-permute-start | bytes 393224 | tf_op jit(solution)/shard_map/ppermute | solution.py:284
  18.0 0.3 turn.1
  18.3 0.2 collective-permute-done.1.refs_3_
  18.5 1.8 %collective-permute-done.2.refs_6_ = bf16[256,256]{1,0:T(8,128)(2,1)S(1)} collective-permute-done((bf16[256,256]{1,0:T(8,128)(2,1)S(1)}, bf16[256,256]{1,0:T(8,128)(2,1)S(1)}, u32[]{:S(2)}, u32[]{:S(2)}) %collective-permute-start.2) | collective-permute-done | bytes 131104 | tf_op jit(solution)/shard_map/ppermute | solution.py:284
  20.3 0.0 collective-permute-done.3
  20.3 0.3 convert_add_fusion
  20.7 0.0 copy-start.6
  20.7 0.0 copy-start.7
  20.7 0.1 slice.100
  20.8 1.5 %collective-permute-start.4 = (bf16[8,64,512]{2,1,0:T(8,128)(2,1)S(1)}, bf16[8,64,512]{2,1,0:T(8,128)(2,1)S(1)}, u32[]{:S(2)}, u32[]{:S(2)}) collective-permute-start(bf16[8,64,512]{2,1,0:T(8,128)(2,1)S(1)} %slice.100), channel_id=1, source_target_pairs={{0,2},{1,5},{2,0},{3,7},{4,6},{5,1},{6,4},{7,3},{8,10},{9,13},{10,... | collective-permute-start | bytes 1572872 | tf_op jit(solution)/shard_map/ppermute | solution.py:284
  22.3 0.1 slice.63.kept
  22.4 5.3 %conv.2 = (f32[512,256]{1,0:T(8,128)S(1)}, bf16[8,216,256]{2,1,0:T(8,128)(2,1)S(1)}, bf16[8,216,256]{2,1,0:T(8,128)(2,1)S(1)}) custom-call(s32[1]{0:T(128)} %bitcast.me.refs_0_, s32[8,27]{1,0:T(8,128)S(1)} %bitcast.17, s32[8,27]{1,0:T(8,128)S(1)} %bitcast.19, bf16[256,256]{1,0:T(8,128)(2,1)S(1)} %collective-permute-done.1.refs_3_, ...), custom_call_target="tpu_custom_call" | custom-call | flops 1048576 | bytes 1024 | tf_op jit(solution)/shard_map/conv/pallas_call | solution.py:257
  27.7 2.6 %collective-permute-start.5 = (bf16[8,216,256]{2,1,0:T(8,128)(2,1)S(1)}, bf16[8,216,256]{2,1,0:T(8,128)(2,1)S(1)}, u32[]{:S(2)}, u32[]{:S(2)}) collective-permute-start(bf16[8,216,256]{2,1,0:T(8,128)(2,1)S(1)} %get-tuple-element.70), channel_id=1, source_target_pairs={{0,1},{1,0},{2,3},{3,2},{4,5},{5,4},{6,7},{7,6},{8,9},{9,8},{10,11... | collective-permute-start | bytes 2654216 | tf_op jit(solution)/shard_map/ppermute | solution.py:284
  30.3 0.1 fold.3
  30.4 2.0 %collective-permute-done.5 = bf16[8,216,256]{2,1,0:T(8,128)(2,1)S(1)} collective-permute-done((bf16[8,216,256]{2,1,0:T(8,128)(2,1)S(1)}, bf16[8,216,256]{2,1,0:T(8,128)(2,1)S(1)}, u32[]{:S(2)}, u32[]{:S(2)}) %collective-permute-start.5) | collective-permute-done | bytes 884768 | tf_op jit(solution)/shard_map/ppermute | solution.py:284
  32.4 0.2 convert_add_fusion.2
  32.6 0.1 collective-permute-start.6
  32.7 1.4 %collective-permute-start.7 = (bf16[4,64,512]{2,1,0:T(8,128)(2,1)S(1)}, bf16[4,64,512]{2,1,0:T(8,128)(2,1)S(1)}, u32[]{:S(2)}, u32[]{:S(2)}) collective-permute-start(bf16[4,64,512]{2,1,0:T(8,128)(2,1)S(1)} %get-tuple-element.80), channel_id=1, source_target_pairs={{0,4},{1,3},{2,6},{3,1},{4,0},{5,7},{6,2},{7,5},{8,12},{9,11},{10,... | collective-permute-start | bytes 786440 | tf_op jit(solution)/shard_map/ppermute | solution.py:284
  34.0 0.1 slice.66.kept
  34.1 6.7 %conv.3 = (bf16[512,256]{1,0:T(8,128)(2,1)}, bf16[8,216,256]{2,1,0:T(8,128)(2,1)S(1)}, bf16[8,216,256]{2,1,0:T(8,128)(2,1)S(1)}) custom-call(s32[1]{0:T(128)} %bitcast.me.refs_0_, s32[8,27]{1,0:T(8,128)S(1)} %bitcast.18, s32[8,27]{1,0:T(8,128)S(1)} %bitcast.20, bf16[256,256]{1,0:T(8,128)(2,1)S(1)} %collective-permute-done.1.refs_3_, ...), custom_call_target="tpu_custom_call" | custom-call | flops 1048576 | bytes 1024 | tf_op jit(solution)/shard_map/conv/pallas_call | solution.py:257
  40.8 0.0 collective-permute-start.11
  40.8 1.0 %collective-permute-done.7 = bf16[4,64,512]{2,1,0:T(8,128)(2,1)S(1)} collective-permute-done((bf16[4,64,512]{2,1,0:T(8,128)(2,1)S(1)}, bf16[4,64,512]{2,1,0:T(8,128)(2,1)S(1)}, u32[]{:S(2)}, u32[]{:S(2)}) %collective-permute-start.7) | collective-permute-done | bytes 262176 | tf_op jit(solution)/shard_map/ppermute | solution.py:284
  41.9 1.9 %collective-permute-done.6.got = bf16[4,216,256]{2,1,0:T(8,128)(2,1)S(1)} collective-permute-done((bf16[4,216,256]{2,1,0:T(8,128)(2,1)S(1)}, bf16[4,216,256]{2,1,0:T(8,128)(2,1)S(1)}, u32[]{:S(2)}, u32[]{:S(2)}) %collective-permute-start.6) | collective-permute-done | bytes 442400 | tf_op jit(solution)/shard_map/ppermute | solution.py:284
  43.8 0.1 fold.4
  43.9 1.2 %collective-permute-start.8 = (bf16[2,216,256]{2,1,0:T(8,128)(2,1)S(1)}, bf16[2,216,256]{2,1,0:T(8,128)(2,1)S(1)}, u32[]{:S(2)}, u32[]{:S(2)}) collective-permute-start(bf16[2,216,256]{2,1,0:T(8,128)(2,1)S(1)} %get-tuple-element.85), channel_id=1, source_target_pairs={{0,4},{1,3},{2,6},{3,1},{4,0},{5,7},{6,2},{7,5},{8,12},{9,11},{10,... | collective-permute-start | bytes 663560 | tf_op jit(solution)/shard_map/ppermute | solution.py:284
  45.1 0.2 convert_add_fusion.1
  45.3 0.8 %slice.101 = bf16[4,216,256]{2,1,0:T(8,128)(2,1)} slice(f32[8,216,256]{2,1,0:T(8,128)S(1)} %convert_add_fusion.1), slice={[4:8], [0:216], [0:256]} | slice | bytes 884736 | tf_op jit(solution)/shard_map/slice | solution.py:290
  46.1 0.2 collective-permute-start.12
  46.3 5.9 %collective-permute-done.8 = bf16[2,216,256]{2,1,0:T(8,128)(2,1)S(1)} collective-permute-done((bf16[2,216,256]{2,1,0:T(8,128)(2,1)S(1)}, bf16[2,216,256]{2,1,0:T(8,128)(2,1)S(1)}, u32[]{:S(2)}, u32[]{:S(2)}) %collective-permute-start.8) | collective-permute-done | bytes 221216 | tf_op jit(solution)/shard_map/ppermute | solution.py:284
  52.2 0.1 convert_add_fusion.5
  52.3 0.7 slice.105
  53.0 0.4 collective-permute-start.9
  53.4 4.5 %collective-permute-done.9 = bf16[1,216,256]{2,1,0:T(8,128)(2,1)S(1)} collective-permute-done((bf16[1,216,256]{2,1,0:T(8,128)(2,1)}, bf16[1,216,256]{2,1,0:T(8,128)(2,1)S(1)}, u32[]{:S(2)}, u32[]{:S(2)}) %collective-permute-start.9) | collective-permute-done | bytes 110624 | tf_op jit(solution)/shard_map/ppermute | solution.py:284
  57.9 3.0 %collective-permute-start.10 = (bf16[1,216,256]{2,1,0:T(8,128)(2,1)S(1)}, bf16[1,216,256]{2,1,0:T(8,128)(2,1)S(1)}, u32[]{:S(2)}, u32[]{:S(2)}) collective-permute-start(bf16[1,216,256]{2,1,0:T(8,128)(2,1)S(1)} %fusion), channel_id=1, source_target_pairs={{8,24},{9,25},{10,26},{11,27},{12,28},{13,29},{14,30},{15,31},{16,... | collective-permute-start | bytes 331784 | tf_op jit(solution)/shard_map/ppermute | solution.py:284
  60.9 0.1 slice.69.kept
  61.0 0.1 fold.5
  61.1 1.2 %collective-permute-start.13 = (bf16[2,216,256]{2,1,0:T(8,128)(2,1)S(1)}, bf16[2,216,256]{2,1,0:T(8,128)(2,1)S(1)}, u32[]{:S(2)}, u32[]{:S(2)}) collective-permute-start(bf16[2,216,256]{2,1,0:T(8,128)(2,1)S(1)} %get-tuple-element.92), channel_id=1, source_target_pairs={{0,4},{1,3},{2,6},{3,1},{4,0},{5,7},{6,2},{7,5},{8,12},{9,11},{10,... | collective-permute-start | bytes 663560 | tf_op jit(solution)/shard_map/ppermute | solution.py:284
  62.3 0.1 convert_add_fusion.3
  62.4 0.1 collective-permute-start.16
  62.5 4.6 %collective-permute-done.13 = bf16[2,216,256]{2,1,0:T(8,128)(2,1)S(1)} collective-permute-done((bf16[2,216,256]{2,1,0:T(8,128)(2,1)S(1)}, bf16[2,216,256]{2,1,0:T(8,128)(2,1)S(1)}, u32[]{:S(2)}, u32[]{:S(2)}) %collective-permute-start.13) | collective-permute-done | bytes 221216 | tf_op jit(solution)/shard_map/ppermute | solution.py:284
  67.1 0.1 convert_add_fusion.4
  67.2 0.1 collective-permute-start.14
  67.2 0.3 collective-permute-done.16
  67.6 2.1 %collective-permute-start.17 = (bf16[1,64,512]{2,1,0:T(8,128)(2,1)S(1)}, bf16[1,64,512]{2,1,0:T(8,128)(2,1)S(1)}, u32[]{:S(2)}, u32[]{:S(2)}) collective-permute-start(bf16[1,64,512]{2,1,0:T(8,128)(2,1)S(1)} %slice.106), channel_id=1, source_target_pairs={{0,16},{1,17},{2,18},{3,19},{4,20},{5,21},{6,22},{7,23},{8,24},{9,... | collective-permute-start | bytes 196616 | tf_op jit(solution)/shard_map/ppermute | solution.py:284
  69.7 3.5 %collective-permute-done.14 = bf16[1,216,256]{2,1,0:T(8,128)(2,1)S(1)} collective-permute-done((bf16[1,216,256]{2,1,0:T(8,128)(2,1)S(1)}, bf16[1,216,256]{2,1,0:T(8,128)(2,1)S(1)}, u32[]{:S(2)}, u32[]{:S(2)}) %collective-permute-start.14) | collective-permute-done | bytes 110624 | tf_op jit(solution)/shard_map/ppermute | solution.py:284
  73.2 1.3 %collective-permute-start.15 = (bf16[1,216,256]{2,1,0:T(8,128)(2,1)S(1)}, bf16[1,216,256]{2,1,0:T(8,128)(2,1)S(1)}, u32[]{:S(2)}, u32[]{:S(2)}) collective-permute-start(bf16[1,216,256]{2,1,0:T(8,128)(2,1)S(1)} %fusion.1), channel_id=1, source_target_pairs={{0,16},{1,17},{2,18},{3,19},{4,20},{5,21},{6,22},{7,23},{24,8},{25... | collective-permute-start | bytes 331784 | tf_op jit(solution)/shard_map/ppermute | solution.py:284
  74.5 0.7 fusion.3
  75.2 5.5 %collective-permute-done.15 = bf16[1,216,256]{2,1,0:T(8,128)(2,1)S(1)} collective-permute-done((bf16[1,216,256]{2,1,0:T(8,128)(2,1)S(1)}, bf16[1,216,256]{2,1,0:T(8,128)(2,1)S(1)}, u32[]{:S(2)}, u32[]{:S(2)}) %collective-permute-start.15) | collective-permute-done | bytes 110624 | tf_op jit(solution)/shard_map/ppermute | solution.py:284
  80.7 0.1 multiply_bitcast_fusion
  80.8 0.8 copy.13
  (22 shorter events, 0.2 us)
Async XLA Ops:
  0.6 7.7 %collective-permute-start = (bf16[128,512]{1,0:T(8,128)(2,1)}, bf16[128,512]{1,0:T(8,128)(2,1)S(1)}, u32[]{:S(2)}, u32[]{:S(2)}) collective-permute-start(bf16[128,512]{1,0:T(8,128)(2,1)} %cur_in.1), channel_id=1, source_target_pairs={{0,1},{1,2},{2,3},{3,4},{4,5},{5,6},{6,7},{7,8},{8,9},{9,10},{10,1... | collective-permute-start | bytes 393224 | tf_op jit(solution)/shard_map/ppermute | solution.py:284
  2.6 1.6 %copy-start.1 = (bf16[2048,512]{1,0:T(8,128)(2,1)S(1)}, bf16[2048,512]{1,0:T(8,128)(2,1)}, u32[]{:S(2)}) copy-start(bf16[2048,512]{1,0:T(8,128)(2,1)} %w_in.1) | copy-start | bytes 6291460
  4.2 0.9 %copy-start.4 = (bf16[512,256]{1,0:T(8,128)(2,1)S(1)}, bf16[512,256]{1,0:T(8,128)(2,1)}, u32[]{:S(2)}) copy-start(bf16[512,256]{1,0:T(8,128)(2,1)} %pre.1) | copy-start | bytes 786436
  5.1 0.9 %copy-start.5 = (bf16[128,512]{1,0:T(8,128)(2,1)S(1)}, bf16[128,512]{1,0:T(8,128)(2,1)}, u32[]{:S(2)}) copy-start(bf16[128,512]{1,0:T(8,128)(2,1)} %cur_in.1) | copy-start | bytes 393220
  6.0 0.7 copy-start.8
  6.7 0.7 copy-start.9
  8.3 9.7 %copy-start = (bf16[6912,256]{1,0:T(8,128)(2,1)S(1)}, bf16[6912,256]{1,0:T(8,128)(2,1)}, u32[]{:S(2)}) copy-start(bf16[6912,256]{1,0:T(8,128)(2,1)} %refs_7_.3) | copy-start | bytes 10616836
  8.3 9.7 %copy-start.2 = (bf16[512,256]{1,0:T(8,128)(2,1)S(1)}, bf16[512,256]{1,0:T(8,128)(2,1)}, u32[]{:S(2)}) copy-start(bf16[512,256]{1,0:T(8,128)(2,1)} %refs_9_.1) | copy-start | bytes 786436
  8.3 9.7 %copy-start.3 = (s32[1,27,8,128]{3,2,1,0:T(8,128)S(1)}, s32[1,27,8,128]{3,2,1,0:T(8,128)}, u32[]{:S(2)}) copy-start(s32[1,27,8,128]{3,2,1,0:T(8,128)} %param.17) | copy-start | bytes 331780
  10.6 9.7 %collective-permute-start.3 = (bf16[16,64,512]{2,1,0:T(8,128)(2,1)S(1)}, bf16[16,64,512]{2,1,0:T(8,128)(2,1)S(1)}, u32[]{:S(2)}, u32[]{:S(2)}) collective-permute-start(bf16[16,64,512]{2,1,0:T(8,128)(2,1)S(1)} %get-tuple-element.60), channel_id=1, source_target_pairs={{0,1},{1,0},{2,3},{3,2},{4,5},{5,4},{6,7},{7,6},{8,9},{9,8},{10,11... | collective-permute-start | bytes 3145736 | tf_op jit(solution)/shard_map/ppermute | solution.py:284
  12.3 6.3 %collective-permute-start.1 = (bf16[256,256]{1,0:T(8,128)(2,1)S(1)}, bf16[256,256]{1,0:T(8,128)(2,1)S(1)}, u32[]{:S(2)}, u32[]{:S(2)}) collective-permute-start(bf16[256,256]{1,0:T(8,128)(2,1)S(1)} %get-tuple-element.55.refs_5_), channel_id=1, source_target_pairs={{0,1},{1,2},{2,3},{3,4},{4,5},{5,6},{6,7},{7,8},{8,9},{9,10},{10,1... | collective-permute-start | bytes 393224 | tf_op jit(solution)/shard_map/ppermute | solution.py:284
  14.2 6.1 %collective-permute-start.2 = (bf16[256,256]{1,0:T(8,128)(2,1)S(1)}, bf16[256,256]{1,0:T(8,128)(2,1)S(1)}, u32[]{:S(2)}, u32[]{:S(2)}) collective-permute-start(bf16[256,256]{1,0:T(8,128)(2,1)S(1)} %get-tuple-element.56.refs_4_), channel_id=1, source_target_pairs={{1,0},{2,1},{3,2},{4,3},{5,4},{6,5},{7,6},{8,7},{9,8},{10,9},{11,1... | collective-permute-start | bytes 393224 | tf_op jit(solution)/shard_map/ppermute | solution.py:284
  20.7 1.7 %copy-start.6 = (s32[1,27,8]{1,2,0:T(8,128)S(1)}, s32[1,27,8]{1,2,0:T(8,128)}, u32[]{:S(2)}) copy-start(s32[1,27,8]{1,2,0:T(8,128)} %param.15) | copy-start | bytes 2596
  20.7 1.7 %copy-start.7 = (s32[1,27,8]{1,2,0:T(8,128)S(1)}, s32[1,27,8]{1,2,0:T(8,128)}, u32[]{:S(2)}) copy-start(s32[1,27,8]{1,2,0:T(8,128)} %param.16) | copy-start | bytes 2596
  20.8 9.5 %collective-permute-start.4 = (bf16[8,64,512]{2,1,0:T(8,128)(2,1)S(1)}, bf16[8,64,512]{2,1,0:T(8,128)(2,1)S(1)}, u32[]{:S(2)}, u32[]{:S(2)}) collective-permute-start(bf16[8,64,512]{2,1,0:T(8,128)(2,1)S(1)} %slice.100), channel_id=1, source_target_pairs={{0,2},{1,5},{2,0},{3,7},{4,6},{5,1},{6,4},{7,3},{8,10},{9,13},{10,... | collective-permute-start | bytes 1572872 | tf_op jit(solution)/shard_map/ppermute | solution.py:284
  27.7 4.6 %collective-permute-start.5 = (bf16[8,216,256]{2,1,0:T(8,128)(2,1)S(1)}, bf16[8,216,256]{2,1,0:T(8,128)(2,1)S(1)}, u32[]{:S(2)}, u32[]{:S(2)}) collective-permute-start(bf16[8,216,256]{2,1,0:T(8,128)(2,1)S(1)} %get-tuple-element.70), channel_id=1, source_target_pairs={{0,1},{1,0},{2,3},{3,2},{4,5},{5,4},{6,7},{7,6},{8,9},{9,8},{10,11... | collective-permute-start | bytes 2654216 | tf_op jit(solution)/shard_map/ppermute | solution.py:284
  32.6 11.2 %collective-permute-start.6 = (bf16[4,216,256]{2,1,0:T(8,128)(2,1)S(1)}, bf16[4,216,256]{2,1,0:T(8,128)(2,1)S(1)}, u32[]{:S(2)}, u32[]{:S(2)}) collective-permute-start(bf16[4,216,256]{2,1,0:T(8,128)(2,1)S(1)} %slice.102), channel_id=1, source_target_pairs={{0,2},{1,5},{2,0},{3,7},{4,6},{5,1},{6,4},{7,3},{8,10},{9,13},{10,... | collective-permute-start | bytes 1327112 | tf_op jit(solution)/shard_map/ppermute | solution.py:284
  32.7 9.2 %collective-permute-start.7 = (bf16[4,64,512]{2,1,0:T(8,128)(2,1)S(1)}, bf16[4,64,512]{2,1,0:T(8,128)(2,1)S(1)}, u32[]{:S(2)}, u32[]{:S(2)}) collective-permute-start(bf16[4,64,512]{2,1,0:T(8,128)(2,1)S(1)} %get-tuple-element.80), channel_id=1, source_target_pairs={{0,4},{1,3},{2,6},{3,1},{4,0},{5,7},{6,2},{7,5},{8,12},{9,11},{10,... | collective-permute-start | bytes 786440 | tf_op jit(solution)/shard_map/ppermute | solution.py:284
  40.8 4.3 %collective-permute-start.11 = (bf16[8,216,256]{2,1,0:T(8,128)(2,1)S(1)}, bf16[8,216,256]{2,1,0:T(8,128)(2,1)S(1)}, u32[]{:S(2)}, u32[]{:S(2)}) collective-permute-start(bf16[8,216,256]{2,1,0:T(8,128)(2,1)S(1)} %get-tuple-element.87), channel_id=1, source_target_pairs={{0,1},{1,0},{2,3},{3,2},{4,5},{5,4},{6,7},{7,6},{8,9},{9,8},{10,11... | collective-permute-start | bytes 2654216 | tf_op jit(solution)/shard_map/ppermute | solution.py:284
  43.9 8.4 %collective-permute-start.8 = (bf16[2,216,256]{2,1,0:T(8,128)(2,1)S(1)}, bf16[2,216,256]{2,1,0:T(8,128)(2,1)S(1)}, u32[]{:S(2)}, u32[]{:S(2)}) collective-permute-start(bf16[2,216,256]{2,1,0:T(8,128)(2,1)S(1)} %get-tuple-element.85), channel_id=1, source_target_pairs={{0,4},{1,3},{2,6},{3,1},{4,0},{5,7},{6,2},{7,5},{8,12},{9,11},{10,... | collective-permute-start | bytes 663560 | tf_op jit(solution)/shard_map/ppermute | solution.py:284
  46.1 14.9 %collective-permute-start.12 = (bf16[4,216,256]{2,1,0:T(8,128)(2,1)}, bf16[4,216,256]{2,1,0:T(8,128)(2,1)S(1)}, u32[]{:S(2)}, u32[]{:S(2)}) collective-permute-start(bf16[4,216,256]{2,1,0:T(8,128)(2,1)} %slice.101), channel_id=1, source_target_pairs={{0,2},{1,5},{2,0},{3,7},{4,6},{5,1},{6,4},{7,3},{8,10},{9,13},{10,... | collective-permute-start | bytes 1327112 | tf_op jit(solution)/shard_map/ppermute | solution.py:284
  53.0 5.0 %collective-permute-start.9 = (bf16[1,216,256]{2,1,0:T(8,128)(2,1)}, bf16[1,216,256]{2,1,0:T(8,128)(2,1)S(1)}, u32[]{:S(2)}, u32[]{:S(2)}) collective-permute-start(bf16[1,216,256]{2,1,0:T(8,128)(2,1)} %slice.105), channel_id=1, source_target_pairs={{0,8},{1,9},{2,10},{3,11},{4,12},{5,13},{6,14},{7,15},{8,0},{9,1},... | collective-permute-start | bytes 331784 | tf_op jit(solution)/shard_map/ppermute | solution.py:284
  57.9 17.2 %collective-permute-start.10 = (bf16[1,216,256]{2,1,0:T(8,128)(2,1)S(1)}, bf16[1,216,256]{2,1,0:T(8,128)(2,1)S(1)}, u32[]{:S(2)}, u32[]{:S(2)}) collective-permute-start(bf16[1,216,256]{2,1,0:T(8,128)(2,1)S(1)} %fusion), channel_id=1, source_target_pairs={{8,24},{9,25},{10,26},{11,27},{12,28},{13,29},{14,30},{15,31},{16,... | collective-permute-start | bytes 331784 | tf_op jit(solution)/shard_map/ppermute | solution.py:284
  61.1 6.0 %collective-permute-start.13 = (bf16[2,216,256]{2,1,0:T(8,128)(2,1)S(1)}, bf16[2,216,256]{2,1,0:T(8,128)(2,1)S(1)}, u32[]{:S(2)}, u32[]{:S(2)}) collective-permute-start(bf16[2,216,256]{2,1,0:T(8,128)(2,1)S(1)} %get-tuple-element.92), channel_id=1, source_target_pairs={{0,4},{1,3},{2,6},{3,1},{4,0},{5,7},{6,2},{7,5},{8,12},{9,11},{10,... | collective-permute-start | bytes 663560 | tf_op jit(solution)/shard_map/ppermute | solution.py:284
  62.4 5.2 %collective-permute-start.16 = (bf16[2,64,512]{2,1,0:T(8,128)(2,1)S(1)}, bf16[2,64,512]{2,1,0:T(8,128)(2,1)S(1)}, u32[]{:S(2)}, u32[]{:S(2)}) collective-permute-start(bf16[2,64,512]{2,1,0:T(8,128)(2,1)S(1)} %slice.103), channel_id=1, source_target_pairs={{0,8},{1,9},{2,10},{3,11},{4,12},{5,13},{6,14},{7,15},{8,0},{9,1},... | collective-permute-start | bytes 393224 | tf_op jit(solution)/shard_map/ppermute | solution.py:284
  67.2 6.0 %collective-permute-start.14 = (bf16[1,216,256]{2,1,0:T(8,128)(2,1)S(1)}, bf16[1,216,256]{2,1,0:T(8,128)(2,1)S(1)}, u32[]{:S(2)}, u32[]{:S(2)}) collective-permute-start(bf16[1,216,256]{2,1,0:T(8,128)(2,1)S(1)} %slice.104), channel_id=1, source_target_pairs={{0,8},{1,9},{2,10},{3,11},{4,12},{5,13},{6,14},{7,15},{8,0},{9,1},... | collective-permute-start | bytes 331784 | tf_op jit(solution)/shard_map/ppermute | solution.py:284
  67.6 6.9 %collective-permute-start.17 = (bf16[1,64,512]{2,1,0:T(8,128)(2,1)S(1)}, bf16[1,64,512]{2,1,0:T(8,128)(2,1)S(1)}, u32[]{:S(2)}, u32[]{:S(2)}) collective-permute-start(bf16[1,64,512]{2,1,0:T(8,128)(2,1)S(1)} %slice.106), channel_id=1, source_target_pairs={{0,16},{1,17},{2,18},{3,19},{4,20},{5,21},{6,22},{7,23},{8,24},{9,... | collective-permute-start | bytes 196616 | tf_op jit(solution)/shard_map/ppermute | solution.py:284
  73.2 7.5 %collective-permute-start.15 = (bf16[1,216,256]{2,1,0:T(8,128)(2,1)S(1)}, bf16[1,216,256]{2,1,0:T(8,128)(2,1)S(1)}, u32[]{:S(2)}, u32[]{:S(2)}) collective-permute-start(bf16[1,216,256]{2,1,0:T(8,128)(2,1)S(1)} %fusion.1), channel_id=1, source_target_pairs={{0,16},{1,17},{2,18},{3,19},{4,20},{5,21},{6,22},{7,23},{24,8},{25... | collective-permute-start | bytes 331784 | tf_op jit(solution)/shard_map/ppermute | solution.py:284

commit v9 on v8

--- a/solution.py
+++ b/solution.py
@@ -399,33 +399,36 @@
     inner_got = across(inner_send)
     outer, outer_send = middle(outer, outer_got)
     outer_got = xy(outer_send, bits - 1)
+    low, low_send = fold_long(low, low_got)
+    low_got = z_near(low_send)
+    inner_got, outer, low = pinned((inner_got, outer, low))
     inner, inner_send = fold(inner, inner_got)
-    inner_send, low, low_got = pinned((inner_send, low, low_got))
     inner_got = xy(inner_send, 0)
-    low, low_send = fold(low, low_got)
-    low_got = z_near(low_send)
-
-    outer, outer_send = fold(outer, outer_got)
+
+    outer, outer_send = fold_long(outer, outer_got)
     outer_got = z_near(outer_send)
+    inner_got, outer, low_got = pinned((inner_got, outer, low_got))
+    inner, inner_send = middle(inner, inner_got)
+    inner_got = xy(inner_send, bits - 1)
+
     low, low_send = fold(low, low_got)
     low_got = z_far(low_send)
-    inner, inner_send = middle(inner, inner_got)
-    inner_got = xy(inner_send, bits - 1)
-
+    outer = outer + outer_got.astype(F32)
+    outer_got = z_far(outer.astype(BF), (0, 3))
+    inner_got, outer, low_got = pinned((inner_got, outer, low_got))
     inner, inner_send = fold(inner, inner_got)
     inner_got = z_near(inner_send)
-
-    def last_step(kept, got, wanted):
-        total = kept + got.astype(F32)
-        return total + z_far(total.astype(BF), wanted).astype(F32)
+    inner = inner + inner_got.astype(F32)
+    low_sum = (low + low_got.astype(F32)).reshape(-1, out_width) * scale
+
+    outer_sum = outer + outer_got.astype(F32)
+    inner, outer_sum = pinned((inner, outer_sum))
+    inner_sum = inner + z_far(inner.astype(BF), (1, 2)).astype(F32)
 
     digit = me // near
     is_outer = (digit == 0) | (digit == 3)
-    outer_sum = last_step(outer, outer_got, (0, 3))
-    inner_sum = last_step(inner, inner_got, (1, 2))
     sub_sum = jnp.where(is_outer, outer_sum, inner_sum)
-    low_sum = (low + low_got.astype(F32)).reshape(-1, out_width)
-    return (grad_in, sub_sum.reshape(-1) * scale, low_sum * scale)
+    return (grad_in, sub_sum.reshape(-1) * scale, low_sum)
 
 
 def solution(mesh):

time: 82 us -> 82.4 us (level)
  the two profiles are of different devices: /device:TPU:14 before, /device:TPU:0 now
where the time goes in v9:
time: 82.4 us; the launch traced here: 81.5 us
  starting transfers between devices  32.6 us (40%)
  Pallas kernels  18.3 us (22%)
  waiting for transfers between devices  17.5 us (21%)
  local copies, waits for them, and re-layouts  10.4 us (13%)
  other arithmetic  1.7 us (2%)
  between operations  1.04 us (1%)
    ppermute x18, starting transfers between devices, moved(): lax.ppermute(x, 'space', [(i, j) for i, j in pairs if j is not None and 0...  32.6 us
    ppermute x18, waiting for transfers between devices, moved(): lax.ppermute(x, 'space', [(i, j) for i, j in pairs if j is not None and 0...  17.5 us
    pallas_call x2, Pallas kernels, conv(): pl.pallas_call(functools.partial(conv_kernel, conv_plan(kernel, channels,...  11.8 us
    unnamed x55, local copies, waits for them, and re-layouts  7.92 us
    pallas_call x5, Pallas kernels, fold_long(): pl.pallas_call(fold_kernel, out_shape=(jax.ShapeDtypeStruct(shape, F32),...  3.07 us
    slice x8, local copies, waits for them, and re-layouts, fold(): return (total[:half], total[half:].astype(BF))  2.48 us
    pallas_call x1, Pallas kernels, down(): pl.pallas_call(functools.partial(down_kernel, bits), out_shape=(side, sid...  2.22 us
  transfers between devices with their start and end apart: 18, of which 10 were waited for; matrix products, arithmetic and copies ran while one was open for 3% of the time, Pallas kernels for 20%

profile of v9, /device:TPU:0, one launch (start us, length us, event | category | flops | bytes accessed | tf_op | source)
XLA Modules:
  0.0 81.5 jit_solution(5324780632145593897)
XLA Ops:
  0.6 2.4 %collective-permute-start = (bf16[128,512]{1,0:T(8,128)(2,1)}, bf16[128,512]{1,0:T(8,128)(2,1)S(1)}, u32[]{:S(2)}, u32[]{:S(2)}) collective-permute-start(bf16[128,512]{1,0:T(8,128)(2,1)} %cur_in.1), channel_id=1, source_target_pairs={{0,1},{1,2},{2,3},{3,4},{4,5},{5,6},{6,7},{7,8},{8,9},{9,10},{10,1... | collective-permute-start | bytes 393224 | tf_op jit(solution)/shard_map/ppermute | solution.py:284
  3.0 1.6 %copy-done.1 = bf16[2048,512]{1,0:T(8,128)(2,1)S(1)} copy-done((bf16[2048,512]{1,0:T(8,128)(2,1)S(1)}, bf16[2048,512]{1,0:T(8,128)(2,1)}, u32[]{:S(2)}) %copy-start.1) | copy-done | bytes 2097176
  4.6 0.9 %copy-done.16 = bf16[512,256]{1,0:T(8,128)(2,1)S(1)} copy-done((bf16[512,256]{1,0:T(8,128)(2,1)S(1)}, bf16[512,256]{1,0:T(8,128)(2,1)}, u32[]{:S(2)}) %copy-start.16) | copy-done | bytes 262168
  5.6 0.9 %copy-done.17 = bf16[128,512]{1,0:T(8,128)(2,1)S(1)} copy-done((bf16[128,512]{1,0:T(8,128)(2,1)S(1)}, bf16[128,512]{1,0:T(8,128)(2,1)}, u32[]{:S(2)}) %copy-start.17) | copy-done | bytes 131096
  6.5 0.7 copy-done.22
  7.1 0.7 copy-done.23
  7.8 0.9 %prep.1 = (bf16[512,256]{1,0:T(8,128)(2,1)S(1)}, bf16[512,1024]{1,0:T(8,128)(2,1)S(1)}, bf16[1024,256]{1,0:T(8,128)(2,1)S(1)}, bf16[256,1024]{1,0:T(8,128)(2,1)S...) custom-call(bf16[512,256]{1,0:T(8,128)(2,1)S(1)} %copy-done.16, s32[8,128]{1,0:T(8,128)S(1)} %bitcast.21, ...), custom_call_target="tpu_custom_call" | custom-call | flops 1048576 | bytes 1024 | tf_op jit(solution)/shard_map/prep/pallas_call | solution.py:114
  8.8 0.6 copy-done.18
  9.4 0.9 %copy-done.19 = bf16[128,512]{1,0:T(8,128)(2,1)S(1)} copy-done((bf16[128,512]{1,0:T(8,128)(2,1)S(1)}, bf16[128,512]{1,0:T(8,128)(2,1)}, u32[]{:S(2)}) %copy-start.19) | copy-done | bytes 131096
  10.3 2.2 %down.1 = (bf16[256,256]{1,0:T(8,128)(2,1)S(1)}, bf16[256,256]{1,0:T(8,128)(2,1)S(1)}, bf16[16,64,512]{2,1,0:T(8,128)(2,1)S(1)}, bf16[16,64,512]{2,1,0:T(8,128)(2,1)S(1)}) custom-call(s32[1]{0:T(128)} %bitcast.me.refs_0_, bf16[128,512]{1,0:T(8,128)(2,1)S(1)} %copy-done.19, bf16[512,256]{1,0:T(8,128)(2,1)S(1)} %get-tuple-element.61.act, ...), custom_call_target="tpu_custom_call" | custom-call | flops 1048576 | bytes 1024 | tf_op jit(solution)/shard_map/down/pallas_call | solution.py:154
  12.6 2.7 %collective-permute-start.3 = (bf16[16,64,512]{2,1,0:T(8,128)(2,1)S(1)}, bf16[16,64,512]{2,1,0:T(8,128)(2,1)S(1)}, u32[]{:S(2)}, u32[]{:S(2)}) collective-permute-start(bf16[16,64,512]{2,1,0:T(8,128)(2,1)S(1)} %get-tuple-element.72), channel_id=1, source_target_pairs={{0,1},{1,0},{2,3},{3,2},{4,5},{5,4},{6,7},{7,6},{8,9},{9,8},{10,11... | collective-permute-start | bytes 3145736 | tf_op jit(solution)/shard_map/ppermute | solution.py:284
  15.2 1.9 %collective-permute-start.1 = (bf16[256,256]{1,0:T(8,128)(2,1)S(1)}, bf16[256,256]{1,0:T(8,128)(2,1)S(1)}, u32[]{:S(2)}, u32[]{:S(2)}) collective-permute-start(bf16[256,256]{1,0:T(8,128)(2,1)S(1)} %get-tuple-element.67.refs_5_), channel_id=1, source_target_pairs={{0,1},{1,2},{2,3},{3,4},{4,5},{5,6},{6,7},{7,8},{8,9},{9,10},{10,1... | collective-permute-start | bytes 393224 | tf_op jit(solution)/shard_map/ppermute | solution.py:284
  17.2 1.5 %collective-permute-start.2 = (bf16[256,256]{1,0:T(8,128)(2,1)S(1)}, bf16[256,256]{1,0:T(8,128)(2,1)S(1)}, u32[]{:S(2)}, u32[]{:S(2)}) collective-permute-start(bf16[256,256]{1,0:T(8,128)(2,1)S(1)} %get-tuple-element.68.refs_4_), channel_id=1, source_target_pairs={{1,0},{2,1},{3,2},{4,3},{5,4},{6,5},{7,6},{8,7},{9,8},{10,9},{11,1... | collective-permute-start | bytes 393224 | tf_op jit(solution)/shard_map/ppermute | solution.py:284
  18.7 0.3 turn.1
  19.0 0.0 copy-start.10
  19.0 2.5 %collective-permute-done.2.refs_6_ = bf16[256,256]{1,0:T(8,128)(2,1)S(1)} collective-permute-done((bf16[256,256]{1,0:T(8,128)(2,1)S(1)}, bf16[256,256]{1,0:T(8,128)(2,1)S(1)}, u32[]{:S(2)}, u32[]{:S(2)}) %collective-permute-start.2) | collective-permute-done | bytes 131104 | tf_op jit(solution)/shard_map/ppermute | solution.py:284
  21.5 0.3 convert_add_fusion
  21.9 0.1 slice.66
  21.9 3.4 %collective-permute-start.4 = (bf16[8,64,512]{2,1,0:T(8,128)(2,1)S(1)}, bf16[8,64,512]{2,1,0:T(8,128)(2,1)S(1)}, u32[]{:S(2)}, u32[]{:S(2)}) collective-permute-start(bf16[8,64,512]{2,1,0:T(8,128)(2,1)S(1)} %slice.66), channel_id=1, source_target_pairs={{0,2},{1,5},{2,0},{3,7},{4,6},{5,1},{6,4},{7,3},{8,10},{9,13},{10,... | collective-permute-start | bytes 1572872 | tf_op jit(solution)/shard_map/ppermute | solution.py:284
  25.3 0.1 slice.45.kept
  25.4 5.1 %conv.2 = (f32[512,256]{1,0:T(8,128)S(1)}, bf16[8,216,256]{2,1,0:T(8,128)(2,1)S(1)}, bf16[8,216,256]{2,1,0:T(8,128)(2,1)S(1)}) custom-call(s32[1]{0:T(128)} %bitcast.me.refs_0_, s32[8,27]{1,0:T(8,128)S(1)} %bitcast.17, s32[8,27]{1,0:T(8,128)S(1)} %bitcast.19, bf16[256,256]{1,0:T(8,128)(2,1)S(1)} %collective-permute-done.1.refs_3_, ...), custom_call_target="tpu_custom_call" | custom-call | flops 1048576 | bytes 1024 | tf_op jit(solution)/shard_map/conv/pallas_call | solution.py:257
  30.6 1.5 %collective-permute-start.5 = (bf16[8,216,256]{2,1,0:T(8,128)(2,1)S(1)}, bf16[8,216,256]{2,1,0:T(8,128)(2,1)S(1)}, u32[]{:S(2)}, u32[]{:S(2)}) collective-permute-start(bf16[8,216,256]{2,1,0:T(8,128)(2,1)S(1)} %get-tuple-element.82), channel_id=1, source_target_pairs={{0,1},{1,0},{2,3},{3,2},{4,5},{5,4},{6,7},{7,6},{8,9},{9,8},{10,11... | collective-permute-start | bytes 2654216 | tf_op jit(solution)/shard_map/ppermute | solution.py:284
  32.1 0.3 collective-permute-done.4.got
  32.5 0.8 fold.5
  33.3 0.9 %collective-permute-done.5 = bf16[8,216,256]{2,1,0:T(8,128)(2,1)S(1)} collective-permute-done((bf16[8,216,256]{2,1,0:T(8,128)(2,1)S(1)}, bf16[8,216,256]{2,1,0:T(8,128)(2,1)S(1)}, u32[]{:S(2)}, u32[]{:S(2)}) %collective-permute-start.5) | collective-permute-done | bytes 884768 | tf_op jit(solution)/shard_map/ppermute | solution.py:284
  34.2 0.2 convert_add_fusion.2
  34.4 0.9 %slice.68 = bf16[4,216,256]{2,1,0:T(8,128)(2,1)} slice(f32[8,216,256]{2,1,0:T(8,128)S(1)} %convert_add_fusion.2), slice={[4:8], [0:216], [0:256]} | slice | bytes 884736 | tf_op jit(solution)/shard_map/slice | solution.py:290
  35.3 0.5 copy-done.26
  35.8 3.3 %collective-permute-start.6 = (bf16[4,216,256]{2,1,0:T(8,128)(2,1)}, bf16[4,216,256]{2,1,0:T(8,128)(2,1)}, u32[]{:S(2)}, u32[]{:S(2)}) collective-permute-start(bf16[4,216,256]{2,1,0:T(8,128)(2,1)} %slice.68), channel_id=1, source_target_pairs={{0,2},{1,5},{2,0},{3,7},{4,6},{5,1},{6,4},{7,3},{8,10},{9,13},{10,... | collective-permute-start | bytes 1327112 | tf_op jit(solution)/shard_map/ppermute | solution.py:284
  39.1 0.7 collective-permute-start.7
  39.9 1.3 %slice.48.kept = f32[4,216,256]{2,1,0:T(8,128)S(1)} slice(f32[8,216,256]{2,1,0:T(8,128)} %copy-done.26), slice={[0:4], [0:216], [0:256]} | slice | bytes 1769472 | tf_op jit(solution)/shard_map/slice | solution.py:290
  41.2 0.0 copy-done.5
  41.2 0.0 copy-done.7
  41.2 0.0 copy-done.9
  41.3 0.0 copy-done.11
  41.3 0.0 copy-done.13
  41.3 0.0 copy-done.15
  41.4 6.7 %conv.3 = (bf16[512,256]{1,0:T(8,128)(2,1)}, bf16[8,216,256]{2,1,0:T(8,128)(2,1)S(1)}, bf16[8,216,256]{2,1,0:T(8,128)(2,1)S(1)}) custom-call(s32[1]{0:T(128)} %bitcast.me.refs_0_, s32[8,27]{1,0:T(8,128)S(1)} %bitcast.18, s32[8,27]{1,0:T(8,128)S(1)} %bitcast.20, bf16[256,256]{1,0:T(8,128)(2,1)S(1)} %copy-done.11, bf16[256,256]{1,0:T(8,128)(2,1)S(1)} %copy-done.7, ...), custom_call_target="tpu_custom_call" | custom-call | flops 1048576 | bytes 1024 | tf_op jit(solution)/shard_map/conv/pallas_call | solution.py:257
  48.0 1.0 %collective-permute-start.8 = (bf16[8,216,256]{2,1,0:T(8,128)(2,1)S(1)}, bf16[8,216,256]{2,1,0:T(8,128)(2,1)S(1)}, u32[]{:S(2)}, u32[]{:S(2)}) collective-permute-start(bf16[8,216,256]{2,1,0:T(8,128)(2,1)S(1)} %get-tuple-element.95), channel_id=1, source_target_pairs={{0,1},{1,0},{2,3},{3,2},{4,5},{5,4},{6,7},{7,6},{8,9},{9,8},{10,11... | collective-permute-start | bytes 2654216 | tf_op jit(solution)/shard_map/ppermute | solution.py:284
  49.1 1.1 %fold.6 = (f32[2,216,256]{2,1,0:T(8,128)S(1)}, bf16[2,216,256]{2,1,0:T(8,128)(2,1)S(1)}) custom-call(f32[4,216,256]{2,1,0:T(8,128)S(1)} %slice.48.kept, bf16[4,216,256]{2,1,0:T(8,128)(2,1)} %collective-permute-done.6.got), custom_call_target="tpu_custom_call" | custom-call | flops 12884901888 | bytes 1024 | tf_op jit(solution)/shard_map/fold/pallas_call | solution.py:301
  50.2 0.9 %collective-permute-start.10 = (bf16[2,216,256]{2,1,0:T(8,128)(2,1)S(1)}, bf16[2,216,256]{2,1,0:T(8,128)(2,1)S(1)}, u32[]{:S(2)}, u32[]{:S(2)}) collective-permute-start(bf16[2,216,256]{2,1,0:T(8,128)(2,1)S(1)} %get-tuple-element.104), channel_id=1, source_target_pairs={{0,4},{1,3},{2,6},{3,1},{4,0},{5,7},{6,2},{7,5},{8,12},{9,11},{10,... | collective-permute-start | bytes 663560 | tf_op jit(solution)/shard_map/ppermute | solution.py:284
  51.1 1.0 %fold.7 = (f32[2,64,512]{2,1,0:T(8,128)S(1)}, bf16[2,64,512]{2,1,0:T(8,128)(2,1)S(1)}) custom-call(f32[4,64,512]{2,1,0:T(8,128)S(1)} %copy-done.25, bf16[4,64,512]{2,1,0:T(8,128)(2,1)} %collective-permute-done.7.got), custom_call_target="tpu_custom_call" | custom-call | flops 12884901888 | bytes 1024 | tf_op jit(solution)/shard_map/fold/pallas_call | solution.py:301
  52.1 1.6 %collective-permute-start.11 = (bf16[2,64,512]{2,1,0:T(8,128)(2,1)S(1)}, bf16[2,64,512]{2,1,0:T(8,128)(2,1)S(1)}, u32[]{:S(2)}, u32[]{:S(2)}) collective-permute-start(bf16[2,64,512]{2,1,0:T(8,128)(2,1)S(1)} %get-tuple-element.106), channel_id=1, source_target_pairs={{0,8},{1,9},{2,10},{3,11},{4,12},{5,13},{6,14},{7,15},{8,0},{9,1},... | collective-permute-start | bytes 393224 | tf_op jit(solution)/shard_map/ppermute | solution.py:284
  53.7 0.2 convert_add_fusion.1
  54.0 1.5 %collective-permute-start.9 = (bf16[4,216,256]{2,1,0:T(8,128)(2,1)S(1)}, bf16[4,216,256]{2,1,0:T(8,128)(2,1)S(1)}, u32[]{:S(2)}, u32[]{:S(2)}) collective-permute-start(bf16[4,216,256]{2,1,0:T(8,128)(2,1)S(1)} %slice.67), channel_id=1, source_target_pairs={{0,2},{1,5},{2,0},{3,7},{4,6},{5,1},{6,4},{7,3},{8,10},{9,13},{10,... | collective-permute-start | bytes 1327112 | tf_op jit(solution)/shard_map/ppermute | solution.py:284
  55.5 0.7 collective-permute-done.10.got
  56.2 0.1 fold.8
  56.3 0.1 slice.49.kept
  56.3 2.8 %collective-permute-start.13 = (bf16[1,216,256]{2,1,0:T(8,128)(2,1)S(1)}, bf16[1,216,256]{2,1,0:T(8,128)(2,1)S(1)}, u32[]{:S(2)}, u32[]{:S(2)}) collective-permute-start(bf16[1,216,256]{2,1,0:T(8,128)(2,1)S(1)} %get-tuple-element.111), channel_id=1, source_target_pairs={{0,8},{1,9},{2,10},{3,11},{4,12},{5,13},{6,14},{7,15},{8,0},{9,1},... | collective-permute-start | bytes 331784 | tf_op jit(solution)/shard_map/ppermute | solution.py:284
  59.1 3.2 %collective-permute-done.9.got = bf16[4,216,256]{2,1,0:T(8,128)(2,1)S(1)} collective-permute-done((bf16[4,216,256]{2,1,0:T(8,128)(2,1)S(1)}, bf16[4,216,256]{2,1,0:T(8,128)(2,1)S(1)}, u32[]{:S(2)}, u32[]{:S(2)}) %collective-permute-start.9) | collective-permute-done | bytes 442400 | tf_op jit(solution)/shard_map/ppermute | solution.py:284
  62.4 2.2 %collective-permute-start.14 = (bf16[1,64,512]{2,1,0:T(8,128)(2,1)S(1)}, bf16[1,64,512]{2,1,0:T(8,128)(2,1)S(1)}, u32[]{:S(2)}, u32[]{:S(2)}) collective-permute-start(bf16[1,64,512]{2,1,0:T(8,128)(2,1)S(1)} %slice.70), channel_id=1, source_target_pairs={{0,16},{1,17},{2,18},{3,19},{4,20},{5,21},{6,22},{7,23},{8,24},{9,... | collective-permute-start | bytes 196616 | tf_op jit(solution)/shard_map/ppermute | solution.py:284
  64.7 0.1 fold.9
  64.7 0.4 collective-permute-start.12
  65.1 1.3 %collective-permute-start.16 = (bf16[1,216,256]{2,1,0:T(8,128)(2,1)S(1)}, bf16[1,216,256]{2,1,0:T(8,128)(2,1)S(1)}, u32[]{:S(2)}, u32[]{:S(2)}) collective-permute-start(bf16[1,216,256]{2,1,0:T(8,128)(2,1)S(1)} %get-tuple-element.119), channel_id=1, source_target_pairs={{8,24},{9,25},{10,26},{11,27},{12,28},{13,29},{14,30},{15,31},{16,... | collective-permute-start | bytes 331784 | tf_op jit(solution)/shard_map/ppermute | solution.py:284
  66.4 1.8 %collective-permute-done.14 = bf16[1,64,512]{2,1,0:T(8,128)(2,1)S(1)} collective-permute-done((bf16[1,64,512]{2,1,0:T(8,128)(2,1)S(1)}, bf16[1,64,512]{2,1,0:T(8,128)(2,1)S(1)}, u32[]{:S(2)}, u32[]{:S(2)}) %collective-permute-start.14) | collective-permute-done | bytes 65568 | tf_op jit(solution)/shard_map/ppermute | solution.py:284
  68.2 2.5 %collective-permute-done.12 = bf16[2,216,256]{2,1,0:T(8,128)(2,1)S(1)} collective-permute-done((bf16[2,216,256]{2,1,0:T(8,128)(2,1)S(1)}, bf16[2,216,256]{2,1,0:T(8,128)(2,1)S(1)}, u32[]{:S(2)}, u32[]{:S(2)}) %collective-permute-start.12) | collective-permute-done | bytes 221216 | tf_op jit(solution)/shard_map/ppermute | solution.py:284
  70.7 0.1 convert_add_fusion.3
  70.8 0.9 %collective-permute-start.15 = (bf16[1,216,256]{2,1,0:T(8,128)(2,1)S(1)}, bf16[1,216,256]{2,1,0:T(8,128)(2,1)S(1)}, u32[]{:S(2)}, u32[]{:S(2)}) collective-permute-start(bf16[1,216,256]{2,1,0:T(8,128)(2,1)S(1)} %slice.69), channel_id=1, source_target_pairs={{0,8},{1,9},{2,10},{3,11},{4,12},{5,13},{6,14},{7,15},{8,0},{9,1},... | collective-permute-start | bytes 331784 | tf_op jit(solution)/shard_map/ppermute | solution.py:284
  71.7 1.0 %collective-permute-done.16 = bf16[1,216,256]{2,1,0:T(8,128)(2,1)S(1)} collective-permute-done((bf16[1,216,256]{2,1,0:T(8,128)(2,1)S(1)}, bf16[1,216,256]{2,1,0:T(8,128)(2,1)S(1)}, u32[]{:S(2)}, u32[]{:S(2)}) %collective-permute-start.16) | collective-permute-done | bytes 110624 | tf_op jit(solution)/shard_map/ppermute | solution.py:284
  72.8 2.8 %collective-permute-done.15 = bf16[1,216,256]{2,1,0:T(8,128)(2,1)S(1)} collective-permute-done((bf16[1,216,256]{2,1,0:T(8,128)(2,1)S(1)}, bf16[1,216,256]{2,1,0:T(8,128)(2,1)S(1)}, u32[]{:S(2)}, u32[]{:S(2)}) %collective-permute-start.15) | collective-permute-done | bytes 110624 | tf_op jit(solution)/shard_map/ppermute | solution.py:284
  75.7 2.7 %collective-permute-start.17 = (bf16[1,216,256]{2,1,0:T(8,128)(2,1)S(1)}, bf16[1,216,256]{2,1,0:T(8,128)(2,1)S(1)}, u32[]{:S(2)}, u32[]{:S(2)}) collective-permute-start(bf16[1,216,256]{2,1,0:T(8,128)(2,1)S(1)} %convert_element_type.62), channel_id=1, source_target_pairs={{0,16},{1,17},{2,18},{3,19},{4,20},{5,21},{6,22},{7,23},{24,8},{25... | collective-permute-start | bytes 331784 | tf_op jit(solution)/shard_map/ppermute | solution.py:284
  78.3 0.7 fusion.1
  79.0 1.6 %collective-permute-done.17 = bf16[1,216,256]{2,1,0:T(8,128)(2,1)S(1)} collective-permute-done((bf16[1,216,256]{2,1,0:T(8,128)(2,1)S(1)}, bf16[1,216,256]{2,1,0:T(8,128)(2,1)S(1)}, u32[]{:S(2)}, u32[]{:S(2)}) %collective-permute-start.17) | collective-permute-done | bytes 110624 | tf_op jit(solution)/shard_map/ppermute | solution.py:284
  80.7 0.8 copy.13
  (56 shorter events, 0.3 us)
Async XLA Ops:
  0.6 8.1 %collective-permute-start = (bf16[128,512]{1,0:T(8,128)(2,1)}, bf16[128,512]{1,0:T(8,128)(2,1)S(1)}, u32[]{:S(2)}, u32[]{:S(2)}) collective-permute-start(bf16[128,512]{1,0:T(8,128)(2,1)} %cur_in.1), channel_id=1, source_target_pairs={{0,1},{1,2},{2,3},{3,4},{4,5},{5,6},{6,7},{7,8},{8,9},{9,10},{10,1... | collective-permute-start | bytes 393224 | tf_op jit(solution)/shard_map/ppermute | solution.py:284
  3.0 1.6 %copy-start.1 = (bf16[2048,512]{1,0:T(8,128)(2,1)S(1)}, bf16[2048,512]{1,0:T(8,128)(2,1)}, u32[]{:S(2)}) copy-start(bf16[2048,512]{1,0:T(8,128)(2,1)} %w_in.1) | copy-start | bytes 6291460
  4.6 0.9 %copy-start.16 = (bf16[512,256]{1,0:T(8,128)(2,1)S(1)}, bf16[512,256]{1,0:T(8,128)(2,1)}, u32[]{:S(2)}) copy-start(bf16[512,256]{1,0:T(8,128)(2,1)} %pre.1) | copy-start | bytes 786436
  5.6 0.9 %copy-start.17 = (bf16[128,512]{1,0:T(8,128)(2,1)S(1)}, bf16[128,512]{1,0:T(8,128)(2,1)}, u32[]{:S(2)}) copy-start(bf16[128,512]{1,0:T(8,128)(2,1)} %cur_in.1) | copy-start | bytes 393220
  6.5 0.7 copy-start.22
  7.1 0.7 copy-start.23
  8.7 0.7 copy-start.18
  9.4 0.9 %copy-start.19 = (bf16[128,512]{1,0:T(8,128)(2,1)S(1)}, bf16[128,512]{1,0:T(8,128)(2,1)}, u32[]{:S(2)}) copy-start(bf16[128,512]{1,0:T(8,128)(2,1)} %copy-done.18) | copy-start | bytes 393220
  10.3 8.3 %copy-start = (bf16[6912,256]{1,0:T(8,128)(2,1)S(1)}, bf16[6912,256]{1,0:T(8,128)(2,1)}, u32[]{:S(2)}) copy-start(bf16[6912,256]{1,0:T(8,128)(2,1)} %refs_7_.3) | copy-start | bytes 10616836
  10.3 8.3 %copy-start.2 = (bf16[512,256]{1,0:T(8,128)(2,1)S(1)}, bf16[512,256]{1,0:T(8,128)(2,1)}, u32[]{:S(2)}) copy-start(bf16[512,256]{1,0:T(8,128)(2,1)} %refs_9_.1) | copy-start | bytes 786436
  10.3 8.4 %copy-start.14 = (s32[1,27,8,128]{3,2,1,0:T(8,128)S(1)}, s32[1,27,8,128]{3,2,1,0:T(8,128)}, u32[]{:S(2)}) copy-start(s32[1,27,8,128]{3,2,1,0:T(8,128)} %param.17) | copy-start | bytes 331780
  12.5 12.8 %copy-start.6 = (bf16[256,256]{1,0:T(8,128)(2,1)}, bf16[256,256]{1,0:T(8,128)(2,1)S(1)}, u32[]{:S(2)}) copy-start(bf16[256,256]{1,0:T(8,128)(2,1)S(1)} %get-tuple-element.68.refs_4_) | copy-start | bytes 393220
  12.5 12.8 %copy-start.8 = (bf16[256,256]{1,0:T(8,128)(2,1)}, bf16[256,256]{1,0:T(8,128)(2,1)S(1)}, u32[]{:S(2)}) copy-start(bf16[256,256]{1,0:T(8,128)(2,1)S(1)} %get-tuple-element.67.refs_5_) | copy-start | bytes 393220
  12.6 8.9 %collective-permute-start.3 = (bf16[16,64,512]{2,1,0:T(8,128)(2,1)S(1)}, bf16[16,64,512]{2,1,0:T(8,128)(2,1)S(1)}, u32[]{:S(2)}, u32[]{:S(2)}) collective-permute-start(bf16[16,64,512]{2,1,0:T(8,128)(2,1)S(1)} %get-tuple-element.72), channel_id=1, source_target_pairs={{0,1},{1,0},{2,3},{3,2},{4,5},{5,4},{6,7},{7,6},{8,9},{9,8},{10,11... | collective-permute-start | bytes 3145736 | tf_op jit(solution)/shard_map/ppermute | solution.py:284
  15.2 3.8 %collective-permute-start.1 = (bf16[256,256]{1,0:T(8,128)(2,1)S(1)}, bf16[256,256]{1,0:T(8,128)(2,1)S(1)}, u32[]{:S(2)}, u32[]{:S(2)}) collective-permute-start(bf16[256,256]{1,0:T(8,128)(2,1)S(1)} %get-tuple-element.67.refs_5_), channel_id=1, source_target_pairs={{0,1},{1,2},{2,3},{3,4},{4,5},{5,6},{6,7},{7,8},{8,9},{9,10},{10,1... | collective-permute-start | bytes 393224 | tf_op jit(solution)/shard_map/ppermute | solution.py:284
  17.2 4.3 %collective-permute-start.2 = (bf16[256,256]{1,0:T(8,128)(2,1)S(1)}, bf16[256,256]{1,0:T(8,128)(2,1)S(1)}, u32[]{:S(2)}, u32[]{:S(2)}) collective-permute-start(bf16[256,256]{1,0:T(8,128)(2,1)S(1)} %get-tuple-element.68.refs_4_), channel_id=1, source_target_pairs={{1,0},{2,1},{3,2},{4,3},{5,4},{6,5},{7,6},{8,7},{9,8},{10,9},{11,1... | collective-permute-start | bytes 393224 | tf_op jit(solution)/shard_map/ppermute | solution.py:284
  19.0 6.4 %copy-start.10 = (bf16[256,256]{1,0:T(8,128)(2,1)}, bf16[256,256]{1,0:T(8,128)(2,1)S(1)}, u32[]{:S(2)}) copy-start(bf16[256,256]{1,0:T(8,128)(2,1)S(1)} %collective-permute-done.1.refs_3_) | copy-start | bytes 393220
  21.5 3.9 %copy-start.12 = (bf16[256,256]{1,0:T(8,128)(2,1)}, bf16[256,256]{1,0:T(8,128)(2,1)S(1)}, u32[]{:S(2)}) copy-start(bf16[256,256]{1,0:T(8,128)(2,1)S(1)} %collective-permute-done.2.refs_6_) | copy-start | bytes 393220
  21.8 3.6 %copy-start.20 = (s32[1,27,8]{1,2,0:T(8,128)S(1)}, s32[1,27,8]{1,2,0:T(8,128)}, u32[]{:S(2)}) copy-start(s32[1,27,8]{1,2,0:T(8,128)} %param.15) | copy-start | bytes 2596
  21.8 3.6 %copy-start.21 = (s32[1,27,8]{1,2,0:T(8,128)S(1)}, s32[1,27,8]{1,2,0:T(8,128)}, u32[]{:S(2)}) copy-start(s32[1,27,8]{1,2,0:T(8,128)} %param.16) | copy-start | bytes 2596
  21.9 10.5 %collective-permute-start.4 = (bf16[8,64,512]{2,1,0:T(8,128)(2,1)S(1)}, bf16[8,64,512]{2,1,0:T(8,128)(2,1)S(1)}, u32[]{:S(2)}, u32[]{:S(2)}) collective-permute-start(bf16[8,64,512]{2,1,0:T(8,128)(2,1)S(1)} %slice.66), channel_id=1, source_target_pairs={{0,2},{1,5},{2,0},{3,7},{4,6},{5,1},{6,4},{7,3},{8,10},{9,13},{10,... | collective-permute-start | bytes 1572872 | tf_op jit(solution)/shard_map/ppermute | solution.py:284
  30.6 2.7 %copy-start.4 = (f32[512,256]{1,0:T(8,128)}, f32[512,256]{1,0:T(8,128)S(1)}, u32[]{:S(2)}) copy-start(f32[512,256]{1,0:T(8,128)S(1)} %get-tuple-element.88.refs_10_) | copy-start | bytes 1572868
  30.6 3.6 %collective-permute-start.5 = (bf16[8,216,256]{2,1,0:T(8,128)(2,1)S(1)}, bf16[8,216,256]{2,1,0:T(8,128)(2,1)S(1)}, u32[]{:S(2)}, u32[]{:S(2)}) collective-permute-start(bf16[8,216,256]{2,1,0:T(8,128)(2,1)S(1)} %get-tuple-element.82), channel_id=1, source_target_pairs={{0,1},{1,0},{2,3},{3,2},{4,5},{5,4},{6,7},{7,6},{8,9},{9,8},{10,11... | collective-permute-start | bytes 2654216 | tf_op jit(solution)/shard_map/ppermute | solution.py:284
  33.3 1.2 %copy-start.24 = (f32[4,64,512]{2,1,0:T(8,128)}, f32[4,64,512]{2,1,0:T(8,128)S(1)}, u32[]{:S(2)}) copy-start(f32[4,64,512]{2,1,0:T(8,128)S(1)} %get-tuple-element.99.kept) | copy-start | bytes 1572868
  34.4 1.4 %copy-start.26 = (f32[8,216,256]{2,1,0:T(8,128)}, f32[8,216,256]{2,1,0:T(8,128)S(1)}, u32[]{:S(2)}) copy-start(f32[8,216,256]{2,1,0:T(8,128)S(1)} %convert_add_fusion.2) | copy-start | bytes 5308420
  35.8 13.2 %collective-permute-start.6 = (bf16[4,216,256]{2,1,0:T(8,128)(2,1)}, bf16[4,216,256]{2,1,0:T(8,128)(2,1)}, u32[]{:S(2)}, u32[]{:S(2)}) collective-permute-start(bf16[4,216,256]{2,1,0:T(8,128)(2,1)} %slice.68), channel_id=1, source_target_pairs={{0,2},{1,5},{2,0},{3,7},{4,6},{5,1},{6,4},{7,3},{8,10},{9,13},{10,... | collective-permute-start | bytes 1327112 | tf_op jit(solution)/shard_map/ppermute | solution.py:284
  39.1 9.9 %collective-permute-start.7 = (bf16[4,64,512]{2,1,0:T(8,128)(2,1)}, bf16[4,64,512]{2,1,0:T(8,128)(2,1)}, u32[]{:S(2)}, u32[]{:S(2)}) collective-permute-start(bf16[4,64,512]{2,1,0:T(8,128)(2,1)} %get-tuple-element.92), channel_id=1, source_target_pairs={{0,4},{1,3},{2,6},{3,1},{4,0},{5,7},{6,2},{7,5},{8,12},{9,11},{10,... | collective-permute-start | bytes 786440 | tf_op jit(solution)/shard_map/ppermute | solution.py:284
  39.8 1.4 %copy-start.3 = (bf16[512,256]{1,0:T(8,128)(2,1)S(1)}, bf16[512,256]{1,0:T(8,128)(2,1)}, u32[]{:S(2)}) copy-start(bf16[512,256]{1,0:T(8,128)(2,1)} %refs_9_.1) | copy-start | bytes 786436
  39.8 1.4 %copy-start.5 = (f32[512,256]{1,0:T(8,128)S(1)}, f32[512,256]{1,0:T(8,128)}, u32[]{:S(2)}) copy-start(f32[512,256]{1,0:T(8,128)} %copy-done.4) | copy-start | bytes 1572868
  39.8 1.4 %copy-start.7 = (bf16[256,256]{1,0:T(8,128)(2,1)S(1)}, bf16[256,256]{1,0:T(8,128)(2,1)}, u32[]{:S(2)}) copy-start(bf16[256,256]{1,0:T(8,128)(2,1)} %copy-done.6) | copy-start | bytes 393220
  39.8 1.4 %copy-start.9 = (bf16[256,256]{1,0:T(8,128)(2,1)S(1)}, bf16[256,256]{1,0:T(8,128)(2,1)}, u32[]{:S(2)}) copy-start(bf16[256,256]{1,0:T(8,128)(2,1)} %copy-done.8) | copy-start | bytes 393220
  39.8 1.5 %copy-start.11 = (bf16[256,256]{1,0:T(8,128)(2,1)S(1)}, bf16[256,256]{1,0:T(8,128)(2,1)}, u32[]{:S(2)}) copy-start(bf16[256,256]{1,0:T(8,128)(2,1)} %copy-done.10) | copy-start | bytes 393220
  39.8 1.5 %copy-start.13 = (bf16[256,256]{1,0:T(8,128)(2,1)S(1)}, bf16[256,256]{1,0:T(8,128)(2,1)}, u32[]{:S(2)}) copy-start(bf16[256,256]{1,0:T(8,128)(2,1)} %copy-done.12) | copy-start | bytes 393220
  39.9 1.5 %copy-start.15 = (s32[1,27,8,128]{3,2,1,0:T(8,128)S(1)}, s32[1,27,8,128]{3,2,1,0:T(8,128)}, u32[]{:S(2)}) copy-start(s32[1,27,8,128]{3,2,1,0:T(8,128)} %param.17) | copy-start | bytes 331780
  48.0 5.7 %collective-permute-start.8 = (bf16[8,216,256]{2,1,0:T(8,128)(2,1)S(1)}, bf16[8,216,256]{2,1,0:T(8,128)(2,1)S(1)}, u32[]{:S(2)}, u32[]{:S(2)}) collective-permute-start(bf16[8,216,256]{2,1,0:T(8,128)(2,1)S(1)} %get-tuple-element.95), channel_id=1, source_target_pairs={{0,1},{1,0},{2,3},{3,2},{4,5},{5,4},{6,7},{7,6},{8,9},{9,8},{10,11... | collective-permute-start | bytes 2654216 | tf_op jit(solution)/shard_map/ppermute | solution.py:284
  49.0 2.0 %copy-start.25 = (f32[4,64,512]{2,1,0:T(8,128)S(1)}, f32[4,64,512]{2,1,0:T(8,128)}, u32[]{:S(2)}) copy-start(f32[4,64,512]{2,1,0:T(8,128)} %copy-done.24) | copy-start | bytes 1572868
  50.2 6.0 %collective-permute-start.10 = (bf16[2,216,256]{2,1,0:T(8,128)(2,1)S(1)}, bf16[2,216,256]{2,1,0:T(8,128)(2,1)S(1)}, u32[]{:S(2)}, u32[]{:S(2)}) collective-permute-start(bf16[2,216,256]{2,1,0:T(8,128)(2,1)S(1)} %get-tuple-element.104), channel_id=1, source_target_pairs={{0,4},{1,3},{2,6},{3,1},{4,0},{5,7},{6,2},{7,5},{8,12},{9,11},{10,... | collective-permute-start | bytes 663560 | tf_op jit(solution)/shard_map/ppermute | solution.py:284
  52.1 7.1 %collective-permute-start.11 = (bf16[2,64,512]{2,1,0:T(8,128)(2,1)S(1)}, bf16[2,64,512]{2,1,0:T(8,128)(2,1)S(1)}, u32[]{:S(2)}, u32[]{:S(2)}) collective-permute-start(bf16[2,64,512]{2,1,0:T(8,128)(2,1)S(1)} %get-tuple-element.106), channel_id=1, source_target_pairs={{0,8},{1,9},{2,10},{3,11},{4,12},{5,13},{6,14},{7,15},{8,0},{9,1},... | collective-permute-start | bytes 393224 | tf_op jit(solution)/shard_map/ppermute | solution.py:284
  54.0 8.4 %collective-permute-start.9 = (bf16[4,216,256]{2,1,0:T(8,128)(2,1)S(1)}, bf16[4,216,256]{2,1,0:T(8,128)(2,1)S(1)}, u32[]{:S(2)}, u32[]{:S(2)}) collective-permute-start(bf16[4,216,256]{2,1,0:T(8,128)(2,1)S(1)} %slice.67), channel_id=1, source_target_pairs={{0,2},{1,5},{2,0},{3,7},{4,6},{5,1},{6,4},{7,3},{8,10},{9,13},{10,... | collective-permute-start | bytes 1327112 | tf_op jit(solution)/shard_map/ppermute | solution.py:284
  56.3 8.8 %collective-permute-start.13 = (bf16[1,216,256]{2,1,0:T(8,128)(2,1)S(1)}, bf16[1,216,256]{2,1,0:T(8,128)(2,1)S(1)}, u32[]{:S(2)}, u32[]{:S(2)}) collective-permute-start(bf16[1,216,256]{2,1,0:T(8,128)(2,1)S(1)} %get-tuple-element.111), channel_id=1, source_target_pairs={{0,8},{1,9},{2,10},{3,11},{4,12},{5,13},{6,14},{7,15},{8,0},{9,1},... | collective-permute-start | bytes 331784 | tf_op jit(solution)/shard_map/ppermute | solution.py:284
  62.4 5.8 %collective-permute-start.14 = (bf16[1,64,512]{2,1,0:T(8,128)(2,1)S(1)}, bf16[1,64,512]{2,1,0:T(8,128)(2,1)S(1)}, u32[]{:S(2)}, u32[]{:S(2)}) collective-permute-start(bf16[1,64,512]{2,1,0:T(8,128)(2,1)S(1)} %slice.70), channel_id=1, source_target_pairs={{0,16},{1,17},{2,18},{3,19},{4,20},{5,21},{6,22},{7,23},{8,24},{9,... | collective-permute-start | bytes 196616 | tf_op jit(solution)/shard_map/ppermute | solution.py:284
  64.7 6.0 %collective-permute-start.12 = (bf16[2,216,256]{2,1,0:T(8,128)(2,1)S(1)}, bf16[2,216,256]{2,1,0:T(8,128)(2,1)S(1)}, u32[]{:S(2)}, u32[]{:S(2)}) collective-permute-start(bf16[2,216,256]{2,1,0:T(8,128)(2,1)S(1)} %get-tuple-element.109), channel_id=1, source_target_pairs={{0,4},{1,3},{2,6},{3,1},{4,0},{5,7},{6,2},{7,5},{8,12},{9,11},{10,... | collective-permute-start | bytes 663560 | tf_op jit(solution)/shard_map/ppermute | solution.py:284
  65.1 7.6 %collective-permute-start.16 = (bf16[1,216,256]{2,1,0:T(8,128)(2,1)S(1)}, bf16[1,216,256]{2,1,0:T(8,128)(2,1)S(1)}, u32[]{:S(2)}, u32[]{:S(2)}) collective-permute-start(bf16[1,216,256]{2,1,0:T(8,128)(2,1)S(1)} %get-tuple-element.119), channel_id=1, source_target_pairs={{8,24},{9,25},{10,26},{11,27},{12,28},{13,29},{14,30},{15,31},{16,... | collective-permute-start | bytes 331784 | tf_op jit(solution)/shard_map/ppermute | solution.py:284
  70.8 4.8 %collective-permute-start.15 = (bf16[1,216,256]{2,1,0:T(8,128)(2,1)S(1)}, bf16[1,216,256]{2,1,0:T(8,128)(2,1)S(1)}, u32[]{:S(2)}, u32[]{:S(2)}) collective-permute-start(bf16[1,216,256]{2,1,0:T(8,128)(2,1)S(1)} %slice.69), channel_id=1, source_target_pairs={{0,8},{1,9},{2,10},{3,11},{4,12},{5,13},{6,14},{7,15},{8,0},{9,1},... | collective-permute-start | bytes 331784 | tf_op jit(solution)/shard_map/ppermute | solution.py:284
  75.7 5.0 %collective-permute-start.17 = (bf16[1,216,256]{2,1,0:T(8,128)(2,1)S(1)}, bf16[1,216,256]{2,1,0:T(8,128)(2,1)S(1)}, u32[]{:S(2)}, u32[]{:S(2)}) collective-permute-start(bf16[1,216,256]{2,1,0:T(8,128)(2,1)S(1)} %convert_element_type.62), channel_id=1, source_target_pairs={{0,16},{1,17},{2,18},{3,19},{4,20},{5,21},{6,22},{7,23},{24,8},{25... | collective-permute-start | bytes 331784 | tf_op jit(solution)/shard_map/ppermute | solution.py:284

commit v10 on v9

--- a/solution.py
+++ b/solution.py
@@ -304,7 +304,7 @@
         in_specs=[VMEM] * 2,
         out_specs=(VMEM,) * 2,
         compiler_params=pltpu.CompilerParams(vmem_limit_bytes=16 << 20),
-        cost_estimate=pl.CostEstimate(flops=12 << 30, bytes_accessed=1 << 10, transcendentals=0),
+        cost_estimate=pl.CostEstimate(flops=6 << 30, bytes_accessed=1 << 10, transcendentals=0),
         name="fold",
     )(kept, got)
 

time: 82.4 us -> 82.4 us (level)
  no operation moved by 1% of the time
where the time goes in v10:
time: 82.4 us; the launch traced here: 81.5 us
  starting transfers between devices  32.4 us (39%)
  Pallas kernels  18.3 us (22%)
  waiting for transfers between devices  17.7 us (21%)
  local copies, waits for them, and re-layouts  10.4 us (13%)
  other arithmetic  1.7 us (2%)
  between operations  1.01 us (1%)
    ppermute x18, starting transfers between devices, moved(): lax.ppermute(x, 'space', [(i, j) for i, j in pairs if j is not None and 0...  32.4 us
    ppermute x18, waiting for transfers between devices, moved(): lax.ppermute(x, 'space', [(i, j) for i, j in pairs if j is not None and 0...  17.7 us
    pallas_call x2, Pallas kernels, conv(): pl.pallas_call(functools.partial(conv_kernel, conv_plan(kernel, channels,...  11.8 us
    unnamed x55, local copies, waits for them, and re-layouts  7.91 us
    pallas_call x5, Pallas kernels, fold_long(): pl.pallas_call(fold_kernel, out_shape=(jax.ShapeDtypeStruct(shape, F32),...  3.07 us
    slice x8, local copies, waits for them, and re-layouts, fold(): return (total[:half], total[half:].astype(BF))  2.48 us
    pallas_call x1, Pallas kernels, down(): pl.pallas_call(functools.partial(down_kernel, bits), out_shape=(side, sid...  2.22 us
  transfers between devices with their start and end apart: 18, of which 10 were waited for; matrix products, arithmetic and copies ran while one was open for 3% of the time, Pallas kernels for 20%

profile of v10, /device:TPU:0, one launch (start us, length us, event | category | flops | bytes accessed | tf_op | source)
XLA Modules:
  0.0 81.5 jit_solution(12746503626158527085)
XLA Ops:
  0.6 2.4 %collective-permute-start = (bf16[128,512]{1,0:T(8,128)(2,1)}, bf16[128,512]{1,0:T(8,128)(2,1)S(1)}, u32[]{:S(2)}, u32[]{:S(2)}) collective-permute-start(bf16[128,512]{1,0:T(8,128)(2,1)} %cur_in.1), channel_id=1, source_target_pairs={{0,1},{1,2},{2,3},{3,4},{4,5},{5,6},{6,7},{7,8},{8,9},{9,10},{10,1... | collective-permute-start | bytes 393224 | tf_op jit(solution)/shard_map/ppermute | solution.py:284
  3.0 1.6 %copy-done.1 = bf16[2048,512]{1,0:T(8,128)(2,1)S(1)} copy-done((bf16[2048,512]{1,0:T(8,128)(2,1)S(1)}, bf16[2048,512]{1,0:T(8,128)(2,1)}, u32[]{:S(2)}) %copy-start.1) | copy-done | bytes 2097176
  4.6 0.9 %copy-done.16 = bf16[512,256]{1,0:T(8,128)(2,1)S(1)} copy-done((bf16[512,256]{1,0:T(8,128)(2,1)S(1)}, bf16[512,256]{1,0:T(8,128)(2,1)}, u32[]{:S(2)}) %copy-start.16) | copy-done | bytes 262168
  5.6 0.9 %copy-done.17 = bf16[128,512]{1,0:T(8,128)(2,1)S(1)} copy-done((bf16[128,512]{1,0:T(8,128)(2,1)S(1)}, bf16[128,512]{1,0:T(8,128)(2,1)}, u32[]{:S(2)}) %copy-start.17) | copy-done | bytes 131096
  6.5 0.7 copy-done.22
  7.1 0.7 copy-done.23
  7.8 0.9 %prep.1 = (bf16[512,256]{1,0:T(8,128)(2,1)S(1)}, bf16[512,1024]{1,0:T(8,128)(2,1)S(1)}, bf16[1024,256]{1,0:T(8,128)(2,1)S(1)}, bf16[256,1024]{1,0:T(8,128)(2,1)S...) custom-call(bf16[512,256]{1,0:T(8,128)(2,1)S(1)} %copy-done.16, s32[8,128]{1,0:T(8,128)S(1)} %bitcast.21, ...), custom_call_target="tpu_custom_call" | custom-call | flops 1048576 | bytes 1024 | tf_op jit(solution)/shard_map/prep/pallas_call | solution.py:114
  8.7 0.0 copy-start.18
  8.8 0.6 copy-done.18
  9.4 0.9 %copy-done.19 = bf16[128,512]{1,0:T(8,128)(2,1)S(1)} copy-done((bf16[128,512]{1,0:T(8,128)(2,1)S(1)}, bf16[128,512]{1,0:T(8,128)(2,1)}, u32[]{:S(2)}) %copy-start.19) | copy-done | bytes 131096
  10.3 2.2 %down.1 = (bf16[256,256]{1,0:T(8,128)(2,1)S(1)}, bf16[256,256]{1,0:T(8,128)(2,1)S(1)}, bf16[16,64,512]{2,1,0:T(8,128)(2,1)S(1)}, bf16[16,64,512]{2,1,0:T(8,128)(2,1)S(1)}) custom-call(s32[1]{0:T(128)} %bitcast.me.refs_0_, bf16[128,512]{1,0:T(8,128)(2,1)S(1)} %copy-done.19, bf16[512,256]{1,0:T(8,128)(2,1)S(1)} %get-tuple-element.61.act, ...), custom_call_target="tpu_custom_call" | custom-call | flops 1048576 | bytes 1024 | tf_op jit(solution)/shard_map/down/pallas_call | solution.py:154
  12.6 2.7 %collective-permute-start.3 = (bf16[16,64,512]{2,1,0:T(8,128)(2,1)S(1)}, bf16[16,64,512]{2,1,0:T(8,128)(2,1)S(1)}, u32[]{:S(2)}, u32[]{:S(2)}) collective-permute-start(bf16[16,64,512]{2,1,0:T(8,128)(2,1)S(1)} %get-tuple-element.72), channel_id=1, source_target_pairs={{0,1},{1,0},{2,3},{3,2},{4,5},{5,4},{6,7},{7,6},{8,9},{9,8},{10,11... | collective-permute-start | bytes 3145736 | tf_op jit(solution)/shard_map/ppermute | solution.py:284
  15.2 1.9 %collective-permute-start.1 = (bf16[256,256]{1,0:T(8,128)(2,1)S(1)}, bf16[256,256]{1,0:T(8,128)(2,1)S(1)}, u32[]{:S(2)}, u32[]{:S(2)}) collective-permute-start(bf16[256,256]{1,0:T(8,128)(2,1)S(1)} %get-tuple-element.67.refs_5_), channel_id=1, source_target_pairs={{0,1},{1,2},{2,3},{3,4},{4,5},{5,6},{6,7},{7,8},{8,9},{9,10},{10,1... | collective-permute-start | bytes 393224 | tf_op jit(solution)/shard_map/ppermute | solution.py:284
  17.2 1.5 %collective-permute-start.2 = (bf16[256,256]{1,0:T(8,128)(2,1)S(1)}, bf16[256,256]{1,0:T(8,128)(2,1)S(1)}, u32[]{:S(2)}, u32[]{:S(2)}) collective-permute-start(bf16[256,256]{1,0:T(8,128)(2,1)S(1)} %get-tuple-element.68.refs_4_), channel_id=1, source_target_pairs={{1,0},{2,1},{3,2},{4,3},{5,4},{6,5},{7,6},{8,7},{9,8},{10,9},{11,1... | collective-permute-start | bytes 393224 | tf_op jit(solution)/shard_map/ppermute | solution.py:284
  18.7 0.3 turn.1
  19.0 2.5 %collective-permute-done.2.refs_6_ = bf16[256,256]{1,0:T(8,128)(2,1)S(1)} collective-permute-done((bf16[256,256]{1,0:T(8,128)(2,1)S(1)}, bf16[256,256]{1,0:T(8,128)(2,1)S(1)}, u32[]{:S(2)}, u32[]{:S(2)}) %collective-permute-start.2) | collective-permute-done | bytes 131104 | tf_op jit(solution)/shard_map/ppermute | solution.py:284
  21.5 0.3 convert_add_fusion
  21.8 0.1 slice.66
  21.9 3.4 %collective-permute-start.4 = (bf16[8,64,512]{2,1,0:T(8,128)(2,1)S(1)}, bf16[8,64,512]{2,1,0:T(8,128)(2,1)S(1)}, u32[]{:S(2)}, u32[]{:S(2)}) collective-permute-start(bf16[8,64,512]{2,1,0:T(8,128)(2,1)S(1)} %slice.66), channel_id=1, source_target_pairs={{0,2},{1,5},{2,0},{3,7},{4,6},{5,1},{6,4},{7,3},{8,10},{9,13},{10,... | collective-permute-start | bytes 1572872 | tf_op jit(solution)/shard_map/ppermute | solution.py:284
  25.3 5.2 %conv.2 = (f32[512,256]{1,0:T(8,128)S(1)}, bf16[8,216,256]{2,1,0:T(8,128)(2,1)S(1)}, bf16[8,216,256]{2,1,0:T(8,128)(2,1)S(1)}) custom-call(s32[1]{0:T(128)} %bitcast.me.refs_0_, s32[8,27]{1,0:T(8,128)S(1)} %bitcast.17, s32[8,27]{1,0:T(8,128)S(1)} %bitcast.19, bf16[256,256]{1,0:T(8,128)(2,1)S(1)} %collective-permute-done.1.refs_3_, ...), custom_call_target="tpu_custom_call" | custom-call | flops 1048576 | bytes 1024 | tf_op jit(solution)/shard_map/conv/pallas_call | solution.py:257
  30.5 1.5 %collective-permute-start.5 = (bf16[8,216,256]{2,1,0:T(8,128)(2,1)S(1)}, bf16[8,216,256]{2,1,0:T(8,128)(2,1)S(1)}, u32[]{:S(2)}, u32[]{:S(2)}) collective-permute-start(bf16[8,216,256]{2,1,0:T(8,128)(2,1)S(1)} %get-tuple-element.82), channel_id=1, source_target_pairs={{0,1},{1,0},{2,3},{3,2},{4,5},{5,4},{6,7},{7,6},{8,9},{9,8},{10,11... | collective-permute-start | bytes 2654216 | tf_op jit(solution)/shard_map/ppermute | solution.py:284
  32.0 0.1 slice.45.kept
  32.1 0.3 collective-permute-done.4.got
  32.4 0.8 fold.5
  33.2 0.8 %collective-permute-done.5 = bf16[8,216,256]{2,1,0:T(8,128)(2,1)S(1)} collective-permute-done((bf16[8,216,256]{2,1,0:T(8,128)(2,1)S(1)}, bf16[8,216,256]{2,1,0:T(8,128)(2,1)S(1)}, u32[]{:S(2)}, u32[]{:S(2)}) %collective-permute-start.5) | collective-permute-done | bytes 884768 | tf_op jit(solution)/shard_map/ppermute | solution.py:284
  34.1 0.2 convert_add_fusion.2
  34.3 0.9 %slice.68 = bf16[4,216,256]{2,1,0:T(8,128)(2,1)} slice(f32[8,216,256]{2,1,0:T(8,128)S(1)} %convert_add_fusion.2), slice={[4:8], [0:216], [0:256]} | slice | bytes 884736 | tf_op jit(solution)/shard_map/slice | solution.py:290
  35.2 0.5 copy-done.26
  35.7 3.3 %collective-permute-start.6 = (bf16[4,216,256]{2,1,0:T(8,128)(2,1)}, bf16[4,216,256]{2,1,0:T(8,128)(2,1)}, u32[]{:S(2)}, u32[]{:S(2)}) collective-permute-start(bf16[4,216,256]{2,1,0:T(8,128)(2,1)} %slice.68), channel_id=1, source_target_pairs={{0,2},{1,5},{2,0},{3,7},{4,6},{5,1},{6,4},{7,3},{8,10},{9,13},{10,... | collective-permute-start | bytes 1327112 | tf_op jit(solution)/shard_map/ppermute | solution.py:284
  39.0 0.5 collective-permute-start.7
  39.6 1.3 %slice.48.kept = f32[4,216,256]{2,1,0:T(8,128)S(1)} slice(f32[8,216,256]{2,1,0:T(8,128)} %copy-done.26), slice={[0:4], [0:216], [0:256]} | slice | bytes 1769472 | tf_op jit(solution)/shard_map/slice | solution.py:290
  40.9 0.0 copy-done.5
  40.9 0.0 copy-done.7
  40.9 0.0 copy-done.9
  41.0 0.0 copy-done.11
  41.0 0.0 copy-done.13
  41.0 0.0 copy-done.15
  41.1 6.7 %conv.3 = (bf16[512,256]{1,0:T(8,128)(2,1)}, bf16[8,216,256]{2,1,0:T(8,128)(2,1)S(1)}, bf16[8,216,256]{2,1,0:T(8,128)(2,1)S(1)}) custom-call(s32[1]{0:T(128)} %bitcast.me.refs_0_, s32[8,27]{1,0:T(8,128)S(1)} %bitcast.18, s32[8,27]{1,0:T(8,128)S(1)} %bitcast.20, bf16[256,256]{1,0:T(8,128)(2,1)S(1)} %copy-done.11, bf16[256,256]{1,0:T(8,128)(2,1)S(1)} %copy-done.7, ...), custom_call_target="tpu_custom_call" | custom-call | flops 1048576 | bytes 1024 | tf_op jit(solution)/shard_map/conv/pallas_call | solution.py:257
  47.7 1.3 %collective-permute-start.8 = (bf16[8,216,256]{2,1,0:T(8,128)(2,1)S(1)}, bf16[8,216,256]{2,1,0:T(8,128)(2,1)S(1)}, u32[]{:S(2)}, u32[]{:S(2)}) collective-permute-start(bf16[8,216,256]{2,1,0:T(8,128)(2,1)S(1)} %get-tuple-element.95), channel_id=1, source_target_pairs={{0,1},{1,0},{2,3},{3,2},{4,5},{5,4},{6,7},{7,6},{8,9},{9,8},{10,11... | collective-permute-start | bytes 2654216 | tf_op jit(solution)/shard_map/ppermute | solution.py:284
  49.0 1.1 %fold.6 = (f32[2,216,256]{2,1,0:T(8,128)S(1)}, bf16[2,216,256]{2,1,0:T(8,128)(2,1)S(1)}) custom-call(f32[4,216,256]{2,1,0:T(8,128)S(1)} %slice.48.kept, bf16[4,216,256]{2,1,0:T(8,128)(2,1)} %collective-permute-done.6.got), custom_call_target="tpu_custom_call" | custom-call | flops 6442450944 | bytes 1024 | tf_op jit(solution)/shard_map/fold/pallas_call | solution.py:301
  50.2 0.8 %collective-permute-start.10 = (bf16[2,216,256]{2,1,0:T(8,128)(2,1)S(1)}, bf16[2,216,256]{2,1,0:T(8,128)(2,1)S(1)}, u32[]{:S(2)}, u32[]{:S(2)}) collective-permute-start(bf16[2,216,256]{2,1,0:T(8,128)(2,1)S(1)} %get-tuple-element.104), channel_id=1, source_target_pairs={{0,4},{1,3},{2,6},{3,1},{4,0},{5,7},{6,2},{7,5},{8,12},{9,11},{10,... | collective-permute-start | bytes 663560 | tf_op jit(solution)/shard_map/ppermute | solution.py:284
  51.0 1.0 %fold.7 = (f32[2,64,512]{2,1,0:T(8,128)S(1)}, bf16[2,64,512]{2,1,0:T(8,128)(2,1)S(1)}) custom-call(f32[4,64,512]{2,1,0:T(8,128)S(1)} %copy-done.25, bf16[4,64,512]{2,1,0:T(8,128)(2,1)} %collective-permute-done.7.got), custom_call_target="tpu_custom_call" | custom-call | flops 6442450944 | bytes 1024 | tf_op jit(solution)/shard_map/fold/pallas_call | solution.py:301
  52.0 1.6 %collective-permute-start.11 = (bf16[2,64,512]{2,1,0:T(8,128)(2,1)S(1)}, bf16[2,64,512]{2,1,0:T(8,128)(2,1)S(1)}, u32[]{:S(2)}, u32[]{:S(2)}) collective-permute-start(bf16[2,64,512]{2,1,0:T(8,128)(2,1)S(1)} %get-tuple-element.106), channel_id=1, source_target_pairs={{0,8},{1,9},{2,10},{3,11},{4,12},{5,13},{6,14},{7,15},{8,0},{9,1},... | collective-permute-start | bytes 393224 | tf_op jit(solution)/shard_map/ppermute | solution.py:284
  53.7 0.2 convert_add_fusion.1
  54.0 1.2 %collective-permute-start.9 = (bf16[4,216,256]{2,1,0:T(8,128)(2,1)S(1)}, bf16[4,216,256]{2,1,0:T(8,128)(2,1)S(1)}, u32[]{:S(2)}, u32[]{:S(2)}) collective-permute-start(bf16[4,216,256]{2,1,0:T(8,128)(2,1)S(1)} %slice.67), channel_id=1, source_target_pairs={{0,2},{1,5},{2,0},{3,7},{4,6},{5,1},{6,4},{7,3},{8,10},{9,13},{10,... | collective-permute-start | bytes 1327112 | tf_op jit(solution)/shard_map/ppermute | solution.py:284
  55.2 1.0 %collective-permute-done.10.got = bf16[2,216,256]{2,1,0:T(8,128)(2,1)S(1)} collective-permute-done((bf16[2,216,256]{2,1,0:T(8,128)(2,1)S(1)}, bf16[2,216,256]{2,1,0:T(8,128)(2,1)S(1)}, u32[]{:S(2)}, u32[]{:S(2)}) %collective-permute-start.10) | collective-permute-done | bytes 221216 | tf_op jit(solution)/shard_map/ppermute | solution.py:284
  56.2 0.1 fold.8
  56.3 0.1 slice.49.kept
  56.3 2.8 %collective-permute-start.13 = (bf16[1,216,256]{2,1,0:T(8,128)(2,1)S(1)}, bf16[1,216,256]{2,1,0:T(8,128)(2,1)S(1)}, u32[]{:S(2)}, u32[]{:S(2)}) collective-permute-start(bf16[1,216,256]{2,1,0:T(8,128)(2,1)S(1)} %get-tuple-element.111), channel_id=1, source_target_pairs={{0,8},{1,9},{2,10},{3,11},{4,12},{5,13},{6,14},{7,15},{8,0},{9,1},... | collective-permute-start | bytes 331784 | tf_op jit(solution)/shard_map/ppermute | solution.py:284
  59.1 3.2 %collective-permute-done.9.got = bf16[4,216,256]{2,1,0:T(8,128)(2,1)S(1)} collective-permute-done((bf16[4,216,256]{2,1,0:T(8,128)(2,1)S(1)}, bf16[4,216,256]{2,1,0:T(8,128)(2,1)S(1)}, u32[]{:S(2)}, u32[]{:S(2)}) %collective-permute-start.9) | collective-permute-done | bytes 442400 | tf_op jit(solution)/shard_map/ppermute | solution.py:284
  62.4 2.2 %collective-permute-start.14 = (bf16[1,64,512]{2,1,0:T(8,128)(2,1)S(1)}, bf16[1,64,512]{2,1,0:T(8,128)(2,1)S(1)}, u32[]{:S(2)}, u32[]{:S(2)}) collective-permute-start(bf16[1,64,512]{2,1,0:T(8,128)(2,1)S(1)} %slice.70), channel_id=1, source_target_pairs={{0,16},{1,17},{2,18},{3,19},{4,20},{5,21},{6,22},{7,23},{8,24},{9,... | collective-permute-start | bytes 196616 | tf_op jit(solution)/shard_map/ppermute | solution.py:284
  64.6 0.1 fold.9
  64.7 0.4 collective-permute-start.12
  65.1 1.3 %collective-permute-start.16 = (bf16[1,216,256]{2,1,0:T(8,128)(2,1)S(1)}, bf16[1,216,256]{2,1,0:T(8,128)(2,1)S(1)}, u32[]{:S(2)}, u32[]{:S(2)}) collective-permute-start(bf16[1,216,256]{2,1,0:T(8,128)(2,1)S(1)} %get-tuple-element.119), channel_id=1, source_target_pairs={{8,24},{9,25},{10,26},{11,27},{12,28},{13,29},{14,30},{15,31},{16,... | collective-permute-start | bytes 331784 | tf_op jit(solution)/shard_map/ppermute | solution.py:284
  66.4 1.8 %collective-permute-done.14 = bf16[1,64,512]{2,1,0:T(8,128)(2,1)S(1)} collective-permute-done((bf16[1,64,512]{2,1,0:T(8,128)(2,1)S(1)}, bf16[1,64,512]{2,1,0:T(8,128)(2,1)S(1)}, u32[]{:S(2)}, u32[]{:S(2)}) %collective-permute-start.14) | collective-permute-done | bytes 65568 | tf_op jit(solution)/shard_map/ppermute | solution.py:284
  68.2 2.5 %collective-permute-done.12 = bf16[2,216,256]{2,1,0:T(8,128)(2,1)S(1)} collective-permute-done((bf16[2,216,256]{2,1,0:T(8,128)(2,1)S(1)}, bf16[2,216,256]{2,1,0:T(8,128)(2,1)S(1)}, u32[]{:S(2)}, u32[]{:S(2)}) %collective-permute-start.12) | collective-permute-done | bytes 221216 | tf_op jit(solution)/shard_map/ppermute | solution.py:284
  70.7 0.1 convert_add_fusion.3
  70.8 0.9 %collective-permute-start.15 = (bf16[1,216,256]{2,1,0:T(8,128)(2,1)S(1)}, bf16[1,216,256]{2,1,0:T(8,128)(2,1)S(1)}, u32[]{:S(2)}, u32[]{:S(2)}) collective-permute-start(bf16[1,216,256]{2,1,0:T(8,128)(2,1)S(1)} %slice.69), channel_id=1, source_target_pairs={{0,8},{1,9},{2,10},{3,11},{4,12},{5,13},{6,14},{7,15},{8,0},{9,1},... | collective-permute-start | bytes 331784 | tf_op jit(solution)/shard_map/ppermute | solution.py:284
  71.7 1.0 %collective-permute-done.16 = bf16[1,216,256]{2,1,0:T(8,128)(2,1)S(1)} collective-permute-done((bf16[1,216,256]{2,1,0:T(8,128)(2,1)S(1)}, bf16[1,216,256]{2,1,0:T(8,128)(2,1)S(1)}, u32[]{:S(2)}, u32[]{:S(2)}) %collective-permute-start.16) | collective-permute-done | bytes 110624 | tf_op jit(solution)/shard_map/ppermute | solution.py:284
  72.8 2.8 %collective-permute-done.15 = bf16[1,216,256]{2,1,0:T(8,128)(2,1)S(1)} collective-permute-done((bf16[1,216,256]{2,1,0:T(8,128)(2,1)S(1)}, bf16[1,216,256]{2,1,0:T(8,128)(2,1)S(1)}, u32[]{:S(2)}, u32[]{:S(2)}) %collective-permute-start.15) | collective-permute-done | bytes 110624 | tf_op jit(solution)/shard_map/ppermute | solution.py:284
  75.7 2.7 %collective-permute-start.17 = (bf16[1,216,256]{2,1,0:T(8,128)(2,1)S(1)}, bf16[1,216,256]{2,1,0:T(8,128)(2,1)S(1)}, u32[]{:S(2)}, u32[]{:S(2)}) collective-permute-start(bf16[1,216,256]{2,1,0:T(8,128)(2,1)S(1)} %convert_element_type.62), channel_id=1, source_target_pairs={{0,16},{1,17},{2,18},{3,19},{4,20},{5,21},{6,22},{7,23},{24,8},{25... | collective-permute-start | bytes 331784 | tf_op jit(solution)/shard_map/ppermute | solution.py:284
  78.3 0.7 fusion.1
  79.0 1.6 %collective-permute-done.17 = bf16[1,216,256]{2,1,0:T(8,128)(2,1)S(1)} collective-permute-done((bf16[1,216,256]{2,1,0:T(8,128)(2,1)S(1)}, bf16[1,216,256]{2,1,0:T(8,128)(2,1)S(1)}, u32[]{:S(2)}, u32[]{:S(2)}) %collective-permute-start.17) | collective-permute-done | bytes 110624 | tf_op jit(solution)/shard_map/ppermute | solution.py:284
  80.7 0.8 copy.13
  (56 shorter events, 0.3 us)
Async XLA Ops:
  0.6 8.1 %collective-permute-start = (bf16[128,512]{1,0:T(8,128)(2,1)}, bf16[128,512]{1,0:T(8,128)(2,1)S(1)}, u32[]{:S(2)}, u32[]{:S(2)}) collective-permute-start(bf16[128,512]{1,0:T(8,128)(2,1)} %cur_in.1), channel_id=1, source_target_pairs={{0,1},{1,2},{2,3},{3,4},{4,5},{5,6},{6,7},{7,8},{8,9},{9,10},{10,1... | collective-permute-start | bytes 393224 | tf_op jit(solution)/shard_map/ppermute | solution.py:284
  3.0 1.6 %copy-start.1 = (bf16[2048,512]{1,0:T(8,128)(2,1)S(1)}, bf16[2048,512]{1,0:T(8,128)(2,1)}, u32[]{:S(2)}) copy-start(bf16[2048,512]{1,0:T(8,128)(2,1)} %w_in.1) | copy-start | bytes 6291460
  4.6 0.9 %copy-start.16 = (bf16[512,256]{1,0:T(8,128)(2,1)S(1)}, bf16[512,256]{1,0:T(8,128)(2,1)}, u32[]{:S(2)}) copy-start(bf16[512,256]{1,0:T(8,128)(2,1)} %pre.1) | copy-start | bytes 786436
  5.6 0.9 %copy-start.17 = (bf16[128,512]{1,0:T(8,128)(2,1)S(1)}, bf16[128,512]{1,0:T(8,128)(2,1)}, u32[]{:S(2)}) copy-start(bf16[128,512]{1,0:T(8,128)(2,1)} %cur_in.1) | copy-start | bytes 393220
  6.5 0.7 copy-start.22
  7.1 0.7 copy-start.23
  8.7 0.7 copy-start.18
  9.4 0.9 %copy-start.19 = (bf16[128,512]{1,0:T(8,128)(2,1)S(1)}, bf16[128,512]{1,0:T(8,128)(2,1)}, u32[]{:S(2)}) copy-start(bf16[128,512]{1,0:T(8,128)(2,1)} %copy-done.18) | copy-start | bytes 393220
  10.3 8.3 %copy-start = (bf16[6912,256]{1,0:T(8,128)(2,1)S(1)}, bf16[6912,256]{1,0:T(8,128)(2,1)}, u32[]{:S(2)}) copy-start(bf16[6912,256]{1,0:T(8,128)(2,1)} %refs_7_.3) | copy-start | bytes 10616836
  10.3 8.3 %copy-start.2 = (bf16[512,256]{1,0:T(8,128)(2,1)S(1)}, bf16[512,256]{1,0:T(8,128)(2,1)}, u32[]{:S(2)}) copy-start(bf16[512,256]{1,0:T(8,128)(2,1)} %refs_9_.1) | copy-start | bytes 786436
  10.3 8.4 %copy-start.14 = (s32[1,27,8,128]{3,2,1,0:T(8,128)S(1)}, s32[1,27,8,128]{3,2,1,0:T(8,128)}, u32[]{:S(2)}) copy-start(s32[1,27,8,128]{3,2,1,0:T(8,128)} %param.17) | copy-start | bytes 331780
  12.5 12.7 %copy-start.6 = (bf16[256,256]{1,0:T(8,128)(2,1)}, bf16[256,256]{1,0:T(8,128)(2,1)S(1)}, u32[]{:S(2)}) copy-start(bf16[256,256]{1,0:T(8,128)(2,1)S(1)} %get-tuple-element.68.refs_4_) | copy-start | bytes 393220
  12.5 12.7 %copy-start.8 = (bf16[256,256]{1,0:T(8,128)(2,1)}, bf16[256,256]{1,0:T(8,128)(2,1)S(1)}, u32[]{:S(2)}) copy-start(bf16[256,256]{1,0:T(8,128)(2,1)S(1)} %get-tuple-element.67.refs_5_) | copy-start | bytes 393220
  12.6 8.9 %collective-permute-start.3 = (bf16[16,64,512]{2,1,0:T(8,128)(2,1)S(1)}, bf16[16,64,512]{2,1,0:T(8,128)(2,1)S(1)}, u32[]{:S(2)}, u32[]{:S(2)}) collective-permute-start(bf16[16,64,512]{2,1,0:T(8,128)(2,1)S(1)} %get-tuple-element.72), channel_id=1, source_target_pairs={{0,1},{1,0},{2,3},{3,2},{4,5},{5,4},{6,7},{7,6},{8,9},{9,8},{10,11... | collective-permute-start | bytes 3145736 | tf_op jit(solution)/shard_map/ppermute | solution.py:284
  15.2 3.8 %collective-permute-start.1 = (bf16[256,256]{1,0:T(8,128)(2,1)S(1)}, bf16[256,256]{1,0:T(8,128)(2,1)S(1)}, u32[]{:S(2)}, u32[]{:S(2)}) collective-permute-start(bf16[256,256]{1,0:T(8,128)(2,1)S(1)} %get-tuple-element.67.refs_5_), channel_id=1, source_target_pairs={{0,1},{1,2},{2,3},{3,4},{4,5},{5,6},{6,7},{7,8},{8,9},{9,10},{10,1... | collective-permute-start | bytes 393224 | tf_op jit(solution)/shard_map/ppermute | solution.py:284
  17.2 4.3 %collective-permute-start.2 = (bf16[256,256]{1,0:T(8,128)(2,1)S(1)}, bf16[256,256]{1,0:T(8,128)(2,1)S(1)}, u32[]{:S(2)}, u32[]{:S(2)}) collective-permute-start(bf16[256,256]{1,0:T(8,128)(2,1)S(1)} %get-tuple-element.68.refs_4_), channel_id=1, source_target_pairs={{1,0},{2,1},{3,2},{4,3},{5,4},{6,5},{7,6},{8,7},{9,8},{10,9},{11,1... | collective-permute-start | bytes 393224 | tf_op jit(solution)/shard_map/ppermute | solution.py:284
  19.0 6.3 %copy-start.10 = (bf16[256,256]{1,0:T(8,128)(2,1)}, bf16[256,256]{1,0:T(8,128)(2,1)S(1)}, u32[]{:S(2)}) copy-start(bf16[256,256]{1,0:T(8,128)(2,1)S(1)} %collective-permute-done.1.refs_3_) | copy-start | bytes 393220
  21.5 3.8 %copy-start.12 = (bf16[256,256]{1,0:T(8,128)(2,1)}, bf16[256,256]{1,0:T(8,128)(2,1)S(1)}, u32[]{:S(2)}) copy-start(bf16[256,256]{1,0:T(8,128)(2,1)S(1)} %collective-permute-done.2.refs_6_) | copy-start | bytes 393220
  21.5 3.8 %copy-start.20 = (s32[1,27,8]{1,2,0:T(8,128)S(1)}, s32[1,27,8]{1,2,0:T(8,128)}, u32[]{:S(2)}) copy-start(s32[1,27,8]{1,2,0:T(8,128)} %param.15) | copy-start | bytes 2596
  21.5 3.8 %copy-start.21 = (s32[1,27,8]{1,2,0:T(8,128)S(1)}, s32[1,27,8]{1,2,0:T(8,128)}, u32[]{:S(2)}) copy-start(s32[1,27,8]{1,2,0:T(8,128)} %param.16) | copy-start | bytes 2596
  21.9 10.5 %collective-permute-start.4 = (bf16[8,64,512]{2,1,0:T(8,128)(2,1)S(1)}, bf16[8,64,512]{2,1,0:T(8,128)(2,1)S(1)}, u32[]{:S(2)}, u32[]{:S(2)}) collective-permute-start(bf16[8,64,512]{2,1,0:T(8,128)(2,1)S(1)} %slice.66), channel_id=1, source_target_pairs={{0,2},{1,5},{2,0},{3,7},{4,6},{5,1},{6,4},{7,3},{8,10},{9,13},{10,... | collective-permute-start | bytes 1572872 | tf_op jit(solution)/shard_map/ppermute | solution.py:284
  30.5 2.8 %copy-start.4 = (f32[512,256]{1,0:T(8,128)}, f32[512,256]{1,0:T(8,128)S(1)}, u32[]{:S(2)}) copy-start(f32[512,256]{1,0:T(8,128)S(1)} %get-tuple-element.88.refs_10_) | copy-start | bytes 1572868
  30.5 3.6 %collective-permute-start.5 = (bf16[8,216,256]{2,1,0:T(8,128)(2,1)S(1)}, bf16[8,216,256]{2,1,0:T(8,128)(2,1)S(1)}, u32[]{:S(2)}, u32[]{:S(2)}) collective-permute-start(bf16[8,216,256]{2,1,0:T(8,128)(2,1)S(1)} %get-tuple-element.82), channel_id=1, source_target_pairs={{0,1},{1,0},{2,3},{3,2},{4,5},{5,4},{6,7},{7,6},{8,9},{9,8},{10,11... | collective-permute-start | bytes 2654216 | tf_op jit(solution)/shard_map/ppermute | solution.py:284
  33.2 1.1 %copy-start.24 = (f32[4,64,512]{2,1,0:T(8,128)}, f32[4,64,512]{2,1,0:T(8,128)S(1)}, u32[]{:S(2)}) copy-start(f32[4,64,512]{2,1,0:T(8,128)S(1)} %get-tuple-element.99.kept) | copy-start | bytes 1572868
  34.3 1.4 %copy-start.26 = (f32[8,216,256]{2,1,0:T(8,128)}, f32[8,216,256]{2,1,0:T(8,128)S(1)}, u32[]{:S(2)}) copy-start(f32[8,216,256]{2,1,0:T(8,128)S(1)} %convert_add_fusion.2) | copy-start | bytes 5308420
  35.7 13.3 %collective-permute-start.6 = (bf16[4,216,256]{2,1,0:T(8,128)(2,1)}, bf16[4,216,256]{2,1,0:T(8,128)(2,1)}, u32[]{:S(2)}, u32[]{:S(2)}) collective-permute-start(bf16[4,216,256]{2,1,0:T(8,128)(2,1)} %slice.68), channel_id=1, source_target_pairs={{0,2},{1,5},{2,0},{3,7},{4,6},{5,1},{6,4},{7,3},{8,10},{9,13},{10,... | collective-permute-start | bytes 1327112 | tf_op jit(solution)/shard_map/ppermute | solution.py:284
  39.0 10.0 %collective-permute-start.7 = (bf16[4,64,512]{2,1,0:T(8,128)(2,1)}, bf16[4,64,512]{2,1,0:T(8,128)(2,1)}, u32[]{:S(2)}, u32[]{:S(2)}) collective-permute-start(bf16[4,64,512]{2,1,0:T(8,128)(2,1)} %get-tuple-element.92), channel_id=1, source_target_pairs={{0,4},{1,3},{2,6},{3,1},{4,0},{5,7},{6,2},{7,5},{8,12},{9,11},{10,... | collective-permute-start | bytes 786440 | tf_op jit(solution)/shard_map/ppermute | solution.py:284
  39.5 1.4 %copy-start.3 = (bf16[512,256]{1,0:T(8,128)(2,1)S(1)}, bf16[512,256]{1,0:T(8,128)(2,1)}, u32[]{:S(2)}) copy-start(bf16[512,256]{1,0:T(8,128)(2,1)} %refs_9_.1) | copy-start | bytes 786436
  39.5 1.4 %copy-start.5 = (f32[512,256]{1,0:T(8,128)S(1)}, f32[512,256]{1,0:T(8,128)}, u32[]{:S(2)}) copy-start(f32[512,256]{1,0:T(8,128)} %copy-done.4) | copy-start | bytes 1572868
  39.5 1.4 %copy-start.7 = (bf16[256,256]{1,0:T(8,128)(2,1)S(1)}, bf16[256,256]{1,0:T(8,128)(2,1)}, u32[]{:S(2)}) copy-start(bf16[256,256]{1,0:T(8,128)(2,1)} %copy-done.6) | copy-start | bytes 393220
  39.5 1.4 %copy-start.9 = (bf16[256,256]{1,0:T(8,128)(2,1)S(1)}, bf16[256,256]{1,0:T(8,128)(2,1)}, u32[]{:S(2)}) copy-start(bf16[256,256]{1,0:T(8,128)(2,1)} %copy-done.8) | copy-start | bytes 393220
  39.5 1.5 %copy-start.11 = (bf16[256,256]{1,0:T(8,128)(2,1)S(1)}, bf16[256,256]{1,0:T(8,128)(2,1)}, u32[]{:S(2)}) copy-start(bf16[256,256]{1,0:T(8,128)(2,1)} %copy-done.10) | copy-start | bytes 393220
  39.5 1.5 %copy-start.13 = (bf16[256,256]{1,0:T(8,128)(2,1)S(1)}, bf16[256,256]{1,0:T(8,128)(2,1)}, u32[]{:S(2)}) copy-start(bf16[256,256]{1,0:T(8,128)(2,1)} %copy-done.12) | copy-start | bytes 393220
  39.5 1.5 %copy-start.15 = (s32[1,27,8,128]{3,2,1,0:T(8,128)S(1)}, s32[1,27,8,128]{3,2,1,0:T(8,128)}, u32[]{:S(2)}) copy-start(s32[1,27,8,128]{3,2,1,0:T(8,128)} %param.17) | copy-start | bytes 331780
  47.7 5.9 %collective-permute-start.8 = (bf16[8,216,256]{2,1,0:T(8,128)(2,1)S(1)}, bf16[8,216,256]{2,1,0:T(8,128)(2,1)S(1)}, u32[]{:S(2)}, u32[]{:S(2)}) collective-permute-start(bf16[8,216,256]{2,1,0:T(8,128)(2,1)S(1)} %get-tuple-element.95), channel_id=1, source_target_pairs={{0,1},{1,0},{2,3},{3,2},{4,5},{5,4},{6,7},{7,6},{8,9},{9,8},{10,11... | collective-permute-start | bytes 2654216 | tf_op jit(solution)/shard_map/ppermute | solution.py:284
  49.0 2.0 %copy-start.25 = (f32[4,64,512]{2,1,0:T(8,128)S(1)}, f32[4,64,512]{2,1,0:T(8,128)}, u32[]{:S(2)}) copy-start(f32[4,64,512]{2,1,0:T(8,128)} %copy-done.24) | copy-start | bytes 1572868
  50.2 6.0 %collective-permute-start.10 = (bf16[2,216,256]{2,1,0:T(8,128)(2,1)S(1)}, bf16[2,216,256]{2,1,0:T(8,128)(2,1)S(1)}, u32[]{:S(2)}, u32[]{:S(2)}) collective-permute-start(bf16[2,216,256]{2,1,0:T(8,128)(2,1)S(1)} %get-tuple-element.104), channel_id=1, source_target_pairs={{0,4},{1,3},{2,6},{3,1},{4,0},{5,7},{6,2},{7,5},{8,12},{9,11},{10,... | collective-permute-start | bytes 663560 | tf_op jit(solution)/shard_map/ppermute | solution.py:284
  52.0 7.1 %collective-permute-start.11 = (bf16[2,64,512]{2,1,0:T(8,128)(2,1)S(1)}, bf16[2,64,512]{2,1,0:T(8,128)(2,1)S(1)}, u32[]{:S(2)}, u32[]{:S(2)}) collective-permute-start(bf16[2,64,512]{2,1,0:T(8,128)(2,1)S(1)} %get-tuple-element.106), channel_id=1, source_target_pairs={{0,8},{1,9},{2,10},{3,11},{4,12},{5,13},{6,14},{7,15},{8,0},{9,1},... | collective-permute-start | bytes 393224 | tf_op jit(solution)/shard_map/ppermute | solution.py:284
  54.0 8.4 %collective-permute-start.9 = (bf16[4,216,256]{2,1,0:T(8,128)(2,1)S(1)}, bf16[4,216,256]{2,1,0:T(8,128)(2,1)S(1)}, u32[]{:S(2)}, u32[]{:S(2)}) collective-permute-start(bf16[4,216,256]{2,1,0:T(8,128)(2,1)S(1)} %slice.67), channel_id=1, source_target_pairs={{0,2},{1,5},{2,0},{3,7},{4,6},{5,1},{6,4},{7,3},{8,10},{9,13},{10,... | collective-permute-start | bytes 1327112 | tf_op jit(solution)/shard_map/ppermute | solution.py:284
  56.3 8.8 %collective-permute-start.13 = (bf16[1,216,256]{2,1,0:T(8,128)(2,1)S(1)}, bf16[1,216,256]{2,1,0:T(8,128)(2,1)S(1)}, u32[]{:S(2)}, u32[]{:S(2)}) collective-permute-start(bf16[1,216,256]{2,1,0:T(8,128)(2,1)S(1)} %get-tuple-element.111), channel_id=1, source_target_pairs={{0,8},{1,9},{2,10},{3,11},{4,12},{5,13},{6,14},{7,15},{8,0},{9,1},... | collective-permute-start | bytes 331784 | tf_op jit(solution)/shard_map/ppermute | solution.py:284
  62.4 5.8 %collective-permute-start.14 = (bf16[1,64,512]{2,1,0:T(8,128)(2,1)S(1)}, bf16[1,64,512]{2,1,0:T(8,128)(2,1)S(1)}, u32[]{:S(2)}, u32[]{:S(2)}) collective-permute-start(bf16[1,64,512]{2,1,0:T(8,128)(2,1)S(1)} %slice.70), channel_id=1, source_target_pairs={{0,16},{1,17},{2,18},{3,19},{4,20},{5,21},{6,22},{7,23},{8,24},{9,... | collective-permute-start | bytes 196616 | tf_op jit(solution)/shard_map/ppermute | solution.py:284
  64.7 6.0 %collective-permute-start.12 = (bf16[2,216,256]{2,1,0:T(8,128)(2,1)S(1)}, bf16[2,216,256]{2,1,0:T(8,128)(2,1)S(1)}, u32[]{:S(2)}, u32[]{:S(2)}) collective-permute-start(bf16[2,216,256]{2,1,0:T(8,128)(2,1)S(1)} %get-tuple-element.109), channel_id=1, source_target_pairs={{0,4},{1,3},{2,6},{3,1},{4,0},{5,7},{6,2},{7,5},{8,12},{9,11},{10,... | collective-permute-start | bytes 663560 | tf_op jit(solution)/shard_map/ppermute | solution.py:284
  65.1 7.6 %collective-permute-start.16 = (bf16[1,216,256]{2,1,0:T(8,128)(2,1)S(1)}, bf16[1,216,256]{2,1,0:T(8,128)(2,1)S(1)}, u32[]{:S(2)}, u32[]{:S(2)}) collective-permute-start(bf16[1,216,256]{2,1,0:T(8,128)(2,1)S(1)} %get-tuple-element.119), channel_id=1, source_target_pairs={{8,24},{9,25},{10,26},{11,27},{12,28},{13,29},{14,30},{15,31},{16,... | collective-permute-start | bytes 331784 | tf_op jit(solution)/shard_map/ppermute | solution.py:284
  70.8 4.8 %collective-permute-start.15 = (bf16[1,216,256]{2,1,0:T(8,128)(2,1)S(1)}, bf16[1,216,256]{2,1,0:T(8,128)(2,1)S(1)}, u32[]{:S(2)}, u32[]{:S(2)}) collective-permute-start(bf16[1,216,256]{2,1,0:T(8,128)(2,1)S(1)} %slice.69), channel_id=1, source_target_pairs={{0,8},{1,9},{2,10},{3,11},{4,12},{5,13},{6,14},{7,15},{8,0},{9,1},... | collective-permute-start | bytes 331784 | tf_op jit(solution)/shard_map/ppermute | solution.py:284
  75.7 5.0 %collective-permute-start.17 = (bf16[1,216,256]{2,1,0:T(8,128)(2,1)S(1)}, bf16[1,216,256]{2,1,0:T(8,128)(2,1)S(1)}, u32[]{:S(2)}, u32[]{:S(2)}) collective-permute-start(bf16[1,216,256]{2,1,0:T(8,128)(2,1)S(1)} %convert_element_type.62), channel_id=1, source_target_pairs={{0,16},{1,17},{2,18},{3,19},{4,20},{5,21},{6,22},{7,23},{24,8},{25... | collective-permute-start | bytes 331784 | tf_op jit(solution)/shard_map/ppermute | solution.py:284

commit v11 on v10

--- a/solution.py
+++ b/solution.py
@@ -399,13 +399,13 @@
     inner_got = across(inner_send)
     outer, outer_send = middle(outer, outer_got)
     outer_got = xy(outer_send, bits - 1)
-    low, low_send = fold_long(low, low_got)
+    low, low_send = fold(low, low_got)
     low_got = z_near(low_send)
     inner_got, outer, low = pinned((inner_got, outer, low))
     inner, inner_send = fold(inner, inner_got)
     inner_got = xy(inner_send, 0)
 
-    outer, outer_send = fold_long(outer, outer_got)
+    outer, outer_send = fold(outer, outer_got)
     outer_got = z_near(outer_send)
     inner_got, outer, low_got = pinned((inner_got, outer, low_got))
     inner, inner_send = middle(inner, inner_got)

time: 82.4 us -> 76.9 us (0.933)
  the two profiles are of different devices: /device:TPU:0 before, /device:TPU:10 now
where the time goes in v11:
time: 76.9 us; the launch traced here: 76.5 us
  starting transfers between devices  25.4 us (33%)
  waiting for transfers between devices  24.7 us (32%)
  Pallas kernels  15.8 us (21%)
  local copies, waits for them, and re-layouts  6.87 us (9%)
  other arithmetic  2.72 us (4%)
  between operations  0.96 us (1%)
    ppermute x18, starting transfers between devices, moved(): lax.ppermute(x, 'space', [(i, j) for i, j in pairs if j is not None and 0...  25.4 us
    ppermute x18, waiting for transfers between devices, moved(): lax.ppermute(x, 'space', [(i, j) for i, j in pairs if j is not None and 0...  24.7 us
    pallas_call x2, Pallas kernels, conv(): pl.pallas_call(functools.partial(conv_kernel, conv_plan(kernel, channels,...  12 us
    unnamed x23, local copies, waits for them, and re-layouts  5.64 us
    pallas_call x1, Pallas kernels, down(): pl.pallas_call(functools.partial(down_kernel, bits), out_shape=(side, sid...  2.26 us
    add x7, other arithmetic, fold(): total = kept.astype(F32) + got.astype(F32)  1.9 us
  transfers between devices with their start and end apart: 18, of which 11 were waited for; matrix products, arithmetic and copies ran while one was open for 4% of the time, Pallas kernels for 18%

profile of v11, /device:TPU:10, one launch (start us, length us, event | category | flops | bytes accessed | tf_op | source)
XLA Modules:
  0.0 76.5 jit_solution(8776875020805238183)
XLA Ops:
  0.6 1.9 %collective-permute-start = (bf16[128,512]{1,0:T(8,128)(2,1)}, bf16[128,512]{1,0:T(8,128)(2,1)S(1)}, u32[]{:S(2)}, u32[]{:S(2)}) collective-permute-start(bf16[128,512]{1,0:T(8,128)(2,1)} %cur_in.1), channel_id=1, source_target_pairs={{0,1},{1,2},{2,3},{3,4},{4,5},{5,6},{6,7},{7,8},{8,9},{9,10},{10,1... | collective-permute-start | bytes 393224 | tf_op jit(solution)/shard_map/ppermute | solution.py:284
  2.6 1.6 %copy-done.1 = bf16[2048,512]{1,0:T(8,128)(2,1)S(1)} copy-done((bf16[2048,512]{1,0:T(8,128)(2,1)S(1)}, bf16[2048,512]{1,0:T(8,128)(2,1)}, u32[]{:S(2)}) %copy-start.1) | copy-done | bytes 2097176
  4.2 0.9 %copy-done.4 = bf16[512,256]{1,0:T(8,128)(2,1)S(1)} copy-done((bf16[512,256]{1,0:T(8,128)(2,1)S(1)}, bf16[512,256]{1,0:T(8,128)(2,1)}, u32[]{:S(2)}) %copy-start.4) | copy-done | bytes 262168
  5.1 0.9 %copy-done.5 = bf16[128,512]{1,0:T(8,128)(2,1)S(1)} copy-done((bf16[128,512]{1,0:T(8,128)(2,1)S(1)}, bf16[128,512]{1,0:T(8,128)(2,1)}, u32[]{:S(2)}) %copy-start.5) | copy-done | bytes 131096
  6.0 0.7 copy-done.8
  6.7 0.7 copy-done.9
  7.4 0.9 %prep.1 = (bf16[512,256]{1,0:T(8,128)(2,1)S(1)}, bf16[512,1024]{1,0:T(8,128)(2,1)S(1)}, bf16[1024,256]{1,0:T(8,128)(2,1)S(1)}, bf16[256,1024]{1,0:T(8,128)(2,1)S...) custom-call(bf16[512,256]{1,0:T(8,128)(2,1)S(1)} %copy-done.4, s32[8,128]{1,0:T(8,128)S(1)} %bitcast.21, ...), custom_call_target="tpu_custom_call" | custom-call | flops 1048576 | bytes 1024 | tf_op jit(solution)/shard_map/prep/pallas_call | solution.py:114
  8.3 0.0 collective-permute-done.prev
  8.3 0.0 copy-start
  8.3 0.0 copy-start.2
  8.3 0.0 copy-start.3
  8.3 2.3 %down.1 = (bf16[256,256]{1,0:T(8,128)(2,1)S(1)}, bf16[256,256]{1,0:T(8,128)(2,1)S(1)}, bf16[16,64,512]{2,1,0:T(8,128)(2,1)S(1)}, bf16[16,64,512]{2,1,0:T(8,128)(2,1)S(1)}) custom-call(s32[1]{0:T(128)} %bitcast.me.refs_0_, bf16[128,512]{1,0:T(8,128)(2,1)S(1)} %collective-permute-done.prev, bf16[512,256]{1,0:T(8,128)(2,1)S(1)} %get-tuple-element.57.act, ...), custom_call_target="tpu_custom_call" | custom-call | flops 1048576 | bytes 1024 | tf_op jit(solution)/shard_map/down/pallas_call | solution.py:154
  10.6 1.7 %collective-permute-start.3 = (bf16[16,64,512]{2,1,0:T(8,128)(2,1)S(1)}, bf16[16,64,512]{2,1,0:T(8,128)(2,1)S(1)}, u32[]{:S(2)}, u32[]{:S(2)}) collective-permute-start(bf16[16,64,512]{2,1,0:T(8,128)(2,1)S(1)} %get-tuple-element.68), channel_id=1, source_target_pairs={{0,1},{1,0},{2,3},{3,2},{4,5},{5,4},{6,7},{7,6},{8,9},{9,8},{10,11... | collective-permute-start | bytes 3145736 | tf_op jit(solution)/shard_map/ppermute | solution.py:284
  12.3 1.9 %collective-permute-start.1 = (bf16[256,256]{1,0:T(8,128)(2,1)S(1)}, bf16[256,256]{1,0:T(8,128)(2,1)S(1)}, u32[]{:S(2)}, u32[]{:S(2)}) collective-permute-start(bf16[256,256]{1,0:T(8,128)(2,1)S(1)} %get-tuple-element.63.refs_5_), channel_id=1, source_target_pairs={{0,1},{1,2},{2,3},{3,4},{4,5},{5,6},{6,7},{7,8},{8,9},{9,10},{10,1... | collective-permute-start | bytes 393224 | tf_op jit(solution)/shard_map/ppermute | solution.py:284
  14.2 3.8 %collective-permute-start.2 = (bf16[256,256]{1,0:T(8,128)(2,1)S(1)}, bf16[256,256]{1,0:T(8,128)(2,1)S(1)}, u32[]{:S(2)}, u32[]{:S(2)}) collective-permute-start(bf16[256,256]{1,0:T(8,128)(2,1)S(1)} %get-tuple-element.64.refs_4_), channel_id=1, source_target_pairs={{1,0},{2,1},{3,2},{4,3},{5,4},{6,5},{7,6},{8,7},{9,8},{10,9},{11,1... | collective-permute-start | bytes 393224 | tf_op jit(solution)/shard_map/ppermute | solution.py:284
  18.0 0.3 turn.1
  18.4 0.2 collective-permute-done.1.refs_3_
  18.5 1.8 %collective-permute-done.2.refs_6_ = bf16[256,256]{1,0:T(8,128)(2,1)S(1)} collective-permute-done((bf16[256,256]{1,0:T(8,128)(2,1)S(1)}, bf16[256,256]{1,0:T(8,128)(2,1)S(1)}, u32[]{:S(2)}, u32[]{:S(2)}) %collective-permute-start.2) | collective-permute-done | bytes 131104 | tf_op jit(solution)/shard_map/ppermute | solution.py:284
  20.3 0.0 collective-permute-done.3
  20.3 0.3 convert_add_fusion
  20.7 0.1 slice.90
  20.7 2.4 %collective-permute-start.4 = (bf16[8,64,512]{2,1,0:T(8,128)(2,1)S(1)}, bf16[8,64,512]{2,1,0:T(8,128)(2,1)S(1)}, u32[]{:S(2)}, u32[]{:S(2)}) collective-permute-start(bf16[8,64,512]{2,1,0:T(8,128)(2,1)S(1)} %slice.90), channel_id=1, source_target_pairs={{0,2},{1,5},{2,0},{3,7},{4,6},{5,1},{6,4},{7,3},{8,10},{9,13},{10,... | collective-permute-start | bytes 1572872 | tf_op jit(solution)/shard_map/ppermute | solution.py:284
  23.1 5.3 %conv.2 = (f32[512,256]{1,0:T(8,128)S(1)}, bf16[8,216,256]{2,1,0:T(8,128)(2,1)S(1)}, bf16[8,216,256]{2,1,0:T(8,128)(2,1)S(1)}) custom-call(s32[1]{0:T(128)} %bitcast.me.refs_0_, s32[8,27]{1,0:T(8,128)S(1)} %bitcast.17, s32[8,27]{1,0:T(8,128)S(1)} %bitcast.19, bf16[256,256]{1,0:T(8,128)(2,1)S(1)} %collective-permute-done.1.refs_3_, ...), custom_call_target="tpu_custom_call" | custom-call | flops 1048576 | bytes 1024 | tf_op jit(solution)/shard_map/conv/pallas_call | solution.py:257
  28.5 2.5 %collective-permute-start.5 = (bf16[8,216,256]{2,1,0:T(8,128)(2,1)S(1)}, bf16[8,216,256]{2,1,0:T(8,128)(2,1)S(1)}, u32[]{:S(2)}, u32[]{:S(2)}) collective-permute-start(bf16[8,216,256]{2,1,0:T(8,128)(2,1)S(1)} %get-tuple-element.78), channel_id=1, source_target_pairs={{0,1},{1,0},{2,3},{3,2},{4,5},{5,4},{6,7},{7,6},{8,9},{9,8},{10,11... | collective-permute-start | bytes 2654216 | tf_op jit(solution)/shard_map/ppermute | solution.py:284
  31.0 0.1 slice.63.kept
  31.1 0.1 fold.3
  31.2 1.8 %collective-permute-done.5 = bf16[8,216,256]{2,1,0:T(8,128)(2,1)S(1)} collective-permute-done((bf16[8,216,256]{2,1,0:T(8,128)(2,1)S(1)}, bf16[8,216,256]{2,1,0:T(8,128)(2,1)S(1)}, u32[]{:S(2)}, u32[]{:S(2)}) %collective-permute-start.5) | collective-permute-done | bytes 884768 | tf_op jit(solution)/shard_map/ppermute | solution.py:284
  33.0 0.2 convert_add_fusion.2
  33.3 0.1 collective-permute-start.6
  33.4 0.6 collective-permute-start.7
  34.0 6.7 %conv.3 = (bf16[512,256]{1,0:T(8,128)(2,1)}, bf16[8,216,256]{2,1,0:T(8,128)(2,1)S(1)}, bf16[8,216,256]{2,1,0:T(8,128)(2,1)S(1)}) custom-call(s32[1]{0:T(128)} %bitcast.me.refs_0_, s32[8,27]{1,0:T(8,128)S(1)} %bitcast.18, s32[8,27]{1,0:T(8,128)S(1)} %bitcast.20, bf16[256,256]{1,0:T(8,128)(2,1)S(1)} %collective-permute-done.1.refs_3_, ...), custom_call_target="tpu_custom_call" | custom-call | flops 1048576 | bytes 1024 | tf_op jit(solution)/shard_map/conv/pallas_call | solution.py:257
  40.7 0.1 collective-permute-start.8
  40.8 0.1 slice.66.kept
  40.8 1.7 %collective-permute-done.7 = bf16[4,64,512]{2,1,0:T(8,128)(2,1)S(1)} collective-permute-done((bf16[4,64,512]{2,1,0:T(8,128)(2,1)S(1)}, bf16[4,64,512]{2,1,0:T(8,128)(2,1)S(1)}, u32[]{:S(2)}, u32[]{:S(2)}) %collective-permute-start.7) | collective-permute-done | bytes 262176 | tf_op jit(solution)/shard_map/ppermute | solution.py:284
  42.6 1.6 %collective-permute-done.6.got = bf16[4,216,256]{2,1,0:T(8,128)(2,1)S(1)} collective-permute-done((bf16[4,216,256]{2,1,0:T(8,128)(2,1)S(1)}, bf16[4,216,256]{2,1,0:T(8,128)(2,1)S(1)}, u32[]{:S(2)}, u32[]{:S(2)}) %collective-permute-start.6) | collective-permute-done | bytes 442400 | tf_op jit(solution)/shard_map/ppermute | solution.py:284
  44.2 0.1 convert_add_fusion.3
  44.3 0.1 fold.4
  44.4 0.8 %collective-permute-start.10 = (bf16[2,216,256]{2,1,0:T(8,128)(2,1)S(1)}, bf16[2,216,256]{2,1,0:T(8,128)(2,1)}, u32[]{:S(2)}, u32[]{:S(2)}) collective-permute-start(bf16[2,216,256]{2,1,0:T(8,128)(2,1)S(1)} %get-tuple-element.99), channel_id=1, source_target_pairs={{0,4},{1,3},{2,6},{3,1},{4,0},{5,7},{6,2},{7,5},{8,12},{9,11},{10,... | collective-permute-start | bytes 663560 | tf_op jit(solution)/shard_map/ppermute | solution.py:284
  45.3 0.0 collective-permute-done.8
  45.3 0.2 convert_add_fusion.1
  45.5 0.8 %slice.91 = bf16[4,216,256]{2,1,0:T(8,128)(2,1)} slice(f32[8,216,256]{2,1,0:T(8,128)S(1)} %convert_add_fusion.1), slice={[4:8], [0:216], [0:256]} | slice | bytes 884736 | tf_op jit(solution)/shard_map/slice | solution.py:290
  46.3 0.0 collective-permute-start.9
  46.3 0.0 slice-start
  46.3 0.5 collective-permute-start.11
  46.9 5.9 %collective-permute-done.10 = bf16[2,216,256]{2,1,0:T(8,128)(2,1)} collective-permute-done((bf16[2,216,256]{2,1,0:T(8,128)(2,1)S(1)}, bf16[2,216,256]{2,1,0:T(8,128)(2,1)}, u32[]{:S(2)}, u32[]{:S(2)}) %collective-permute-start.10) | collective-permute-done | bytes 221216 | tf_op jit(solution)/shard_map/ppermute | solution.py:284
  52.8 1.0 %convert_add_fusion.5 = f32[2,216,256]{2,1,0:T(8,128)S(1)} fusion(f32[2,216,256]{2,1,0:T(8,128)S(1)} %get-tuple-element.98, bf16[2,216,256]{2,1,0:T(8,128)(2,1)} %collective-permute-done.10), kind=kLoop, calls=%fused_computation.8 | loop fusion | flops 221184 | bytes 1105920 | tf_op jit(solution)/shard_map/add | solution.py:289
  53.8 0.1 slice.68.kept
  53.9 0.5 collective-permute-start.13
  54.4 0.4 collective-permute-done.9.got
  54.9 2.2 %collective-permute-start.14 = (bf16[1,64,512]{2,1,0:T(8,128)(2,1)S(1)}, bf16[1,64,512]{2,1,0:T(8,128)(2,1)S(1)}, u32[]{:S(2)}, u32[]{:S(2)}) collective-permute-start(bf16[1,64,512]{2,1,0:T(8,128)(2,1)S(1)} %slice.96), channel_id=1, source_target_pairs={{0,16},{1,17},{2,18},{3,19},{4,20},{5,21},{6,22},{7,23},{8,24},{9,... | collective-permute-start | bytes 196616 | tf_op jit(solution)/shard_map/ppermute | solution.py:284
  57.1 0.1 fold.5
  57.2 0.9 %collective-permute-start.12 = (bf16[2,216,256]{2,1,0:T(8,128)(2,1)S(1)}, bf16[2,216,256]{2,1,0:T(8,128)(2,1)S(1)}, u32[]{:S(2)}, u32[]{:S(2)}) collective-permute-start(bf16[2,216,256]{2,1,0:T(8,128)(2,1)S(1)} %get-tuple-element.102), channel_id=1, source_target_pairs={{0,4},{1,3},{2,6},{3,1},{4,0},{5,7},{6,2},{7,5},{8,12},{9,11},{10,... | collective-permute-start | bytes 663560 | tf_op jit(solution)/shard_map/ppermute | solution.py:284
  58.1 0.6 collective-permute-done.13
  58.7 3.2 %collective-permute-start.16 = (bf16[1,216,256]{2,1,0:T(8,128)(2,1)S(1)}, bf16[1,216,256]{2,1,0:T(8,128)(2,1)S(1)}, u32[]{:S(2)}, u32[]{:S(2)}) collective-permute-start(bf16[1,216,256]{2,1,0:T(8,128)(2,1)S(1)} %get-tuple-element.111), channel_id=1, source_target_pairs={{8,24},{9,25},{10,26},{11,27},{12,28},{13,29},{14,30},{15,31},{16,... | collective-permute-start | bytes 331784 | tf_op jit(solution)/shard_map/ppermute | solution.py:284
  61.9 0.0 collective-permute-done.14
  61.9 1.3 %collective-permute-done.12 = bf16[2,216,256]{2,1,0:T(8,128)(2,1)S(1)} collective-permute-done((bf16[2,216,256]{2,1,0:T(8,128)(2,1)S(1)}, bf16[2,216,256]{2,1,0:T(8,128)(2,1)S(1)}, u32[]{:S(2)}, u32[]{:S(2)}) %collective-permute-start.12) | collective-permute-done | bytes 221216 | tf_op jit(solution)/shard_map/ppermute | solution.py:284
  63.2 0.1 convert_add_fusion.4
  63.3 0.9 %collective-permute-start.15 = (bf16[1,216,256]{2,1,0:T(8,128)(2,1)S(1)}, bf16[1,216,256]{2,1,0:T(8,128)(2,1)S(1)}, u32[]{:S(2)}, u32[]{:S(2)}) collective-permute-start(bf16[1,216,256]{2,1,0:T(8,128)(2,1)S(1)} %slice.94), channel_id=1, source_target_pairs={{0,8},{1,9},{2,10},{3,11},{4,12},{5,13},{6,14},{7,15},{8,0},{9,1},... | collective-permute-start | bytes 331784 | tf_op jit(solution)/shard_map/ppermute | solution.py:284
  64.2 0.0 collective-permute-done.16
  64.2 3.8 %collective-permute-done.15 = bf16[1,216,256]{2,1,0:T(8,128)(2,1)S(1)} collective-permute-done((bf16[1,216,256]{2,1,0:T(8,128)(2,1)S(1)}, bf16[1,216,256]{2,1,0:T(8,128)(2,1)S(1)}, u32[]{:S(2)}, u32[]{:S(2)}) %collective-permute-start.15) | collective-permute-done | bytes 110624 | tf_op jit(solution)/shard_map/ppermute | solution.py:284
  68.1 1.3 %collective-permute-start.17 = (bf16[1,216,256]{2,1,0:T(8,128)(2,1)S(1)}, bf16[1,216,256]{2,1,0:T(8,128)(2,1)S(1)}, u32[]{:S(2)}, u32[]{:S(2)}) collective-permute-start(bf16[1,216,256]{2,1,0:T(8,128)(2,1)S(1)} %convert_element_type.72), channel_id=1, source_target_pairs={{0,16},{1,17},{2,18},{3,19},{4,20},{5,21},{6,22},{7,23},{24,8},{25... | collective-permute-start | bytes 331784 | tf_op jit(solution)/shard_map/ppermute | solution.py:284
  69.4 0.7 fusion.1
  70.1 5.6 %collective-permute-done.17 = bf16[1,216,256]{2,1,0:T(8,128)(2,1)S(1)} collective-permute-done((bf16[1,216,256]{2,1,0:T(8,128)(2,1)S(1)}, bf16[1,216,256]{2,1,0:T(8,128)(2,1)S(1)}, u32[]{:S(2)}, u32[]{:S(2)}) %collective-permute-start.17) | collective-permute-done | bytes 110624 | tf_op jit(solution)/shard_map/ppermute | solution.py:284
  75.7 0.8 %copy.13 = f32[27,2,8,128]{3,1,2,0:T(2,128)} copy(f32[27,2,8,128]{3,2,1,0:T(8,128)S(1)} %multiply_bitcast_fusion) | data formatting | bytes 442368
  (29 shorter events, 0.3 us)
Async XLA Ops:
  0.6 7.7 %collective-permute-start = (bf16[128,512]{1,0:T(8,128)(2,1)}, bf16[128,512]{1,0:T(8,128)(2,1)S(1)}, u32[]{:S(2)}, u32[]{:S(2)}) collective-permute-start(bf16[128,512]{1,0:T(8,128)(2,1)} %cur_in.1), channel_id=1, source_target_pairs={{0,1},{1,2},{2,3},{3,4},{4,5},{5,6},{6,7},{7,8},{8,9},{9,10},{10,1... | collective-permute-start | bytes 393224 | tf_op jit(solution)/shard_map/ppermute | solution.py:284
  2.6 1.6 %copy-start.1 = (bf16[2048,512]{1,0:T(8,128)(2,1)S(1)}, bf16[2048,512]{1,0:T(8,128)(2,1)}, u32[]{:S(2)}) copy-start(bf16[2048,512]{1,0:T(8,128)(2,1)} %w_in.1) | copy-start | bytes 6291460
  4.2 0.9 %copy-start.4 = (bf16[512,256]{1,0:T(8,128)(2,1)S(1)}, bf16[512,256]{1,0:T(8,128)(2,1)}, u32[]{:S(2)}) copy-start(bf16[512,256]{1,0:T(8,128)(2,1)} %pre.1) | copy-start | bytes 786436
  5.1 0.9 %copy-start.5 = (bf16[128,512]{1,0:T(8,128)(2,1)S(1)}, bf16[128,512]{1,0:T(8,128)(2,1)}, u32[]{:S(2)}) copy-start(bf16[128,512]{1,0:T(8,128)(2,1)} %cur_in.1) | copy-start | bytes 393220
  6.0 0.7 copy-start.8
  6.7 0.7 copy-start.9
  8.3 9.7 %copy-start = (bf16[6912,256]{1,0:T(8,128)(2,1)S(1)}, bf16[6912,256]{1,0:T(8,128)(2,1)}, u32[]{:S(2)}) copy-start(bf16[6912,256]{1,0:T(8,128)(2,1)} %refs_7_.3) | copy-start | bytes 10616836
  8.3 9.7 %copy-start.2 = (bf16[512,256]{1,0:T(8,128)(2,1)S(1)}, bf16[512,256]{1,0:T(8,128)(2,1)}, u32[]{:S(2)}) copy-start(bf16[512,256]{1,0:T(8,128)(2,1)} %refs_9_.1) | copy-start | bytes 786436
  8.3 9.7 %copy-start.3 = (s32[1,27,8,128]{3,2,1,0:T(8,128)S(1)}, s32[1,27,8,128]{3,2,1,0:T(8,128)}, u32[]{:S(2)}) copy-start(s32[1,27,8,128]{3,2,1,0:T(8,128)} %param.17) | copy-start | bytes 331780
  10.6 9.7 %collective-permute-start.3 = (bf16[16,64,512]{2,1,0:T(8,128)(2,1)S(1)}, bf16[16,64,512]{2,1,0:T(8,128)(2,1)S(1)}, u32[]{:S(2)}, u32[]{:S(2)}) collective-permute-start(bf16[16,64,512]{2,1,0:T(8,128)(2,1)S(1)} %get-tuple-element.68), channel_id=1, source_target_pairs={{0,1},{1,0},{2,3},{3,2},{4,5},{5,4},{6,7},{7,6},{8,9},{9,8},{10,11... | collective-permute-start | bytes 3145736 | tf_op jit(solution)/shard_map/ppermute | solution.py:284
  12.3 6.3 %collective-permute-start.1 = (bf16[256,256]{1,0:T(8,128)(2,1)S(1)}, bf16[256,256]{1,0:T(8,128)(2,1)S(1)}, u32[]{:S(2)}, u32[]{:S(2)}) collective-permute-start(bf16[256,256]{1,0:T(8,128)(2,1)S(1)} %get-tuple-element.63.refs_5_), channel_id=1, source_target_pairs={{0,1},{1,2},{2,3},{3,4},{4,5},{5,6},{6,7},{7,8},{8,9},{9,10},{10,1... | collective-permute-start | bytes 393224 | tf_op jit(solution)/shard_map/ppermute | solution.py:284
  14.2 6.1 %collective-permute-start.2 = (bf16[256,256]{1,0:T(8,128)(2,1)S(1)}, bf16[256,256]{1,0:T(8,128)(2,1)S(1)}, u32[]{:S(2)}, u32[]{:S(2)}) collective-permute-start(bf16[256,256]{1,0:T(8,128)(2,1)S(1)} %get-tuple-element.64.refs_4_), channel_id=1, source_target_pairs={{1,0},{2,1},{3,2},{4,3},{5,4},{6,5},{7,6},{8,7},{9,8},{10,9},{11,1... | collective-permute-start | bytes 393224 | tf_op jit(solution)/shard_map/ppermute | solution.py:284
  20.3 2.8 %copy-start.6 = (s32[1,27,8]{1,2,0:T(8,128)S(1)}, s32[1,27,8]{1,2,0:T(8,128)}, u32[]{:S(2)}) copy-start(s32[1,27,8]{1,2,0:T(8,128)} %param.15) | copy-start | bytes 2596
  20.3 2.8 %copy-start.7 = (s32[1,27,8]{1,2,0:T(8,128)S(1)}, s32[1,27,8]{1,2,0:T(8,128)}, u32[]{:S(2)}) copy-start(s32[1,27,8]{1,2,0:T(8,128)} %param.16) | copy-start | bytes 2596
  20.7 10.3 %collective-permute-start.4 = (bf16[8,64,512]{2,1,0:T(8,128)(2,1)S(1)}, bf16[8,64,512]{2,1,0:T(8,128)(2,1)S(1)}, u32[]{:S(2)}, u32[]{:S(2)}) collective-permute-start(bf16[8,64,512]{2,1,0:T(8,128)(2,1)S(1)} %slice.90), channel_id=1, source_target_pairs={{0,2},{1,5},{2,0},{3,7},{4,6},{5,1},{6,4},{7,3},{8,10},{9,13},{10,... | collective-permute-start | bytes 1572872 | tf_op jit(solution)/shard_map/ppermute | solution.py:284
  28.5 4.5 %collective-permute-start.5 = (bf16[8,216,256]{2,1,0:T(8,128)(2,1)S(1)}, bf16[8,216,256]{2,1,0:T(8,128)(2,1)S(1)}, u32[]{:S(2)}, u32[]{:S(2)}) collective-permute-start(bf16[8,216,256]{2,1,0:T(8,128)(2,1)S(1)} %get-tuple-element.78), channel_id=1, source_target_pairs={{0,1},{1,0},{2,3},{3,2},{4,5},{5,4},{6,7},{7,6},{8,9},{9,8},{10,11... | collective-permute-start | bytes 2654216 | tf_op jit(solution)/shard_map/ppermute | solution.py:284
  33.3 10.9 %collective-permute-start.6 = (bf16[4,216,256]{2,1,0:T(8,128)(2,1)S(1)}, bf16[4,216,256]{2,1,0:T(8,128)(2,1)S(1)}, u32[]{:S(2)}, u32[]{:S(2)}) collective-permute-start(bf16[4,216,256]{2,1,0:T(8,128)(2,1)S(1)} %slice.92), channel_id=1, source_target_pairs={{0,2},{1,5},{2,0},{3,7},{4,6},{5,1},{6,4},{7,3},{8,10},{9,13},{10,... | collective-permute-start | bytes 1327112 | tf_op jit(solution)/shard_map/ppermute | solution.py:284
  33.4 9.2 %collective-permute-start.7 = (bf16[4,64,512]{2,1,0:T(8,128)(2,1)S(1)}, bf16[4,64,512]{2,1,0:T(8,128)(2,1)S(1)}, u32[]{:S(2)}, u32[]{:S(2)}) collective-permute-start(bf16[4,64,512]{2,1,0:T(8,128)(2,1)S(1)} %get-tuple-element.88), channel_id=1, source_target_pairs={{0,4},{1,3},{2,6},{3,1},{4,0},{5,7},{6,2},{7,5},{8,12},{9,11},{10,... | collective-permute-start | bytes 786440 | tf_op jit(solution)/shard_map/ppermute | solution.py:284
  40.7 4.6 %collective-permute-start.8 = (bf16[8,216,256]{2,1,0:T(8,128)(2,1)S(1)}, bf16[8,216,256]{2,1,0:T(8,128)(2,1)S(1)}, u32[]{:S(2)}, u32[]{:S(2)}) collective-permute-start(bf16[8,216,256]{2,1,0:T(8,128)(2,1)S(1)} %get-tuple-element.91), channel_id=1, source_target_pairs={{0,1},{1,0},{2,3},{3,2},{4,5},{5,4},{6,7},{7,6},{8,9},{9,8},{10,11... | collective-permute-start | bytes 2654216 | tf_op jit(solution)/shard_map/ppermute | solution.py:284
  44.3 2.0 %copy-start.10 = (f32[4,64,512]{2,1,0:T(8,128)}, f32[4,64,512]{2,1,0:T(8,128)S(1)}, u32[]{:S(2)}) copy-start(f32[4,64,512]{2,1,0:T(8,128)S(1)} %convert_add_fusion.3) | copy-start | bytes 1572868
  44.4 8.4 %collective-permute-start.10 = (bf16[2,216,256]{2,1,0:T(8,128)(2,1)S(1)}, bf16[2,216,256]{2,1,0:T(8,128)(2,1)}, u32[]{:S(2)}, u32[]{:S(2)}) collective-permute-start(bf16[2,216,256]{2,1,0:T(8,128)(2,1)S(1)} %get-tuple-element.99), channel_id=1, source_target_pairs={{0,4},{1,3},{2,6},{3,1},{4,0},{5,7},{6,2},{7,5},{8,12},{9,11},{10,... | collective-permute-start | bytes 663560 | tf_op jit(solution)/shard_map/ppermute | solution.py:284
  46.3 8.5 %collective-permute-start.9 = (bf16[4,216,256]{2,1,0:T(8,128)(2,1)}, bf16[4,216,256]{2,1,0:T(8,128)(2,1)S(1)}, u32[]{:S(2)}, u32[]{:S(2)}) collective-permute-start(bf16[4,216,256]{2,1,0:T(8,128)(2,1)} %slice.91), channel_id=1, source_target_pairs={{0,2},{1,5},{2,0},{3,7},{4,6},{5,1},{6,4},{7,3},{8,10},{9,13},{10,... | collective-permute-start | bytes 1327112 | tf_op jit(solution)/shard_map/ppermute | solution.py:284
  46.3 8.5 %slice-start = ((f32[4,64,512]{2,1,0:T(8,128)}), f32[2,64,512]{2,1,0:T(8,128)S(1)}, s32[]{:S(2)}) async-start(f32[4,64,512]{2,1,0:T(8,128)} %copy-done.10), calls=%async_computation | async-start | bytes 524288 | tf_op jit(solution)/shard_map/slice | solution.py:290
  46.3 8.1 %collective-permute-start.11 = (bf16[2,64,512]{2,1,0:T(8,128)(2,1)S(1)}, bf16[2,64,512]{2,1,0:T(8,128)(2,1)S(1)}, u32[]{:S(2)}, u32[]{:S(2)}) collective-permute-start(bf16[2,64,512]{2,1,0:T(8,128)(2,1)S(1)} %slice.93), channel_id=1, source_target_pairs={{0,8},{1,9},{2,10},{3,11},{4,12},{5,13},{6,14},{7,15},{8,0},{9,1},... | collective-permute-start | bytes 393224 | tf_op jit(solution)/shard_map/ppermute | solution.py:284
  53.9 4.8 %collective-permute-start.13 = (bf16[1,216,256]{2,1,0:T(8,128)(2,1)S(1)}, bf16[1,216,256]{2,1,0:T(8,128)(2,1)S(1)}, u32[]{:S(2)}, u32[]{:S(2)}) collective-permute-start(bf16[1,216,256]{2,1,0:T(8,128)(2,1)S(1)} %slice.95), channel_id=1, source_target_pairs={{0,8},{1,9},{2,10},{3,11},{4,12},{5,13},{6,14},{7,15},{8,0},{9,1},... | collective-permute-start | bytes 331784 | tf_op jit(solution)/shard_map/ppermute | solution.py:284
  54.9 7.0 %collective-permute-start.14 = (bf16[1,64,512]{2,1,0:T(8,128)(2,1)S(1)}, bf16[1,64,512]{2,1,0:T(8,128)(2,1)S(1)}, u32[]{:S(2)}, u32[]{:S(2)}) collective-permute-start(bf16[1,64,512]{2,1,0:T(8,128)(2,1)S(1)} %slice.96), channel_id=1, source_target_pairs={{0,16},{1,17},{2,18},{3,19},{4,20},{5,21},{6,22},{7,23},{8,24},{9,... | collective-permute-start | bytes 196616 | tf_op jit(solution)/shard_map/ppermute | solution.py:284
  57.2 6.0 %collective-permute-start.12 = (bf16[2,216,256]{2,1,0:T(8,128)(2,1)S(1)}, bf16[2,216,256]{2,1,0:T(8,128)(2,1)S(1)}, u32[]{:S(2)}, u32[]{:S(2)}) collective-permute-start(bf16[2,216,256]{2,1,0:T(8,128)(2,1)S(1)} %get-tuple-element.102), channel_id=1, source_target_pairs={{0,4},{1,3},{2,6},{3,1},{4,0},{5,7},{6,2},{7,5},{8,12},{9,11},{10,... | collective-permute-start | bytes 663560 | tf_op jit(solution)/shard_map/ppermute | solution.py:284
  58.7 5.5 %collective-permute-start.16 = (bf16[1,216,256]{2,1,0:T(8,128)(2,1)S(1)}, bf16[1,216,256]{2,1,0:T(8,128)(2,1)S(1)}, u32[]{:S(2)}, u32[]{:S(2)}) collective-permute-start(bf16[1,216,256]{2,1,0:T(8,128)(2,1)S(1)} %get-tuple-element.111), channel_id=1, source_target_pairs={{8,24},{9,25},{10,26},{11,27},{12,28},{13,29},{14,30},{15,31},{16,... | collective-permute-start | bytes 331784 | tf_op jit(solution)/shard_map/ppermute | solution.py:284
  63.3 4.8 %collective-permute-start.15 = (bf16[1,216,256]{2,1,0:T(8,128)(2,1)S(1)}, bf16[1,216,256]{2,1,0:T(8,128)(2,1)S(1)}, u32[]{:S(2)}, u32[]{:S(2)}) collective-permute-start(bf16[1,216,256]{2,1,0:T(8,128)(2,1)S(1)} %slice.94), channel_id=1, source_target_pairs={{0,8},{1,9},{2,10},{3,11},{4,12},{5,13},{6,14},{7,15},{8,0},{9,1},... | collective-permute-start | bytes 331784 | tf_op jit(solution)/shard_map/ppermute | solution.py:284
  68.1 7.5 %collective-permute-start.17 = (bf16[1,216,256]{2,1,0:T(8,128)(2,1)S(1)}, bf16[1,216,256]{2,1,0:T(8,128)(2,1)S(1)}, u32[]{:S(2)}, u32[]{:S(2)}) collective-permute-start(bf16[1,216,256]{2,1,0:T(8,128)(2,1)S(1)} %convert_element_type.72), channel_id=1, source_target_pairs={{0,16},{1,17},{2,18},{3,19},{4,20},{5,21},{6,22},{7,23},{24,8},{25... | collective-permute-start | bytes 331784 | tf_op jit(solution)/shard_map/ppermute | solution.py:284

commit v12 on v11

--- a/solution.py
+++ b/solution.py
@@ -85,10 +85,11 @@
 SMALL = pl.CostEstimate(flops=1 << 20, bytes_accessed=1 << 10, transcendentals=0)
 
 
-def prep_kernel(pre, rows, parents, w_in, cur_in, act, pick, parent_pick, chosen, w, cur):
-    children, slots = rows.shape
+def prep_kernel(pre, lists, w_in, cur_in, act, pick, parent_pick, chosen, w, cur):
+    children, slots = lists.shape[0] // 2, lists.shape[1]
+    rows, parents = lists[:children], lists[children:]
     count, channels = pre.shape
-    columns = turned(parents[...])
+    columns = turned(parents)
     for c in range(children):
         mine = pl.ds(c * slots, slots)
         pick[:, mine] = one_hot(rows[c : c + 1, :], (count, slots), 0)
@@ -100,9 +101,9 @@
     cur[...] = cur_in[...]
 
 
-def prep(pre, rows, parents, w, cur, parent_rows):
+def prep(pre, lists, w, cur, parent_rows):
     count, channels = pre.shape
-    children, slots = rows.shape
+    children, slots = lists.shape[0] // 2, lists.shape[1]
     shapes = (
         (count, channels),
         (count, children * slots),
@@ -114,12 +115,12 @@
     return pl.pallas_call(
         prep_kernel,
         out_shape=tuple(jax.ShapeDtypeStruct(shape, BF) for shape in shapes),
-        in_specs=[VMEM] * 5,
+        in_specs=[VMEM] * 4,
         out_specs=(VMEM,) * len(shapes),
         compiler_params=pltpu.CompilerParams(vmem_limit_bytes=16 << 20),
         cost_estimate=SMALL,
         name="prep",
-    )(pre, rows, parents, w, cur)
+    )(pre, lists, w, cur)
 
 
 def down_kernel(
@@ -286,8 +287,9 @@
 
 def fold(kept, got):
     half = kept.shape[0] // 2
-    total = kept.astype(F32) + got.astype(F32)
-    return total[:half], total[half:].astype(BF)
+    keep = kept[:half].astype(F32) + got[:half].astype(F32)
+    send = kept[half:].astype(F32) + got[half:].astype(F32)
+    return keep, send.astype(BF)
 
 
 def fold_kernel(kept, got, keep, send):
@@ -358,8 +360,7 @@
     previous = moved(coarse_grad[-block_rows:], peers, lambda i: i + 1)
     prepared = prep(
         pre_act,
-        down_rows[0],
-        down_parent[0],
+        jnp.concatenate([down_rows[0], down_parent[0]], 0),
         w_down,
         coarse_grad,
         block_rows + coarse_grad.shape[0],
@@ -410,6 +411,7 @@
     inner_got, outer, low_got = pinned((inner_got, outer, low_got))
     inner, inner_send = middle(inner, inner_got)
     inner_got = xy(inner_send, bits - 1)
+    inner, low_got = pinned((inner, low_got))
 
     low, low_send = fold(low, low_got)
     low_got = z_far(low_send)

time: 76.9 us -> 74.7 us (0.971)
  the two profiles are of different devices: /device:TPU:10 before, /device:TPU:0 now
where the time goes in v12:
time: 74.7 us; the launch traced here: 73.7 us
  starting transfers between devices  30.1 us (40%)
  waiting for transfers between devices  20.2 us (27%)
  Pallas kernels  15.8 us (21%)
  local copies, waits for them, and re-layouts  4.28 us (6%)
  other arithmetic  2.46 us (3%)
  between operations  0.87 us (1%)
    ppermute x18, starting transfers between devices, moved(): lax.ppermute(x, 'space', [(i, j) for i, j in pairs if j is not None and 0...  30.1 us
    ppermute x18, waiting for transfers between devices, moved(): lax.ppermute(x, 'space', [(i, j) for i, j in pairs if j is not None and 0...  20.2 us
    pallas_call x2, Pallas kernels, conv(): pl.pallas_call(functools.partial(conv_kernel, conv_plan(kernel, channels,...  12 us
    unnamed x17, local copies, waits for them, and re-layouts  4.28 us
    pallas_call x1, Pallas kernels, down(): pl.pallas_call(functools.partial(down_kernel, bits), out_shape=(side, sid...  2.27 us
  transfers between devices with their start and end apart: 18, of which 12 were waited for; matrix products, arithmetic and copies ran while one was open for 2% of the time, Pallas kernels for 18%

profile of v12, /device:TPU:0, one launch (start us, length us, event | category | flops | bytes accessed | tf_op | source)
XLA Modules:
  0.0 73.7 jit_solution(1221355773583322312)
XLA Ops:
  0.6 2.4 %collective-permute-start = (bf16[128,512]{1,0:T(8,128)(2,1)}, bf16[128,512]{1,0:T(8,128)(2,1)S(1)}, u32[]{:S(2)}, u32[]{:S(2)}) collective-permute-start(bf16[128,512]{1,0:T(8,128)(2,1)} %cur_in.1), channel_id=1, source_target_pairs={{0,1},{1,2},{2,3},{3,4},{4,5},{5,6},{6,7},{7,8},{8,9},{9,10},{10,1... | collective-permute-start | bytes 393224 | tf_op jit(solution)/shard_map/ppermute | solution.py:285
  3.0 0.7 pad_add_fusion.lists
  3.7 1.6 %copy-done.1 = bf16[2048,512]{1,0:T(8,128)(2,1)S(1)} copy-done((bf16[2048,512]{1,0:T(8,128)(2,1)S(1)}, bf16[2048,512]{1,0:T(8,128)(2,1)}, u32[]{:S(2)}) %copy-start.1) | copy-done | bytes 2097176
  5.3 0.9 %copy-done.4 = bf16[512,256]{1,0:T(8,128)(2,1)S(1)} copy-done((bf16[512,256]{1,0:T(8,128)(2,1)S(1)}, bf16[512,256]{1,0:T(8,128)(2,1)}, u32[]{:S(2)}) %copy-start.4) | copy-done | bytes 262168
  6.3 0.9 %copy-done.5 = bf16[128,512]{1,0:T(8,128)(2,1)S(1)} copy-done((bf16[128,512]{1,0:T(8,128)(2,1)S(1)}, bf16[128,512]{1,0:T(8,128)(2,1)}, u32[]{:S(2)}) %copy-start.5) | copy-done | bytes 131096
  7.2 0.9 %prep.1 = (bf16[512,256]{1,0:T(8,128)(2,1)S(1)}, bf16[512,1024]{1,0:T(8,128)(2,1)S(1)}, bf16[1024,256]{1,0:T(8,128)(2,1)S(1)}, bf16[256,1024]{1,0:T(8,128)(2,1)S...) custom-call(bf16[512,256]{1,0:T(8,128)(2,1)S(1)} %copy-done.4, s32[16,128]{1,0:T(8,128)S(1)} %pad_add_fusion.lists, ...), custom_call_target="tpu_custom_call" | custom-call | flops 1048576 | bytes 1024 | tf_op jit(solution)/shard_map/prep/pallas_call | solution.py:115
  8.1 0.0 collective-permute-done.prev
  8.1 0.0 copy-start
  8.1 0.0 copy-start.2
  8.1 0.0 copy-start.3
  8.1 2.3 %down.1 = (bf16[256,256]{1,0:T(8,128)(2,1)S(1)}, bf16[256,256]{1,0:T(8,128)(2,1)S(1)}, bf16[16,64,512]{2,1,0:T(8,128)(2,1)S(1)}, bf16[16,64,512]{2,1,0:T(8,128)(2,1)S(1)}) custom-call(s32[1]{0:T(128)} %bitcast.me.refs_0_, bf16[128,512]{1,0:T(8,128)(2,1)S(1)} %collective-permute-done.prev, bf16[512,256]{1,0:T(8,128)(2,1)S(1)} %get-tuple-element.59.act, ...), custom_call_target="tpu_custom_call" | custom-call | flops 1048576 | bytes 1024 | tf_op jit(solution)/shard_map/down/pallas_call | solution.py:155
  10.4 2.7 %collective-permute-start.3 = (bf16[16,64,512]{2,1,0:T(8,128)(2,1)S(1)}, bf16[16,64,512]{2,1,0:T(8,128)(2,1)S(1)}, u32[]{:S(2)}, u32[]{:S(2)}) collective-permute-start(bf16[16,64,512]{2,1,0:T(8,128)(2,1)S(1)} %get-tuple-element.70), channel_id=1, source_target_pairs={{0,1},{1,0},{2,3},{3,2},{4,5},{5,4},{6,7},{7,6},{8,9},{9,8},{10,11... | collective-permute-start | bytes 3145736 | tf_op jit(solution)/shard_map/ppermute | solution.py:285
  13.1 1.9 %collective-permute-start.1 = (bf16[256,256]{1,0:T(8,128)(2,1)S(1)}, bf16[256,256]{1,0:T(8,128)(2,1)S(1)}, u32[]{:S(2)}, u32[]{:S(2)}) collective-permute-start(bf16[256,256]{1,0:T(8,128)(2,1)S(1)} %get-tuple-element.65.refs_5_), channel_id=1, source_target_pairs={{0,1},{1,2},{2,3},{3,4},{4,5},{5,6},{6,7},{7,8},{8,9},{9,10},{10,1... | collective-permute-start | bytes 393224 | tf_op jit(solution)/shard_map/ppermute | solution.py:285
  15.0 1.5 %collective-permute-start.2 = (bf16[256,256]{1,0:T(8,128)(2,1)S(1)}, bf16[256,256]{1,0:T(8,128)(2,1)S(1)}, u32[]{:S(2)}, u32[]{:S(2)}) collective-permute-start(bf16[256,256]{1,0:T(8,128)(2,1)S(1)} %get-tuple-element.66.refs_4_), channel_id=1, source_target_pairs={{1,0},{2,1},{3,2},{4,3},{5,4},{6,5},{7,6},{8,7},{9,8},{10,9},{11,1... | collective-permute-start | bytes 393224 | tf_op jit(solution)/shard_map/ppermute | solution.py:285
  16.5 0.0 copy-done
  16.5 0.0 copy-done.2
  16.5 0.0 copy-done.3
  16.5 0.3 turn.1
  16.8 0.0 copy-start.6
  16.8 0.0 copy-start.7
  16.8 0.0 collective-permute-done.1.refs_3_
  16.8 2.5 %collective-permute-done.2.refs_6_ = bf16[256,256]{1,0:T(8,128)(2,1)S(1)} collective-permute-done((bf16[256,256]{1,0:T(8,128)(2,1)S(1)}, bf16[256,256]{1,0:T(8,128)(2,1)S(1)}, u32[]{:S(2)}, u32[]{:S(2)}) %collective-permute-start.2) | collective-permute-done | bytes 131104 | tf_op jit(solution)/shard_map/ppermute | solution.py:285
  19.3 0.0 collective-permute-done.3
  19.3 0.3 add_convert_fusion
  19.6 3.4 %collective-permute-start.4 = (bf16[8,64,512]{2,1,0:T(8,128)(2,1)S(1)}, bf16[8,64,512]{2,1,0:T(8,128)(2,1)S(1)}, u32[]{:S(2)}, u32[]{:S(2)}) collective-permute-start(bf16[8,64,512]{2,1,0:T(8,128)(2,1)S(1)} %get-tuple-element.117), channel_id=1, source_target_pairs={{0,2},{1,5},{2,0},{3,7},{4,6},{5,1},{6,4},{7,3},{8,10},{9,13},{10,... | collective-permute-start | bytes 1572872 | tf_op jit(solution)/shard_map/ppermute | solution.py:285
  23.0 0.0 copy-done.6
  23.0 5.3 %conv.2 = (f32[512,256]{1,0:T(8,128)S(1)}, bf16[8,216,256]{2,1,0:T(8,128)(2,1)S(1)}, bf16[8,216,256]{2,1,0:T(8,128)(2,1)S(1)}) custom-call(s32[1]{0:T(128)} %bitcast.me.refs_0_, s32[8,27]{1,0:T(8,128)S(1)} %bitcast.17, s32[8,27]{1,0:T(8,128)S(1)} %bitcast.19, bf16[256,256]{1,0:T(8,128)(2,1)S(1)} %collective-permute-done.1.refs_3_, ...), custom_call_target="tpu_custom_call" | custom-call | flops 1048576 | bytes 1024 | tf_op jit(solution)/shard_map/conv/pallas_call | solution.py:258
  28.3 1.5 %collective-permute-start.5 = (bf16[8,216,256]{2,1,0:T(8,128)(2,1)S(1)}, bf16[8,216,256]{2,1,0:T(8,128)(2,1)S(1)}, u32[]{:S(2)}, u32[]{:S(2)}) collective-permute-start(bf16[8,216,256]{2,1,0:T(8,128)(2,1)S(1)} %get-tuple-element.80), channel_id=1, source_target_pairs={{0,1},{1,0},{2,3},{3,2},{4,5},{5,4},{6,7},{7,6},{8,9},{9,8},{10,11... | collective-permute-start | bytes 2654216 | tf_op jit(solution)/shard_map/ppermute | solution.py:285
  29.9 0.3 collective-permute-done.4.got
  30.2 0.1 fold.3
  30.3 1.7 %collective-permute-done.5 = bf16[8,216,256]{2,1,0:T(8,128)(2,1)S(1)} collective-permute-done((bf16[8,216,256]{2,1,0:T(8,128)(2,1)S(1)}, bf16[8,216,256]{2,1,0:T(8,128)(2,1)S(1)}, u32[]{:S(2)}, u32[]{:S(2)}) %collective-permute-start.5) | collective-permute-done | bytes 884768 | tf_op jit(solution)/shard_map/ppermute | solution.py:285
  31.9 0.2 convert_add_fusion.2
  32.2 3.4 %collective-permute-start.6 = (bf16[4,216,256]{2,1,0:T(8,128)(2,1)S(1)}, bf16[4,216,256]{2,1,0:T(8,128)(2,1)S(1)}, u32[]{:S(2)}, u32[]{:S(2)}) collective-permute-start(bf16[4,216,256]{2,1,0:T(8,128)(2,1)S(1)} %get-tuple-element.88), channel_id=1, source_target_pairs={{0,2},{1,5},{2,0},{3,7},{4,6},{5,1},{6,4},{7,3},{8,10},{9,13},{10,... | collective-permute-start | bytes 1327112 | tf_op jit(solution)/shard_map/ppermute | solution.py:285
  35.5 0.3 collective-permute-start.7
  35.8 6.7 %conv.3 = (bf16[512,256]{1,0:T(8,128)(2,1)}, bf16[8,216,256]{2,1,0:T(8,128)(2,1)S(1)}, bf16[8,216,256]{2,1,0:T(8,128)(2,1)S(1)}) custom-call(s32[1]{0:T(128)} %bitcast.me.refs_0_, s32[8,27]{1,0:T(8,128)S(1)} %bitcast.18, s32[8,27]{1,0:T(8,128)S(1)} %bitcast.20, bf16[256,256]{1,0:T(8,128)(2,1)S(1)} %collective-permute-done.1.refs_3_, ...), custom_call_target="tpu_custom_call" | custom-call | flops 1048576 | bytes 1024 | tf_op jit(solution)/shard_map/conv/pallas_call | solution.py:258
  42.5 0.1 collective-permute-start.8
  42.6 0.1 collective-permute-done.7
  42.7 1.8 %collective-permute-done.6.got = bf16[4,216,256]{2,1,0:T(8,128)(2,1)S(1)} collective-permute-done((bf16[4,216,256]{2,1,0:T(8,128)(2,1)S(1)}, bf16[4,216,256]{2,1,0:T(8,128)(2,1)S(1)}, u32[]{:S(2)}, u32[]{:S(2)}) %collective-permute-start.6) | collective-permute-done | bytes 442400 | tf_op jit(solution)/shard_map/ppermute | solution.py:285
  44.6 0.1 fold.4
  44.7 0.4 collective-permute-start.10
  45.1 0.1 add_convert_fusion.3
  45.1 0.0 collective-permute-done.8
  45.2 0.2 add_convert_fusion.1
  45.4 2.1 %collective-permute-start.9 = (bf16[4,216,256]{2,1,0:T(8,128)(2,1)S(1)}, bf16[4,216,256]{2,1,0:T(8,128)(2,1)S(1)}, u32[]{:S(2)}, u32[]{:S(2)}) collective-permute-start(bf16[4,216,256]{2,1,0:T(8,128)(2,1)S(1)} %get-tuple-element.119), channel_id=1, source_target_pairs={{0,2},{1,5},{2,0},{3,7},{4,6},{5,1},{6,4},{7,3},{8,10},{9,13},{10,... | collective-permute-start | bytes 1327112 | tf_op jit(solution)/shard_map/ppermute | solution.py:285
  47.5 1.6 %collective-permute-start.11 = (bf16[2,64,512]{2,1,0:T(8,128)(2,1)S(1)}, bf16[2,64,512]{2,1,0:T(8,128)(2,1)S(1)}, u32[]{:S(2)}, u32[]{:S(2)}) collective-permute-start(bf16[2,64,512]{2,1,0:T(8,128)(2,1)S(1)} %get-tuple-element.123), channel_id=1, source_target_pairs={{0,8},{1,9},{2,10},{3,11},{4,12},{5,13},{6,14},{7,15},{8,0},{9,1},... | collective-permute-start | bytes 393224 | tf_op jit(solution)/shard_map/ppermute | solution.py:285
  49.0 3.4 %collective-permute-done.10 = bf16[2,216,256]{2,1,0:T(8,128)(2,1)S(1)} collective-permute-done((bf16[2,216,256]{2,1,0:T(8,128)(2,1)S(1)}, bf16[2,216,256]{2,1,0:T(8,128)(2,1)S(1)}, u32[]{:S(2)}, u32[]{:S(2)}) %collective-permute-start.10) | collective-permute-done | bytes 221216 | tf_op jit(solution)/shard_map/ppermute | solution.py:285
  52.4 0.1 add_convert_fusion.5
  52.5 1.6 %collective-permute-start.13 = (bf16[1,216,256]{2,1,0:T(8,128)(2,1)S(1)}, bf16[1,216,256]{2,1,0:T(8,128)(2,1)S(1)}, u32[]{:S(2)}, u32[]{:S(2)}) collective-permute-start(bf16[1,216,256]{2,1,0:T(8,128)(2,1)S(1)} %get-tuple-element.125), channel_id=1, source_target_pairs={{0,8},{1,9},{2,10},{3,11},{4,12},{5,13},{6,14},{7,15},{8,0},{9,1},... | collective-permute-start | bytes 331784 | tf_op jit(solution)/shard_map/ppermute | solution.py:285
  54.1 0.0 collective-permute-done.11
  54.1 0.1 collective-permute-done.9.got
  54.3 0.1 fold.5
  54.4 2.7 %collective-permute-start.14 = (bf16[1,64,512]{2,1,0:T(8,128)(2,1)S(1)}, bf16[1,64,512]{2,1,0:T(8,128)(2,1)S(1)}, u32[]{:S(2)}, u32[]{:S(2)}) collective-permute-start(bf16[1,64,512]{2,1,0:T(8,128)(2,1)S(1)} %add_convert_fusion.6), channel_id=1, source_target_pairs={{0,16},{1,17},{2,18},{3,19},{4,20},{5,21},{6,22},{7,23},{8,24},{9,... | collective-permute-start | bytes 196616 | tf_op jit(solution)/shard_map/ppermute | solution.py:285
  57.0 1.2 %collective-permute-start.12 = (bf16[2,216,256]{2,1,0:T(8,128)(2,1)S(1)}, bf16[2,216,256]{2,1,0:T(8,128)(2,1)S(1)}, u32[]{:S(2)}, u32[]{:S(2)}) collective-permute-start(bf16[2,216,256]{2,1,0:T(8,128)(2,1)S(1)} %get-tuple-element.106), channel_id=1, source_target_pairs={{0,4},{1,3},{2,6},{3,1},{4,0},{5,7},{6,2},{7,5},{8,12},{9,11},{10,... | collective-permute-start | bytes 663560 | tf_op jit(solution)/shard_map/ppermute | solution.py:285
  58.2 0.0 collective-permute-done.13
  58.2 1.3 %collective-permute-start.16 = (bf16[1,216,256]{2,1,0:T(8,128)(2,1)S(1)}, bf16[1,216,256]{2,1,0:T(8,128)(2,1)S(1)}, u32[]{:S(2)}, u32[]{:S(2)}) collective-permute-start(bf16[1,216,256]{2,1,0:T(8,128)(2,1)S(1)} %get-tuple-element.115), channel_id=1, source_target_pairs={{8,24},{9,25},{10,26},{11,27},{12,28},{13,29},{14,30},{15,31},{16,... | collective-permute-start | bytes 331784 | tf_op jit(solution)/shard_map/ppermute | solution.py:285
  59.5 2.1 %collective-permute-done.14 = bf16[1,64,512]{2,1,0:T(8,128)(2,1)S(1)} collective-permute-done((bf16[1,64,512]{2,1,0:T(8,128)(2,1)S(1)}, bf16[1,64,512]{2,1,0:T(8,128)(2,1)S(1)}, u32[]{:S(2)}, u32[]{:S(2)}) %collective-permute-start.14) | collective-permute-done | bytes 65568 | tf_op jit(solution)/shard_map/ppermute | solution.py:285
  61.7 1.3 %collective-permute-done.12 = bf16[2,216,256]{2,1,0:T(8,128)(2,1)S(1)} collective-permute-done((bf16[2,216,256]{2,1,0:T(8,128)(2,1)S(1)}, bf16[2,216,256]{2,1,0:T(8,128)(2,1)S(1)}, u32[]{:S(2)}, u32[]{:S(2)}) %collective-permute-start.12) | collective-permute-done | bytes 221216 | tf_op jit(solution)/shard_map/ppermute | solution.py:285
  63.0 0.4 collective-permute-start.15
  63.4 2.9 %collective-permute-done.16 = bf16[1,216,256]{2,1,0:T(8,128)(2,1)S(1)} collective-permute-done((bf16[1,216,256]{2,1,0:T(8,128)(2,1)S(1)}, bf16[1,216,256]{2,1,0:T(8,128)(2,1)S(1)}, u32[]{:S(2)}, u32[]{:S(2)}) %collective-permute-start.16) | collective-permute-done | bytes 110624 | tf_op jit(solution)/shard_map/ppermute | solution.py:285
  66.3 2.3 %collective-permute-done.15 = bf16[1,216,256]{2,1,0:T(8,128)(2,1)S(1)} collective-permute-done((bf16[1,216,256]{2,1,0:T(8,128)(2,1)S(1)}, bf16[1,216,256]{2,1,0:T(8,128)(2,1)S(1)}, u32[]{:S(2)}, u32[]{:S(2)}) %collective-permute-start.15) | collective-permute-done | bytes 110624 | tf_op jit(solution)/shard_map/ppermute | solution.py:285
  68.6 1.8 %collective-permute-start.17 = (bf16[1,216,256]{2,1,0:T(8,128)(2,1)S(1)}, bf16[1,216,256]{2,1,0:T(8,128)(2,1)S(1)}, u32[]{:S(2)}, u32[]{:S(2)}) collective-permute-start(bf16[1,216,256]{2,1,0:T(8,128)(2,1)S(1)} %convert_element_type.132), channel_id=1, source_target_pairs={{0,16},{1,17},{2,18},{3,19},{4,20},{5,21},{6,22},{7,23},{24,8},{25... | collective-permute-start | bytes 331784 | tf_op jit(solution)/shard_map/ppermute | solution.py:285
  70.5 0.7 multiply_bitcast_fusion.1
  71.1 1.7 %collective-permute-done.17 = bf16[1,216,256]{2,1,0:T(8,128)(2,1)S(1)} collective-permute-done((bf16[1,216,256]{2,1,0:T(8,128)(2,1)S(1)}, bf16[1,216,256]{2,1,0:T(8,128)(2,1)S(1)}, u32[]{:S(2)}, u32[]{:S(2)}) %collective-permute-start.17) | collective-permute-done | bytes 110624 | tf_op jit(solution)/shard_map/ppermute | solution.py:285
  72.9 0.8 %copy.13 = f32[27,2,8,128]{3,1,2,0:T(2,128)} copy(f32[27,2,8,128]{3,2,1,0:T(8,128)S(1)} %multiply_bitcast_fusion) | data formatting | bytes 442368
  (11 shorter events, 0.2 us)
Async XLA Ops:
  0.6 7.4 %collective-permute-start = (bf16[128,512]{1,0:T(8,128)(2,1)}, bf16[128,512]{1,0:T(8,128)(2,1)S(1)}, u32[]{:S(2)}, u32[]{:S(2)}) collective-permute-start(bf16[128,512]{1,0:T(8,128)(2,1)} %cur_in.1), channel_id=1, source_target_pairs={{0,1},{1,2},{2,3},{3,4},{4,5},{5,6},{6,7},{7,8},{8,9},{9,10},{10,1... | collective-permute-start | bytes 393224 | tf_op jit(solution)/shard_map/ppermute | solution.py:285
  3.7 1.6 %copy-start.1 = (bf16[2048,512]{1,0:T(8,128)(2,1)S(1)}, bf16[2048,512]{1,0:T(8,128)(2,1)}, u32[]{:S(2)}) copy-start(bf16[2048,512]{1,0:T(8,128)(2,1)} %w_in.1) | copy-start | bytes 6291460
  5.3 0.9 %copy-start.4 = (bf16[512,256]{1,0:T(8,128)(2,1)S(1)}, bf16[512,256]{1,0:T(8,128)(2,1)}, u32[]{:S(2)}) copy-start(bf16[512,256]{1,0:T(8,128)(2,1)} %pre.1) | copy-start | bytes 786436
  6.3 0.9 %copy-start.5 = (bf16[128,512]{1,0:T(8,128)(2,1)S(1)}, bf16[128,512]{1,0:T(8,128)(2,1)}, u32[]{:S(2)}) copy-start(bf16[128,512]{1,0:T(8,128)(2,1)} %cur_in.1) | copy-start | bytes 393220
  8.1 8.4 %copy-start = (bf16[6912,256]{1,0:T(8,128)(2,1)S(1)}, bf16[6912,256]{1,0:T(8,128)(2,1)}, u32[]{:S(2)}) copy-start(bf16[6912,256]{1,0:T(8,128)(2,1)} %refs_7_.3) | copy-start | bytes 10616836
  8.1 8.4 %copy-start.2 = (bf16[512,256]{1,0:T(8,128)(2,1)S(1)}, bf16[512,256]{1,0:T(8,128)(2,1)}, u32[]{:S(2)}) copy-start(bf16[512,256]{1,0:T(8,128)(2,1)} %refs_9_.1) | copy-start | bytes 786436
  8.1 8.4 %copy-start.3 = (s32[1,27,8,128]{3,2,1,0:T(8,128)S(1)}, s32[1,27,8,128]{3,2,1,0:T(8,128)}, u32[]{:S(2)}) copy-start(s32[1,27,8,128]{3,2,1,0:T(8,128)} %param.17) | copy-start | bytes 331780
  10.4 8.9 %collective-permute-start.3 = (bf16[16,64,512]{2,1,0:T(8,128)(2,1)S(1)}, bf16[16,64,512]{2,1,0:T(8,128)(2,1)S(1)}, u32[]{:S(2)}, u32[]{:S(2)}) collective-permute-start(bf16[16,64,512]{2,1,0:T(8,128)(2,1)S(1)} %get-tuple-element.70), channel_id=1, source_target_pairs={{0,1},{1,0},{2,3},{3,2},{4,5},{5,4},{6,7},{7,6},{8,9},{9,8},{10,11... | collective-permute-start | bytes 3145736 | tf_op jit(solution)/shard_map/ppermute | solution.py:285
  13.1 3.8 %collective-permute-start.1 = (bf16[256,256]{1,0:T(8,128)(2,1)S(1)}, bf16[256,256]{1,0:T(8,128)(2,1)S(1)}, u32[]{:S(2)}, u32[]{:S(2)}) collective-permute-start(bf16[256,256]{1,0:T(8,128)(2,1)S(1)} %get-tuple-element.65.refs_5_), channel_id=1, source_target_pairs={{0,1},{1,2},{2,3},{3,4},{4,5},{5,6},{6,7},{7,8},{8,9},{9,10},{10,1... | collective-permute-start | bytes 393224 | tf_op jit(solution)/shard_map/ppermute | solution.py:285
  15.0 4.3 %collective-permute-start.2 = (bf16[256,256]{1,0:T(8,128)(2,1)S(1)}, bf16[256,256]{1,0:T(8,128)(2,1)S(1)}, u32[]{:S(2)}, u32[]{:S(2)}) collective-permute-start(bf16[256,256]{1,0:T(8,128)(2,1)S(1)} %get-tuple-element.66.refs_4_), channel_id=1, source_target_pairs={{1,0},{2,1},{3,2},{4,3},{5,4},{6,5},{7,6},{8,7},{9,8},{10,9},{11,1... | collective-permute-start | bytes 393224 | tf_op jit(solution)/shard_map/ppermute | solution.py:285
  16.8 6.2 %copy-start.6 = (s32[1,27,8]{1,2,0:T(8,128)S(1)}, s32[1,27,8]{1,2,0:T(8,128)}, u32[]{:S(2)}) copy-start(s32[1,27,8]{1,2,0:T(8,128)} %param.15) | copy-start | bytes 2596
  16.8 6.2 %copy-start.7 = (s32[1,27,8]{1,2,0:T(8,128)S(1)}, s32[1,27,8]{1,2,0:T(8,128)}, u32[]{:S(2)}) copy-start(s32[1,27,8]{1,2,0:T(8,128)} %param.16) | copy-start | bytes 2596
  19.6 10.5 %collective-permute-start.4 = (bf16[8,64,512]{2,1,0:T(8,128)(2,1)S(1)}, bf16[8,64,512]{2,1,0:T(8,128)(2,1)S(1)}, u32[]{:S(2)}, u32[]{:S(2)}) collective-permute-start(bf16[8,64,512]{2,1,0:T(8,128)(2,1)S(1)} %get-tuple-element.117), channel_id=1, source_target_pairs={{0,2},{1,5},{2,0},{3,7},{4,6},{5,1},{6,4},{7,3},{8,10},{9,13},{10,... | collective-permute-start | bytes 1572872 | tf_op jit(solution)/shard_map/ppermute | solution.py:285
  28.3 3.6 %collective-permute-start.5 = (bf16[8,216,256]{2,1,0:T(8,128)(2,1)S(1)}, bf16[8,216,256]{2,1,0:T(8,128)(2,1)S(1)}, u32[]{:S(2)}, u32[]{:S(2)}) collective-permute-start(bf16[8,216,256]{2,1,0:T(8,128)(2,1)S(1)} %get-tuple-element.80), channel_id=1, source_target_pairs={{0,1},{1,0},{2,3},{3,2},{4,5},{5,4},{6,7},{7,6},{8,9},{9,8},{10,11... | collective-permute-start | bytes 2654216 | tf_op jit(solution)/shard_map/ppermute | solution.py:285
  32.2 12.4 %collective-permute-start.6 = (bf16[4,216,256]{2,1,0:T(8,128)(2,1)S(1)}, bf16[4,216,256]{2,1,0:T(8,128)(2,1)S(1)}, u32[]{:S(2)}, u32[]{:S(2)}) collective-permute-start(bf16[4,216,256]{2,1,0:T(8,128)(2,1)S(1)} %get-tuple-element.88), channel_id=1, source_target_pairs={{0,2},{1,5},{2,0},{3,7},{4,6},{5,1},{6,4},{7,3},{8,10},{9,13},{10,... | collective-permute-start | bytes 1327112 | tf_op jit(solution)/shard_map/ppermute | solution.py:285
  35.5 7.2 %collective-permute-start.7 = (bf16[4,64,512]{2,1,0:T(8,128)(2,1)S(1)}, bf16[4,64,512]{2,1,0:T(8,128)(2,1)S(1)}, u32[]{:S(2)}, u32[]{:S(2)}) collective-permute-start(bf16[4,64,512]{2,1,0:T(8,128)(2,1)S(1)} %get-tuple-element.90), channel_id=1, source_target_pairs={{0,4},{1,3},{2,6},{3,1},{4,0},{5,7},{6,2},{7,5},{8,12},{9,11},{10,... | collective-permute-start | bytes 786440 | tf_op jit(solution)/shard_map/ppermute | solution.py:285
  42.5 2.6 %collective-permute-start.8 = (bf16[8,216,256]{2,1,0:T(8,128)(2,1)S(1)}, bf16[8,216,256]{2,1,0:T(8,128)(2,1)S(1)}, u32[]{:S(2)}, u32[]{:S(2)}) collective-permute-start(bf16[8,216,256]{2,1,0:T(8,128)(2,1)S(1)} %get-tuple-element.93), channel_id=1, source_target_pairs={{0,1},{1,0},{2,3},{3,2},{4,5},{5,4},{6,7},{7,6},{8,9},{9,8},{10,11... | collective-permute-start | bytes 2654216 | tf_op jit(solution)/shard_map/ppermute | solution.py:285
  44.7 7.7 %collective-permute-start.10 = (bf16[2,216,256]{2,1,0:T(8,128)(2,1)S(1)}, bf16[2,216,256]{2,1,0:T(8,128)(2,1)S(1)}, u32[]{:S(2)}, u32[]{:S(2)}) collective-permute-start(bf16[2,216,256]{2,1,0:T(8,128)(2,1)S(1)} %get-tuple-element.101), channel_id=1, source_target_pairs={{0,4},{1,3},{2,6},{3,1},{4,0},{5,7},{6,2},{7,5},{8,12},{9,11},{10,... | collective-permute-start | bytes 663560 | tf_op jit(solution)/shard_map/ppermute | solution.py:285
  45.4 8.9 %collective-permute-start.9 = (bf16[4,216,256]{2,1,0:T(8,128)(2,1)S(1)}, bf16[4,216,256]{2,1,0:T(8,128)(2,1)S(1)}, u32[]{:S(2)}, u32[]{:S(2)}) collective-permute-start(bf16[4,216,256]{2,1,0:T(8,128)(2,1)S(1)} %get-tuple-element.119), channel_id=1, source_target_pairs={{0,2},{1,5},{2,0},{3,7},{4,6},{5,1},{6,4},{7,3},{8,10},{9,13},{10,... | collective-permute-start | bytes 1327112 | tf_op jit(solution)/shard_map/ppermute | solution.py:285
  47.5 6.7 %collective-permute-start.11 = (bf16[2,64,512]{2,1,0:T(8,128)(2,1)S(1)}, bf16[2,64,512]{2,1,0:T(8,128)(2,1)S(1)}, u32[]{:S(2)}, u32[]{:S(2)}) collective-permute-start(bf16[2,64,512]{2,1,0:T(8,128)(2,1)S(1)} %get-tuple-element.123), channel_id=1, source_target_pairs={{0,8},{1,9},{2,10},{3,11},{4,12},{5,13},{6,14},{7,15},{8,0},{9,1},... | collective-permute-start | bytes 393224 | tf_op jit(solution)/shard_map/ppermute | solution.py:285
  52.5 5.7 %collective-permute-start.13 = (bf16[1,216,256]{2,1,0:T(8,128)(2,1)S(1)}, bf16[1,216,256]{2,1,0:T(8,128)(2,1)S(1)}, u32[]{:S(2)}, u32[]{:S(2)}) collective-permute-start(bf16[1,216,256]{2,1,0:T(8,128)(2,1)S(1)} %get-tuple-element.125), channel_id=1, source_target_pairs={{0,8},{1,9},{2,10},{3,11},{4,12},{5,13},{6,14},{7,15},{8,0},{9,1},... | collective-permute-start | bytes 331784 | tf_op jit(solution)/shard_map/ppermute | solution.py:285
  54.4 7.3 %collective-permute-start.14 = (bf16[1,64,512]{2,1,0:T(8,128)(2,1)S(1)}, bf16[1,64,512]{2,1,0:T(8,128)(2,1)S(1)}, u32[]{:S(2)}, u32[]{:S(2)}) collective-permute-start(bf16[1,64,512]{2,1,0:T(8,128)(2,1)S(1)} %add_convert_fusion.6), channel_id=1, source_target_pairs={{0,16},{1,17},{2,18},{3,19},{4,20},{5,21},{6,22},{7,23},{8,24},{9,... | collective-permute-start | bytes 196616 | tf_op jit(solution)/shard_map/ppermute | solution.py:285
  57.0 5.9 %collective-permute-start.12 = (bf16[2,216,256]{2,1,0:T(8,128)(2,1)S(1)}, bf16[2,216,256]{2,1,0:T(8,128)(2,1)S(1)}, u32[]{:S(2)}, u32[]{:S(2)}) collective-permute-start(bf16[2,216,256]{2,1,0:T(8,128)(2,1)S(1)} %get-tuple-element.106), channel_id=1, source_target_pairs={{0,4},{1,3},{2,6},{3,1},{4,0},{5,7},{6,2},{7,5},{8,12},{9,11},{10,... | collective-permute-start | bytes 663560 | tf_op jit(solution)/shard_map/ppermute | solution.py:285
  58.2 8.0 %collective-permute-start.16 = (bf16[1,216,256]{2,1,0:T(8,128)(2,1)S(1)}, bf16[1,216,256]{2,1,0:T(8,128)(2,1)S(1)}, u32[]{:S(2)}, u32[]{:S(2)}) collective-permute-start(bf16[1,216,256]{2,1,0:T(8,128)(2,1)S(1)} %get-tuple-element.115), channel_id=1, source_target_pairs={{8,24},{9,25},{10,26},{11,27},{12,28},{13,29},{14,30},{15,31},{16,... | collective-permute-start | bytes 331784 | tf_op jit(solution)/shard_map/ppermute | solution.py:285
  63.0 5.6 %collective-permute-start.15 = (bf16[1,216,256]{2,1,0:T(8,128)(2,1)S(1)}, bf16[1,216,256]{2,1,0:T(8,128)(2,1)S(1)}, u32[]{:S(2)}, u32[]{:S(2)}) collective-permute-start(bf16[1,216,256]{2,1,0:T(8,128)(2,1)S(1)} %add_convert_fusion.4), channel_id=1, source_target_pairs={{0,8},{1,9},{2,10},{3,11},{4,12},{5,13},{6,14},{7,15},{8,0},{9,1},... | collective-permute-start | bytes 331784 | tf_op jit(solution)/shard_map/ppermute | solution.py:285
  68.6 4.2 %collective-permute-start.17 = (bf16[1,216,256]{2,1,0:T(8,128)(2,1)S(1)}, bf16[1,216,256]{2,1,0:T(8,128)(2,1)S(1)}, u32[]{:S(2)}, u32[]{:S(2)}) collective-permute-start(bf16[1,216,256]{2,1,0:T(8,128)(2,1)S(1)} %convert_element_type.132), channel_id=1, source_target_pairs={{0,16},{1,17},{2,18},{3,19},{4,20},{5,21},{6,22},{7,23},{24,8},{25... | collective-permute-start | bytes 331784 | tf_op jit(solution)/shard_map/ppermute | solution.py:285

commit v13 on v12

--- a/solution.py
+++ b/solution.py
@@ -205,11 +205,11 @@
 def conv_kernel(plan, bits, quarters, begun, *refs):
     me, src, tgt, before, head, tail, after, w, *rest = refs
     if begun:
-        pairs, feats, partial, grad, keep, send, both, ext, acc, col0, col1, tab, feats_t = rest
+        pairs, feats, partial, grad, keep, send, both, ext, acc, col0, col1, col2, tab, feats_t = rest
         turn_kernel(pairs, feats, w, tab, feats_t)
     else:
-        tab, feats_t, grad, keep, send, both, ext, acc, col0, col1 = rest
-    cols = (col0, col1)
+        tab, feats_t, grad, keep, send, both, ext, acc, col0, col1, col2 = rest
+    cols = (col0, col1, col2)
     slots = src.shape[0]
     blocks, rows, channels = col0.shape
     count = feats_t.shape[1]
@@ -233,14 +233,22 @@
             col[owner] = col[owner] + piece
 
     gather(plan[0][0], cols[0])
+    waiting = []
     for at, (k, first, last, out) in enumerate(plan):
         if at + 1 < len(plan):
-            gather(plan[at + 1][0], cols[(at + 1) % 2])
-        column = cols[at % 2][...].reshape(count, channels)
+            gather(plan[at + 1][0], cols[(at + 1) % 3])
+        column = cols[at % 3][...].reshape(count, channels)
         value = dot(feats_t[pl.ds(first, last - first), :], column)
         place(both, value, out, me[0], bits, quarters)
         if first == 0:
-            acc[...] += dot_nt(column, w[pl.ds(k * channels, channels), :])
+            waiting.append((cols[at % 3], k))
+        if len(waiting) == 2 or (waiting and (first > 0 or at + 1 == len(plan))):
+            terms = [
+                dot_nt(col[...].reshape(count, channels), w[pl.ds(j * channels, channels), :])
+                for col, j in waiting
+            ]
+            acc[...] += sum(terms[1:], terms[0])
+            waiting = []
     grad[...] = acc[...].astype(grad.dtype)
     part(both, keep, send)
 
@@ -268,6 +276,7 @@
             pltpu.VMEM((count, channels), F32),
             pltpu.VMEM((count // rows,) + block, BF),
             pltpu.VMEM((count // rows,) + block, BF),
+            pltpu.VMEM((count // rows,) + block, BF),
         ]
         + [
             pltpu.VMEM((rows, listed), jnp.int32),

time: 74.7 us -> 74.9 us (level)
  transfers between devices with their start and end apart: 18 -> 18, of which waited for: 12 -> 11; matrix products, arithmetic and copies ran while one was open for 2% -> 2% of each run, Pallas kernels for 18% -> 19%
where the time goes in v13:
time: 74.9 us; the launch traced here: 73.9 us
  starting transfers between devices  30 us (40%)
  waiting for transfers between devices  19.7 us (26%)
  Pallas kernels  16.5 us (22%)
  local copies, waits for them, and re-layouts  4.28 us (6%)
  other arithmetic  2.46 us (3%)
  between operations  0.87 us (1%)
    ppermute x18, starting transfers between devices, moved(): lax.ppermute(x, 'space', [(i, j) for i, j in pairs if j is not None and 0...  30 us
    ppermute x18, waiting for transfers between devices, moved(): lax.ppermute(x, 'space', [(i, j) for i, j in pairs if j is not None and 0...  19.7 us
    pallas_call x2, Pallas kernels, conv(): pl.pallas_call(functools.partial(conv_kernel, conv_plan(kernel, channels,...  12.8 us
    unnamed x17, local copies, waits for them, and re-layouts  4.28 us
    pallas_call x1, Pallas kernels, down(): pl.pallas_call(functools.partial(down_kernel, bits), out_shape=(side, sid...  2.27 us
  transfers between devices with their start and end apart: 18, of which 11 were waited for; matrix products, arithmetic and copies ran while one was open for 2% of the time, Pallas kernels for 19%

profile of v13, /device:TPU:0, one launch (start us, length us, event | category | flops | bytes accessed | tf_op | source)
XLA Modules:
  0.0 73.9 jit_solution(932501538103384661)
XLA Ops:
  0.6 2.4 %collective-permute-start = (bf16[128,512]{1,0:T(8,128)(2,1)}, bf16[128,512]{1,0:T(8,128)(2,1)S(1)}, u32[]{:S(2)}, u32[]{:S(2)}) collective-permute-start(bf16[128,512]{1,0:T(8,128)(2,1)} %cur_in.1), channel_id=1, source_target_pairs={{0,1},{1,2},{2,3},{3,4},{4,5},{5,6},{6,7},{7,8},{8,9},{9,10},{10,1... | collective-permute-start | bytes 393224 | tf_op jit(solution)/shard_map/ppermute | solution.py:294
  3.0 0.7 pad_add_fusion.lists
  3.7 1.6 %copy-done.1 = bf16[2048,512]{1,0:T(8,128)(2,1)S(1)} copy-done((bf16[2048,512]{1,0:T(8,128)(2,1)S(1)}, bf16[2048,512]{1,0:T(8,128)(2,1)}, u32[]{:S(2)}) %copy-start.1) | copy-done | bytes 2097176
  5.3 0.9 %copy-done.4 = bf16[512,256]{1,0:T(8,128)(2,1)S(1)} copy-done((bf16[512,256]{1,0:T(8,128)(2,1)S(1)}, bf16[512,256]{1,0:T(8,128)(2,1)}, u32[]{:S(2)}) %copy-start.4) | copy-done | bytes 262168
  6.3 0.9 %copy-done.5 = bf16[128,512]{1,0:T(8,128)(2,1)S(1)} copy-done((bf16[128,512]{1,0:T(8,128)(2,1)S(1)}, bf16[128,512]{1,0:T(8,128)(2,1)}, u32[]{:S(2)}) %copy-start.5) | copy-done | bytes 131096
  7.2 0.9 %prep.1 = (bf16[512,256]{1,0:T(8,128)(2,1)S(1)}, bf16[512,1024]{1,0:T(8,128)(2,1)S(1)}, bf16[1024,256]{1,0:T(8,128)(2,1)S(1)}, bf16[256,1024]{1,0:T(8,128)(2,1)S...) custom-call(bf16[512,256]{1,0:T(8,128)(2,1)S(1)} %copy-done.4, s32[16,128]{1,0:T(8,128)S(1)} %pad_add_fusion.lists, ...), custom_call_target="tpu_custom_call" | custom-call | flops 1048576 | bytes 1024 | tf_op jit(solution)/shard_map/prep/pallas_call | solution.py:115
  8.1 0.0 collective-permute-done.prev
  8.1 0.0 copy-start
  8.1 0.0 copy-start.2
  8.1 0.0 copy-start.3
  8.1 2.3 %down.1 = (bf16[256,256]{1,0:T(8,128)(2,1)S(1)}, bf16[256,256]{1,0:T(8,128)(2,1)S(1)}, bf16[16,64,512]{2,1,0:T(8,128)(2,1)S(1)}, bf16[16,64,512]{2,1,0:T(8,128)(2,1)S(1)}) custom-call(s32[1]{0:T(128)} %bitcast.me.refs_0_, bf16[128,512]{1,0:T(8,128)(2,1)S(1)} %collective-permute-done.prev, bf16[512,256]{1,0:T(8,128)(2,1)S(1)} %get-tuple-element.59.act, ...), custom_call_target="tpu_custom_call" | custom-call | flops 1048576 | bytes 1024 | tf_op jit(solution)/shard_map/down/pallas_call | solution.py:155
  10.4 2.7 %collective-permute-start.3 = (bf16[16,64,512]{2,1,0:T(8,128)(2,1)S(1)}, bf16[16,64,512]{2,1,0:T(8,128)(2,1)S(1)}, u32[]{:S(2)}, u32[]{:S(2)}) collective-permute-start(bf16[16,64,512]{2,1,0:T(8,128)(2,1)S(1)} %get-tuple-element.70), channel_id=1, source_target_pairs={{0,1},{1,0},{2,3},{3,2},{4,5},{5,4},{6,7},{7,6},{8,9},{9,8},{10,11... | collective-permute-start | bytes 3145736 | tf_op jit(solution)/shard_map/ppermute | solution.py:294
  13.1 1.9 %collective-permute-start.1 = (bf16[256,256]{1,0:T(8,128)(2,1)S(1)}, bf16[256,256]{1,0:T(8,128)(2,1)S(1)}, u32[]{:S(2)}, u32[]{:S(2)}) collective-permute-start(bf16[256,256]{1,0:T(8,128)(2,1)S(1)} %get-tuple-element.65.refs_5_), channel_id=1, source_target_pairs={{0,1},{1,2},{2,3},{3,4},{4,5},{5,6},{6,7},{7,8},{8,9},{9,10},{10,1... | collective-permute-start | bytes 393224 | tf_op jit(solution)/shard_map/ppermute | solution.py:294
  15.0 1.5 %collective-permute-start.2 = (bf16[256,256]{1,0:T(8,128)(2,1)S(1)}, bf16[256,256]{1,0:T(8,128)(2,1)S(1)}, u32[]{:S(2)}, u32[]{:S(2)}) collective-permute-start(bf16[256,256]{1,0:T(8,128)(2,1)S(1)} %get-tuple-element.66.refs_4_), channel_id=1, source_target_pairs={{1,0},{2,1},{3,2},{4,3},{5,4},{6,5},{7,6},{8,7},{9,8},{10,9},{11,1... | collective-permute-start | bytes 393224 | tf_op jit(solution)/shard_map/ppermute | solution.py:294
  16.5 0.0 copy-done
  16.5 0.0 copy-done.2
  16.5 0.0 copy-done.3
  16.5 0.3 turn.1
  16.8 0.0 copy-start.6
  16.8 0.0 copy-start.7
  16.8 0.0 collective-permute-done.1.refs_3_
  16.8 2.5 %collective-permute-done.2.refs_6_ = bf16[256,256]{1,0:T(8,128)(2,1)S(1)} collective-permute-done((bf16[256,256]{1,0:T(8,128)(2,1)S(1)}, bf16[256,256]{1,0:T(8,128)(2,1)S(1)}, u32[]{:S(2)}, u32[]{:S(2)}) %collective-permute-start.2) | collective-permute-done | bytes 131104 | tf_op jit(solution)/shard_map/ppermute | solution.py:294
  19.3 0.0 collective-permute-done.3
  19.3 0.3 add_convert_fusion
  19.6 3.4 %collective-permute-start.4 = (bf16[8,64,512]{2,1,0:T(8,128)(2,1)S(1)}, bf16[8,64,512]{2,1,0:T(8,128)(2,1)S(1)}, u32[]{:S(2)}, u32[]{:S(2)}) collective-permute-start(bf16[8,64,512]{2,1,0:T(8,128)(2,1)S(1)} %get-tuple-element.117), channel_id=1, source_target_pairs={{0,2},{1,5},{2,0},{3,7},{4,6},{5,1},{6,4},{7,3},{8,10},{9,13},{10,... | collective-permute-start | bytes 1572872 | tf_op jit(solution)/shard_map/ppermute | solution.py:294
  23.0 0.0 copy-done.7
  23.0 5.8 %conv.2 = (f32[512,256]{1,0:T(8,128)S(1)}, bf16[8,216,256]{2,1,0:T(8,128)(2,1)S(1)}, bf16[8,216,256]{2,1,0:T(8,128)(2,1)S(1)}) custom-call(s32[1]{0:T(128)} %bitcast.me.refs_0_, s32[8,27]{1,0:T(8,128)S(1)} %bitcast.17, s32[8,27]{1,0:T(8,128)S(1)} %bitcast.19, bf16[256,256]{1,0:T(8,128)(2,1)S(1)} %collective-permute-done.1.refs_3_, ...), custom_call_target="tpu_custom_call" | custom-call | flops 1048576 | bytes 1024 | tf_op jit(solution)/shard_map/conv/pallas_call | solution.py:266
  28.8 1.5 %collective-permute-start.5 = (bf16[8,216,256]{2,1,0:T(8,128)(2,1)S(1)}, bf16[8,216,256]{2,1,0:T(8,128)(2,1)S(1)}, u32[]{:S(2)}, u32[]{:S(2)}) collective-permute-start(bf16[8,216,256]{2,1,0:T(8,128)(2,1)S(1)} %get-tuple-element.80), channel_id=1, source_target_pairs={{0,1},{1,0},{2,3},{3,2},{4,5},{5,4},{6,7},{7,6},{8,9},{9,8},{10,11... | collective-permute-start | bytes 2654216 | tf_op jit(solution)/shard_map/ppermute | solution.py:294
  30.4 0.0 collective-permute-done.4.got
  30.4 0.1 fold.3
  30.5 2.0 %collective-permute-done.5 = bf16[8,216,256]{2,1,0:T(8,128)(2,1)S(1)} collective-permute-done((bf16[8,216,256]{2,1,0:T(8,128)(2,1)S(1)}, bf16[8,216,256]{2,1,0:T(8,128)(2,1)S(1)}, u32[]{:S(2)}, u32[]{:S(2)}) %collective-permute-start.5) | collective-permute-done | bytes 884768 | tf_op jit(solution)/shard_map/ppermute | solution.py:294
  32.4 0.2 convert_add_fusion.2
  32.6 3.4 %collective-permute-start.6 = (bf16[4,216,256]{2,1,0:T(8,128)(2,1)S(1)}, bf16[4,216,256]{2,1,0:T(8,128)(2,1)S(1)}, u32[]{:S(2)}, u32[]{:S(2)}) collective-permute-start(bf16[4,216,256]{2,1,0:T(8,128)(2,1)S(1)} %get-tuple-element.88), channel_id=1, source_target_pairs={{0,2},{1,5},{2,0},{3,7},{4,6},{5,1},{6,4},{7,3},{8,10},{9,13},{10,... | collective-permute-start | bytes 1327112 | tf_op jit(solution)/shard_map/ppermute | solution.py:294
  36.0 0.3 collective-permute-start.7
  36.3 7.0 %conv.3 = (bf16[512,256]{1,0:T(8,128)(2,1)}, bf16[8,216,256]{2,1,0:T(8,128)(2,1)S(1)}, bf16[8,216,256]{2,1,0:T(8,128)(2,1)S(1)}) custom-call(s32[1]{0:T(128)} %bitcast.me.refs_0_, s32[8,27]{1,0:T(8,128)S(1)} %bitcast.18, s32[8,27]{1,0:T(8,128)S(1)} %bitcast.20, bf16[256,256]{1,0:T(8,128)(2,1)S(1)} %collective-permute-done.1.refs_3_, ...), custom_call_target="tpu_custom_call" | custom-call | flops 1048576 | bytes 1024 | tf_op jit(solution)/shard_map/conv/pallas_call | solution.py:266
  43.3 0.0 collective-permute-start.8
  43.3 0.0 collective-permute-done.7
  43.3 1.6 %collective-permute-done.6.got = bf16[4,216,256]{2,1,0:T(8,128)(2,1)S(1)} collective-permute-done((bf16[4,216,256]{2,1,0:T(8,128)(2,1)S(1)}, bf16[4,216,256]{2,1,0:T(8,128)(2,1)S(1)}, u32[]{:S(2)}, u32[]{:S(2)}) %collective-permute-start.6) | collective-permute-done | bytes 442400 | tf_op jit(solution)/shard_map/ppermute | solution.py:294
  44.8 0.1 fold.4
  44.9 0.6 collective-permute-start.10
  45.6 0.1 add_convert_fusion.3
  45.6 0.1 collective-permute-done.8
  45.7 0.2 add_convert_fusion.1
  45.9 2.0 %collective-permute-start.9 = (bf16[4,216,256]{2,1,0:T(8,128)(2,1)S(1)}, bf16[4,216,256]{2,1,0:T(8,128)(2,1)S(1)}, u32[]{:S(2)}, u32[]{:S(2)}) collective-permute-start(bf16[4,216,256]{2,1,0:T(8,128)(2,1)S(1)} %get-tuple-element.119), channel_id=1, source_target_pairs={{0,2},{1,5},{2,0},{3,7},{4,6},{5,1},{6,4},{7,3},{8,10},{9,13},{10,... | collective-permute-start | bytes 1327112 | tf_op jit(solution)/shard_map/ppermute | solution.py:294
  47.9 1.6 %collective-permute-start.11 = (bf16[2,64,512]{2,1,0:T(8,128)(2,1)S(1)}, bf16[2,64,512]{2,1,0:T(8,128)(2,1)S(1)}, u32[]{:S(2)}, u32[]{:S(2)}) collective-permute-start(bf16[2,64,512]{2,1,0:T(8,128)(2,1)S(1)} %get-tuple-element.123), channel_id=1, source_target_pairs={{0,8},{1,9},{2,10},{3,11},{4,12},{5,13},{6,14},{7,15},{8,0},{9,1},... | collective-permute-start | bytes 393224 | tf_op jit(solution)/shard_map/ppermute | solution.py:294
  49.5 2.9 %collective-permute-done.10 = bf16[2,216,256]{2,1,0:T(8,128)(2,1)S(1)} collective-permute-done((bf16[2,216,256]{2,1,0:T(8,128)(2,1)S(1)}, bf16[2,216,256]{2,1,0:T(8,128)(2,1)S(1)}, u32[]{:S(2)}, u32[]{:S(2)}) %collective-permute-start.10) | collective-permute-done | bytes 221216 | tf_op jit(solution)/shard_map/ppermute | solution.py:294
  52.4 0.1 add_convert_fusion.5
  52.5 1.6 %collective-permute-start.13 = (bf16[1,216,256]{2,1,0:T(8,128)(2,1)S(1)}, bf16[1,216,256]{2,1,0:T(8,128)(2,1)S(1)}, u32[]{:S(2)}, u32[]{:S(2)}) collective-permute-start(bf16[1,216,256]{2,1,0:T(8,128)(2,1)S(1)} %get-tuple-element.125), channel_id=1, source_target_pairs={{0,8},{1,9},{2,10},{3,11},{4,12},{5,13},{6,14},{7,15},{8,0},{9,1},... | collective-permute-start | bytes 331784 | tf_op jit(solution)/shard_map/ppermute | solution.py:294
  54.1 0.0 collective-permute-done.11
  54.1 0.6 collective-permute-done.9.got
  54.7 0.1 fold.5
  54.9 2.7 %collective-permute-start.14 = (bf16[1,64,512]{2,1,0:T(8,128)(2,1)S(1)}, bf16[1,64,512]{2,1,0:T(8,128)(2,1)S(1)}, u32[]{:S(2)}, u32[]{:S(2)}) collective-permute-start(bf16[1,64,512]{2,1,0:T(8,128)(2,1)S(1)} %add_convert_fusion.6), channel_id=1, source_target_pairs={{0,16},{1,17},{2,18},{3,19},{4,20},{5,21},{6,22},{7,23},{8,24},{9,... | collective-permute-start | bytes 196616 | tf_op jit(solution)/shard_map/ppermute | solution.py:294
  57.5 1.2 %collective-permute-start.12 = (bf16[2,216,256]{2,1,0:T(8,128)(2,1)S(1)}, bf16[2,216,256]{2,1,0:T(8,128)(2,1)S(1)}, u32[]{:S(2)}, u32[]{:S(2)}) collective-permute-start(bf16[2,216,256]{2,1,0:T(8,128)(2,1)S(1)} %get-tuple-element.106), channel_id=1, source_target_pairs={{0,4},{1,3},{2,6},{3,1},{4,0},{5,7},{6,2},{7,5},{8,12},{9,11},{10,... | collective-permute-start | bytes 663560 | tf_op jit(solution)/shard_map/ppermute | solution.py:294
  58.7 0.0 collective-permute-done.13
  58.8 1.3 %collective-permute-start.16 = (bf16[1,216,256]{2,1,0:T(8,128)(2,1)S(1)}, bf16[1,216,256]{2,1,0:T(8,128)(2,1)S(1)}, u32[]{:S(2)}, u32[]{:S(2)}) collective-permute-start(bf16[1,216,256]{2,1,0:T(8,128)(2,1)S(1)} %get-tuple-element.115), channel_id=1, source_target_pairs={{8,24},{9,25},{10,26},{11,27},{12,28},{13,29},{14,30},{15,31},{16,... | collective-permute-start | bytes 331784 | tf_op jit(solution)/shard_map/ppermute | solution.py:294
  60.1 1.9 %collective-permute-done.14 = bf16[1,64,512]{2,1,0:T(8,128)(2,1)S(1)} collective-permute-done((bf16[1,64,512]{2,1,0:T(8,128)(2,1)S(1)}, bf16[1,64,512]{2,1,0:T(8,128)(2,1)S(1)}, u32[]{:S(2)}, u32[]{:S(2)}) %collective-permute-start.14) | collective-permute-done | bytes 65568 | tf_op jit(solution)/shard_map/ppermute | solution.py:294
  62.0 1.5 %collective-permute-done.12 = bf16[2,216,256]{2,1,0:T(8,128)(2,1)S(1)} collective-permute-done((bf16[2,216,256]{2,1,0:T(8,128)(2,1)S(1)}, bf16[2,216,256]{2,1,0:T(8,128)(2,1)S(1)}, u32[]{:S(2)}, u32[]{:S(2)}) %collective-permute-start.12) | collective-permute-done | bytes 221216 | tf_op jit(solution)/shard_map/ppermute | solution.py:294
  63.5 0.5 collective-permute-start.15
  63.9 2.9 %collective-permute-done.16 = bf16[1,216,256]{2,1,0:T(8,128)(2,1)S(1)} collective-permute-done((bf16[1,216,256]{2,1,0:T(8,128)(2,1)S(1)}, bf16[1,216,256]{2,1,0:T(8,128)(2,1)S(1)}, u32[]{:S(2)}, u32[]{:S(2)}) %collective-permute-start.16) | collective-permute-done | bytes 110624 | tf_op jit(solution)/shard_map/ppermute | solution.py:294
  66.8 2.2 %collective-permute-done.15 = bf16[1,216,256]{2,1,0:T(8,128)(2,1)S(1)} collective-permute-done((bf16[1,216,256]{2,1,0:T(8,128)(2,1)S(1)}, bf16[1,216,256]{2,1,0:T(8,128)(2,1)S(1)}, u32[]{:S(2)}, u32[]{:S(2)}) %collective-permute-start.15) | collective-permute-done | bytes 110624 | tf_op jit(solution)/shard_map/ppermute | solution.py:294
  69.1 1.5 %collective-permute-start.17 = (bf16[1,216,256]{2,1,0:T(8,128)(2,1)S(1)}, bf16[1,216,256]{2,1,0:T(8,128)(2,1)S(1)}, u32[]{:S(2)}, u32[]{:S(2)}) collective-permute-start(bf16[1,216,256]{2,1,0:T(8,128)(2,1)S(1)} %convert_element_type.132), channel_id=1, source_target_pairs={{0,16},{1,17},{2,18},{3,19},{4,20},{5,21},{6,22},{7,23},{24,8},{25... | collective-permute-start | bytes 331784 | tf_op jit(solution)/shard_map/ppermute | solution.py:294
  70.7 0.7 multiply_bitcast_fusion.1
  71.4 1.7 %collective-permute-done.17 = bf16[1,216,256]{2,1,0:T(8,128)(2,1)S(1)} collective-permute-done((bf16[1,216,256]{2,1,0:T(8,128)(2,1)S(1)}, bf16[1,216,256]{2,1,0:T(8,128)(2,1)S(1)}, u32[]{:S(2)}, u32[]{:S(2)}) %collective-permute-start.17) | collective-permute-done | bytes 110624 | tf_op jit(solution)/shard_map/ppermute | solution.py:294
  73.1 0.8 %copy.13 = f32[27,2,8,128]{3,1,2,0:T(2,128)} copy(f32[27,2,8,128]{3,2,1,0:T(8,128)S(1)} %multiply_bitcast_fusion) | data formatting | bytes 442368
  (11 shorter events, 0.2 us)
Async XLA Ops:
  0.6 7.4 %collective-permute-start = (bf16[128,512]{1,0:T(8,128)(2,1)}, bf16[128,512]{1,0:T(8,128)(2,1)S(1)}, u32[]{:S(2)}, u32[]{:S(2)}) collective-permute-start(bf16[128,512]{1,0:T(8,128)(2,1)} %cur_in.1), channel_id=1, source_target_pairs={{0,1},{1,2},{2,3},{3,4},{4,5},{5,6},{6,7},{7,8},{8,9},{9,10},{10,1... | collective-permute-start | bytes 393224 | tf_op jit(solution)/shard_map/ppermute | solution.py:294
  3.7 1.6 %copy-start.1 = (bf16[2048,512]{1,0:T(8,128)(2,1)S(1)}, bf16[2048,512]{1,0:T(8,128)(2,1)}, u32[]{:S(2)}) copy-start(bf16[2048,512]{1,0:T(8,128)(2,1)} %w_in.1) | copy-start | bytes 6291460
  5.3 0.9 %copy-start.4 = (bf16[512,256]{1,0:T(8,128)(2,1)S(1)}, bf16[512,256]{1,0:T(8,128)(2,1)}, u32[]{:S(2)}) copy-start(bf16[512,256]{1,0:T(8,128)(2,1)} %pre.1) | copy-start | bytes 786436
  6.3 0.9 %copy-start.5 = (bf16[128,512]{1,0:T(8,128)(2,1)S(1)}, bf16[128,512]{1,0:T(8,128)(2,1)}, u32[]{:S(2)}) copy-start(bf16[128,512]{1,0:T(8,128)(2,1)} %cur_in.1) | copy-start | bytes 393220
  8.1 8.4 %copy-start = (bf16[6912,256]{1,0:T(8,128)(2,1)S(1)}, bf16[6912,256]{1,0:T(8,128)(2,1)}, u32[]{:S(2)}) copy-start(bf16[6912,256]{1,0:T(8,128)(2,1)} %refs_7_.3) | copy-start | bytes 10616836
  8.1 8.4 %copy-start.2 = (bf16[512,256]{1,0:T(8,128)(2,1)S(1)}, bf16[512,256]{1,0:T(8,128)(2,1)}, u32[]{:S(2)}) copy-start(bf16[512,256]{1,0:T(8,128)(2,1)} %refs_9_.1) | copy-start | bytes 786436
  8.1 8.4 %copy-start.3 = (s32[1,27,8,128]{3,2,1,0:T(8,128)S(1)}, s32[1,27,8,128]{3,2,1,0:T(8,128)}, u32[]{:S(2)}) copy-start(s32[1,27,8,128]{3,2,1,0:T(8,128)} %param.17) | copy-start | bytes 331780
  10.4 8.9 %collective-permute-start.3 = (bf16[16,64,512]{2,1,0:T(8,128)(2,1)S(1)}, bf16[16,64,512]{2,1,0:T(8,128)(2,1)S(1)}, u32[]{:S(2)}, u32[]{:S(2)}) collective-permute-start(bf16[16,64,512]{2,1,0:T(8,128)(2,1)S(1)} %get-tuple-element.70), channel_id=1, source_target_pairs={{0,1},{1,0},{2,3},{3,2},{4,5},{5,4},{6,7},{7,6},{8,9},{9,8},{10,11... | collective-permute-start | bytes 3145736 | tf_op jit(solution)/shard_map/ppermute | solution.py:294
  13.1 3.8 %collective-permute-start.1 = (bf16[256,256]{1,0:T(8,128)(2,1)S(1)}, bf16[256,256]{1,0:T(8,128)(2,1)S(1)}, u32[]{:S(2)}, u32[]{:S(2)}) collective-permute-start(bf16[256,256]{1,0:T(8,128)(2,1)S(1)} %get-tuple-element.65.refs_5_), channel_id=1, source_target_pairs={{0,1},{1,2},{2,3},{3,4},{4,5},{5,6},{6,7},{7,8},{8,9},{9,10},{10,1... | collective-permute-start | bytes 393224 | tf_op jit(solution)/shard_map/ppermute | solution.py:294
  15.0 4.3 %collective-permute-start.2 = (bf16[256,256]{1,0:T(8,128)(2,1)S(1)}, bf16[256,256]{1,0:T(8,128)(2,1)S(1)}, u32[]{:S(2)}, u32[]{:S(2)}) collective-permute-start(bf16[256,256]{1,0:T(8,128)(2,1)S(1)} %get-tuple-element.66.refs_4_), channel_id=1, source_target_pairs={{1,0},{2,1},{3,2},{4,3},{5,4},{6,5},{7,6},{8,7},{9,8},{10,9},{11,1... | collective-permute-start | bytes 393224 | tf_op jit(solution)/shard_map/ppermute | solution.py:294
  16.8 6.2 %copy-start.6 = (s32[1,27,8]{1,2,0:T(8,128)S(1)}, s32[1,27,8]{1,2,0:T(8,128)}, u32[]{:S(2)}) copy-start(s32[1,27,8]{1,2,0:T(8,128)} %param.15) | copy-start | bytes 2596
  16.8 6.2 %copy-start.7 = (s32[1,27,8]{1,2,0:T(8,128)S(1)}, s32[1,27,8]{1,2,0:T(8,128)}, u32[]{:S(2)}) copy-start(s32[1,27,8]{1,2,0:T(8,128)} %param.16) | copy-start | bytes 2596
  19.6 10.7 %collective-permute-start.4 = (bf16[8,64,512]{2,1,0:T(8,128)(2,1)S(1)}, bf16[8,64,512]{2,1,0:T(8,128)(2,1)S(1)}, u32[]{:S(2)}, u32[]{:S(2)}) collective-permute-start(bf16[8,64,512]{2,1,0:T(8,128)(2,1)S(1)} %get-tuple-element.117), channel_id=1, source_target_pairs={{0,2},{1,5},{2,0},{3,7},{4,6},{5,1},{6,4},{7,3},{8,10},{9,13},{10,... | collective-permute-start | bytes 1572872 | tf_op jit(solution)/shard_map/ppermute | solution.py:294
  28.8 3.6 %collective-permute-start.5 = (bf16[8,216,256]{2,1,0:T(8,128)(2,1)S(1)}, bf16[8,216,256]{2,1,0:T(8,128)(2,1)S(1)}, u32[]{:S(2)}, u32[]{:S(2)}) collective-permute-start(bf16[8,216,256]{2,1,0:T(8,128)(2,1)S(1)} %get-tuple-element.80), channel_id=1, source_target_pairs={{0,1},{1,0},{2,3},{3,2},{4,5},{5,4},{6,7},{7,6},{8,9},{9,8},{10,11... | collective-permute-start | bytes 2654216 | tf_op jit(solution)/shard_map/ppermute | solution.py:294
  32.6 12.2 %collective-permute-start.6 = (bf16[4,216,256]{2,1,0:T(8,128)(2,1)S(1)}, bf16[4,216,256]{2,1,0:T(8,128)(2,1)S(1)}, u32[]{:S(2)}, u32[]{:S(2)}) collective-permute-start(bf16[4,216,256]{2,1,0:T(8,128)(2,1)S(1)} %get-tuple-element.88), channel_id=1, source_target_pairs={{0,2},{1,5},{2,0},{3,7},{4,6},{5,1},{6,4},{7,3},{8,10},{9,13},{10,... | collective-permute-start | bytes 1327112 | tf_op jit(solution)/shard_map/ppermute | solution.py:294
  36.0 7.3 %collective-permute-start.7 = (bf16[4,64,512]{2,1,0:T(8,128)(2,1)S(1)}, bf16[4,64,512]{2,1,0:T(8,128)(2,1)S(1)}, u32[]{:S(2)}, u32[]{:S(2)}) collective-permute-start(bf16[4,64,512]{2,1,0:T(8,128)(2,1)S(1)} %get-tuple-element.90), channel_id=1, source_target_pairs={{0,4},{1,3},{2,6},{3,1},{4,0},{5,7},{6,2},{7,5},{8,12},{9,11},{10,... | collective-permute-start | bytes 786440 | tf_op jit(solution)/shard_map/ppermute | solution.py:294
  43.3 2.4 %collective-permute-start.8 = (bf16[8,216,256]{2,1,0:T(8,128)(2,1)S(1)}, bf16[8,216,256]{2,1,0:T(8,128)(2,1)S(1)}, u32[]{:S(2)}, u32[]{:S(2)}) collective-permute-start(bf16[8,216,256]{2,1,0:T(8,128)(2,1)S(1)} %get-tuple-element.93), channel_id=1, source_target_pairs={{0,1},{1,0},{2,3},{3,2},{4,5},{5,4},{6,7},{7,6},{8,9},{9,8},{10,11... | collective-permute-start | bytes 2654216 | tf_op jit(solution)/shard_map/ppermute | solution.py:294
  44.9 7.5 %collective-permute-start.10 = (bf16[2,216,256]{2,1,0:T(8,128)(2,1)S(1)}, bf16[2,216,256]{2,1,0:T(8,128)(2,1)S(1)}, u32[]{:S(2)}, u32[]{:S(2)}) collective-permute-start(bf16[2,216,256]{2,1,0:T(8,128)(2,1)S(1)} %get-tuple-element.101), channel_id=1, source_target_pairs={{0,4},{1,3},{2,6},{3,1},{4,0},{5,7},{6,2},{7,5},{8,12},{9,11},{10,... | collective-permute-start | bytes 663560 | tf_op jit(solution)/shard_map/ppermute | solution.py:294
  45.9 8.8 %collective-permute-start.9 = (bf16[4,216,256]{2,1,0:T(8,128)(2,1)S(1)}, bf16[4,216,256]{2,1,0:T(8,128)(2,1)S(1)}, u32[]{:S(2)}, u32[]{:S(2)}) collective-permute-start(bf16[4,216,256]{2,1,0:T(8,128)(2,1)S(1)} %get-tuple-element.119), channel_id=1, source_target_pairs={{0,2},{1,5},{2,0},{3,7},{4,6},{5,1},{6,4},{7,3},{8,10},{9,13},{10,... | collective-permute-start | bytes 1327112 | tf_op jit(solution)/shard_map/ppermute | solution.py:294
  47.9 6.2 %collective-permute-start.11 = (bf16[2,64,512]{2,1,0:T(8,128)(2,1)S(1)}, bf16[2,64,512]{2,1,0:T(8,128)(2,1)S(1)}, u32[]{:S(2)}, u32[]{:S(2)}) collective-permute-start(bf16[2,64,512]{2,1,0:T(8,128)(2,1)S(1)} %get-tuple-element.123), channel_id=1, source_target_pairs={{0,8},{1,9},{2,10},{3,11},{4,12},{5,13},{6,14},{7,15},{8,0},{9,1},... | collective-permute-start | bytes 393224 | tf_op jit(solution)/shard_map/ppermute | solution.py:294
  52.5 6.3 %collective-permute-start.13 = (bf16[1,216,256]{2,1,0:T(8,128)(2,1)S(1)}, bf16[1,216,256]{2,1,0:T(8,128)(2,1)S(1)}, u32[]{:S(2)}, u32[]{:S(2)}) collective-permute-start(bf16[1,216,256]{2,1,0:T(8,128)(2,1)S(1)} %get-tuple-element.125), channel_id=1, source_target_pairs={{0,8},{1,9},{2,10},{3,11},{4,12},{5,13},{6,14},{7,15},{8,0},{9,1},... | collective-permute-start | bytes 331784 | tf_op jit(solution)/shard_map/ppermute | solution.py:294
  54.9 7.1 %collective-permute-start.14 = (bf16[1,64,512]{2,1,0:T(8,128)(2,1)S(1)}, bf16[1,64,512]{2,1,0:T(8,128)(2,1)S(1)}, u32[]{:S(2)}, u32[]{:S(2)}) collective-permute-start(bf16[1,64,512]{2,1,0:T(8,128)(2,1)S(1)} %add_convert_fusion.6), channel_id=1, source_target_pairs={{0,16},{1,17},{2,18},{3,19},{4,20},{5,21},{6,22},{7,23},{8,24},{9,... | collective-permute-start | bytes 196616 | tf_op jit(solution)/shard_map/ppermute | solution.py:294
  57.5 5.9 %collective-permute-start.12 = (bf16[2,216,256]{2,1,0:T(8,128)(2,1)S(1)}, bf16[2,216,256]{2,1,0:T(8,128)(2,1)S(1)}, u32[]{:S(2)}, u32[]{:S(2)}) collective-permute-start(bf16[2,216,256]{2,1,0:T(8,128)(2,1)S(1)} %get-tuple-element.106), channel_id=1, source_target_pairs={{0,4},{1,3},{2,6},{3,1},{4,0},{5,7},{6,2},{7,5},{8,12},{9,11},{10,... | collective-permute-start | bytes 663560 | tf_op jit(solution)/shard_map/ppermute | solution.py:294
  58.8 8.0 %collective-permute-start.16 = (bf16[1,216,256]{2,1,0:T(8,128)(2,1)S(1)}, bf16[1,216,256]{2,1,0:T(8,128)(2,1)S(1)}, u32[]{:S(2)}, u32[]{:S(2)}) collective-permute-start(bf16[1,216,256]{2,1,0:T(8,128)(2,1)S(1)} %get-tuple-element.115), channel_id=1, source_target_pairs={{8,24},{9,25},{10,26},{11,27},{12,28},{13,29},{14,30},{15,31},{16,... | collective-permute-start | bytes 331784 | tf_op jit(solution)/shard_map/ppermute | solution.py:294
  63.5 5.6 %collective-permute-start.15 = (bf16[1,216,256]{2,1,0:T(8,128)(2,1)S(1)}, bf16[1,216,256]{2,1,0:T(8,128)(2,1)S(1)}, u32[]{:S(2)}, u32[]{:S(2)}) collective-permute-start(bf16[1,216,256]{2,1,0:T(8,128)(2,1)S(1)} %add_convert_fusion.4), channel_id=1, source_target_pairs={{0,8},{1,9},{2,10},{3,11},{4,12},{5,13},{6,14},{7,15},{8,0},{9,1},... | collective-permute-start | bytes 331784 | tf_op jit(solution)/shard_map/ppermute | solution.py:294
  69.1 3.9 %collective-permute-start.17 = (bf16[1,216,256]{2,1,0:T(8,128)(2,1)S(1)}, bf16[1,216,256]{2,1,0:T(8,128)(2,1)S(1)}, u32[]{:S(2)}, u32[]{:S(2)}) collective-permute-start(bf16[1,216,256]{2,1,0:T(8,128)(2,1)S(1)} %convert_element_type.132), channel_id=1, source_target_pairs={{0,16},{1,17},{2,18},{3,19},{4,20},{5,21},{6,22},{7,23},{24,8},{25... | collective-permute-start | bytes 331784 | tf_op jit(solution)/shard_map/ppermute | solution.py:294

commit v14 on v12

--- a/solution.py
+++ b/solution.py
@@ -234,11 +234,11 @@
 
     gather(plan[0][0], cols[0])
     for at, (k, first, last, out) in enumerate(plan):
-        if at + 1 < len(plan):
-            gather(plan[at + 1][0], cols[(at + 1) % 2])
         column = cols[at % 2][...].reshape(count, channels)
         value = dot(feats_t[pl.ds(first, last - first), :], column)
         place(both, value, out, me[0], bits, quarters)
+        if at + 1 < len(plan):
+            gather(plan[at + 1][0], cols[(at + 1) % 2])
         if first == 0:
             acc[...] += dot_nt(column, w[pl.ds(k * channels, channels), :])
     grad[...] = acc[...].astype(grad.dtype)

time: 74.7 us -> 78.4 us (1.050)
  Pallas kernels: 15.8 us -> 20.4 us
  waiting for transfers between devices: 20.2 us -> 18.5 us
  starting transfers between devices: 30.1 us -> 31.1 us
    pallas_call x2, Pallas kernels: 12 us -> 16.7 us  [conv(): pl.pallas_call(functools.partial(conv_kernel, conv_plan(kernel, channels,...]
    ppermute x18, waiting for transfers between devices: 20.2 us -> 18.5 us  [moved(): lax.ppermute(x, 'space', [(i, j) for i, j in pairs if j is not None and 0...]
    ppermute x18, starting transfers between devices: 30.1 us -> 31.1 us  [moved(): lax.ppermute(x, 'space', [(i, j) for i, j in pairs if j is not None and 0...]
  transfers between devices with their start and end apart: 18 -> 18, of which waited for: 12 -> 11; matrix products, arithmetic and copies ran while one was open for 2% -> 2% of each run, Pallas kernels for 18% -> 23%
where the time goes in v14:
time: 78.4 us; the launch traced here: 77.6 us
  starting transfers between devices  31.1 us (40%)
  Pallas kernels  20.4 us (26%)
  waiting for transfers between devices  18.5 us (24%)
  local copies, waits for them, and re-layouts  4.28 us (5%)
  other arithmetic  2.46 us (3%)
  between operations  0.87 us (1%)
    ppermute x18, starting transfers between devices, moved(): lax.ppermute(x, 'space', [(i, j) for i, j in pairs if j is not None and 0...  31.1 us
    ppermute x18, waiting for transfers between devices, moved(): lax.ppermute(x, 'space', [(i, j) for i, j in pairs if j is not None and 0...  18.5 us
    pallas_call x2, Pallas kernels, conv(): pl.pallas_call(functools.partial(conv_kernel, conv_plan(kernel, channels,...  16.7 us
    unnamed x17, local copies, waits for them, and re-layouts  4.28 us
    pallas_call x1, Pallas kernels, down(): pl.pallas_call(functools.partial(down_kernel, bits), out_shape=(side, sid...  2.27 us
  transfers between devices with their start and end apart: 18, of which 11 were waited for; matrix products, arithmetic and copies ran while one was open for 2% of the time, Pallas kernels for 23%

profile of v14, /device:TPU:0, one launch (start us, length us, event | category | flops | bytes accessed | tf_op | source)
XLA Modules:
  0.0 77.6 jit_solution(11590751810082214933)
XLA Ops:
  0.6 2.4 %collective-permute-start = (bf16[128,512]{1,0:T(8,128)(2,1)}, bf16[128,512]{1,0:T(8,128)(2,1)S(1)}, u32[]{:S(2)}, u32[]{:S(2)}) collective-permute-start(bf16[128,512]{1,0:T(8,128)(2,1)} %cur_in.1), channel_id=1, source_target_pairs={{0,1},{1,2},{2,3},{3,4},{4,5},{5,6},{6,7},{7,8},{8,9},{9,10},{10,1... | collective-permute-start | bytes 393224 | tf_op jit(solution)/shard_map/ppermute | solution.py:285
  3.0 0.7 pad_add_fusion.lists
  3.7 1.6 %copy-done.1 = bf16[2048,512]{1,0:T(8,128)(2,1)S(1)} copy-done((bf16[2048,512]{1,0:T(8,128)(2,1)S(1)}, bf16[2048,512]{1,0:T(8,128)(2,1)}, u32[]{:S(2)}) %copy-start.1) | copy-done | bytes 2097176
  5.3 0.9 %copy-done.4 = bf16[512,256]{1,0:T(8,128)(2,1)S(1)} copy-done((bf16[512,256]{1,0:T(8,128)(2,1)S(1)}, bf16[512,256]{1,0:T(8,128)(2,1)}, u32[]{:S(2)}) %copy-start.4) | copy-done | bytes 262168
  6.3 0.9 %copy-done.5 = bf16[128,512]{1,0:T(8,128)(2,1)S(1)} copy-done((bf16[128,512]{1,0:T(8,128)(2,1)S(1)}, bf16[128,512]{1,0:T(8,128)(2,1)}, u32[]{:S(2)}) %copy-start.5) | copy-done | bytes 131096
  7.2 0.9 %prep.1 = (bf16[512,256]{1,0:T(8,128)(2,1)S(1)}, bf16[512,1024]{1,0:T(8,128)(2,1)S(1)}, bf16[1024,256]{1,0:T(8,128)(2,1)S(1)}, bf16[256,1024]{1,0:T(8,128)(2,1)S...) custom-call(bf16[512,256]{1,0:T(8,128)(2,1)S(1)} %copy-done.4, s32[16,128]{1,0:T(8,128)S(1)} %pad_add_fusion.lists, ...), custom_call_target="tpu_custom_call" | custom-call | flops 1048576 | bytes 1024 | tf_op jit(solution)/shard_map/prep/pallas_call | solution.py:115
  8.1 0.0 collective-permute-done.prev
  8.1 0.0 copy-start
  8.1 0.0 copy-start.2
  8.1 0.0 copy-start.3
  8.1 2.3 %down.1 = (bf16[256,256]{1,0:T(8,128)(2,1)S(1)}, bf16[256,256]{1,0:T(8,128)(2,1)S(1)}, bf16[16,64,512]{2,1,0:T(8,128)(2,1)S(1)}, bf16[16,64,512]{2,1,0:T(8,128)(2,1)S(1)}) custom-call(s32[1]{0:T(128)} %bitcast.me.refs_0_, bf16[128,512]{1,0:T(8,128)(2,1)S(1)} %collective-permute-done.prev, bf16[512,256]{1,0:T(8,128)(2,1)S(1)} %get-tuple-element.59.act, ...), custom_call_target="tpu_custom_call" | custom-call | flops 1048576 | bytes 1024 | tf_op jit(solution)/shard_map/down/pallas_call | solution.py:155
  10.4 2.7 %collective-permute-start.3 = (bf16[16,64,512]{2,1,0:T(8,128)(2,1)S(1)}, bf16[16,64,512]{2,1,0:T(8,128)(2,1)S(1)}, u32[]{:S(2)}, u32[]{:S(2)}) collective-permute-start(bf16[16,64,512]{2,1,0:T(8,128)(2,1)S(1)} %get-tuple-element.70), channel_id=1, source_target_pairs={{0,1},{1,0},{2,3},{3,2},{4,5},{5,4},{6,7},{7,6},{8,9},{9,8},{10,11... | collective-permute-start | bytes 3145736 | tf_op jit(solution)/shard_map/ppermute | solution.py:285
  13.1 1.9 %collective-permute-start.1 = (bf16[256,256]{1,0:T(8,128)(2,1)S(1)}, bf16[256,256]{1,0:T(8,128)(2,1)S(1)}, u32[]{:S(2)}, u32[]{:S(2)}) collective-permute-start(bf16[256,256]{1,0:T(8,128)(2,1)S(1)} %get-tuple-element.65.refs_5_), channel_id=1, source_target_pairs={{0,1},{1,2},{2,3},{3,4},{4,5},{5,6},{6,7},{7,8},{8,9},{9,10},{10,1... | collective-permute-start | bytes 393224 | tf_op jit(solution)/shard_map/ppermute | solution.py:285
  15.0 1.5 %collective-permute-start.2 = (bf16[256,256]{1,0:T(8,128)(2,1)S(1)}, bf16[256,256]{1,0:T(8,128)(2,1)S(1)}, u32[]{:S(2)}, u32[]{:S(2)}) collective-permute-start(bf16[256,256]{1,0:T(8,128)(2,1)S(1)} %get-tuple-element.66.refs_4_), channel_id=1, source_target_pairs={{1,0},{2,1},{3,2},{4,3},{5,4},{6,5},{7,6},{8,7},{9,8},{10,9},{11,1... | collective-permute-start | bytes 393224 | tf_op jit(solution)/shard_map/ppermute | solution.py:285
  16.5 0.0 copy-done
  16.5 0.0 copy-done.2
  16.5 0.0 copy-done.3
  16.5 0.3 turn.1
  16.8 0.0 copy-start.6
  16.8 0.0 copy-start.7
  16.8 0.0 collective-permute-done.1.refs_3_
  16.8 2.5 %collective-permute-done.2.refs_6_ = bf16[256,256]{1,0:T(8,128)(2,1)S(1)} collective-permute-done((bf16[256,256]{1,0:T(8,128)(2,1)S(1)}, bf16[256,256]{1,0:T(8,128)(2,1)S(1)}, u32[]{:S(2)}, u32[]{:S(2)}) %collective-permute-start.2) | collective-permute-done | bytes 131104 | tf_op jit(solution)/shard_map/ppermute | solution.py:285
  19.3 0.0 collective-permute-done.3
  19.3 0.3 add_convert_fusion
  19.6 3.4 %collective-permute-start.4 = (bf16[8,64,512]{2,1,0:T(8,128)(2,1)S(1)}, bf16[8,64,512]{2,1,0:T(8,128)(2,1)S(1)}, u32[]{:S(2)}, u32[]{:S(2)}) collective-permute-start(bf16[8,64,512]{2,1,0:T(8,128)(2,1)S(1)} %get-tuple-element.117), channel_id=1, source_target_pairs={{0,2},{1,5},{2,0},{3,7},{4,6},{5,1},{6,4},{7,3},{8,10},{9,13},{10,... | collective-permute-start | bytes 1572872 | tf_op jit(solution)/shard_map/ppermute | solution.py:285
  23.0 0.0 copy-done.6
  23.0 7.4 %conv.2 = (f32[512,256]{1,0:T(8,128)S(1)}, bf16[8,216,256]{2,1,0:T(8,128)(2,1)S(1)}, bf16[8,216,256]{2,1,0:T(8,128)(2,1)S(1)}) custom-call(s32[1]{0:T(128)} %bitcast.me.refs_0_, s32[8,27]{1,0:T(8,128)S(1)} %bitcast.17, s32[8,27]{1,0:T(8,128)S(1)} %bitcast.19, bf16[256,256]{1,0:T(8,128)(2,1)S(1)} %collective-permute-done.1.refs_3_, ...), custom_call_target="tpu_custom_call" | custom-call | flops 1048576 | bytes 1024 | tf_op jit(solution)/shard_map/conv/pallas_call | solution.py:258
  30.5 1.6 %collective-permute-start.5 = (bf16[8,216,256]{2,1,0:T(8,128)(2,1)S(1)}, bf16[8,216,256]{2,1,0:T(8,128)(2,1)S(1)}, u32[]{:S(2)}, u32[]{:S(2)}) collective-permute-start(bf16[8,216,256]{2,1,0:T(8,128)(2,1)S(1)} %get-tuple-element.80), channel_id=1, source_target_pairs={{0,1},{1,0},{2,3},{3,2},{4,5},{5,4},{6,7},{7,6},{8,9},{9,8},{10,11... | collective-permute-start | bytes 2654216 | tf_op jit(solution)/shard_map/ppermute | solution.py:285
  32.0 0.0 collective-permute-done.4.got
  32.0 0.1 fold.3
  32.1 2.0 %collective-permute-done.5 = bf16[8,216,256]{2,1,0:T(8,128)(2,1)S(1)} collective-permute-done((bf16[8,216,256]{2,1,0:T(8,128)(2,1)S(1)}, bf16[8,216,256]{2,1,0:T(8,128)(2,1)S(1)}, u32[]{:S(2)}, u32[]{:S(2)}) %collective-permute-start.5) | collective-permute-done | bytes 884768 | tf_op jit(solution)/shard_map/ppermute | solution.py:285
  34.1 0.2 convert_add_fusion.2
  34.3 3.4 %collective-permute-start.6 = (bf16[4,216,256]{2,1,0:T(8,128)(2,1)S(1)}, bf16[4,216,256]{2,1,0:T(8,128)(2,1)S(1)}, u32[]{:S(2)}, u32[]{:S(2)}) collective-permute-start(bf16[4,216,256]{2,1,0:T(8,128)(2,1)S(1)} %get-tuple-element.88), channel_id=1, source_target_pairs={{0,2},{1,5},{2,0},{3,7},{4,6},{5,1},{6,4},{7,3},{8,10},{9,13},{10,... | collective-permute-start | bytes 1327112 | tf_op jit(solution)/shard_map/ppermute | solution.py:285
  37.6 0.3 collective-permute-start.7
  38.0 9.3 %conv.3 = (bf16[512,256]{1,0:T(8,128)(2,1)}, bf16[8,216,256]{2,1,0:T(8,128)(2,1)S(1)}, bf16[8,216,256]{2,1,0:T(8,128)(2,1)S(1)}) custom-call(s32[1]{0:T(128)} %bitcast.me.refs_0_, s32[8,27]{1,0:T(8,128)S(1)} %bitcast.18, s32[8,27]{1,0:T(8,128)S(1)} %bitcast.20, bf16[256,256]{1,0:T(8,128)(2,1)S(1)} %collective-permute-done.1.refs_3_, ...), custom_call_target="tpu_custom_call" | custom-call | flops 1048576 | bytes 1024 | tf_op jit(solution)/shard_map/conv/pallas_call | solution.py:258
  47.2 0.0 collective-permute-start.8
  47.2 0.0 collective-permute-done.7
  47.2 0.0 collective-permute-done.6.got
  47.2 0.1 fold.4
  47.3 1.8 %collective-permute-start.10 = (bf16[2,216,256]{2,1,0:T(8,128)(2,1)S(1)}, bf16[2,216,256]{2,1,0:T(8,128)(2,1)S(1)}, u32[]{:S(2)}, u32[]{:S(2)}) collective-permute-start(bf16[2,216,256]{2,1,0:T(8,128)(2,1)S(1)} %get-tuple-element.101), channel_id=1, source_target_pairs={{0,4},{1,3},{2,6},{3,1},{4,0},{5,7},{6,2},{7,5},{8,12},{9,11},{10,... | collective-permute-start | bytes 663560 | tf_op jit(solution)/shard_map/ppermute | solution.py:285
  49.1 0.1 add_convert_fusion.3
  49.2 0.5 collective-permute-done.8
  49.7 0.2 add_convert_fusion.1
  49.9 0.1 collective-permute-start.9
  50.0 1.6 %collective-permute-start.11 = (bf16[2,64,512]{2,1,0:T(8,128)(2,1)S(1)}, bf16[2,64,512]{2,1,0:T(8,128)(2,1)S(1)}, u32[]{:S(2)}, u32[]{:S(2)}) collective-permute-start(bf16[2,64,512]{2,1,0:T(8,128)(2,1)S(1)} %get-tuple-element.123), channel_id=1, source_target_pairs={{0,8},{1,9},{2,10},{3,11},{4,12},{5,13},{6,14},{7,15},{8,0},{9,1},... | collective-permute-start | bytes 393224 | tf_op jit(solution)/shard_map/ppermute | solution.py:285
  51.6 2.4 %collective-permute-done.10 = bf16[2,216,256]{2,1,0:T(8,128)(2,1)S(1)} collective-permute-done((bf16[2,216,256]{2,1,0:T(8,128)(2,1)S(1)}, bf16[2,216,256]{2,1,0:T(8,128)(2,1)S(1)}, u32[]{:S(2)}, u32[]{:S(2)}) %collective-permute-start.10) | collective-permute-done | bytes 221216 | tf_op jit(solution)/shard_map/ppermute | solution.py:285
  54.0 0.1 add_convert_fusion.5
  54.0 1.6 %collective-permute-start.13 = (bf16[1,216,256]{2,1,0:T(8,128)(2,1)S(1)}, bf16[1,216,256]{2,1,0:T(8,128)(2,1)S(1)}, u32[]{:S(2)}, u32[]{:S(2)}) collective-permute-start(bf16[1,216,256]{2,1,0:T(8,128)(2,1)S(1)} %get-tuple-element.125), channel_id=1, source_target_pairs={{0,8},{1,9},{2,10},{3,11},{4,12},{5,13},{6,14},{7,15},{8,0},{9,1},... | collective-permute-start | bytes 331784 | tf_op jit(solution)/shard_map/ppermute | solution.py:285
  55.6 0.3 collective-permute-done.11
  56.0 2.3 %collective-permute-done.9.got = bf16[4,216,256]{2,1,0:T(8,128)(2,1)S(1)} collective-permute-done((bf16[4,216,256]{2,1,0:T(8,128)(2,1)S(1)}, bf16[4,216,256]{2,1,0:T(8,128)(2,1)S(1)}, u32[]{:S(2)}, u32[]{:S(2)}) %collective-permute-start.9) | collective-permute-done | bytes 442400 | tf_op jit(solution)/shard_map/ppermute | solution.py:285
  58.2 0.1 fold.5
  58.3 2.6 %collective-permute-start.14 = (bf16[1,64,512]{2,1,0:T(8,128)(2,1)S(1)}, bf16[1,64,512]{2,1,0:T(8,128)(2,1)S(1)}, u32[]{:S(2)}, u32[]{:S(2)}) collective-permute-start(bf16[1,64,512]{2,1,0:T(8,128)(2,1)S(1)} %add_convert_fusion.6), channel_id=1, source_target_pairs={{0,16},{1,17},{2,18},{3,19},{4,20},{5,21},{6,22},{7,23},{8,24},{9,... | collective-permute-start | bytes 196616 | tf_op jit(solution)/shard_map/ppermute | solution.py:285
  61.0 1.7 %collective-permute-start.12 = (bf16[2,216,256]{2,1,0:T(8,128)(2,1)S(1)}, bf16[2,216,256]{2,1,0:T(8,128)(2,1)S(1)}, u32[]{:S(2)}, u32[]{:S(2)}) collective-permute-start(bf16[2,216,256]{2,1,0:T(8,128)(2,1)S(1)} %get-tuple-element.106), channel_id=1, source_target_pairs={{0,4},{1,3},{2,6},{3,1},{4,0},{5,7},{6,2},{7,5},{8,12},{9,11},{10,... | collective-permute-start | bytes 663560 | tf_op jit(solution)/shard_map/ppermute | solution.py:285
  62.7 0.0 collective-permute-done.13
  62.7 1.3 %collective-permute-start.16 = (bf16[1,216,256]{2,1,0:T(8,128)(2,1)S(1)}, bf16[1,216,256]{2,1,0:T(8,128)(2,1)S(1)}, u32[]{:S(2)}, u32[]{:S(2)}) collective-permute-start(bf16[1,216,256]{2,1,0:T(8,128)(2,1)S(1)} %get-tuple-element.115), channel_id=1, source_target_pairs={{8,24},{9,25},{10,26},{11,27},{12,28},{13,29},{14,30},{15,31},{16,... | collective-permute-start | bytes 331784 | tf_op jit(solution)/shard_map/ppermute | solution.py:285
  64.0 0.9 %collective-permute-done.14 = bf16[1,64,512]{2,1,0:T(8,128)(2,1)S(1)} collective-permute-done((bf16[1,64,512]{2,1,0:T(8,128)(2,1)S(1)}, bf16[1,64,512]{2,1,0:T(8,128)(2,1)S(1)}, u32[]{:S(2)}, u32[]{:S(2)}) %collective-permute-start.14) | collective-permute-done | bytes 65568 | tf_op jit(solution)/shard_map/ppermute | solution.py:285
  65.0 2.0 %collective-permute-done.12 = bf16[2,216,256]{2,1,0:T(8,128)(2,1)S(1)} collective-permute-done((bf16[2,216,256]{2,1,0:T(8,128)(2,1)S(1)}, bf16[2,216,256]{2,1,0:T(8,128)(2,1)S(1)}, u32[]{:S(2)}, u32[]{:S(2)}) %collective-permute-start.12) | collective-permute-done | bytes 221216 | tf_op jit(solution)/shard_map/ppermute | solution.py:285
  67.0 0.9 %collective-permute-start.15 = (bf16[1,216,256]{2,1,0:T(8,128)(2,1)S(1)}, bf16[1,216,256]{2,1,0:T(8,128)(2,1)S(1)}, u32[]{:S(2)}, u32[]{:S(2)}) collective-permute-start(bf16[1,216,256]{2,1,0:T(8,128)(2,1)S(1)} %add_convert_fusion.4), channel_id=1, source_target_pairs={{0,8},{1,9},{2,10},{3,11},{4,12},{5,13},{6,14},{7,15},{8,0},{9,1},... | collective-permute-start | bytes 331784 | tf_op jit(solution)/shard_map/ppermute | solution.py:285
  67.9 2.5 %collective-permute-done.16 = bf16[1,216,256]{2,1,0:T(8,128)(2,1)S(1)} collective-permute-done((bf16[1,216,256]{2,1,0:T(8,128)(2,1)S(1)}, bf16[1,216,256]{2,1,0:T(8,128)(2,1)S(1)}, u32[]{:S(2)}, u32[]{:S(2)}) %collective-permute-start.16) | collective-permute-done | bytes 110624 | tf_op jit(solution)/shard_map/ppermute | solution.py:285
  70.4 1.6 %collective-permute-done.15 = bf16[1,216,256]{2,1,0:T(8,128)(2,1)S(1)} collective-permute-done((bf16[1,216,256]{2,1,0:T(8,128)(2,1)S(1)}, bf16[1,216,256]{2,1,0:T(8,128)(2,1)S(1)}, u32[]{:S(2)}, u32[]{:S(2)}) %collective-permute-start.15) | collective-permute-done | bytes 110624 | tf_op jit(solution)/shard_map/ppermute | solution.py:285
  72.1 2.4 %collective-permute-start.17 = (bf16[1,216,256]{2,1,0:T(8,128)(2,1)S(1)}, bf16[1,216,256]{2,1,0:T(8,128)(2,1)S(1)}, u32[]{:S(2)}, u32[]{:S(2)}) collective-permute-start(bf16[1,216,256]{2,1,0:T(8,128)(2,1)S(1)} %convert_element_type.132), channel_id=1, source_target_pairs={{0,16},{1,17},{2,18},{3,19},{4,20},{5,21},{6,22},{7,23},{24,8},{25... | collective-permute-start | bytes 331784 | tf_op jit(solution)/shard_map/ppermute | solution.py:285
  74.4 0.7 multiply_bitcast_fusion.1
  75.1 1.6 %collective-permute-done.17 = bf16[1,216,256]{2,1,0:T(8,128)(2,1)S(1)} collective-permute-done((bf16[1,216,256]{2,1,0:T(8,128)(2,1)S(1)}, bf16[1,216,256]{2,1,0:T(8,128)(2,1)S(1)}, u32[]{:S(2)}, u32[]{:S(2)}) %collective-permute-start.17) | collective-permute-done | bytes 110624 | tf_op jit(solution)/shard_map/ppermute | solution.py:285
  76.8 0.8 %copy.13 = f32[27,2,8,128]{3,1,2,0:T(2,128)} copy(f32[27,2,8,128]{3,2,1,0:T(8,128)S(1)} %multiply_bitcast_fusion) | data formatting | bytes 442368
  (11 shorter events, 0.2 us)
Async XLA Ops:
  0.6 7.4 %collective-permute-start = (bf16[128,512]{1,0:T(8,128)(2,1)}, bf16[128,512]{1,0:T(8,128)(2,1)S(1)}, u32[]{:S(2)}, u32[]{:S(2)}) collective-permute-start(bf16[128,512]{1,0:T(8,128)(2,1)} %cur_in.1), channel_id=1, source_target_pairs={{0,1},{1,2},{2,3},{3,4},{4,5},{5,6},{6,7},{7,8},{8,9},{9,10},{10,1... | collective-permute-start | bytes 393224 | tf_op jit(solution)/shard_map/ppermute | solution.py:285
  3.7 1.6 %copy-start.1 = (bf16[2048,512]{1,0:T(8,128)(2,1)S(1)}, bf16[2048,512]{1,0:T(8,128)(2,1)}, u32[]{:S(2)}) copy-start(bf16[2048,512]{1,0:T(8,128)(2,1)} %w_in.1) | copy-start | bytes 6291460
  5.3 0.9 %copy-start.4 = (bf16[512,256]{1,0:T(8,128)(2,1)S(1)}, bf16[512,256]{1,0:T(8,128)(2,1)}, u32[]{:S(2)}) copy-start(bf16[512,256]{1,0:T(8,128)(2,1)} %pre.1) | copy-start | bytes 786436
  6.3 0.9 %copy-start.5 = (bf16[128,512]{1,0:T(8,128)(2,1)S(1)}, bf16[128,512]{1,0:T(8,128)(2,1)}, u32[]{:S(2)}) copy-start(bf16[128,512]{1,0:T(8,128)(2,1)} %cur_in.1) | copy-start | bytes 393220
  8.1 8.4 %copy-start = (bf16[6912,256]{1,0:T(8,128)(2,1)S(1)}, bf16[6912,256]{1,0:T(8,128)(2,1)}, u32[]{:S(2)}) copy-start(bf16[6912,256]{1,0:T(8,128)(2,1)} %refs_7_.3) | copy-start | bytes 10616836
  8.1 8.4 %copy-start.2 = (bf16[512,256]{1,0:T(8,128)(2,1)S(1)}, bf16[512,256]{1,0:T(8,128)(2,1)}, u32[]{:S(2)}) copy-start(bf16[512,256]{1,0:T(8,128)(2,1)} %refs_9_.1) | copy-start | bytes 786436
  8.1 8.4 %copy-start.3 = (s32[1,27,8,128]{3,2,1,0:T(8,128)S(1)}, s32[1,27,8,128]{3,2,1,0:T(8,128)}, u32[]{:S(2)}) copy-start(s32[1,27,8,128]{3,2,1,0:T(8,128)} %param.17) | copy-start | bytes 331780
  10.4 8.9 %collective-permute-start.3 = (bf16[16,64,512]{2,1,0:T(8,128)(2,1)S(1)}, bf16[16,64,512]{2,1,0:T(8,128)(2,1)S(1)}, u32[]{:S(2)}, u32[]{:S(2)}) collective-permute-start(bf16[16,64,512]{2,1,0:T(8,128)(2,1)S(1)} %get-tuple-element.70), channel_id=1, source_target_pairs={{0,1},{1,0},{2,3},{3,2},{4,5},{5,4},{6,7},{7,6},{8,9},{9,8},{10,11... | collective-permute-start | bytes 3145736 | tf_op jit(solution)/shard_map/ppermute | solution.py:285
  13.1 3.8 %collective-permute-start.1 = (bf16[256,256]{1,0:T(8,128)(2,1)S(1)}, bf16[256,256]{1,0:T(8,128)(2,1)S(1)}, u32[]{:S(2)}, u32[]{:S(2)}) collective-permute-start(bf16[256,256]{1,0:T(8,128)(2,1)S(1)} %get-tuple-element.65.refs_5_), channel_id=1, source_target_pairs={{0,1},{1,2},{2,3},{3,4},{4,5},{5,6},{6,7},{7,8},{8,9},{9,10},{10,1... | collective-permute-start | bytes 393224 | tf_op jit(solution)/shard_map/ppermute | solution.py:285
  15.0 4.3 %collective-permute-start.2 = (bf16[256,256]{1,0:T(8,128)(2,1)S(1)}, bf16[256,256]{1,0:T(8,128)(2,1)S(1)}, u32[]{:S(2)}, u32[]{:S(2)}) collective-permute-start(bf16[256,256]{1,0:T(8,128)(2,1)S(1)} %get-tuple-element.66.refs_4_), channel_id=1, source_target_pairs={{1,0},{2,1},{3,2},{4,3},{5,4},{6,5},{7,6},{8,7},{9,8},{10,9},{11,1... | collective-permute-start | bytes 393224 | tf_op jit(solution)/shard_map/ppermute | solution.py:285
  16.8 6.2 %copy-start.6 = (s32[1,27,8]{1,2,0:T(8,128)S(1)}, s32[1,27,8]{1,2,0:T(8,128)}, u32[]{:S(2)}) copy-start(s32[1,27,8]{1,2,0:T(8,128)} %param.15) | copy-start | bytes 2596
  16.8 6.2 %copy-start.7 = (s32[1,27,8]{1,2,0:T(8,128)S(1)}, s32[1,27,8]{1,2,0:T(8,128)}, u32[]{:S(2)}) copy-start(s32[1,27,8]{1,2,0:T(8,128)} %param.16) | copy-start | bytes 2596
  19.6 12.4 %collective-permute-start.4 = (bf16[8,64,512]{2,1,0:T(8,128)(2,1)S(1)}, bf16[8,64,512]{2,1,0:T(8,128)(2,1)S(1)}, u32[]{:S(2)}, u32[]{:S(2)}) collective-permute-start(bf16[8,64,512]{2,1,0:T(8,128)(2,1)S(1)} %get-tuple-element.117), channel_id=1, source_target_pairs={{0,2},{1,5},{2,0},{3,7},{4,6},{5,1},{6,4},{7,3},{8,10},{9,13},{10,... | collective-permute-start | bytes 1572872 | tf_op jit(solution)/shard_map/ppermute | solution.py:285
  30.5 3.6 %collective-permute-start.5 = (bf16[8,216,256]{2,1,0:T(8,128)(2,1)S(1)}, bf16[8,216,256]{2,1,0:T(8,128)(2,1)S(1)}, u32[]{:S(2)}, u32[]{:S(2)}) collective-permute-start(bf16[8,216,256]{2,1,0:T(8,128)(2,1)S(1)} %get-tuple-element.80), channel_id=1, source_target_pairs={{0,1},{1,0},{2,3},{3,2},{4,5},{5,4},{6,7},{7,6},{8,9},{9,8},{10,11... | collective-permute-start | bytes 2654216 | tf_op jit(solution)/shard_map/ppermute | solution.py:285
  34.3 13.0 %collective-permute-start.6 = (bf16[4,216,256]{2,1,0:T(8,128)(2,1)S(1)}, bf16[4,216,256]{2,1,0:T(8,128)(2,1)S(1)}, u32[]{:S(2)}, u32[]{:S(2)}) collective-permute-start(bf16[4,216,256]{2,1,0:T(8,128)(2,1)S(1)} %get-tuple-element.88), channel_id=1, source_target_pairs={{0,2},{1,5},{2,0},{3,7},{4,6},{5,1},{6,4},{7,3},{8,10},{9,13},{10,... | collective-permute-start | bytes 1327112 | tf_op jit(solution)/shard_map/ppermute | solution.py:285
  37.6 9.6 %collective-permute-start.7 = (bf16[4,64,512]{2,1,0:T(8,128)(2,1)S(1)}, bf16[4,64,512]{2,1,0:T(8,128)(2,1)S(1)}, u32[]{:S(2)}, u32[]{:S(2)}) collective-permute-start(bf16[4,64,512]{2,1,0:T(8,128)(2,1)S(1)} %get-tuple-element.90), channel_id=1, source_target_pairs={{0,4},{1,3},{2,6},{3,1},{4,0},{5,7},{6,2},{7,5},{8,12},{9,11},{10,... | collective-permute-start | bytes 786440 | tf_op jit(solution)/shard_map/ppermute | solution.py:285
  47.2 2.4 %collective-permute-start.8 = (bf16[8,216,256]{2,1,0:T(8,128)(2,1)S(1)}, bf16[8,216,256]{2,1,0:T(8,128)(2,1)S(1)}, u32[]{:S(2)}, u32[]{:S(2)}) collective-permute-start(bf16[8,216,256]{2,1,0:T(8,128)(2,1)S(1)} %get-tuple-element.93), channel_id=1, source_target_pairs={{0,1},{1,0},{2,3},{3,2},{4,5},{5,4},{6,7},{7,6},{8,9},{9,8},{10,11... | collective-permute-start | bytes 2654216 | tf_op jit(solution)/shard_map/ppermute | solution.py:285
  47.3 6.6 %collective-permute-start.10 = (bf16[2,216,256]{2,1,0:T(8,128)(2,1)S(1)}, bf16[2,216,256]{2,1,0:T(8,128)(2,1)S(1)}, u32[]{:S(2)}, u32[]{:S(2)}) collective-permute-start(bf16[2,216,256]{2,1,0:T(8,128)(2,1)S(1)} %get-tuple-element.101), channel_id=1, source_target_pairs={{0,4},{1,3},{2,6},{3,1},{4,0},{5,7},{6,2},{7,5},{8,12},{9,11},{10,... | collective-permute-start | bytes 663560 | tf_op jit(solution)/shard_map/ppermute | solution.py:285
  49.9 8.4 %collective-permute-start.9 = (bf16[4,216,256]{2,1,0:T(8,128)(2,1)S(1)}, bf16[4,216,256]{2,1,0:T(8,128)(2,1)S(1)}, u32[]{:S(2)}, u32[]{:S(2)}) collective-permute-start(bf16[4,216,256]{2,1,0:T(8,128)(2,1)S(1)} %get-tuple-element.119), channel_id=1, source_target_pairs={{0,2},{1,5},{2,0},{3,7},{4,6},{5,1},{6,4},{7,3},{8,10},{9,13},{10,... | collective-permute-start | bytes 1327112 | tf_op jit(solution)/shard_map/ppermute | solution.py:285
  50.0 6.0 %collective-permute-start.11 = (bf16[2,64,512]{2,1,0:T(8,128)(2,1)S(1)}, bf16[2,64,512]{2,1,0:T(8,128)(2,1)S(1)}, u32[]{:S(2)}, u32[]{:S(2)}) collective-permute-start(bf16[2,64,512]{2,1,0:T(8,128)(2,1)S(1)} %get-tuple-element.123), channel_id=1, source_target_pairs={{0,8},{1,9},{2,10},{3,11},{4,12},{5,13},{6,14},{7,15},{8,0},{9,1},... | collective-permute-start | bytes 393224 | tf_op jit(solution)/shard_map/ppermute | solution.py:285
  54.0 8.7 %collective-permute-start.13 = (bf16[1,216,256]{2,1,0:T(8,128)(2,1)S(1)}, bf16[1,216,256]{2,1,0:T(8,128)(2,1)S(1)}, u32[]{:S(2)}, u32[]{:S(2)}) collective-permute-start(bf16[1,216,256]{2,1,0:T(8,128)(2,1)S(1)} %get-tuple-element.125), channel_id=1, source_target_pairs={{0,8},{1,9},{2,10},{3,11},{4,12},{5,13},{6,14},{7,15},{8,0},{9,1},... | collective-permute-start | bytes 331784 | tf_op jit(solution)/shard_map/ppermute | solution.py:285
  58.3 6.6 %collective-permute-start.14 = (bf16[1,64,512]{2,1,0:T(8,128)(2,1)S(1)}, bf16[1,64,512]{2,1,0:T(8,128)(2,1)S(1)}, u32[]{:S(2)}, u32[]{:S(2)}) collective-permute-start(bf16[1,64,512]{2,1,0:T(8,128)(2,1)S(1)} %add_convert_fusion.6), channel_id=1, source_target_pairs={{0,16},{1,17},{2,18},{3,19},{4,20},{5,21},{6,22},{7,23},{8,24},{9,... | collective-permute-start | bytes 196616 | tf_op jit(solution)/shard_map/ppermute | solution.py:285
  61.0 5.9 %collective-permute-start.12 = (bf16[2,216,256]{2,1,0:T(8,128)(2,1)S(1)}, bf16[2,216,256]{2,1,0:T(8,128)(2,1)S(1)}, u32[]{:S(2)}, u32[]{:S(2)}) collective-permute-start(bf16[2,216,256]{2,1,0:T(8,128)(2,1)S(1)} %get-tuple-element.106), channel_id=1, source_target_pairs={{0,4},{1,3},{2,6},{3,1},{4,0},{5,7},{6,2},{7,5},{8,12},{9,11},{10,... | collective-permute-start | bytes 663560 | tf_op jit(solution)/shard_map/ppermute | solution.py:285
  62.7 7.6 %collective-permute-start.16 = (bf16[1,216,256]{2,1,0:T(8,128)(2,1)S(1)}, bf16[1,216,256]{2,1,0:T(8,128)(2,1)S(1)}, u32[]{:S(2)}, u32[]{:S(2)}) collective-permute-start(bf16[1,216,256]{2,1,0:T(8,128)(2,1)S(1)} %get-tuple-element.115), channel_id=1, source_target_pairs={{8,24},{9,25},{10,26},{11,27},{12,28},{13,29},{14,30},{15,31},{16,... | collective-permute-start | bytes 331784 | tf_op jit(solution)/shard_map/ppermute | solution.py:285
  67.0 5.0 %collective-permute-start.15 = (bf16[1,216,256]{2,1,0:T(8,128)(2,1)S(1)}, bf16[1,216,256]{2,1,0:T(8,128)(2,1)S(1)}, u32[]{:S(2)}, u32[]{:S(2)}) collective-permute-start(bf16[1,216,256]{2,1,0:T(8,128)(2,1)S(1)} %add_convert_fusion.4), channel_id=1, source_target_pairs={{0,8},{1,9},{2,10},{3,11},{4,12},{5,13},{6,14},{7,15},{8,0},{9,1},... | collective-permute-start | bytes 331784 | tf_op jit(solution)/shard_map/ppermute | solution.py:285
  72.1 4.7 %collective-permute-start.17 = (bf16[1,216,256]{2,1,0:T(8,128)(2,1)S(1)}, bf16[1,216,256]{2,1,0:T(8,128)(2,1)S(1)}, u32[]{:S(2)}, u32[]{:S(2)}) collective-permute-start(bf16[1,216,256]{2,1,0:T(8,128)(2,1)S(1)} %convert_element_type.132), channel_id=1, source_target_pairs={{0,16},{1,17},{2,18},{3,19},{4,20},{5,21},{6,22},{7,23},{24,8},{25... | collective-permute-start | bytes 331784 | tf_op jit(solution)/shard_map/ppermute | solution.py:285
